TPU v7x, 32 devices: a whole 2x2x4 slice. The times are simulated.
32 devices in a mesh: seq: 8 (over z, core), dp: 4 (over y, x).
Axes of the slice: x: 2, y: 2, z: 4, core: 2. Of those that a mesh axis runs over, the one named last changes fastest.
Arguments:
- tokens: bfloat16 [8, 512, 2048], P('dp', 'seq'), may hold values from -6 to 6
- segments: int32 [8, 512], P('dp'), may hold values from 0 to 7, as said below
- cotangent: bfloat16 [8, 512, 2048], P('dp', 'seq'), may hold values from -6 to 6
- attention_weight: float32 [2048, 4, 2048], P(('seq', 'dp'))
- attention_first: float32 [2048, 4, 2048], P(('seq', 'dp'))
- attention_second: float32 [2048, 4, 2048], P(('seq', 'dp'))
- feed_weight: float32 [2048, 3, 5120], P(('seq', 'dp'))
- feed_first: float32 [2048, 3, 5120], P(('seq', 'dp'))
- feed_second: float32 [2048, 3, 5120], P(('seq', 'dp'))
- gains: float32 [2, 2048], replicated, may hold values from 0.5 to 1.5
- gains_first: float32 [2, 2048], replicated, may hold values from -64 to 64
- gains_second: float32 [2, 2048], replicated, may hold values from 409.6 to 1638.4
- rel_table: float32 [32, 32], replicated, may hold values from -4 to 4
- table_first: float32 [32, 32], replicated, may hold values from -128 to 128
- table_second: float32 [32, 32], replicated, may hold values from 2048 to 8192
Outputs:
- block_out: bfloat16 [8, 512, 2048], P('dp', 'seq')
- grad_tokens: bfloat16 [8, 512, 2048], P('dp', 'seq')
- new_attention_weight: float32 [2048, 4, 2048], P(('seq', 'dp'))
- new_attention_first: float32 [2048, 4, 2048], P(('seq', 'dp'))
- new_attention_second: float32 [2048, 3, 2048], P(('seq', 'dp'))
- new_output_second: float32 [2048, 2048], P(('seq', 'dp'))
- new_feed_weight: float32 [2048, 3, 5120], P(('seq', 'dp'))
- new_feed_first: float32 [2048, 3, 5120], P(('seq', 'dp'))
- new_feed_second: float32 [2048, 3, 5120], P(('seq', 'dp'))
- new_gains: float32 [2, 2048], replicated
- new_gains_first: float32 [2, 2048], replicated
- new_gains_second: float32 [2, 2048], replicated
- new_table: float32 [32, 32], replicated
- new_table_first: float32 [32, 32], replicated
- new_table_second: float32 [32, 32], replicated
Inputs may be any that keep to these rules, and one draw needn't show every extreme that they name: `segments`: along each row the numbers start at 0 and never fall, rising by at most one from a position to the next; tokens attend only within equal numbers. Of the 2 rows of each dp index, one holds a single document over all its positions, and every other row holds exactly 8 documents.
All inputs are finite; a program needn't handle non-finite values.
Results may differ from a plain program's by a relative error of at most 0.015.
The roundings to bfloat16 on the way count: a program that leaves them out, or rounds other values in their place, can miss the bound.
Values may be sent and summed in bfloat16 or wider, within the bound.
No kernel may reach another device: no remote copies, remote signals or barrier semaphores. Data moves between devices by JAX's collectives and lax.ppermute only.
A program may use at most 616 MiB of HBM per device.

v0:
```python
import jax
import jax.numpy as jnp
from jax import lax
from jax.sharding import PartitionSpec as P

D = 2048
HEADS = 32
HEAD_DIM = 64
FF = 5120
NUM_BUCKETS = 32
MAX_DIST = 128
STEP = 10


NORM_EPSILON = 1e-06
NEG_BIG = -1000000000.0
BETA_ONE = 0.9
BETA_TWO = 0.95
EPS_ADAM = 1e-08
DECAY = 0.1
HIGHEST = lax.Precision.HIGHEST


def rms_norm(values, gain_vec):
    inv_root = lax.rsqrt(jnp.mean(values * values, axis=-1, keepdims=True) + NORM_EPSILON)
    return values * inv_root * gain_vec


def gelu_tanh(values):
    return jax.nn.gelu(values, approximate=True)


def bucket_edges():
    half_count = NUM_BUCKETS // 2
    exact_count = half_count // 2
    log_count = half_count - exact_count
    far_ratio = MAX_DIST // exact_count
    edge_list = []
    for step_index in range(1, log_count):
        edge_at = exact_count
        while edge_at**log_count < exact_count**log_count * far_ratio**step_index:
            edge_at = edge_at + 1
        edge_list.append(edge_at)
    return edge_list


def rel_bucket(relative):
    half_count = NUM_BUCKETS // 2
    exact_count = half_count // 2
    distance = jnp.abs(relative)
    far_bucket = jnp.full(relative.shape, exact_count, jnp.int32)
    for edge_at in bucket_edges():
        far_bucket = far_bucket + (distance >= edge_at).astype(jnp.int32)
    near_far = jnp.where(distance < exact_count, distance, far_bucket)
    return near_far + jnp.where(relative > 0, half_count, 0)


def contract_last(left, right):
    return lax.dot_general(
        left, right, (((1,), (1,)), ((), ())), preferred_element_type=jnp.float32
    )


def outer_sum(left, right):
    return lax.dot_general(
        left, right, (((0,), (0,)), ((), ())), preferred_element_type=jnp.float32
    )


def group_heads(matrix, group_count):
    rows_here = matrix.shape[0]
    return matrix.reshape(rows_here, group_count, matrix.shape[1] // group_count).transpose(1, 0, 2)


def ungroup_heads(grouped):
    return grouped.transpose(1, 0, 2).reshape(grouped.shape[1], grouped.shape[0] * grouped.shape[2])


def group_scores(query_g, key_g, bias_g, same_doc):
    group_size = bias_g.shape[0]
    query_h = query_g.reshape(query_g.shape[0], group_size, HEAD_DIM)
    key_h = key_g.reshape(key_g.shape[0], group_size, HEAD_DIM)
    dots = jnp.einsum("qhd,khd->hqk", query_h, key_h, preferred_element_type=jnp.float32)
    return jnp.where(same_doc[None], dots + bias_g, NEG_BIG)


def adam_update(weight, first, second, grads, rate, decay):
    first_new = BETA_ONE * first + (1.0 - BETA_ONE) * grads
    second_new = BETA_TWO * second + (1.0 - BETA_TWO) * grads * grads
    first_hat = first_new / (1.0 - BETA_ONE**STEP)
    second_hat = second_new / (1.0 - BETA_TWO**STEP)
    weight_new = weight - rate * (first_hat / (jnp.sqrt(second_hat) + EPS_ADAM) + decay * weight)
    return (weight_new, first_new, second_new)


def attention_rates():
    return 3.0 * jnp.array(
        [D ** (-0.5), (32 * D) ** (-0.5), D ** (-0.5), (HEADS * HEAD_DIM // 64) ** (-0.5)],
        jnp.float32,
    ).reshape(1, 4, 1)


def feed_rates():
    return 3.0 * jnp.array([D ** (-0.5), D ** (-0.5), FF ** (-0.5)], jnp.float32).reshape(1, 3, 1)


def attention_maker(product_factors):
    normed_one, grad_queries, grad_keys, grad_values, grad_branch, attended = product_factors[:6]
    pieces = [
        outer_sum(normed_one, grad_queries),
        outer_sum(normed_one, grad_keys),
        outer_sum(normed_one, grad_values),
        outer_sum(grad_branch, attended),
    ]
    return jnp.stack(pieces, 1)


def feed_maker(product_factors):
    normed_two, grad_gate, grad_up, grad_out, inner = product_factors[6:]
    pieces = [
        outer_sum(normed_two, grad_gate),
        outer_sum(normed_two, grad_up),
        outer_sum(grad_out, inner),
    ]
    return jnp.stack(pieces, 1)


def reduce_single(product_factors):
    attention_grad = lax.psum_scatter(
        attention_maker(product_factors), ("seq", "dp"), scatter_dimension=0, tiled=True
    )
    feed_grad = lax.psum_scatter(
        feed_maker(product_factors), ("seq", "dp"), scatter_dimension=0, tiled=True
    )
    return (attention_grad, feed_grad)


def local(
    tokens,
    segments,
    cotangent,
    attention_weight,
    attention_first,
    attention_second,
    feed_weight,
    feed_first,
    feed_second,
    gains,
    gains_first,
    gains_second,
    rel_table,
    table_first,
    table_second,
):
    micro_count, local_rows, width = tokens.shape
    seq_len = local_rows * lax.axis_size("seq")
    offset = lax.axis_index("seq") * local_rows
    group_size = min(8, HEADS)
    group_count = HEADS // group_size
    query_location = offset + jnp.arange(local_rows, dtype=jnp.int32)
    key_pos = jnp.arange(seq_len, dtype=jnp.int32)
    buckets = rel_bucket(key_pos[None, :] - query_location[:, None])
    bucket_match = buckets[None, :, :] == jnp.arange(NUM_BUCKETS, dtype=jnp.int32)[:, None, None]
    indicator_matrix = bucket_match.astype(jnp.bfloat16)
    onehot_exact = bucket_match.astype(jnp.float32)
    bias_all = jnp.einsum(
        "atj,ao->otj",
        onehot_exact,
        rel_table,
        precision=HIGHEST,
        preferred_element_type=jnp.float32,
    )
    bias_groups = bias_all.reshape(group_count, group_size, local_rows, seq_len)
    results = []
    for index in range(micro_count):
        attention_full = lax.all_gather(
            attention_weight.astype(jnp.bfloat16), ("seq", "dp"), axis=0, tiled=True
        )
        feed_full = lax.all_gather(
            feed_weight.astype(jnp.bfloat16), ("seq", "dp"), axis=0, tiled=True
        )
        inputs = tokens[index].astype(jnp.float32)
        seg_row = segments[index]
        seg_query = lax.dynamic_slice_in_dim(seg_row, offset, local_rows, 0)
        same_doc = seg_query[:, None] == seg_row[None, :]
        normed_one = rms_norm(inputs, gains[0]).astype(jnp.bfloat16)
        queries = jnp.dot(
            normed_one, attention_full[:, 0, :], preferred_element_type=jnp.float32
        ).astype(jnp.bfloat16)
        keys_local = jnp.dot(
            normed_one, attention_full[:, 1, :], preferred_element_type=jnp.float32
        ).astype(jnp.bfloat16)
        values_local = jnp.dot(
            normed_one, attention_full[:, 2, :], preferred_element_type=jnp.float32
        ).astype(jnp.bfloat16)
        keys_all = lax.all_gather(keys_local, "seq", axis=0, tiled=True)
        values_all = lax.all_gather(values_local, "seq", axis=0, tiled=True)
        query_groups = group_heads(queries, group_count)
        key_groups = group_heads(keys_all, group_count)
        value_groups = group_heads(values_all, group_count)

        def forward_group(product_factors):
            query_g, key_g, value_g, bias_g = product_factors
            scores = group_scores(query_g, key_g, bias_g, same_doc)
            row_max = jnp.max(scores, axis=-1, keepdims=True)
            exp_scores = jnp.exp(scores - row_max)
            totals = jnp.sum(exp_scores, axis=-1, keepdims=True)
            probs_low = (exp_scores / totals).astype(jnp.bfloat16)
            value_h = value_g.reshape(value_g.shape[0], group_size, HEAD_DIM)
            attended_g = jnp.einsum(
                "hqk,khd->qhd", probs_low, value_h, preferred_element_type=jnp.float32
            )
            return (
                attended_g.reshape(local_rows, group_size * HEAD_DIM),
                (row_max + jnp.log(totals))[..., 0],
            )

        attended_groups, log_totals = lax.map(
            forward_group, (query_groups, key_groups, value_groups, bias_groups)
        )
        attended = ungroup_heads(attended_groups).astype(jnp.bfloat16)
        attention_out = contract_last(attended, attention_full[:, 3, :])
        hidden_state = inputs + attention_out
        normed_two = rms_norm(hidden_state, gains[1]).astype(jnp.bfloat16)
        gate_pre = jnp.dot(normed_two, feed_full[:, 0, :], preferred_element_type=jnp.float32)
        up_pre = jnp.dot(normed_two, feed_full[:, 1, :], preferred_element_type=jnp.float32)
        gate_act, gate_back = jax.vjp(gelu_tanh, gate_pre)
        inner = (gate_act * up_pre).astype(jnp.bfloat16)
        feed_out = contract_last(inner, feed_full[:, 2, :])
        block_rows = (hidden_state + feed_out).astype(jnp.bfloat16)
        grad_out = cotangent[index]
        grad_inner = jnp.dot(grad_out, feed_full[:, 2, :], preferred_element_type=jnp.float32)
        grad_gate = gate_back(grad_inner * up_pre)[0].astype(jnp.bfloat16)
        grad_up = (grad_inner * gate_act).astype(jnp.bfloat16)
        grad_normed_two = contract_last(grad_gate, feed_full[:, 0, :]) + contract_last(
            grad_up, feed_full[:, 1, :]
        )
        unused_two, norm_back_two = jax.vjp(rms_norm, hidden_state, gains[1])
        grad_hidden_norm, grad_gain_two = norm_back_two(grad_normed_two)
        grad_hidden = grad_out.astype(jnp.float32) + grad_hidden_norm
        grad_branch = grad_hidden.astype(jnp.bfloat16)
        grad_attended = jnp.dot(
            grad_branch, attention_full[:, 3, :], preferred_element_type=jnp.float32
        ).astype(jnp.bfloat16)
        grad_attended_groups = group_heads(grad_attended, group_count)

        def backward_group(product_factors):
            query_g, key_g, value_g, bias_g, grad_att_g, log_total = product_factors
            scores = group_scores(query_g, key_g, bias_g, same_doc)
            probs = jnp.exp(scores - log_total[:, :, None])
            query_h = query_g.reshape(local_rows, group_size, HEAD_DIM)
            key_h = key_g.reshape(key_g.shape[0], group_size, HEAD_DIM)
            value_h = value_g.reshape(value_g.shape[0], group_size, HEAD_DIM)
            grad_att_h = grad_att_g.reshape(local_rows, group_size, HEAD_DIM)
            grad_probs = jnp.einsum(
                "qhd,khd->hqk", grad_att_h, value_h, preferred_element_type=jnp.float32
            )
            row_dot = jnp.sum(probs * grad_probs, axis=-1, keepdims=True)
            score_gradients = (probs * (grad_probs - row_dot)).astype(jnp.bfloat16)
            grad_query = jnp.einsum(
                "hqk,khd->qhd", score_gradients, key_h, preferred_element_type=jnp.float32
            )
            grad_key = jnp.einsum(
                "hqk,qhd->khd", score_gradients, query_h, preferred_element_type=jnp.float32
            )
            grad_value = jnp.einsum(
                "hqk,qhd->khd",
                probs.astype(jnp.bfloat16),
                grad_att_h,
                preferred_element_type=jnp.float32,
            )
            grad_table_g = jnp.einsum(
                "icr,zcr->zi", score_gradients, indicator_matrix, preferred_element_type=jnp.float32
            )
            return (
                grad_query.reshape(local_rows, group_size * HEAD_DIM),
                grad_key.reshape(key_g.shape[0], group_size * HEAD_DIM),
                grad_value.reshape(key_g.shape[0], group_size * HEAD_DIM),
                grad_table_g,
            )

        query_grad_groups, grouped_key_gradients, value_grad_groups, table_grad_groups = lax.map(
            backward_group,
            (query_groups, key_groups, value_groups, bias_groups, grad_attended_groups, log_totals),
        )
        grad_queries = ungroup_heads(query_grad_groups).astype(jnp.bfloat16)
        key_sums = lax.psum_scatter(
            ungroup_heads(grouped_key_gradients).astype(jnp.bfloat16),
            "seq",
            scatter_dimension=0,
            tiled=True,
        )
        value_sums = lax.psum_scatter(
            ungroup_heads(value_grad_groups).astype(jnp.bfloat16),
            "seq",
            scatter_dimension=0,
            tiled=True,
        )
        grad_table = table_grad_groups.transpose(1, 0, 2).reshape(NUM_BUCKETS, HEADS)
        grad_normed_one = (
            contract_last(grad_queries, attention_full[:, 0, :])
            + contract_last(key_sums, attention_full[:, 1, :])
            + contract_last(value_sums, attention_full[:, 2, :])
        )
        unused_one, norm_back_one = jax.vjp(rms_norm, inputs, gains[0])
        grad_input_norm, grad_gain_one = norm_back_one(grad_normed_one)
        grad_rows = (grad_hidden + grad_input_norm).astype(jnp.bfloat16)
        product_factors = (
            normed_one,
            grad_queries,
            key_sums,
            value_sums,
            grad_branch,
            attended,
            normed_two,
            grad_gate,
            grad_up,
            grad_out,
            inner,
        )
        gain_grad = jnp.stack([grad_gain_one, grad_gain_two], 0)
        results.append((block_rows, grad_rows, product_factors, gain_grad, grad_table))
    attention_total, feed_total = reduce_single(results[0][2])
    for result_item in results[1:]:
        attention_more, feed_more = reduce_single(result_item[2])
        attention_total = attention_total + attention_more
        feed_total = feed_total + feed_more
    block_out = jnp.stack([result_item[0] for result_item in results], 0)
    grad_tokens = jnp.stack([result_item[1] for result_item in results], 0)
    gains_local = results[0][3]
    table_local = results[0][4]
    for result_item in results[1:]:
        gains_local = gains_local + result_item[3]
        table_local = table_local + result_item[4]
    gains_total, table_total = lax.psum((gains_local, table_local), ("seq", "dp"))
    new_attention = adam_update(
        attention_weight,
        attention_first,
        attention_second,
        attention_total,
        attention_rates(),
        DECAY,
    )
    new_feed = adam_update(feed_weight, feed_first, feed_second, feed_total, feed_rates(), DECAY)
    new_gains = adam_update(gains, gains_first, gains_second, gains_total, 0.6, 0.0)
    new_table = adam_update(rel_table, table_first, table_second, table_total, 1.5, 0.0)
    return (
        block_out,
        grad_tokens,
        new_attention[0],
        new_attention[1],
        new_attention[2][:, :3, :],
        new_attention[2][:, 3, :],
        new_feed[0],
        new_feed[1],
        new_feed[2],
        new_gains[0],
        new_gains[1],
        new_gains[2],
        new_table[0],
        new_table[1],
        new_table[2],
    )


def solution(mesh):
    in_specs = (
        P("dp", "seq", None),
        P("dp", None),
        P("dp", "seq", None),
        P(("seq", "dp"), None, None),
        P(("seq", "dp"), None, None),
        P(("seq", "dp"), None, None),
        P(("seq", "dp"), None, None),
        P(("seq", "dp"), None, None),
        P(("seq", "dp"), None, None),
        P(),
        P(),
        P(),
        P(),
        P(),
        P(),
    )
    out_specs = (
        P("dp", "seq", None),
        P("dp", "seq", None),
        P(("seq", "dp"), None, None),
        P(("seq", "dp"), None, None),
        P(("seq", "dp"), None, None),
        P(("seq", "dp"), None),
        P(("seq", "dp"), None, None),
        P(("seq", "dp"), None, None),
        P(("seq", "dp"), None, None),
        P(),
        P(),
        P(),
        P(),
        P(),
        P(),
    )
    return jax.shard_map(local, mesh=mesh, in_specs=in_specs, out_specs=out_specs, check_vma=False)
```

profile of v0, /device:TPU:0, one launch (start us, length us, event | category | flops | bytes accessed | tf_op | source)
XLA Modules:
  0.0 5094.5 jit_solution(3984601501299807852)
XLA Ops:
  11.4 197.5 %all-gather.7.cloned.1.call-done = bf16[2048,4,2048]{2,0,1:T(8,128)(2,1)} async-done(((bf16[64,4,2048]{2,0,1:T(8,128)(2,1)}), bf16[2048,4,2048]{2,0,1:T(8,128)(2,1)}) %all-gather.7.cloned.1.call-update) | async-done | bytes 33554448 | tf_op jit(solution)/shard_map/all_gather | solution.py:176
  208.9 5.7 fusion.101
  214.7 5.7 fusion.97
  220.5 5.8 fusion.100
  226.4 5.8 fusion.96
  239.0 4.4 copy.118
  243.5 5.0 fusion.99
  249.3 5.3 fusion.98
  258.5 14.4 all-gather.17.cloned.1.call-done
  272.9 3.9 copy.149
  276.8 26.7 all-gather.9.cloned.1.call-done
  303.5 3.9 copy.145
  307.5 26.7 all-gather.11.cloned.1.call-done
  339.0 29.3 while.60
  368.3 7.2 multiply_reduce_fusion.7
  376.4 28.5 while.61
  405.0 7.9 multiply_reduce_fusion.6
  413.1 260.0 %all-gather.13.cloned.1.call-done = bf16[2048,3,5120]{2,0,1:T(8,128)(2,1)} async-done(((bf16[64,3,5120]{2,0,1:T(8,128)(2,1)}), bf16[2048,3,5120]{2,0,1:T(8,128)(2,1)}) %all-gather.13.cloned.1.call-update) | async-done | bytes 62914576 | tf_op jit(solution)/shard_map/all_gather | solution.py:179
  673.1 8.9 fusion.55
  682.0 8.9 fusion.59
  690.9 9.9 multiply_convert_fusion.3
  700.8 11.4 fusion.53
  712.2 11.3 multiply_reduce_fusion.3
  723.6 9.0 fusion.54
  732.6 8.9 fusion.58
  741.4 9.9 multiply_convert_fusion.2
  751.3 11.1 fusion.52
  762.4 11.7 multiply_reduce_fusion.2
  774.5 5.3 fusion.94
  783.8 38.5 while.62
  822.3 4.0 copy.152
  826.4 5.1 fusion.95
  838.4 40.9 while.63
  879.3 4.1 copy.156
  886.1 9.3 convolution_bitcast_fusion.13
  895.4 9.3 convolution_bitcast_fusion.9
  904.7 8.2 convolution_bitcast_fusion.10
  912.9 8.2 convolution_bitcast_fusion.6
  921.1 9.3 convolution_bitcast_fusion.11
  930.6 9.3 convolution_bitcast_fusion.12
  939.9 9.2 convolution_bitcast_fusion.7
  949.0 23.5 reduce-scatter.23.cloned.1.call-done
  972.5 9.1 convolution_bitcast_fusion.8
  981.7 64.0 %maximum_add_fusion.1 = f32[2048,4,2048]{2,0,1:T(8,128)} fusion(f32[2048,1,2048]{2,0,1:T(8,128)} %convolution_bitcast_fusion.10, f32[2048,1,2048]{2,0,1:T(8,128)} %convolution_bitcast_fusion.11, f32[2048,1,2048]{2,0,1:T(8,128)} %convolution_bitcast_fusion.12, f32[2048,1,2048]{2,0,1:T(8,128)} %convolution_bitcast_fusion.13, ...), kind=kLoop, calls=%fused_computation.81 | loop fusion | flops 117440512 | bytes 201326592 | tf_op jit(solution)/shard_map/add | solution.py:326
  1046.9 16.9 convolution_bitcast_fusion.4
  1063.8 16.4 convolution_bitcast_fusion.5
  1080.2 16.4 convolution_bitcast_fusion.1
  1096.6 16.4 convolution_bitcast_fusion.2
  1113.0 16.5 convolution_bitcast_fusion.3
  1129.5 16.4 convolution_bitcast_fusion
  1145.9 120.3 %maximum_add_fusion = f32[2048,3,5120]{2,0,1:T(8,128)} fusion(f32[2048,1,5120]{2,0,1:T(8,128)} %convolution_bitcast_fusion.3, f32[2048,1,5120]{2,0,1:T(8,128)} %convolution_bitcast_fusion.4, f32[2048,1,5120]{2,0,1:T(8,128)} %convolution_bitcast_fusion.5, f32[2048,1,5120]{2,0,1:T(8,128)} %convolution_bitcast_fusion, ...), kind=kLoop, calls=%fused_computation.80 | loop fusion | flops 157286400 | bytes 377487360 | tf_op jit(solution)/shard_map/add | solution.py:327
  1267.9 10.6 fusion.103
  1278.6 10.8 fusion.102
  1290.3 6.3 fusion.68
  1296.6 6.1 fusion.69
  1302.7 6.1 fusion.64
  1308.8 6.2 fusion.65
  1315.1 6.2 fusion.87
  1322.1 7.1 fusion.137
  1329.4 42.7 all-reduce
  1377.5 1072.9 %reduce-scatter.15.cloned.1.call-done = f32[64,4,2048]{2,0,1:T(8,128)} async-done(((f32[2048,4,2048]{2,0,1:T(8,128)}), f32[64,4,2048]{2,0,1:T(8,128)}) %reduce-scatter.15.cloned.1.call-update) | async-done | bytes 2097168 | tf_op jit(solution)/shard_map/reduce_scatter | solution.py:129
  2450.4 7.3 multiply_subtract_fusion.1
  2465.2 2612.5 %reduce-scatter.17.cloned.1.call-done = f32[64,3,5120]{2,0,1:T(8,128)} async-done(((f32[2048,3,5120]{2,0,1:T(8,128)}), f32[64,3,5120]{2,0,1:T(8,128)}) %reduce-scatter.17.cloned.1.call-update) | async-done | bytes 3932176 | tf_op jit(solution)/shard_map/reduce_scatter | solution.py:132
  5077.7 9.5 multiply_subtract_fusion
  (454 shorter events, 189.4 us)
Async XLA Ops:
  7.2 201.7 %all-gather.7.cloned.1.call-start = ((), (), s32[]{:S(2)}) async-start(), calls=%async_computation.6 | async-start | bytes 34603008 | tf_op jit(solution)/shard_map/all_gather | solution.py:176
  11.0 244.4 %all-gather.15.cloned.1.call-start = ((), (), s32[]{:S(2)}) async-start(), calls=%async_computation.10 | async-start | bytes 2359296 | tf_op jit(solution)/shard_map/all_gather | solution.py:197
  11.3 203.3 %copy-start.77 = (f32[64]{0:T(128)}, f32[64]{0:T(128)S(1)}, u32[]{:S(2)}) copy-start(f32[64]{0:T(128)S(1)} %get-tuple-element.559) | copy-start | bytes 772
  11.3 209.2 %copy-start.75 = (f32[64]{0:T(128)}, f32[64]{0:T(128)S(1)}, u32[]{:S(2)}) copy-start(f32[64]{0:T(128)S(1)} %get-tuple-element.558) | copy-start | bytes 772
  11.3 232.2 %copy-start.62 = (f32[64]{0:T(128)}, f32[64]{0:T(128)S(1)}, u32[]{:S(2)}) copy-start(f32[64]{0:T(128)S(1)} %fusion.187) | copy-start | bytes 772
  11.3 238.0 %copy-start.23 = (f32[1,2048]{1,0:T(1,128)}, f32[1,2048]{1,0:T(1,128)S(1)}, u32[]{:S(2)}) copy-start(f32[1,2048]{1,0:T(1,128)S(1)} %get-tuple-element.693) | copy-start | bytes 24580
  214.6 58.3 %all-gather.17.cloned.1.call-start = ((), (), s32[]{:S(2)}) async-start(), calls=%async_computation.11 | async-start | bytes 2359296 | tf_op jit(solution)/shard_map/all_gather | solution.py:196
  220.4 83.1 %all-gather.9.cloned.1.call-start = ((), (), s32[]{:S(2)}) async-start(), calls=%async_computation.7 | async-start | bytes 2359296 | tf_op jit(solution)/shard_map/all_gather | solution.py:197
  220.5 28.8 copy-start.65
  226.3 107.9 %all-gather.11.cloned.1.call-start = ((), (), s32[]{:S(2)}) async-start(), calls=%async_computation.8 | async-start | bytes 2359296 | tf_op jit(solution)/shard_map/all_gather | solution.py:196
  232.2 440.9 %all-gather.13.cloned.1.call-start = ((), (), s32[]{:S(2)}) async-start(), calls=%async_computation.9 | async-start | bytes 64880640 | tf_op jit(solution)/shard_map/all_gather | solution.py:179
  236.0 685.1 %reduce-scatter.21.cloned.1.call-start = ((), (), s32[]{:S(2)}) async-start(), calls=%async_computation.15 | async-start | bytes 2359296
  368.3 7.2 copy-start.48
  368.3 7.2 copy-start.50
  368.3 7.2 copy-start.60
  404.9 7.9 copy-start
  404.9 7.9 copy-start.46
  405.0 7.9 copy-start.51
  405.0 7.9 copy-start.58
  405.0 7.9 copy-start.15
  413.0 268.9 %copy-start.11 = (bf16[64,2048]{1,0:T(8,128)(2,1)}, bf16[64,2048]{1,0:T(8,128)(2,1)S(1)}, u32[]{:S(2)}) copy-start(bf16[64,2048]{1,0:T(8,128)(2,1)S(1)} %multiply_convert_fusion.7) | copy-start | bytes 786436
  682.0 9.0 copy-start.13
  700.8 11.4 copy-start.29
  700.8 11.4 copy-start.31
  700.8 11.4 copy-start.16
  700.8 11.4 copy-start.37
  723.5 9.0 copy-start.21
  751.3 11.1 copy-start.33
  751.3 11.1 copy-start.35
  774.5 51.9 %copy-start.9 = (f32[64,2048]{1,0:T(8,128)}, f32[64,2048]{1,0:T(8,128)S(1)}, u32[]{:S(2)}) copy-start(f32[64,2048]{1,0:T(8,128)S(1)} %get-tuple-element.691) | copy-start | bytes 1572868
  774.5 130.2 %copy-start.7 = (f32[64,2048]{1,0:T(8,128)}, f32[64,2048]{1,0:T(8,128)S(1)}, u32[]{:S(2)}) copy-start(f32[64,2048]{1,0:T(8,128)S(1)} %get-tuple-element.690) | copy-start | bytes 1572868
  826.3 104.3 %reduce-scatter.19.cloned.1.call-start = ((), (), s32[]{:S(2)}) async-start(), calls=%async_computation.14 | async-start | bytes 2359296
  833.9 105.9 %reduce-scatter.25.cloned.1.call-start = ((), (), s32[]{:S(2)}) async-start(), calls=%async_computation.17 | async-start | bytes 2359296
  883.4 89.1 %reduce-scatter.23.cloned.1.call-start = ((), (), s32[]{:S(2)}) async-start(), calls=%async_computation.16 | async-start | bytes 2359296
  885.9 1564.5 %reduce-scatter.15.cloned.1.call-start = ((), (), s32[]{:S(2)}) async-start(), calls=%async_computation.12 | async-start | bytes 69206016 | tf_op jit(solution)/shard_map/reduce_scatter | solution.py:129
  886.1 9.3 copy-start.63
  895.4 9.3 copy-start.18
  904.7 8.2 copy-start.10
  904.7 8.2 copy-start.19
  1045.8 18.0 copy-start.30
  1045.8 4031.9 %reduce-scatter.17.cloned.1.call-start = ((), (), s32[]{:S(2)}) async-start(), calls=%async_computation.13 | async-start | bytes 129761280 | tf_op jit(solution)/shard_map/reduce_scatter | solution.py:132
  1063.8 16.4 copy-start.22
  1063.8 16.4 copy-start.36
  1080.2 16.4 copy-start.34
  1096.6 16.4 copy-start.14
  1096.6 16.4 copy-start.26
  1113.0 16.5 copy-start.28
  1267.9 10.7 copy-start.17
  1267.9 10.7 copy-start.27
  1315.0 7.0 copy-start.3
  1315.0 7.0 copy-start.25
  1315.0 7.0 copy-start.43
  1315.0 7.0 copy-start.64
  1322.1 7.3 copy-start.72
  1322.1 7.3 copy-start.73
  1322.1 52.1 %copy-start.76 = (f32[64]{0:T(128)S(1)}, f32[64]{0:T(128)}, u32[]{:S(2)}) copy-start(f32[64]{0:T(128)} %copy-done.75) | copy-start | bytes 772
  1322.1 52.1 %copy-start.78 = (f32[64]{0:T(128)S(1)}, f32[64]{0:T(128)}, u32[]{:S(2)}) copy-start(f32[64]{0:T(128)} %copy-done.77) | copy-start | bytes 772
  1322.1 52.1 %copy-start.8 = (f32[64,2048]{1,0:T(8,128)S(1)}, f32[64,2048]{1,0:T(8,128)}, u32[]{:S(2)}) copy-start(f32[64,2048]{1,0:T(8,128)} %copy-done.7) | copy-start | bytes 1572868
  1329.3 47.5 copy-start.55
  1329.3 47.5 copy-start.68
  1329.3 47.5 copy-start.69
  1329.3 1121.0 %copy-start.6 = (f32[64,4,2048]{2,1,0:T(4,128)S(1)}, f32[64,4,2048]{2,1,0:T(4,128)}, u32[]{:S(2)}) copy-start(f32[64,4,2048]{2,1,0:T(4,128)} %param.28) | copy-start | bytes 6291460
  1329.3 1121.0 %copy-start.80 = (f32[4]{0:T(128)S(1)}, f32[4]{0:T(128)}, u32[]{:S(2)}) copy-start(f32[4]{0:T(128)} %constant.204) | copy-start | bytes 52
  2460.4 2617.3 %copy-start.79 = (f32[3]{0:T(128)S(1)}, f32[3]{0:T(128)}, u32[]{:S(2)}) copy-start(f32[3]{0:T(128)} %constant.205) | copy-start | bytes 40
  (29 other events, 105.5 us)
Sparse Core Ops, SparseCore 0:
  11.5 197.3 all-gather.6
  214.8 27.2 all-gather.14
  244.2 28.6 all-gather.16
  274.9 28.5 all-gather.8
  305.6 28.5 all-gather.10
  337.5 335.5 all-gather.12
  826.4 34.0 reduce-scatter.20
  863.4 34.5 reduce-scatter.18
  900.8 34.3 reduce-scatter.24
  937.9 34.5 reduce-scatter.22
  1045.9 1404.4 reduce-scatter.14
  2452.6 2625.0 reduce-scatter.16
where the time goes:
time: 5100 us; the launch traced here: 5090 us
  waiting for transfers between devices  4230 us (83%)
  matrix products  448 us (9%)
  other arithmetic  216 us (4%)
  local copies, waits for them, and re-layouts  134 us (3%)
    reduce_scatter x1, waiting for transfers between devices, reduce_single(): lax.psum_scatter(feed_maker(product_factors), ('seq', 'dp'), scatter_dime...  2610 us
    reduce_scatter x1, waiting for transfers between devices, reduce_single(): lax.psum_scatter(attention_maker(product_factors), ('seq', 'dp'), scatter...  1070 us
    all_gather x1, waiting for transfers between devices, local(): lax.all_gather(feed_weight.astype(jnp.bfloat16), ('seq', 'dp'), axis=0, t...  260 us
    all_gather x1, waiting for transfers between devices, local(): lax.all_gather(attention_weight.astype(jnp.bfloat16), ('seq', 'dp'), axis...  198 us
    dot_general x14, matrix products, outer_sum(): lax.dot_general(left, right, (((0,), (0,)), ((), ())), preferred_element_...  171 us
    add x1, other arithmetic, local(): feed_total = feed_total + feed_more  120 us
    dot_general x14, matrix products, contract_last(): lax.dot_general(left, right, (((1,), (1,)), ((), ())), preferred_element_...  120 us
  transfers between devices with their start and end apart: 12, of which 9 were waited for; matrix products, arithmetic and copies ran while one was open for 11% of the time, Pallas kernels for 0%

commit v1 on v0

v1 whole, which is shorter than its diff:
```python
import jax
import jax.numpy as jnp
from jax import lax
from jax.sharding import PartitionSpec as P

D = 2048
HEADS = 32
HEAD_DIM = 64
FF = 5120
NUM_BUCKETS = 32
MAX_DIST = 128
STEP = 10


NORM_EPSILON = 1e-06
NEG_BIG = -1000000000.0
BETA_ONE = 0.9
BETA_TWO = 0.95
EPS_ADAM = 1e-08
DECAY = 0.1
HIGHEST = lax.Precision.HIGHEST


def rms_norm(values, gain_vec):
    inv_root = lax.rsqrt(jnp.mean(values * values, axis=-1, keepdims=True) + NORM_EPSILON)
    return values * inv_root * gain_vec


def gelu_tanh(values):
    return jax.nn.gelu(values, approximate=True)


def bucket_edges():
    half_count = NUM_BUCKETS // 2
    exact_count = half_count // 2
    log_count = half_count - exact_count
    far_ratio = MAX_DIST // exact_count
    edge_list = []
    for step_index in range(1, log_count):
        edge_at = exact_count
        while edge_at**log_count < exact_count**log_count * far_ratio**step_index:
            edge_at = edge_at + 1
        edge_list.append(edge_at)
    return edge_list


def rel_bucket(relative):
    half_count = NUM_BUCKETS // 2
    exact_count = half_count // 2
    distance = jnp.abs(relative)
    far_bucket = jnp.full(relative.shape, exact_count, jnp.int32)
    for edge_at in bucket_edges():
        far_bucket = far_bucket + (distance >= edge_at).astype(jnp.int32)
    near_far = jnp.where(distance < exact_count, distance, far_bucket)
    return near_far + jnp.where(relative > 0, half_count, 0)


def adam_update(weight, first, second, grads, rate, decay):
    first_new = BETA_ONE * first + (1.0 - BETA_ONE) * grads
    second_new = BETA_TWO * second + (1.0 - BETA_TWO) * grads * grads
    first_hat = first_new / (1.0 - BETA_ONE**STEP)
    second_hat = second_new / (1.0 - BETA_TWO**STEP)
    weight_new = weight - rate * (first_hat / (jnp.sqrt(second_hat) + EPS_ADAM) + decay * weight)
    return (weight_new, first_new, second_new)


def attention_rates():
    return 3.0 * jnp.array(
        [D ** (-0.5), (32 * D) ** (-0.5), D ** (-0.5), (HEADS * HEAD_DIM // 64) ** (-0.5)],
        jnp.float32,
    ).reshape(1, 4, 1)


def feed_rates():
    return 3.0 * jnp.array([D ** (-0.5), D ** (-0.5), FF ** (-0.5)], jnp.float32).reshape(1, 3, 1)


def dot(left, right):
    return jnp.dot(left, right, preferred_element_type=jnp.float32)


def dot_t(left, right):
    return lax.dot_general(
        left, right, (((1,), (1,)), ((), ())), preferred_element_type=jnp.float32
    )


def outer_sum(left, right):
    return lax.dot_general(
        left, right, (((0,), (0,)), ((), ())), preferred_element_type=jnp.float32
    )


def norm_stats(values):
    return lax.rsqrt(jnp.mean(values * values, axis=-1, keepdims=True) + NORM_EPSILON)


def norm_back(values, gain_vec, grads):
    inv_root = norm_stats(values)
    unit = values * inv_root
    scaled = grads * gain_vec
    grad_in = inv_root * (scaled - unit * jnp.mean(unit * scaled, axis=-1, keepdims=True))
    return grad_in, jnp.sum(grads * unit, axis=(0, 1))


def to_columns(weight):
    seq_size = lax.axis_size("seq")
    dp_size = lax.axis_size("dp")
    rows, slots, width = weight.shape
    part = width // seq_size
    send = weight.astype(jnp.bfloat16).reshape(rows, slots, seq_size, part).transpose(2, 0, 1, 3)
    send = send.reshape(seq_size, rows, slots * part)
    mine = lax.all_to_all(send, "seq", 0, 0)
    full = lax.all_gather(mine, "dp", axis=0)
    return full.transpose(1, 0, 2, 3).reshape(seq_size * dp_size * rows, slots * part)


def to_rows(grad, slots):
    seq_size = lax.axis_size("seq")
    dp_size = lax.axis_size("dp")
    rows = grad.shape[0] // (seq_size * dp_size)
    part = grad.shape[1] // slots
    send = grad.astype(jnp.bfloat16).reshape(seq_size, dp_size, rows, slots * part).transpose(1, 0, 2, 3)
    summed = lax.psum_scatter(send, "dp", scatter_dimension=0)
    back = lax.all_to_all(summed, "seq", 0, 0)
    back = back.reshape(seq_size, rows, slots, part).transpose(1, 2, 0, 3)
    return back.reshape(rows, slots, seq_size * part).astype(jnp.float32)


def gather_tokens(local_rows):
    full = lax.all_gather(local_rows, "seq", axis=0)
    return full.reshape(-1, local_rows.shape[-1])


def scatter_tokens(partial, shape):
    send = partial.astype(jnp.bfloat16).reshape((lax.axis_size("seq"),) + shape)
    return lax.psum_scatter(send, "seq", scatter_dimension=0).astype(jnp.float32)


def local(
    tokens,
    segments,
    cotangent,
    attention_weight,
    attention_first,
    attention_second,
    feed_weight,
    feed_first,
    feed_second,
    gains,
    gains_first,
    gains_second,
    rel_table,
    table_first,
    table_second,
):
    micro_count, local_rows, width = tokens.shape
    shape = tokens.shape
    seq_size = lax.axis_size("seq")
    seq_len = local_rows * seq_size
    heads_here = HEADS // seq_size
    part = heads_here * HEAD_DIM
    hidden_part = FF // seq_size
    seq_index = lax.axis_index("seq")

    attention_low = to_columns(attention_weight)
    feed_low = to_columns(feed_weight)
    weight_qkv = attention_low[:, : 3 * part]
    weight_out = attention_low[:, 3 * part :]
    weight_in = feed_low[:, : 2 * hidden_part]
    weight_down = feed_low[:, 2 * hidden_part :]

    positions = jnp.arange(seq_len, dtype=jnp.int32)
    buckets = rel_bucket(positions[None, :] - positions[:, None])
    bucket_match = buckets[None, :, :] == jnp.arange(NUM_BUCKETS, dtype=jnp.int32)[:, None, None]
    table_here = lax.dynamic_slice_in_dim(rel_table, seq_index * heads_here, heads_here, 1)
    bias = jnp.einsum(
        "atj,ao->otj",
        bucket_match.astype(jnp.float32),
        table_here,
        precision=HIGHEST,
        preferred_element_type=jnp.float32,
    )
    same_doc = segments[:, :, None] == segments[:, None, :]

    def to_heads(matrix):
        grouped = matrix.reshape(seq_size, micro_count, local_rows, heads_here, HEAD_DIM)
        return grouped.transpose(1, 3, 0, 2, 4).reshape(micro_count, heads_here, seq_len, HEAD_DIM)

    def from_heads(grouped):
        split = grouped.reshape(micro_count, heads_here, seq_size, local_rows, HEAD_DIM)
        return split.transpose(2, 0, 3, 1, 4).reshape(seq_len * micro_count, part)

    inputs = tokens.astype(jnp.float32)
    normed_one = gather_tokens(rms_norm(inputs, gains[0]).astype(jnp.bfloat16))
    grad_out = gather_tokens(cotangent)
    qkv = dot(normed_one, weight_qkv).astype(jnp.bfloat16)
    query_h = to_heads(qkv[:, :part])
    key_h = to_heads(qkv[:, part : 2 * part])
    value_h = to_heads(qkv[:, 2 * part :])
    scores = jnp.einsum("bhqd,bhkd->bhqk", query_h, key_h, preferred_element_type=jnp.float32)
    scores = jnp.where(same_doc[:, None], scores + bias[None], NEG_BIG)
    row_max = jnp.max(scores, axis=-1, keepdims=True)
    exp_scores = jnp.exp(scores - row_max)
    probs = exp_scores / jnp.sum(exp_scores, axis=-1, keepdims=True)
    probs_low = probs.astype(jnp.bfloat16)
    attended = from_heads(
        jnp.einsum("bhqk,bhkd->bhqd", probs_low, value_h, preferred_element_type=jnp.float32)
    ).astype(jnp.bfloat16)
    hidden_state = inputs + scatter_tokens(dot_t(attended, weight_out), shape)
    normed_two = gather_tokens(rms_norm(hidden_state, gains[1]).astype(jnp.bfloat16))
    pre = dot(normed_two, weight_in)
    gate_pre = pre[:, :hidden_part]
    up_pre = pre[:, hidden_part:]
    gate_act, gate_back = jax.vjp(gelu_tanh, gate_pre)
    inner = (gate_act * up_pre).astype(jnp.bfloat16)
    block_rows = (hidden_state + scatter_tokens(dot_t(inner, weight_down), shape)).astype(jnp.bfloat16)
    grad_inner = dot(grad_out, weight_down)
    grad_gate = gate_back(grad_inner * up_pre)[0].astype(jnp.bfloat16)
    grad_up = (grad_inner * gate_act).astype(jnp.bfloat16)
    grad_pre = jnp.concatenate([grad_gate, grad_up], 1)
    grad_normed_two = scatter_tokens(dot_t(grad_pre, weight_in), shape)
    grad_feed = jnp.concatenate([outer_sum(normed_two, grad_pre), outer_sum(grad_out, inner)], 1)
    feed_total = to_rows(grad_feed, 3)
    grad_hidden_norm, grad_gain_two = norm_back(hidden_state, gains[1], grad_normed_two)
    grad_hidden = cotangent.astype(jnp.float32) + grad_hidden_norm
    grad_branch = gather_tokens(grad_hidden.astype(jnp.bfloat16))
    grad_attended = to_heads(dot(grad_branch, weight_out).astype(jnp.bfloat16))
    grad_probs = jnp.einsum(
        "bhqd,bhkd->bhqk", grad_attended, value_h, preferred_element_type=jnp.float32
    )
    row_dot = jnp.sum(probs * grad_probs, axis=-1, keepdims=True)
    grad_scores = (probs * (grad_probs - row_dot)).astype(jnp.bfloat16)
    grad_query = jnp.einsum("bhqk,bhkd->bhqd", grad_scores, key_h, preferred_element_type=jnp.float32)
    grad_key = jnp.einsum("bhqk,bhqd->bhkd", grad_scores, query_h, preferred_element_type=jnp.float32)
    grad_value = jnp.einsum(
        "bhqk,bhqd->bhkd", probs_low, grad_attended, preferred_element_type=jnp.float32
    )
    grad_table_here = jnp.einsum(
        "bhij,zij->zh",
        grad_scores,
        bucket_match.astype(jnp.bfloat16),
        preferred_element_type=jnp.float32,
    )
    grad_qkv = jnp.concatenate(
        [from_heads(item.astype(jnp.bfloat16)) for item in (grad_query, grad_key, grad_value)], 1
    )
    grad_normed_one = scatter_tokens(dot_t(grad_qkv, weight_qkv), shape)
    grad_attention = jnp.concatenate(
        [outer_sum(normed_one, grad_qkv), outer_sum(grad_branch, attended)], 1
    )
    attention_total = to_rows(grad_attention, 4)
    grad_input_norm, grad_gain_one = norm_back(inputs, gains[0], grad_normed_one)
    grad_rows = (grad_hidden + grad_input_norm).astype(jnp.bfloat16)
    grad_table = lax.dynamic_update_slice_in_dim(
        jnp.zeros((NUM_BUCKETS, HEADS), jnp.float32), grad_table_here, seq_index * heads_here, 1
    )
    gains_total, table_total = lax.psum(
        (jnp.stack([grad_gain_one, grad_gain_two], 0), grad_table), ("seq", "dp")
    )
    new_attention = adam_update(
        attention_weight,
        attention_first,
        attention_second,
        attention_total,
        attention_rates(),
        DECAY,
    )
    new_feed = adam_update(feed_weight, feed_first, feed_second, feed_total, feed_rates(), DECAY)
    new_gains = adam_update(gains, gains_first, gains_second, gains_total, 0.6, 0.0)
    new_table = adam_update(rel_table, table_first, table_second, table_total, 1.5, 0.0)
    return (
        block_rows,
        grad_rows,
        new_attention[0],
        new_attention[1],
        new_attention[2][:, :3, :],
        new_attention[2][:, 3, :],
        new_feed[0],
        new_feed[1],
        new_feed[2],
        new_gains[0],
        new_gains[1],
        new_gains[2],
        new_table[0],
        new_table[1],
        new_table[2],
    )


def solution(mesh):
    in_specs = (
        P("dp", "seq", None),
        P("dp", None),
        P("dp", "seq", None),
        P(("seq", "dp"), None, None),
        P(("seq", "dp"), None, None),
        P(("seq", "dp"), None, None),
        P(("seq", "dp"), None, None),
        P(("seq", "dp"), None, None),
        P(("seq", "dp"), None, None),
        P(),
        P(),
        P(),
        P(),
        P(),
        P(),
    )
    out_specs = (
        P("dp", "seq", None),
        P("dp", "seq", None),
        P(("seq", "dp"), None, None),
        P(("seq", "dp"), None, None),
        P(("seq", "dp"), None, None),
        P(("seq", "dp"), None),
        P(("seq", "dp"), None, None),
        P(("seq", "dp"), None, None),
        P(("seq", "dp"), None, None),
        P(),
        P(),
        P(),
        P(),
        P(),
        P(),
    )
    return jax.shard_map(local, mesh=mesh, in_specs=in_specs, out_specs=out_specs, check_vma=False)
```

time: 5100 us -> 1100 us (0.22)
  waiting for transfers between devices: 4230 us -> 574 us
  matrix products: 448 us -> 129 us
  other arithmetic: 216 us -> 52.2 us
  blocking collectives: 42.7 us -> 179 us
    reduce_scatter x2 -> x4, waiting for transfers between devices: 3690 us -> 80.6 us  [scatter_tokens(): lax.psum_scatter(send, 'seq', scatter_dimension=0).astype(jnp.float32)]
    all_gather x6, waiting for transfers between devices: 525 us -> 241 us  [the longest x4 126 us: gather_tokens(): full = lax.all_gather(local_rows, 'seq', axis=0)]
    unnamed x16 -> x12, waiting for transfers between devices: 23.9 us -> 215 us
    add x6 -> x0, other arithmetic: 185 us -> none  [the longest x1 120 us: local(): feed_total = feed_total + feed_more]
    dot_general x93 -> x15, matrix products: 278 us -> 98.9 us  [the longest x4 31.3 us: dot(): return jnp.dot(left, right, preferred_element_type=jnp.float32)]
    dot_general x14 -> x4, matrix products: 171 us -> 23.1 us  [outer_sum(): lax.dot_general(left, right, (((0,), (0,)), ((), ())), preferred_element_...]
    all_to_all x0 -> x2, blocking collectives: none -> 110 us  [to_columns(): mine = lax.all_to_all(send, 'seq', 0, 0)]
  transfers between devices with their start and end apart: 12 -> 13, of which waited for: 9 -> 11; matrix products, arithmetic and copies ran while one was open for 11% -> 14% of each run, Pallas kernels for 0% -> 0%
where the time goes in v1:
time: 1100 us
  waiting for transfers between devices  574 us (52%)
  blocking collectives  179 us (16%)
  local copies, waits for them, and re-layouts  136 us (12%)
  matrix products  129 us (12%)
  other arithmetic  52.2 us (5%)
  between operations  14.8 us (1%)
    unnamed x12, waiting for transfers between devices  215 us
    all_gather x4, waiting for transfers between devices, gather_tokens(): full = lax.all_gather(local_rows, 'seq', axis=0)  126 us
    all_gather x2, waiting for transfers between devices, to_columns(): full = lax.all_gather(mine, 'dp', axis=0)  115 us
    all_to_all x2, blocking collectives, to_columns(): mine = lax.all_to_all(send, 'seq', 0, 0)  110 us
    reduce_scatter x4, waiting for transfers between devices, scatter_tokens(): lax.psum_scatter(send, 'seq', scatter_dimension=0).astype(jnp.float32)  80.6 us
    psum x1, blocking collectives, local(): lax.psum((jnp.stack([grad_gain_one, grad_gain_two], 0), grad_table), ('se...  69.2 us
    all_to_all x2, waiting for transfers between devices, to_rows(): back = lax.all_to_all(summed, 'seq', 0, 0)  37.3 us
    dot_general x4, matrix products, dot(): return jnp.dot(left, right, preferred_element_type=jnp.float32)  31.3 us
  transfers between devices with their start and end apart: 13, of which 11 were waited for; matrix products, arithmetic and copies ran while one was open for 14% of the time, Pallas kernels for 0%

profile of v1, /device:TPU:0, one launch (start us, length us, event | category | flops | bytes accessed | tf_op | source)
XLA Modules:
  0.0 1095.5 jit_solution(509703530454587204)
XLA Ops:
  10.5 32.8 %all_to_all.20 = bf16[8,64,1024]{2,1,0:T(8,128)(2,1)} all-to-all(bf16[8,64,1024]{2,1,0:T(8,128)(2,1)S(1)} %reshape.230), channel_id=1, replica_groups=mesh['seq'=8,'dp'=4] {'seq'}, dimensions={0} | all-to-all | bytes 2097152 | tf_op jit(solution)/shard_map/all_to_all | solution.py:113
  46.6 12.2 %fusion.2 = f32[4,512,512]{2,0,1:T(4,128)} fusion(s32[512,512]{1,0:T(8,128)S(1)} %fusion.67, f32[32,32]{1,0:T(8,128)S(1)} %copy-done.26, s32[]{:T(128)S(6)} %select_n.28), kind=kOutput, calls=%fused_computation.3 | convolution fusion | flops 411041792 | bytes 5246980 | tf_op jit(solution)/shard_map/atj,ao->otj/dot_general | solution.py:177
  58.9 5.3 copy.163
  65.3 29.8 %all-gather.15.cloned.1.call-done = bf16[32,64,1024]{2,1,0:T(8,128)(2,1)} async-done(((bf16[8,64,1024]{2,1,0:T(8,128)(2,1)}), bf16[32,64,1024]{2,1,0:T(8,128)(2,1)}) %all-gather.15.cloned.1.call-update) | async-done | bytes 4194320 | tf_op jit(solution)/shard_map/all_gather | solution.py:114
  95.1 4.9 copy.159
  99.9 44.5 %all-gather.13.cloned.1.call-done = bf16[16,64,2048]{2,1,0:T(8,128)(2,1)} async-done(((bf16[2,64,2048]{2,1,0:T(8,128)(2,1)}), bf16[16,64,2048]{2,1,0:T(8,128)(2,1)}) %all-gather.13.cloned.1.call-update) | async-done | bytes 4194320 | tf_op jit(solution)/shard_map/all_gather | solution.py:131
  144.4 6.6 fusion.38
  162.3 7.0 fusion.100
  169.3 4.2 fusion.46
  175.8 4.5 convolution_convert_fusion.2
  184.8 2.8 reshape.241
  187.7 77.4 %all_to_all.21 = bf16[8,64,1920]{2,1,0:T(8,128)(2,1)} all-to-all(bf16[8,64,1920]{2,1,0:T(8,128)(2,1)} %reshape.241), channel_id=1, replica_groups=mesh['seq'=8,'dp'=4] {'seq'}, dimensions={0} | all-to-all | bytes 3932160 | tf_op jit(solution)/shard_map/all_to_all | solution.py:113
  269.4 85.3 %all-gather.19.cloned.1.call-done = bf16[32,64,1920]{2,1,0:T(8,128)(2,1)} async-done(((bf16[8,64,1920]{2,1,0:T(8,128)(2,1)}), bf16[32,64,1920]{2,1,0:T(8,128)(2,1)}) %all-gather.19.cloned.1.call-update) | async-done | bytes 7864336 | tf_op jit(solution)/shard_map/all_gather | solution.py:114
  354.7 7.2 copy.168
  361.8 42.0 %all-gather.17.cloned.1.call-done = bf16[16,64,2048]{2,1,0:T(8,128)(2,1)} async-done(((bf16[2,64,2048]{2,1,0:T(8,128)(2,1)}), bf16[16,64,2048]{2,1,0:T(8,128)(2,1)}) %all-gather.17.cloned.1.call-update) | async-done | bytes 4194320 | tf_op jit(solution)/shard_map/all_gather | solution.py:131
  403.9 10.4 fusion.8
  414.2 37.0 %all-gather.21.cloned.1.call-done = bf16[16,64,2048]{2,1,0:T(8,128)(2,1)} async-done(((bf16[2,64,2048]{2,1,0:T(8,128)(2,1)}), bf16[16,64,2048]{2,1,0:T(8,128)(2,1)}) %all-gather.21.cloned.1.call-update) | async-done | bytes 4194320 | tf_op jit(solution)/shard_map/all_gather | solution.py:131
  451.2 10.6 fusion.27
  461.8 7.3 fusion.14
  469.2 48.8 %reduce-scatter.15.cloned.1.call-done = bf16[1,2,64,2048]{3,2,1,0:T(8,128)(2,1)} async-done(((bf16[8,2,64,2048]{3,2,1,0:T(8,128)(2,1)}), bf16[1,2,64,2048]{3,2,1,0:T(8,128)(2,1)}) %reduce-scatter.15.cloned.1.call-update) | async-done | bytes 524304 | tf_op jit(solution)/shard_map/reduce_scatter | solution.py:137
  522.4 6.4 copy.179
  530.3 6.6 copy.185
  536.9 6.6 fusion.17
  543.5 4.5 copy.186
  547.9 9.2 convolution_convert_fusion
  557.1 7.5 maximum_bitcast_fusion
  564.7 2.7 all-gather.23.cloned.1.call-done
  567.4 3.7 convolution_convert_fusion.9
  571.1 6.4 copy.180
  579.6 5.7 fusion.49
  585.4 8.2 multiply_reduce_fusion
  593.6 5.2 convert_reduce_fusion
  604.9 2.7 copy.177
  607.7 2.7 reshape.254
  612.8 2.7 copy.173
  615.5 2.7 reshape.250
  620.7 2.7 copy.175
  623.4 3.1 reshape.252
  627.7 3.7 convolution_convert_fusion.6
  632.7 3.6 convolution_convert_fusion.5
  636.3 2.5 maximum_bitcast_fusion.1
  638.8 7.7 convolution_convert_fusion.3
  646.6 7.6 convolution_convert_fusion.1
  655.4 213.9 %all-reduce.6.cloned.1.call-done = (bf16[4,8,64,1024]{3,2,0,1:T(8,128)(2,1)}, bf16[4,8,64,1920]{3,2,0,1:T(8,128)(2,1)}) async-done(((bf16[4,8,64,1024]{3,2,0,1:T(8,128)(2,1)}, bf16[4,8,64,1920]{3,2,0,1:T(8,128)(2,1)}), (bf16[4,8,64,1024]{3,2,0,1:T(8,128)(2,1)}, bf16[4,8,64,1920]{3,2,0,1:T(8,128)(2,1)})) %all-reduce.6.cloned.1.call-update) | async-done | bytes 12058640
  869.3 2.9 dynamic-slice_bitcast_fusion.1
  872.2 4.6 all-to-all-start.2
  876.8 3.1 copy.188
  879.9 3.7 dynamic-slice_bitcast_fusion
  883.6 37.3 %all-to-all-done.2 = bf16[8,64,1024]{2,1,0:T(8,128)(2,1)} async-done(((bf16[8,64,1024]{2,1,0:T(8,128)(2,1)}), bf16[8,64,1024]{2,1,0:T(8,128)(2,1)}, u32[]{:S(2)}, u32[]{:S(2)}) %all-to-all-start.2) | async-done | bytes 1048608 | tf_op jit(solution)/shard_map/all_to_all | solution.py:125
  920.9 4.3 all-to-all-start.3
  925.4 6.4 fusion.55
  932.1 23.9 %reduce-scatter.17.cloned.1.call-done = bf16[1,2,64,2048]{3,2,1,0:T(8,128)(2,1)} async-done(((bf16[8,2,64,2048]{3,2,1,0:T(8,128)(2,1)}), bf16[1,2,64,2048]{3,2,1,0:T(8,128)(2,1)}) %reduce-scatter.17.cloned.1.call-update) | async-done | bytes 524304 | tf_op jit(solution)/shard_map/reduce_scatter | solution.py:137
  957.5 69.2 %all-reduce.2 = (f32[2,2048]{1,0:T(2,128)S(1)}, f32[32,32]{1,0:T(8,128)S(1)}) all-reduce(f32[2,2048]{1,0:T(2,128)S(1)} %pad_maximum_fusion.3, f32[32,32]{1,0:T(8,128)S(1)} %dynamic_update_slice.3), channel_id=1, replica_groups=mesh['seq'=8,'dp'=4] {'seq','dp'}, use_global_device_ids=true, to_apply=%region_15.16 | all-reduce | flops 5120 | bytes 40960 | tf_op jit(solution)/shard_map/psum | solution.py:258
  1028.1 7.8 reduce-scatter.13.cloned.1.call-done
  1035.9 3.0 fusion.61
  1041.0 2.5 copy.181
  1043.5 2.8 reshape.260
  1046.4 7.3 multiply_subtract_fusion.1
  1053.7 2.7 copy.190
  1057.7 2.7 copy.191
  1061.2 6.5 reshape.263
  1067.7 6.7 copy.187
  1074.3 4.9 reshape.261
  1079.3 9.5 multiply_subtract_fusion
  (165 shorter events, 59.6 us)
Async XLA Ops:
  7.2 87.9 %all-gather.15.cloned.1.call-start = ((), (), s32[]{:S(2)}) async-start(), calls=%async_computation.13 | async-start | bytes 5242880 | tf_op jit(solution)/shard_map/all_gather | solution.py:114
  9.3 34.1 %copy-start = (bf16[2,64,2048]{2,1,0:T(8,128)(2,1)S(1)}, bf16[2,64,2048]{2,1,0:T(8,128)(2,1)}, u32[]{:S(2)}) copy-start(bf16[2,64,2048]{2,1,0:T(8,128)(2,1)} %param.17) | copy-start | bytes 1572868
  9.3 34.3 %copy-start.23 = (f32[2,2048]{1,0:T(2,128)S(1)}, f32[2,2048]{1,0:T(2,128)}, u32[]{:S(2)}) copy-start(f32[2,2048]{1,0:T(2,128)} %param.26) | copy-start | bytes 49156
  9.7 37.0 %copy-start.26 = (f32[32,32]{1,0:T(8,128)S(1)}, f32[32,32]{1,0:T(8,128)}, u32[]{:S(2)}) copy-start(f32[32,32]{1,0:T(8,128)} %param.29) | copy-start | bytes 12292
  43.3 101.1 %all-gather.13.cloned.1.call-start = ((), (), s32[]{:S(2)}) async-start(), calls=%async_computation.12 | async-start | bytes 4718592 | tf_op jit(solution)/shard_map/all_gather | solution.py:131
  43.6 15.3 %copy-start.32 = (f32[2,64]{1,0:T(2,128)}, f32[2,64]{1,0:T(2,128)S(1)}, u32[]{:S(2)}) copy-start(f32[2,64]{1,0:T(2,128)S(1)} %add_rsqrt_fusion.1) | copy-start | bytes 1540
  43.6 0.6 copy-start.21
  45.2 219.9 %reduce-scatter.11.cloned.1.call-start = ((), (), s32[]{:S(2)}) async-start(), calls=%async_computation.8 | async-start | bytes 4718592 | tf_op jit(solution)/shard_map/reduce_scatter | solution.py:137
  45.7 1.0 copy-start.16
  58.9 5.3 copy-start.25
  154.0 8.3 copy-start.10
  162.3 7.1 copy-start.12
  162.3 7.1 copy-start.18
  175.1 5.2 copy-start.2
  180.4 174.3 %all-gather.19.cloned.1.call-start = ((), (), s32[]{:S(2)}) async-start(), calls=%async_computation.15 | async-start | bytes 9830400 | tf_op jit(solution)/shard_map/all_gather | solution.py:114
  265.1 138.8 %all-gather.17.cloned.1.call-start = ((), (), s32[]{:S(2)}) async-start(), calls=%async_computation.14 | async-start | bytes 4718592 | tf_op jit(solution)/shard_map/all_gather | solution.py:131
  268.5 182.7 %all-gather.21.cloned.1.call-start = ((), (), s32[]{:S(2)}) async-start(), calls=%async_computation.16 | async-start | bytes 4718592 | tf_op jit(solution)/shard_map/all_gather | solution.py:131
  269.1 248.9 %reduce-scatter.15.cloned.1.call-start = ((), (), s32[]{:S(2)}) async-start(), calls=%async_computation.10 | async-start | bytes 4718592 | tf_op jit(solution)/shard_map/reduce_scatter | solution.py:137
  451.2 10.6 copy-start.5
  461.8 7.3 copy-start.38
  461.8 7.3 copy-start.40
  469.1 48.9 %copy-start.1 = (bf16[1,2,64,2048]{3,2,1,0:T(8,128)(2,1)S(1)}, bf16[1,2,64,2048]{3,2,1,0:T(8,128)(2,1)}, u32[]{:S(2)}) copy-start(bf16[1,2,64,2048]{3,2,1,0:T(8,128)(2,1)} %reduce-scatter.11.cloned.1.call-done) | copy-start | bytes 1572868
  469.1 50.5 %copy-start.6 = (bf16[2,64,2048]{2,1,0:T(8,128)(2,1)S(1)}, bf16[2,64,2048]{2,1,0:T(8,128)(2,1)}, u32[]{:S(2)}) copy-start(bf16[2,64,2048]{2,1,0:T(8,128)(2,1)} %param.19) | copy-start | bytes 1572868
  469.2 98.2 %all-gather.23.cloned.1.call-start = ((), (), s32[]{:S(2)}) async-start(), calls=%async_computation.17 | async-start | bytes 4718592 | tf_op jit(solution)/shard_map/all_gather | solution.py:131
  521.9 6.9 copy-start.3
  521.9 347.4 %all-reduce.6.cloned.1.call-start = ((), (), s32[]{:S(2)}) async-start(), calls=%async_computation.18 | async-start | bytes 24117248
  530.3 6.6 copy-start.37
  543.5 4.5 copy-start.39
  579.6 5.8 copy-start.19
  579.6 13.9 %slice-start = ((s8[8388608]{0:T(1024)(128)(4,1)}), s8[4194304]{0:T(1024)(128)(4,1)S(1)}, s32[]{:S(2)}) async-start(s8[8388608]{0:T(1024)(128)(4,1)} %bitcast.198), calls=%async_computation.19 | async-start | bytes 8388608
  585.4 8.2 slice-start.1
  593.6 5.3 copy-start.13
  598.8 2.2 copy-start.11
  626.5 4.9 copy-start.15
  627.7 3.8 copy-start.14
  627.7 5.0 copy-start.9
  631.5 1.1 copy-start.20
  638.8 317.2 %reduce-scatter.17.cloned.1.call-start = ((), (), s32[]{:S(2)}) async-start(), calls=%async_computation.11 | async-start | bytes 4718592 | tf_op jit(solution)/shard_map/reduce_scatter | solution.py:137
  646.6 389.3 %reduce-scatter.13.cloned.1.call-start = ((), (), s32[]{:S(2)}) async-start(), calls=%async_computation.9 | async-start | bytes 4718592 | tf_op jit(solution)/shard_map/reduce_scatter | solution.py:137
  654.2 0.7 copy-start.36
  872.2 48.7 %all-to-all-start.2 = ((bf16[8,64,1024]{2,1,0:T(8,128)(2,1)}), bf16[8,64,1024]{2,1,0:T(8,128)(2,1)}, u32[]{:S(2)}, u32[]{:S(2)}) async-start(bf16[8,64,1024]{2,1,0:T(8,128)(2,1)} %dynamic-slice_bitcast_fusion.1), calls=%async_computation.6 | async-start | bytes 2097152 | tf_op jit(solution)/shard_map/all_to_all | solution.py:125
  879.9 45.4 %copy-start.17 = (s32[512,512]{1,0:T(8,128)S(1)}, s32[512,512]{1,0:T(8,128)}, u32[]{:S(2)}) copy-start(s32[512,512]{1,0:T(8,128)} %copy-done.16) | copy-start | bytes 3145732
  920.9 140.3 %all-to-all-start.3 = ((bf16[8,64,1920]{2,1,0:T(8,128)(2,1)}), bf16[8,64,1920]{2,1,0:T(8,128)(2,1)}, u32[]{:S(2)}, u32[]{:S(2)}) async-start(bf16[8,64,1920]{2,1,0:T(8,128)(2,1)} %dynamic-slice_bitcast_fusion), calls=%async_computation.7 | async-start | bytes 3932160 | tf_op jit(solution)/shard_map/all_to_all | solution.py:125
  925.3 30.7 %copy-start.22 = (f32[1,2048]{1,0:T(1,128)S(1)}, f32[1,2048]{1,0:T(1,128)}, u32[]{:S(2)}) copy-start(f32[1,2048]{1,0:T(1,128)} %copy-done.21) | copy-start | bytes 24580
  925.3 30.7 %copy-start.33 = (f32[2,64]{1,0:T(2,128)S(1)}, f32[2,64]{1,0:T(2,128)}, u32[]{:S(2)}) copy-start(f32[2,64]{1,0:T(2,128)} %copy-done.32) | copy-start | bytes 1540
  925.3 101.4 %copy-start.27 = (f32[32,32]{1,0:T(8,128)S(1)}, f32[32,32]{1,0:T(8,128)}, u32[]{:S(2)}) copy-start(f32[32,32]{1,0:T(8,128)} %param.29) | copy-start | bytes 12292
  925.3 101.4 %copy-start.28 = (f32[32,32]{1,0:T(8,128)S(1)}, f32[32,32]{1,0:T(8,128)}, u32[]{:S(2)}) copy-start(f32[32,32]{1,0:T(8,128)} %param.30) | copy-start | bytes 12292
  925.3 101.4 %copy-start.29 = (f32[32,32]{1,0:T(8,128)S(1)}, f32[32,32]{1,0:T(8,128)}, u32[]{:S(2)}) copy-start(f32[32,32]{1,0:T(8,128)} %param.31) | copy-start | bytes 12292
  925.3 102.1 %copy-start.24 = (f32[2,2048]{1,0:T(2,128)S(1)}, f32[2,2048]{1,0:T(2,128)}, u32[]{:S(2)}) copy-start(f32[2,2048]{1,0:T(2,128)} %param.26) | copy-start | bytes 49156
  925.4 102.1 %copy-start.30 = (f32[2,2048]{1,0:T(2,128)S(1)}, f32[2,2048]{1,0:T(2,128)}, u32[]{:S(2)}) copy-start(f32[2,2048]{1,0:T(2,128)} %param.27) | copy-start | bytes 49156
  925.4 102.0 %copy-start.31 = (f32[2,2048]{1,0:T(2,128)S(1)}, f32[2,2048]{1,0:T(2,128)}, u32[]{:S(2)}) copy-start(f32[2,2048]{1,0:T(2,128)} %param.28) | copy-start | bytes 49156
  925.4 110.6 %copy-start.7 = (bf16[2,64,2048]{2,1,0:T(8,128)(2,1)S(1)}, bf16[2,64,2048]{2,1,0:T(8,128)(2,1)}, u32[]{:S(2)}) copy-start(bf16[2,64,2048]{2,1,0:T(8,128)(2,1)} %param.19) | copy-start | bytes 1572868
  925.4 110.6 %copy-start.8 = (bf16[1,2,64,2048]{3,2,1,0:T(8,128)(2,1)S(1)}, bf16[1,2,64,2048]{3,2,1,0:T(8,128)(2,1)}, u32[]{:S(2)}) copy-start(bf16[1,2,64,2048]{3,2,1,0:T(8,128)(2,1)} %reduce-scatter.15.cloned.1.call-done) | copy-start | bytes 1572868
  1041.0 5.4 copy-start.35
  1043.5 2.9 copy-start.4
  1074.3 4.9 copy-start.34
Sparse Core Ops, SparseCore 0:
  43.4 51.6 all-gather.14
  97.2 47.1 all-gather.12
  180.5 77.8 reduce-scatter.10
  265.2 89.4 all-gather.18
  356.7 47.1 all-gather.16
  405.3 45.8 all-gather.20
  469.3 48.7 reduce-scatter.14
  522.0 45.2 all-gather.22
  638.9 230.3 all-reduce.5
  871.5 84.4 reduce-scatter.16
  958.3 77.6 reduce-scatter.12

commit v2 on v1

--- a/solution.py
+++ b/solution.py
@@ -1,6 +1,8 @@
 import jax
 import jax.numpy as jnp
 from jax import lax
+from jax.experimental import pallas as pl
+from jax.experimental.pallas import tpu as pltpu
 from jax.sharding import PartitionSpec as P
 
 D = 2048
@@ -103,28 +105,232 @@
     return grad_in, jnp.sum(grads * unit, axis=(0, 1))
 
 
+def partner_pairs(axis, offset):
+    return [(index, index ^ offset) for index in range(lax.axis_size(axis))]
+
+
+def swap(value, axis, offset):
+    return lax.ppermute(value, axis, partner_pairs(axis, offset))
+
+
+VMEM_LIMIT = 56 * 1024 * 1024
+
+
+def place_columns(stacked, me):
+    seq_size, slots, rows, part = stacked.shape
+    if part % 128:
+        out = jnp.zeros((slots, rows, seq_size * part), stacked.dtype)
+        for offset in range(seq_size):
+            out = lax.dynamic_update_slice(out, stacked[offset], (0, 0, (me ^ offset) * part))
+        return out
+
+    def body(me_ref, in_ref, out_ref):
+        out_ref[...] = in_ref[0]
+
+    return pl.pallas_call(
+        body,
+        grid_spec=pltpu.PrefetchScalarGridSpec(
+            num_scalar_prefetch=1,
+            grid=(seq_size,),
+            in_specs=[
+                pl.BlockSpec((1, slots, rows, part), lambda j, me_ref: (j ^ me_ref[0], 0, 0, 0))
+            ],
+            out_specs=pl.BlockSpec((slots, rows, part), lambda j, me_ref: (0, 0, j)),
+        ),
+        out_shape=jax.ShapeDtypeStruct((slots, rows, seq_size * part), stacked.dtype),
+        compiler_params=pltpu.CompilerParams(vmem_limit_bytes=VMEM_LIMIT),
+    )(me.reshape(1), stacked)
+
+
+def head_probs(query, key, bias, same_doc):
+    scores = lax.dot_general(
+        query, key, (((1,), (1,)), ((), ())), preferred_element_type=jnp.float32
+    )
+    scores = jnp.where(same_doc, scores + bias, NEG_BIG)
+    exp_scores = jnp.exp(scores - jnp.max(scores, axis=-1, keepdims=True))
+    return exp_scores * (1.0 / jnp.sum(exp_scores, axis=-1, keepdims=True))
+
+
+def attention_specs(seq_size, rows):
+    length = seq_size * rows
+    tokens_spec = pl.BlockSpec((seq_size, 1, rows, 128), lambda pair, m: (0, m, 0, pair))
+    return tokens_spec, [
+        pl.BlockSpec((2, length, length), lambda pair, m: (pair, 0, 0)),
+        pl.BlockSpec((1, length, 1), lambda pair, m: (m, 0, 0)),
+        pl.BlockSpec((1, 1, length), lambda pair, m: (m, 0, 0)),
+    ]
+
+
+def attention_forward(query, key, value, bias, segments):
+    seq_size, micro_count, rows, part = query.shape
+    length = seq_size * rows
+    tokens_spec, other_specs = attention_specs(seq_size, rows)
+
+    def body(q_ref, k_ref, v_ref, bias_ref, seg_q_ref, seg_k_ref, out_ref):
+        q, k, v = [ref[:, 0].reshape(length, 128) for ref in (q_ref, k_ref, v_ref)]
+        same_doc = seg_q_ref[0] == seg_k_ref[0]
+        outs = []
+        for h in range(2):
+            cols = slice(h * HEAD_DIM, (h + 1) * HEAD_DIM)
+            probs = head_probs(q[:, cols], k[:, cols], bias_ref[h], same_doc)
+            outs.append(dot(probs.astype(jnp.bfloat16), v[:, cols]))
+        out = jnp.concatenate(outs, 1).astype(jnp.bfloat16)
+        out_ref[...] = out.reshape(seq_size, 1, rows, 128)
+
+    return pl.pallas_call(
+        body,
+        grid=(part // 128, micro_count),
+        in_specs=[tokens_spec] * 3 + other_specs,
+        out_specs=tokens_spec,
+        out_shape=jax.ShapeDtypeStruct(query.shape, jnp.bfloat16),
+        compiler_params=pltpu.CompilerParams(vmem_limit_bytes=VMEM_LIMIT),
+    )(query, key, value, bias, segments[:, :, None], segments[:, None, :])
+
+
+def attention_backward(query, key, value, grad_out, bias, segments):
+    seq_size, micro_count, rows, part = query.shape
+    length = seq_size * rows
+    tokens_spec, other_specs = attention_specs(seq_size, rows)
+
+    def body(
+        q_ref, k_ref, v_ref, g_ref, bias_ref, seg_q_ref, seg_k_ref, dq_ref, dk_ref, dv_ref, ds_ref
+    ):
+        q, k, v, g = [ref[:, 0].reshape(length, 128) for ref in (q_ref, k_ref, v_ref, g_ref)]
+        same_doc = seg_q_ref[0] == seg_k_ref[0]
+        first = pl.program_id(1) == 0
+        grads = ([], [], [])
+        for h in range(2):
+            cols = slice(h * HEAD_DIM, (h + 1) * HEAD_DIM)
+            probs = head_probs(q[:, cols], k[:, cols], bias_ref[h], same_doc)
+            grad_probs = dot_t(g[:, cols], v[:, cols])
+            row_dot = jnp.sum(probs * grad_probs, axis=-1, keepdims=True)
+            grad_scores = (probs * (grad_probs - row_dot)).astype(jnp.bfloat16)
+            wide = grad_scores.astype(jnp.float32)
+            ds_ref[h] = jnp.where(first, wide, ds_ref[h] + wide)
+            grads[0].append(dot(grad_scores, k[:, cols]))
+            grads[1].append(outer_sum(grad_scores, q[:, cols]))
+            grads[2].append(outer_sum(probs.astype(jnp.bfloat16), g[:, cols]))
+        for ref, parts in zip((dq_ref, dk_ref, dv_ref), grads):
+            joined = jnp.concatenate(parts, 1).astype(jnp.bfloat16)
+            ref[...] = joined.reshape(seq_size, 1, rows, 128)
+
+    return pl.pallas_call(
+        body,
+        grid=(part // 128, micro_count),
+        in_specs=[tokens_spec] * 4 + other_specs,
+        out_specs=[tokens_spec] * 3
+        + [pl.BlockSpec((2, length, length), lambda pair, m: (pair, 0, 0))],
+        out_shape=[jax.ShapeDtypeStruct(query.shape, jnp.bfloat16)] * 3
+        + [jax.ShapeDtypeStruct((part // HEAD_DIM, length, length), jnp.float32)],
+        compiler_params=pltpu.CompilerParams(vmem_limit_bytes=VMEM_LIMIT),
+    )(query, key, value, grad_out, bias, segments[:, :, None], segments[:, None, :])
+
+
+def exchange(values, dim, out_dim):
+    seq_size = lax.axis_size("seq")
+    me = lax.axis_index("seq")
+    received = None
+    for offset in range(seq_size):
+        piece = lax.dynamic_index_in_dim(values, me ^ offset, dim, keepdims=False)
+        if offset:
+            piece = swap(piece, "seq", offset)
+        piece = jnp.expand_dims(piece, out_dim)
+        if received is None:
+            shape = piece.shape[:out_dim] + (seq_size,) + piece.shape[out_dim + 1 :]
+            received = jnp.zeros(shape, values.dtype)
+        received = lax.dynamic_update_slice_in_dim(received, piece, me ^ offset, out_dim)
+    return received
+
+
+def gather_dp(mine):
+    if lax.axis_size("dp") != 4:
+        return lax.all_gather(mine, "dp", axis=2)
+    me = lax.axis_index("dp")
+    half = mine.shape[1] // 2
+    one = swap(mine, "dp", 1)
+    two = swap(mine, "dp", 2)
+    low = swap(one[:, :half], "dp", 2)
+    high = swap(two[:, half:], "dp", 1)
+    full = jnp.zeros(mine.shape[:2] + (4,) + mine.shape[2:], mine.dtype)
+    for piece, source, start in (
+        (mine, 0, 0),
+        (one, 1, 0),
+        (two, 2, 0),
+        (low, 3, 0),
+        (high, 3, half),
+    ):
+        full = lax.dynamic_update_slice(full, piece[:, :, None], (0, start, me ^ source, 0, 0))
+    return full
+
+
+def wide(value):
+    return value.astype(jnp.float32)
+
+
+def scatter_dp_first(partial):
+    if lax.axis_size("dp") != 4:
+        return [lax.psum_scatter(partial, "dp", scatter_dimension=2)]
+    me = lax.axis_index("dp")
+    half = partial.shape[1] // 2
+    pieces = [lax.dynamic_index_in_dim(partial, me ^ k, 2, keepdims=False) for k in range(4)]
+    low = [piece[:, :half] for piece in pieces]
+    high = [piece[:, half:] for piece in pieces]
+    low_two = (wide(low[2]) + wide(swap(low[3], "dp", 1))).astype(jnp.bfloat16)
+    high_one = (wide(high[1]) + wide(swap(high[3], "dp", 2))).astype(jnp.bfloat16)
+    low_zero = wide(low[0]) + wide(swap(low[1], "dp", 1))
+    high_zero = wide(high[0]) + wide(swap(high[2], "dp", 2))
+    return [low_two, high_one, low_zero, high_zero]
+
+
+def scatter_dp_second(items):
+    if len(items) == 1:
+        return items[0]
+    low_two, high_one, low_zero, high_zero = items
+    low_sum = low_zero + wide(swap(low_two, "dp", 2))
+    high_sum = high_zero + wide(swap(high_one, "dp", 1))
+    return jnp.concatenate([low_sum, high_sum], 1).astype(jnp.bfloat16)
+
+
 def to_columns(weight):
     seq_size = lax.axis_size("seq")
-    dp_size = lax.axis_size("dp")
-    rows, slots, width = weight.shape
+    slots, rows, width = weight.shape
     part = width // seq_size
-    send = weight.astype(jnp.bfloat16).reshape(rows, slots, seq_size, part).transpose(2, 0, 1, 3)
-    send = send.reshape(seq_size, rows, slots * part)
-    mine = lax.all_to_all(send, "seq", 0, 0)
-    full = lax.all_gather(mine, "dp", axis=0)
-    return full.transpose(1, 0, 2, 3).reshape(seq_size * dp_size * rows, slots * part)
-
-
-def to_rows(grad, slots):
+    return exchange(weight.astype(jnp.bfloat16).reshape(slots, rows, seq_size, part), 2, 1)
+
+
+def all_rows(mine):
+    return gather_dp(mine).reshape(mine.shape[0], -1, mine.shape[-1])
+
+
+def after(value, *earlier):
+    return lax.optimization_barrier((value,) + earlier)[0]
+
+
+def to_rows_first(grads):
     seq_size = lax.axis_size("seq")
     dp_size = lax.axis_size("dp")
-    rows = grad.shape[0] // (seq_size * dp_size)
-    part = grad.shape[1] // slots
-    send = grad.astype(jnp.bfloat16).reshape(seq_size, dp_size, rows, slots * part).transpose(1, 0, 2, 3)
-    summed = lax.psum_scatter(send, "dp", scatter_dimension=0)
-    back = lax.all_to_all(summed, "seq", 0, 0)
-    back = back.reshape(seq_size, rows, slots, part).transpose(1, 2, 0, 3)
-    return back.reshape(rows, slots, seq_size * part).astype(jnp.float32)
+    partial = jnp.stack([grad.astype(jnp.bfloat16) for grad in grads], 0)
+    slots, total, part = partial.shape
+    rows = total // (seq_size * dp_size)
+    return scatter_dp_first(partial.reshape(slots, seq_size, dp_size, rows, part))
+
+
+def to_rows_last(mine):
+    me = lax.axis_index("seq")
+    pieces = []
+    for offset in range(lax.axis_size("seq")):
+        piece = lax.dynamic_index_in_dim(mine, me ^ offset, 1, keepdims=False)
+        pieces.append(swap(piece, "seq", offset) if offset else piece)
+    return wide(place_columns(jnp.stack(pieces, 0), me))
+
+
+def sum_all(value):
+    for axis in ("seq", "dp"):
+        offset = 1
+        while offset < lax.axis_size(axis):
+            value = value + swap(value, axis, offset)
+            offset = offset * 2
+    return value
 
 
 def gather_tokens(local_rows):
@@ -160,15 +366,15 @@
     seq_len = local_rows * seq_size
     heads_here = HEADS // seq_size
     part = heads_here * HEAD_DIM
-    hidden_part = FF // seq_size
     seq_index = lax.axis_index("seq")
 
-    attention_low = to_columns(attention_weight)
-    feed_low = to_columns(feed_weight)
-    weight_qkv = attention_low[:, : 3 * part]
-    weight_out = attention_low[:, 3 * part :]
-    weight_in = feed_low[:, : 2 * hidden_part]
-    weight_down = feed_low[:, 2 * hidden_part :]
+    attention_slots = attention_weight.transpose(1, 0, 2)
+    feed_slots = feed_weight.transpose(1, 0, 2).astype(jnp.bfloat16)
+    attention_mine = to_columns(attention_slots)
+    attention_mine, feed_slots = lax.optimization_barrier((attention_mine, feed_slots))
+    attention_low = all_rows(attention_mine)
+    feed_mine = to_columns(feed_slots)
+    weight_out = attention_low[3]
 
     positions = jnp.arange(seq_len, dtype=jnp.int32)
     buckets = rel_bucket(positions[None, :] - positions[:, None])
@@ -181,83 +387,80 @@
         precision=HIGHEST,
         preferred_element_type=jnp.float32,
     )
-    same_doc = segments[:, :, None] == segments[:, None, :]
-
-    def to_heads(matrix):
-        grouped = matrix.reshape(seq_size, micro_count, local_rows, heads_here, HEAD_DIM)
-        return grouped.transpose(1, 3, 0, 2, 4).reshape(micro_count, heads_here, seq_len, HEAD_DIM)
-
-    def from_heads(grouped):
-        split = grouped.reshape(micro_count, heads_here, seq_size, local_rows, HEAD_DIM)
-        return split.transpose(2, 0, 3, 1, 4).reshape(seq_len * micro_count, part)
+
+    def as_blocks(matrix):
+        return matrix.astype(jnp.bfloat16).reshape(seq_size, micro_count, local_rows, part)
 
     inputs = tokens.astype(jnp.float32)
     normed_one = gather_tokens(rms_norm(inputs, gains[0]).astype(jnp.bfloat16))
-    grad_out = gather_tokens(cotangent)
-    qkv = dot(normed_one, weight_qkv).astype(jnp.bfloat16)
-    query_h = to_heads(qkv[:, :part])
-    key_h = to_heads(qkv[:, part : 2 * part])
-    value_h = to_heads(qkv[:, 2 * part :])
-    scores = jnp.einsum("bhqd,bhkd->bhqk", query_h, key_h, preferred_element_type=jnp.float32)
-    scores = jnp.where(same_doc[:, None], scores + bias[None], NEG_BIG)
-    row_max = jnp.max(scores, axis=-1, keepdims=True)
-    exp_scores = jnp.exp(scores - row_max)
-    probs = exp_scores / jnp.sum(exp_scores, axis=-1, keepdims=True)
-    probs_low = probs.astype(jnp.bfloat16)
-    attended = from_heads(
-        jnp.einsum("bhqk,bhkd->bhqd", probs_low, value_h, preferred_element_type=jnp.float32)
-    ).astype(jnp.bfloat16)
-    hidden_state = inputs + scatter_tokens(dot_t(attended, weight_out), shape)
+    grad_out = gather_tokens(after(cotangent, normed_one))
+    query, key, value = [
+        as_blocks(dot(normed_one, attention_low[slot])) for slot in range(3)
+    ]
+    attended = attention_forward(query, key, value, bias, segments).reshape(-1, part)
+    attention_partial, feed_mine, grad_out = lax.optimization_barrier(
+        (dot_t(attended, weight_out).astype(jnp.bfloat16), feed_mine, grad_out)
+    )
+    feed_low = all_rows(feed_mine)
+    attention_out = scatter_tokens(attention_partial, shape)
+    weight_gate, weight_up, weight_down = feed_low[0], feed_low[1], feed_low[2]
+    hidden_state = inputs + attention_out
     normed_two = gather_tokens(rms_norm(hidden_state, gains[1]).astype(jnp.bfloat16))
-    pre = dot(normed_two, weight_in)
-    gate_pre = pre[:, :hidden_part]
-    up_pre = pre[:, hidden_part:]
+    gate_pre = dot(normed_two, weight_gate)
+    up_pre = dot(normed_two, weight_up)
     gate_act, gate_back = jax.vjp(gelu_tanh, gate_pre)
     inner = (gate_act * up_pre).astype(jnp.bfloat16)
-    block_rows = (hidden_state + scatter_tokens(dot_t(inner, weight_down), shape)).astype(jnp.bfloat16)
+    feed_partial = dot_t(inner, weight_down).astype(jnp.bfloat16)
     grad_inner = dot(grad_out, weight_down)
     grad_gate = gate_back(grad_inner * up_pre)[0].astype(jnp.bfloat16)
     grad_up = (grad_inner * gate_act).astype(jnp.bfloat16)
-    grad_pre = jnp.concatenate([grad_gate, grad_up], 1)
-    grad_normed_two = scatter_tokens(dot_t(grad_pre, weight_in), shape)
-    grad_feed = jnp.concatenate([outer_sum(normed_two, grad_pre), outer_sum(grad_out, inner)], 1)
-    feed_total = to_rows(grad_feed, 3)
+    grad_normed_two = scatter_tokens(
+        dot_t(grad_gate, weight_gate) + dot_t(grad_up, weight_up), shape
+    )
+    grads_feed = [
+        outer_sum(normed_two, grad_gate).astype(jnp.bfloat16),
+        outer_sum(normed_two, grad_up).astype(jnp.bfloat16),
+        outer_sum(grad_out, inner).astype(jnp.bfloat16),
+    ]
+    grad_normed_two, grads_feed = lax.optimization_barrier((grad_normed_two, grads_feed))
+    feed_first_step = to_rows_first(grads_feed)
     grad_hidden_norm, grad_gain_two = norm_back(hidden_state, gains[1], grad_normed_two)
     grad_hidden = cotangent.astype(jnp.float32) + grad_hidden_norm
     grad_branch = gather_tokens(grad_hidden.astype(jnp.bfloat16))
-    grad_attended = to_heads(dot(grad_branch, weight_out).astype(jnp.bfloat16))
-    grad_probs = jnp.einsum(
-        "bhqd,bhkd->bhqk", grad_attended, value_h, preferred_element_type=jnp.float32
-    )
-    row_dot = jnp.sum(probs * grad_probs, axis=-1, keepdims=True)
-    grad_scores = (probs * (grad_probs - row_dot)).astype(jnp.bfloat16)
-    grad_query = jnp.einsum("bhqk,bhkd->bhqd", grad_scores, key_h, preferred_element_type=jnp.float32)
-    grad_key = jnp.einsum("bhqk,bhqd->bhkd", grad_scores, query_h, preferred_element_type=jnp.float32)
-    grad_value = jnp.einsum(
-        "bhqk,bhqd->bhkd", probs_low, grad_attended, preferred_element_type=jnp.float32
-    )
+    grad_branch, feed_partial, feed_first_step = lax.optimization_barrier(
+        (grad_branch, feed_partial, feed_first_step)
+    )
+    block_rows = (hidden_state + scatter_tokens(feed_partial, shape)).astype(jnp.bfloat16)
+    grad_attended = as_blocks(dot(grad_branch, weight_out))
+    feed_mine_grad = scatter_dp_second(feed_first_step)
+    grad_query, grad_key, grad_value, score_sums = attention_backward(
+        query, key, value, grad_attended, bias, segments
+    )
+    grad_query, feed_mine_grad = lax.optimization_barrier((grad_query, feed_mine_grad))
     grad_table_here = jnp.einsum(
-        "bhij,zij->zh",
-        grad_scores,
+        "hij,zij->zh",
+        score_sums.astype(jnp.bfloat16),
         bucket_match.astype(jnp.bfloat16),
         preferred_element_type=jnp.float32,
     )
-    grad_qkv = jnp.concatenate(
-        [from_heads(item.astype(jnp.bfloat16)) for item in (grad_query, grad_key, grad_value)], 1
-    )
-    grad_normed_one = scatter_tokens(dot_t(grad_qkv, weight_qkv), shape)
-    grad_attention = jnp.concatenate(
-        [outer_sum(normed_one, grad_qkv), outer_sum(grad_branch, attended)], 1
-    )
-    attention_total = to_rows(grad_attention, 4)
+    grad_qkv = [item.reshape(-1, part) for item in (grad_query, grad_key, grad_value)]
+    grad_normed_one = scatter_tokens(
+        sum(dot_t(grad_qkv[slot], attention_low[slot]) for slot in range(3)), shape
+    )
+    attention_steps = to_rows_first(
+        [outer_sum(normed_one, item) for item in grad_qkv] + [outer_sum(grad_branch, attended)]
+    )
+    feed_total = to_rows_last(feed_mine_grad).transpose(1, 0, 2)
+    attention_total = to_rows_last(scatter_dp_second(attention_steps)).transpose(1, 0, 2)
     grad_input_norm, grad_gain_one = norm_back(inputs, gains[0], grad_normed_one)
     grad_rows = (grad_hidden + grad_input_norm).astype(jnp.bfloat16)
     grad_table = lax.dynamic_update_slice_in_dim(
         jnp.zeros((NUM_BUCKETS, HEADS), jnp.float32), grad_table_here, seq_index * heads_here, 1
     )
-    gains_total, table_total = lax.psum(
-        (jnp.stack([grad_gain_one, grad_gain_two], 0), grad_table), ("seq", "dp")
-    )
+    small = jnp.concatenate([grad_gain_one, grad_gain_two, grad_table.reshape(-1)])
+    small = sum_all(small.reshape(-1, 128)).reshape(-1)
+    gains_total = small[: 2 * width].reshape(2, width)
+    table_total = small[2 * width :].reshape(NUM_BUCKETS, HEADS)
     new_attention = adam_update(
         attention_weight,
         attention_first,

time: 1100 us -> 695 us (0.63)
  waiting for transfers between devices: 574 us -> 338 us
  blocking collectives: 179 us -> 0 us
  local copies, waits for them, and re-layouts: 136 us -> 56.2 us
  starting transfers between devices: 10 us -> 78.7 us
  Pallas kernels: 0 us -> 40.1 us
  matrix products: 129 us -> 99.7 us
    ppermute x0 -> x53, waiting for transfers between devices: none -> 216 us  [swap(): return lax.ppermute(value, axis, partner_pairs(axis, offset))]
    unnamed x12 -> x8, waiting for transfers between devices: 215 us -> 0.13 us
    all_gather x2 -> x0, waiting for transfers between devices: 115 us -> none  [to_columns(): full = lax.all_gather(mine, 'dp', axis=0)]
    all_to_all x2 -> x0, blocking collectives: 110 us -> none  [to_columns(): mine = lax.all_to_all(send, 'seq', 0, 0)]
    all_gather x4, waiting for transfers between devices: 126 us -> 29.5 us  [gather_tokens(): full = lax.all_gather(local_rows, 'seq', axis=0)]
    ppermute x0 -> x53, starting transfers between devices: none -> 77.4 us  [swap(): return lax.ppermute(value, axis, partner_pairs(axis, offset))]
    psum x1 -> x0, blocking collectives: 69.2 us -> none  [local(): lax.psum((jnp.stack([grad_gain_one, grad_gain_two], 0), grad_table), ('se...]
    reshape x21 -> x4, local copies, waits for them, and re-layouts: 49 us -> 1.94 us  [the longest x1 1.79 us: to_columns(): weight.astype(jnp.bfloat16).reshape(slots, rows, seq_size, part)]
  transfers between devices with their start and end apart: 13 -> 61, of which waited for: 11 -> 26; matrix products, arithmetic and copies ran while one was open for 14% -> 24% of each run, Pallas kernels for 0% -> 6%
where the time goes in v2:
time: 695 us; the launch traced here: 685 us
  waiting for transfers between devices  338 us (49%)
  matrix products  99.7 us (14%)
  starting transfers between devices  78.7 us (11%)
  other arithmetic  57.3 us (8%)
  local copies, waits for them, and re-layouts  56.2 us (8%)
  Pallas kernels  40.1 us (6%)
  between operations  16 us (2%)
    ppermute x53, waiting for transfers between devices, swap(): return lax.ppermute(value, axis, partner_pairs(axis, offset))  216 us
    reduce_scatter x4, waiting for transfers between devices, scatter_tokens(): lax.psum_scatter(send, 'seq', scatter_dimension=0).astype(jnp.float32)  91.8 us
    ppermute x53, starting transfers between devices, swap(): return lax.ppermute(value, axis, partner_pairs(axis, offset))  77.4 us
    dot_general x7, matrix products, outer_sum(): lax.dot_general(left, right, (((0,), (0,)), ((), ())), preferred_element_...  30.2 us
    all_gather x4, waiting for transfers between devices, gather_tokens(): full = lax.all_gather(local_rows, 'seq', axis=0)  29.5 us
    dot_general x7, matrix products, dot(): return jnp.dot(left, right, preferred_element_type=jnp.float32)  27 us
    dot_general x7, matrix products, dot_t(): lax.dot_general(left, right, (((1,), (1,)), ((), ())), preferred_element_...  24.9 us
    unnamed x154, local copies, waits for them, and re-layouts  20.3 us
  transfers between devices with their start and end apart: 61, of which 26 were waited for; matrix products, arithmetic and copies ran while one was open for 24% of the time, Pallas kernels for 6%

profile of v2, /device:TPU:0, one launch (start us, length us, event | category | flops | bytes accessed | tf_op | source)
XLA Modules:
  0.0 685.4 jit_solution(4256177100717071607)
XLA Ops:
  17.7 2.7 collective-permute-start.1
  20.7 2.8 collective-permute-start.3
  24.1 10.4 %fusion.1 = f32[4,512,512]{2,0,1:T(4,128)S(1)} fusion(s32[512,512]{1,0:T(8,128)S(1)} %fusion.34, f32[32,32]{1,0:T(8,128)S(1)} %copy-done.41, s32[]{:T(128)S(6)} %select_n.132), kind=kOutput, calls=%fused_computation.2 | convolution fusion | flops 411041792 | bytes 5246980 | tf_op jit(solution)/shard_map/atj,ao->otj/dot_general | solution.py:383
  34.6 3.3 copy.156.bias_ref
  39.5 2.4 convert_bitcast_fusion
  42.0 29.5 %all-gather.9.cloned.1.call-done = bf16[16,64,2048]{2,1,0:T(8,128)(2,1)} async-done(((bf16[2,64,2048]{2,1,0:T(8,128)(2,1)}), bf16[16,64,2048]{2,1,0:T(8,128)(2,1)}) %all-gather.9.cloned.1.call-update) | async-done | bytes 4194320 | tf_op jit(solution)/shard_map/all_gather | solution.py:337
  72.0 2.5 collective-permute-start.5
  79.7 3.4 collective-permute-done.6
  86.7 4.6 constant_dynamic-slice_fusion.8
  91.4 5.0 collective-permute-start.12
  97.7 2.8 collective-permute-start.14
  100.5 23.8 %collective-permute-done.12 = bf16[3,64,640]{2,1,0:T(8,128)(2,1)S(1)} collective-permute-done((bf16[3,64,640]{2,1,0:T(8,128)(2,1)S(1)}, bf16[3,64,640]{2,1,0:T(8,128)(2,1)S(1)}, u32[]{:S(2)}, u32[]{:S(2)}) %collective-permute-start.12) | collective-permute-done | bytes 245792 | tf_op jit(solution)/shard_map/ppermute | solution.py:113
  124.5 10.1 %collective-permute-done.13 = bf16[3,64,640]{2,1,0:T(8,128)(2,1)S(1)} collective-permute-done((bf16[3,64,640]{2,1,0:T(8,128)(2,1)S(1)}, bf16[3,64,640]{2,1,0:T(8,128)(2,1)S(1)}, u32[]{:S(2)}, u32[]{:S(2)}) %collective-permute-start.13) | collective-permute-done | bytes 245792 | tf_op jit(solution)/shard_map/ppermute | solution.py:113
  134.6 2.5 collective-permute-start.16
  138.0 15.3 %collective-permute-done.15 = bf16[3,64,640]{2,1,0:T(8,128)(2,1)S(1)} collective-permute-done((bf16[3,64,640]{2,1,0:T(8,128)(2,1)S(1)}, bf16[3,64,640]{2,1,0:T(8,128)(2,1)S(1)}, u32[]{:S(2)}, u32[]{:S(2)}) %collective-permute-start.15) | collective-permute-done | bytes 245792 | tf_op jit(solution)/shard_map/ppermute | solution.py:113
  155.9 11.7 %collective-permute-done.9 = bf16[4,4,64,256]{3,2,1,0:T(8,128)(2,1)S(1)} collective-permute-done((bf16[4,4,64,256]{3,2,1,0:T(8,128)(2,1)S(1)}, bf16[4,4,64,256]{3,2,1,0:T(8,128)(2,1)S(1)}, u32[]{:S(2)}, u32[]{:S(2)}) %collective-permute-start.9) | collective-permute-done | bytes 524320 | tf_op jit(solution)/shard_map/ppermute | solution.py:113
  169.0 3.1 copy-done.49
  178.2 13.4 %shard_map.280 = bf16[8,2,64,256]{3,2,1,0:T(8,128)(2,1)} custom-call(bf16[8,2,64,256]{3,2,1,0:T(8,128)(2,1)} %bitcast.427, bf16[8,2,64,256]{3,2,1,0:T(8,128)(2,1)} %bitcast.425, bf16[8,2,64,256]{3,2,1,0:T(8,128)(2,1)} %bitcast.423, f32[4,512,512]{2,1,0:T(8,128)} %copy.156.bias_ref, s32[2,512,1]{2,1,0:T(8,128)} %copy.157.seg_q_ref, ...), custom_call_target="tpu_custom_call" | custom-call | tf_op jit(solution)/shard_map/pallas_call | solution.py:180
  191.6 4.3 convolution_convert_fusion.1
  196.0 57.8 %reduce-scatter.5.cloned.1.call-done = bf16[1,2,64,2048]{3,2,1,0:T(8,128)(2,1)} async-done(((bf16[8,2,64,2048]{3,2,1,0:T(8,128)(2,1)}), bf16[1,2,64,2048]{3,2,1,0:T(8,128)(2,1)}) %reduce-scatter.5.cloned.1.call-update) | async-done | bytes 524304 | tf_op jit(solution)/shard_map/reduce_scatter | solution.py:343
  260.2 39.5 %collective-permute-done.18 = bf16[3,8,64,640]{3,2,1,0:T(8,128)(2,1)S(1)} collective-permute-done((bf16[3,8,64,640]{3,2,1,0:T(8,128)(2,1)S(1)}, bf16[3,8,64,640]{3,2,1,0:T(8,128)(2,1)S(1)}, u32[]{:S(2)}, u32[]{:S(2)}) %collective-permute-start.18) | collective-permute-done | bytes 1966112 | tf_op jit(solution)/shard_map/ppermute | solution.py:113
  305.2 16.8 %collective-permute-done.20 = bf16[3,4,64,640]{3,2,1,0:T(8,128)(2,1)S(1)} collective-permute-done((bf16[3,4,64,640]{3,2,1,0:T(8,128)(2,1)S(1)}, bf16[3,4,64,640]{3,2,1,0:T(8,128)(2,1)S(1)}, u32[]{:S(2)}, u32[]{:S(2)}) %collective-permute-start.20) | collective-permute-done | bytes 983072 | tf_op jit(solution)/shard_map/ppermute | solution.py:113
  326.1 4.9 fusion.78
  331.0 5.3 fusion.79
  336.4 6.1 multiply_convert_fusion
  342.5 3.4 fusion.80
  345.9 5.0 add_convert_fusion.1
  352.3 7.3 %convolution_convert_fusion.3 = bf16[2048,640]{1,0:T(8,128)(2,1)} fusion(bf16[1024,2048]{1,0:T(8,128)(2,1)} %bitcast.470, bf16[1024,640]{1,0:T(8,128)(2,1)S(1)} %copy-done.58), kind=kOutput, calls=%fused_computation.19 | convolution fusion | flops 2685665280 | bytes 8126464 | tf_op jit(solution)/shard_map/dot_general | solution.py:91
  359.6 4.9 convolution_convert_fusion.4
  364.5 4.8 convolution_convert_fusion.2
  369.4 34.0 %reduce-scatter.7.cloned.1.call-done = bf16[1,2,64,2048]{3,2,1,0:T(8,128)(2,1)} async-done(((bf16[8,2,64,2048]{3,2,1,0:T(8,128)(2,1)}), bf16[1,2,64,2048]{3,2,1,0:T(8,128)(2,1)}) %reduce-scatter.7.cloned.1.call-update) | async-done | bytes 524304 | tf_op jit(solution)/shard_map/reduce_scatter | solution.py:343
  406.6 4.2 pad_maximum_fusion
  418.4 5.1 convolution_convert_fusion
  423.5 13.6 %collective-permute-done.23 = bf16[3,4,64,640]{3,2,0,1:T(8,128)(2,1)S(1)} collective-permute-done((bf16[3,4,64,640]{3,2,0,1:T(8,128)(2,1)S(1)}, bf16[3,4,64,640]{3,2,0,1:T(8,128)(2,1)S(1)}, u32[]{:S(2)}, u32[]{:S(2)}) %collective-permute-start.23) | collective-permute-done | bytes 983072 | tf_op jit(solution)/shard_map/ppermute | solution.py:113
  439.9 16.2 %collective-permute-done.24 = bf16[3,4,64,640]{3,2,0,1:T(8,128)(2,1)S(1)} collective-permute-done((bf16[3,4,64,640]{3,2,0,1:T(8,128)(2,1)S(1)}, bf16[3,4,64,640]{3,2,0,1:T(8,128)(2,1)S(1)}, u32[]{:S(2)}, u32[]{:S(2)}) %collective-permute-start.24) | collective-permute-done | bytes 983072 | tf_op jit(solution)/shard_map/ppermute | solution.py:113
  456.1 2.5 convert_add_fusion
  460.6 4.5 convolution_convert_fusion.6
  465.2 15.4 %shard_map.281 = (bf16[8,2,64,256]{3,2,1,0:T(8,128)(2,1)}, bf16[8,2,64,256]{3,2,1,0:T(8,128)(2,1)}, bf16[8,2,64,256]{3,2,1,0:T(8,128)(2,1)}, f32[4,512,512]{2,1,0:T(8,128)}) custom-call(bf16[8,2,64,256]{3,2,1,0:T(8,128)(2,1)} %bitcast.428, bf16[8,2,64,256]{3,2,1,0:T(8,128)(2,1)} %bitcast.426, bf16[8,2,64,256]{3,2,1,0:T(8,128)(2,1)} %bitcast.424, ...), custom_call_target="tpu_custom_call" | custom-call | tf_op jit(solution)/shard_map/pallas_call | solution.py:217
  480.6 2.5 fusion.82
  488.5 3.3 add_convert_fusion
  491.9 3.8 convert_element_type.323
  495.6 7.2 %fusion.24 = f32[32,4]{1,0:T(8,128)S(1)} fusion(bf16[4,512,512]{2,1,0:T(8,128)(2,1)} %convert_element_type.323, s32[512,512]{1,0:T(8,128)} %copy-done.26), kind=kOutput, calls=%fused_computation.91 | convolution fusion | flops 75497472 | bytes 3146240 | tf_op jit(solution)/shard_map/hij,zij->zh/dot_general | solution.py:440
  503.4 4.7 convolution_convert_fusion.5
  513.8 3.7 fusion.13
  527.8 2.9 collective-permute-start.46
  530.7 15.6 %collective-permute-done.42 = bf16[3,64,640]{2,1,0:T(8,128)(2,1)S(1)} collective-permute-done((bf16[3,64,640]{2,1,0:T(8,128)(2,1)S(1)}, bf16[3,64,640]{2,1,0:T(8,128)(2,1)S(1)}, u32[]{:S(2)}, u32[]{:S(2)}) %collective-permute-start.42) | collective-permute-done | bytes 245792 | tf_op jit(solution)/shard_map/ppermute | solution.py:113
  546.5 10.6 %collective-permute-done.43 = bf16[3,64,640]{2,1,0:T(8,128)(2,1)S(1)} collective-permute-done((bf16[3,64,640]{2,1,0:T(8,128)(2,1)S(1)}, bf16[3,64,640]{2,1,0:T(8,128)(2,1)S(1)}, u32[]{:S(2)}, u32[]{:S(2)}) %collective-permute-start.43) | collective-permute-done | bytes 245792 | tf_op jit(solution)/shard_map/ppermute | solution.py:113
  560.8 6.4 collective-permute-done.46
  568.7 3.5 collective-permute-done.47
  573.5 6.1 shard_map.283
  585.2 8.4 %multiply_subtract_fusion = (f32[64,3,5120]{2,0,1:T(8,128)}, f32[64,3,5120]{2,0,1:T(8,128)}, f32[64,3,5120]{2,0,1:T(8,128)}) fusion(f32[64,3,5120]{2,0,1:T(8,128)S(1)} %copy-done.1, f32[3]{0:T(128)S(1)} %copy-done.48, bf16[3,64,5120]{2,1,0:T(8,128)(2,1)S(1)} %copy-done.8, f32[64,3,5120]{2,0,1:T(8,128)} %param.24, f32[64,3,5120]{2,0,1:T(8,128)} %param.25), kind=kLoop, calls=%fused_computation.13 | loop fusion | flops 15728640 | bytes 25559052 | tf_op jit(solution)/shard_map/sub | solution.py:65
  594.9 2.4 collective-permute-done.30
  600.3 10.6 %collective-permute-start.35 = (bf16[4,64,256]{2,1,0:T(8,128)(2,1)S(1)}, bf16[4,64,256]{2,1,0:T(8,128)(2,1)S(1)}, u32[]{:S(2)}, u32[]{:S(2)}) collective-permute-start(bf16[4,64,256]{2,1,0:T(8,128)(2,1)S(1)} %get-tuple-element.174), channel_id=1, source_target_pairs={{0,8},{4,12},{8,0},{12,4},{16,24},{20,28},{24,16},{28,20},{1,9},{5... | collective-permute-start | bytes 393224 | tf_op jit(solution)/shard_map/ppermute | solution.py:113
  610.9 2.7 collective-permute-start.37
  615.2 3.5 collective-permute-done.35
  621.2 8.0 %collective-permute-done.36 = bf16[4,64,256]{2,1,0:T(8,128)(2,1)S(1)} collective-permute-done((bf16[4,64,256]{2,1,0:T(8,128)(2,1)S(1)}, bf16[4,64,256]{2,1,0:T(8,128)(2,1)S(1)}, u32[]{:S(2)}, u32[]{:S(2)}) %collective-permute-start.36) | collective-permute-done | bytes 131104 | tf_op jit(solution)/shard_map/ppermute | solution.py:113
  630.6 9.1 %collective-permute-done.38 = bf16[4,64,256]{2,1,0:T(8,128)(2,1)S(1)} collective-permute-done((bf16[4,64,256]{2,1,0:T(8,128)(2,1)S(1)}, bf16[4,64,256]{2,1,0:T(8,128)(2,1)S(1)}, u32[]{:S(2)}, u32[]{:S(2)}) %collective-permute-start.38) | collective-permute-done | bytes 131104 | tf_op jit(solution)/shard_map/ppermute | solution.py:113
  644.5 5.2 shard_map.282
  649.7 4.1 collective-permute-start.49
  653.8 7.1 %multiply_subtract_fusion.1 = (f32[64,4,2048]{2,0,1:T(8,128)S(1)}, f32[64,4,2048]{2,0,1:T(8,128)S(1)}, f32[64,4,2048]{2,0,1:T(8,128)S(1)}) fusion(f32[64,4,2048]{2,1,0:T(4,128)S(1)} %copy-done.4, f32[4]{0:T(128)S(1)} %copy-done.47, bf16[4,64,2048]{2,1,0:T(8,128)(2,1)} %shard_map.282, f32[64,4,2048]{2,1,0:T(4,128)} %param.21, f32[64,4,2048]{2,1,0:T(4,128)} %param.22), kind=kLoop, calls=%fused_computation.45 | loop fusion | flops 8388608 | bytes 13631504 | tf_op jit(solution)/shard_map/sub | solution.py:65
  663.1 2.7 copy.186
  665.8 2.7 copy.187
  669.6 2.8 collective-permute-done.51
  673.9 2.8 fusion.29
  (358 shorter events, 122.1 us)
Async XLA Ops:
  7.2 64.3 %all-gather.9.cloned.1.call-start = ((), (), s32[]{:S(2)}) async-start(), calls=%async_computation.8 | async-start | bytes 4718592 | tf_op jit(solution)/shard_map/all_gather | solution.py:337
  11.4 184.5 %all-gather.11.cloned.1.call-start = ((), (), s32[]{:S(2)}) async-start(), calls=%async_computation.9 | async-start | bytes 4718592 | tf_op jit(solution)/shard_map/all_gather | solution.py:337
  17.2 54.9 %collective-permute-start = (bf16[4,64,256]{2,1,0:T(8,128)(2,1)S(1)}, bf16[4,64,256]{2,1,0:T(8,128)(2,1)}, u32[]{:S(2)}, u32[]{:S(2)}) collective-permute-start(bf16[4,64,256]{2,1,0:T(8,128)(2,1)S(1)} %bitcast.455), channel_id=1, source_target_pairs={{0,4},{4,0},{8,12},{12,8},{16,20},{20,16},{24,28},{28,24},{1,5},{5... | collective-permute-start | bytes 393224 | tf_op jit(solution)/shard_map/ppermute | solution.py:113
  17.7 57.8 %collective-permute-start.1 = (bf16[4,64,256]{2,1,0:T(8,128)(2,1)S(1)}, bf16[4,64,256]{2,1,0:T(8,128)(2,1)}, u32[]{:S(2)}, u32[]{:S(2)}) collective-permute-start(bf16[4,64,256]{2,1,0:T(8,128)(2,1)S(1)} %bitcast.454), channel_id=1, source_target_pairs={{0,8},{4,12},{8,0},{12,4},{16,24},{20,28},{24,16},{28,20},{1,9},{5... | collective-permute-start | bytes 393224 | tf_op jit(solution)/shard_map/ppermute | solution.py:113
  20.4 57.0 %collective-permute-start.2 = (bf16[4,64,256]{2,1,0:T(8,128)(2,1)S(1)}, bf16[4,64,256]{2,1,0:T(8,128)(2,1)}, u32[]{:S(2)}, u32[]{:S(2)}) collective-permute-start(bf16[4,64,256]{2,1,0:T(8,128)(2,1)S(1)} %bitcast.453), channel_id=1, source_target_pairs={{0,12},{4,8},{8,4},{12,0},{16,28},{20,24},{24,20},{28,16},{1,13},{... | collective-permute-start | bytes 393224 | tf_op jit(solution)/shard_map/ppermute | solution.py:113
  20.7 57.7 %collective-permute-start.3 = (bf16[4,64,256]{2,1,0:T(8,128)(2,1)S(1)}, bf16[4,64,256]{2,1,0:T(8,128)(2,1)}, u32[]{:S(2)}, u32[]{:S(2)}) collective-permute-start(bf16[4,64,256]{2,1,0:T(8,128)(2,1)S(1)} %bitcast.452), channel_id=1, source_target_pairs={{0,16},{4,20},{8,24},{12,28},{16,0},{20,4},{24,8},{28,12},{1,17},{... | collective-permute-start | bytes 393224 | tf_op jit(solution)/shard_map/ppermute | solution.py:113
  23.5 55.8 %collective-permute-start.4 = (bf16[4,64,256]{2,1,0:T(8,128)(2,1)S(1)}, bf16[4,64,256]{2,1,0:T(8,128)(2,1)S(1)}, u32[]{:S(2)}, u32[]{:S(2)}) collective-permute-start(bf16[4,64,256]{2,1,0:T(8,128)(2,1)S(1)} %bitcast.451), channel_id=1, source_target_pairs={{0,20},{4,16},{8,28},{12,24},{16,4},{20,0},{24,12},{28,8},{1,21},{... | collective-permute-start | bytes 393224 | tf_op jit(solution)/shard_map/ppermute | solution.py:113
  71.5 182.3 %reduce-scatter.5.cloned.1.call-start = ((), (), s32[]{:S(2)}) async-start(), calls=%async_computation.4 | async-start | bytes 4718592 | tf_op jit(solution)/shard_map/reduce_scatter | solution.py:343
  72.0 7.6 %collective-permute-start.5 = (bf16[4,64,256]{2,1,0:T(8,128)(2,1)S(1)}, bf16[4,64,256]{2,1,0:T(8,128)(2,1)S(1)}, u32[]{:S(2)}, u32[]{:S(2)}) collective-permute-start(bf16[4,64,256]{2,1,0:T(8,128)(2,1)S(1)} %bitcast.457), channel_id=1, source_target_pairs={{0,24},{4,28},{8,16},{12,20},{16,8},{20,12},{24,0},{28,4},{1,25},{... | collective-permute-start | bytes 393224 | tf_op jit(solution)/shard_map/ppermute | solution.py:113
  75.5 7.6 %collective-permute-start.6 = (bf16[4,64,256]{2,1,0:T(8,128)(2,1)S(1)}, bf16[4,64,256]{2,1,0:T(8,128)(2,1)S(1)}, u32[]{:S(2)}, u32[]{:S(2)}) collective-permute-start(bf16[4,64,256]{2,1,0:T(8,128)(2,1)S(1)} %bitcast.456), channel_id=1, source_target_pairs={{0,28},{4,24},{8,20},{12,16},{16,12},{20,8},{24,4},{28,0},{1,29},{... | collective-permute-start | bytes 393224 | tf_op jit(solution)/shard_map/ppermute | solution.py:113
  83.1 70.4 %collective-permute-start.7 = (bf16[4,8,64,256]{3,2,1,0:T(8,128)(2,1)S(1)}, bf16[4,8,64,256]{3,2,1,0:T(8,128)(2,1)S(1)}, u32[]{:S(2)}, u32[]{:S(2)}) collective-permute-start(bf16[4,8,64,256]{3,2,1,0:T(8,128)(2,1)S(1)} %bitcast_dynamic-update-slice_fusion.27), channel_id=1, source_target_pairs={{0,1},{1,0},{2,3},{3,2},{4,5},{5,4},{6,7},{7,6},{8,9},{9,8},{10,11... | collective-permute-start | bytes 3145736 | tf_op jit(solution)/shard_map/ppermute | solution.py:113
  84.9 69.6 %collective-permute-start.8 = (bf16[4,8,64,256]{3,2,1,0:T(8,128)(2,1)S(1)}, bf16[4,8,64,256]{3,2,1,0:T(8,128)(2,1)S(1)}, u32[]{:S(2)}, u32[]{:S(2)}) collective-permute-start(bf16[4,8,64,256]{3,2,1,0:T(8,128)(2,1)S(1)} %bitcast_dynamic-update-slice_fusion.27), channel_id=1, source_target_pairs={{0,2},{1,3},{2,0},{3,1},{4,6},{5,7},{6,4},{7,5},{8,10},{9,11},{10,... | collective-permute-start | bytes 3145736 | tf_op jit(solution)/shard_map/ppermute | solution.py:113
  91.3 6.4 collective-permute-start.11
  91.4 32.9 %collective-permute-start.12 = (bf16[3,64,640]{2,1,0:T(8,128)(2,1)S(1)}, bf16[3,64,640]{2,1,0:T(8,128)(2,1)S(1)}, u32[]{:S(2)}, u32[]{:S(2)}) collective-permute-start(bf16[3,64,640]{2,1,0:T(8,128)(2,1)S(1)} %bitcast.442), channel_id=1, source_target_pairs={{0,8},{4,12},{8,0},{12,4},{16,24},{20,28},{24,16},{28,20},{1,9},{5... | collective-permute-start | bytes 737288 | tf_op jit(solution)/shard_map/ppermute | solution.py:113
  96.4 38.2 %collective-permute-start.13 = (bf16[3,64,640]{2,1,0:T(8,128)(2,1)S(1)}, bf16[3,64,640]{2,1,0:T(8,128)(2,1)S(1)}, u32[]{:S(2)}, u32[]{:S(2)}) collective-permute-start(bf16[3,64,640]{2,1,0:T(8,128)(2,1)S(1)} %bitcast.440), channel_id=1, source_target_pairs={{0,12},{4,8},{8,4},{12,0},{16,28},{20,24},{24,20},{28,16},{1,13},{... | collective-permute-start | bytes 737288 | tf_op jit(solution)/shard_map/ppermute | solution.py:113
  97.7 39.4 %collective-permute-start.14 = (bf16[3,64,640]{2,1,0:T(8,128)(2,1)S(1)}, bf16[3,64,640]{2,1,0:T(8,128)(2,1)S(1)}, u32[]{:S(2)}, u32[]{:S(2)}) collective-permute-start(bf16[3,64,640]{2,1,0:T(8,128)(2,1)S(1)} %bitcast.441), channel_id=1, source_target_pairs={{0,16},{4,20},{8,24},{12,28},{16,0},{20,4},{24,8},{28,12},{1,17},{... | collective-permute-start | bytes 737288 | tf_op jit(solution)/shard_map/ppermute | solution.py:113
  124.3 29.0 %collective-permute-start.15 = (bf16[3,64,640]{2,1,0:T(8,128)(2,1)S(1)}, bf16[3,64,640]{2,1,0:T(8,128)(2,1)S(1)}, u32[]{:S(2)}, u32[]{:S(2)}) collective-permute-start(bf16[3,64,640]{2,1,0:T(8,128)(2,1)S(1)} %bitcast.439), channel_id=1, source_target_pairs={{0,20},{4,16},{8,28},{12,24},{16,4},{20,0},{24,12},{28,8},{1,21},{... | collective-permute-start | bytes 737288 | tf_op jit(solution)/shard_map/ppermute | solution.py:113
  134.6 18.8 %collective-permute-start.16 = (bf16[3,64,640]{2,1,0:T(8,128)(2,1)S(1)}, bf16[3,64,640]{2,1,0:T(8,128)(2,1)S(1)}, u32[]{:S(2)}, u32[]{:S(2)}) collective-permute-start(bf16[3,64,640]{2,1,0:T(8,128)(2,1)S(1)} %bitcast.438), channel_id=1, source_target_pairs={{0,24},{4,28},{8,16},{12,20},{16,8},{20,12},{24,0},{28,4},{1,25},{... | collective-permute-start | bytes 737288 | tf_op jit(solution)/shard_map/ppermute | solution.py:113
  137.1 16.3 %collective-permute-start.17 = (bf16[3,64,640]{2,1,0:T(8,128)(2,1)S(1)}, bf16[3,64,640]{2,1,0:T(8,128)(2,1)S(1)}, u32[]{:S(2)}, u32[]{:S(2)}) collective-permute-start(bf16[3,64,640]{2,1,0:T(8,128)(2,1)S(1)} %bitcast.437), channel_id=1, source_target_pairs={{0,28},{4,24},{8,20},{12,16},{16,12},{20,8},{24,4},{28,0},{1,29},{... | collective-permute-start | bytes 737288 | tf_op jit(solution)/shard_map/ppermute | solution.py:113
  153.6 14.0 %collective-permute-start.9 = (bf16[4,4,64,256]{3,2,1,0:T(8,128)(2,1)S(1)}, bf16[4,4,64,256]{3,2,1,0:T(8,128)(2,1)S(1)}, u32[]{:S(2)}, u32[]{:S(2)}) collective-permute-start(bf16[4,4,64,256]{3,2,1,0:T(8,128)(2,1)S(1)} %slice.146), channel_id=1, source_target_pairs={{0,2},{1,3},{2,0},{3,1},{4,6},{5,7},{6,4},{7,5},{8,10},{9,11},{10,... | collective-permute-start | bytes 1572872 | tf_op jit(solution)/shard_map/ppermute | solution.py:113
  154.5 13.8 %collective-permute-start.10 = (bf16[4,4,64,256]{3,2,1,0:T(8,128)(2,1)S(1)}, bf16[4,4,64,256]{3,2,1,0:T(8,128)(2,1)S(1)}, u32[]{:S(2)}, u32[]{:S(2)}) collective-permute-start(bf16[4,4,64,256]{3,2,1,0:T(8,128)(2,1)S(1)} %slice.147), channel_id=1, source_target_pairs={{0,1},{1,0},{2,3},{3,2},{4,5},{5,4},{6,7},{7,6},{8,9},{9,8},{10,11... | collective-permute-start | bytes 1572872 | tf_op jit(solution)/shard_map/ppermute | solution.py:113
  195.9 57.9 %copy-start = (bf16[2,64,2048]{2,1,0:T(8,128)(2,1)S(1)}, bf16[2,64,2048]{2,1,0:T(8,128)(2,1)}, u32[]{:S(2)}) copy-start(bf16[2,64,2048]{2,1,0:T(8,128)(2,1)} %param.17) | copy-start | bytes 1572868
  195.9 135.1 %all-gather.13.cloned.1.call-start = ((), (), s32[]{:S(2)}) async-start(), calls=%async_computation.10 | async-start | bytes 4718592 | tf_op jit(solution)/shard_map/all_gather | solution.py:337
  257.2 146.2 %reduce-scatter.7.cloned.1.call-start = ((), (), s32[]{:S(2)}) async-start(), calls=%async_computation.5 | async-start | bytes 4718592 | tf_op jit(solution)/shard_map/reduce_scatter | solution.py:343
  257.2 42.5 %collective-permute-start.18 = (bf16[3,8,64,640]{3,2,1,0:T(8,128)(2,1)S(1)}, bf16[3,8,64,640]{3,2,1,0:T(8,128)(2,1)S(1)}, u32[]{:S(2)}, u32[]{:S(2)}) collective-permute-start(bf16[3,8,64,640]{3,2,1,0:T(8,128)(2,1)S(1)} %bitcast_dynamic-update-slice_fusion.11), channel_id=1, source_target_pairs={{0,1},{1,0},{2,3},{3,2},{4,5},{5,4},{6,7},{7,6},{8,9},{9,8},{10,11... | collective-permute-start | bytes 5898248 | tf_op jit(solution)/shard_map/ppermute | solution.py:113
  258.7 43.6 %collective-permute-start.19 = (bf16[3,8,64,640]{3,2,1,0:T(8,128)(2,1)S(1)}, bf16[3,8,64,640]{3,2,1,0:T(8,128)(2,1)S(1)}, u32[]{:S(2)}, u32[]{:S(2)}) collective-permute-start(bf16[3,8,64,640]{3,2,1,0:T(8,128)(2,1)S(1)} %bitcast_dynamic-update-slice_fusion.11), channel_id=1, source_target_pairs={{0,2},{1,3},{2,0},{3,1},{4,6},{5,7},{6,4},{7,5},{8,10},{9,11},{10,... | collective-permute-start | bytes 5898248 | tf_op jit(solution)/shard_map/ppermute | solution.py:113
  299.8 22.2 %collective-permute-start.20 = (bf16[3,4,64,640]{3,2,1,0:T(8,128)(2,1)S(1)}, bf16[3,4,64,640]{3,2,1,0:T(8,128)(2,1)S(1)}, u32[]{:S(2)}, u32[]{:S(2)}) collective-permute-start(bf16[3,4,64,640]{3,2,1,0:T(8,128)(2,1)S(1)} %slice.152), channel_id=1, source_target_pairs={{0,2},{1,3},{2,0},{3,1},{4,6},{5,7},{6,4},{7,5},{8,10},{9,11},{10,... | collective-permute-start | bytes 2949128 | tf_op jit(solution)/shard_map/ppermute | solution.py:113
  302.5 19.6 %collective-permute-start.21 = (bf16[3,4,64,640]{3,2,1,0:T(8,128)(2,1)S(1)}, bf16[3,4,64,640]{3,2,1,0:T(8,128)(2,1)S(1)}, u32[]{:S(2)}, u32[]{:S(2)}) collective-permute-start(bf16[3,4,64,640]{3,2,1,0:T(8,128)(2,1)S(1)} %slice.153), channel_id=1, source_target_pairs={{0,1},{1,0},{2,3},{3,2},{4,5},{5,4},{6,7},{7,6},{8,9},{9,8},{10,11... | collective-permute-start | bytes 2949128 | tf_op jit(solution)/shard_map/ppermute | solution.py:113
  351.0 107.6 %all-gather.15.cloned.1.call-start = ((), (), s32[]{:S(2)}) async-start(), calls=%async_computation.11 | async-start | bytes 4718592 | tf_op jit(solution)/shard_map/all_gather | solution.py:337
  406.2 234.9 %reduce-scatter.11.cloned.1.call-start = ((), (), s32[]{:S(2)}) async-start(), calls=%async_computation.7 | async-start | bytes 4718592 | tf_op jit(solution)/shard_map/reduce_scatter | solution.py:343
  412.4 24.8 %collective-permute-start.23 = (bf16[3,4,64,640]{3,2,0,1:T(8,128)(2,1)S(1)}, bf16[3,4,64,640]{3,2,0,1:T(8,128)(2,1)S(1)}, u32[]{:S(2)}, u32[]{:S(2)}) collective-permute-start(bf16[3,4,64,640]{3,2,0,1:T(8,128)(2,1)S(1)} %get-tuple-element.162), channel_id=1, source_target_pairs={{0,2},{1,3},{2,0},{3,1},{4,6},{5,7},{6,4},{7,5},{8,10},{9,11},{10,... | collective-permute-start | bytes 2949128 | tf_op jit(solution)/shard_map/ppermute | solution.py:113
  414.0 24.7 %collective-permute-start.22 = (bf16[3,4,64,640]{3,2,0,1:T(8,128)(2,1)S(1)}, bf16[3,4,64,640]{3,2,0,1:T(8,128)(2,1)S(1)}, u32[]{:S(2)}, u32[]{:S(2)}) collective-permute-start(bf16[3,4,64,640]{3,2,0,1:T(8,128)(2,1)S(1)} %get-tuple-element.163), channel_id=1, source_target_pairs={{0,1},{1,0},{2,3},{3,2},{4,5},{5,4},{6,7},{7,6},{8,9},{9,8},{10,11... | collective-permute-start | bytes 2949128 | tf_op jit(solution)/shard_map/ppermute | solution.py:113
  415.7 40.4 %collective-permute-start.24 = (bf16[3,4,64,640]{3,2,0,1:T(8,128)(2,1)S(1)}, bf16[3,4,64,640]{3,2,0,1:T(8,128)(2,1)S(1)}, u32[]{:S(2)}, u32[]{:S(2)}) collective-permute-start(bf16[3,4,64,640]{3,2,0,1:T(8,128)(2,1)S(1)} %slice.162), channel_id=1, source_target_pairs={{0,1},{1,0},{2,3},{3,2},{4,5},{5,4},{6,7},{7,6},{8,9},{9,8},{10,11... | collective-permute-start | bytes 2949128 | tf_op jit(solution)/shard_map/ppermute | solution.py:113
  416.6 39.5 %collective-permute-start.25 = (bf16[3,4,64,640]{3,2,0,1:T(8,128)(2,1)S(1)}, bf16[3,4,64,640]{3,2,0,1:T(8,128)(2,1)S(1)}, u32[]{:S(2)}, u32[]{:S(2)}) collective-permute-start(bf16[3,4,64,640]{3,2,0,1:T(8,128)(2,1)S(1)} %slice.164), channel_id=1, source_target_pairs={{0,2},{1,3},{2,0},{3,1},{4,6},{5,7},{6,4},{7,5},{8,10},{9,11},{10,... | collective-permute-start | bytes 2949128 | tf_op jit(solution)/shard_map/ppermute | solution.py:113
  458.6 24.5 %collective-permute-start.26 = (bf16[3,4,64,640]{3,2,0,1:T(8,128)(2,1)}, bf16[3,4,64,640]{3,2,0,1:T(8,128)(2,1)}, u32[]{:S(2)}, u32[]{:S(2)}) collective-permute-start(bf16[3,4,64,640]{3,2,0,1:T(8,128)(2,1)} %add_convert_fusion.5), channel_id=1, source_target_pairs={{0,2},{1,3},{2,0},{3,1},{4,6},{5,7},{6,4},{7,5},{8,10},{9,11},{10,... | collective-permute-start | bytes 2949128 | tf_op jit(solution)/shard_map/ppermute | solution.py:113
  459.2 25.6 %collective-permute-start.27 = (bf16[3,4,64,640]{3,2,0,1:T(8,128)(2,1)}, bf16[3,4,64,640]{3,2,0,1:T(8,128)(2,1)S(1)}, u32[]{:S(2)}, u32[]{:S(2)}) collective-permute-start(bf16[3,4,64,640]{3,2,0,1:T(8,128)(2,1)} %add_convert_fusion.4), channel_id=1, source_target_pairs={{0,1},{1,0},{2,3},{3,2},{4,5},{5,4},{6,7},{7,6},{8,9},{9,8},{10,11... | collective-permute-start | bytes 2949128 | tf_op jit(solution)/shard_map/ppermute | solution.py:113
  491.8 182.0 %reduce-scatter.9.cloned.1.call-start = ((), (), s32[]{:S(2)}) async-start(), calls=%async_computation.6 | async-start | bytes 4718592 | tf_op jit(solution)/shard_map/reduce_scatter | solution.py:343
  517.8 10.0 %collective-permute-start.41 = (bf16[3,64,640]{2,1,0:T(8,128)(2,1)S(1)}, bf16[3,64,640]{2,1,0:T(8,128)(2,1)S(1)}, u32[]{:S(2)}, u32[]{:S(2)}) collective-permute-start(bf16[3,64,640]{2,1,0:T(8,128)(2,1)S(1)} %get-tuple-element.159), channel_id=1, source_target_pairs={{0,4},{4,0},{8,12},{12,8},{16,20},{20,16},{24,28},{28,24},{1,5},{5... | collective-permute-start | bytes 737288 | tf_op jit(solution)/shard_map/ppermute | solution.py:113
  517.9 28.4 %collective-permute-start.42 = (bf16[3,64,640]{2,1,0:T(8,128)(2,1)S(1)}, bf16[3,64,640]{2,1,0:T(8,128)(2,1)S(1)}, u32[]{:S(2)}, u32[]{:S(2)}) collective-permute-start(bf16[3,64,640]{2,1,0:T(8,128)(2,1)S(1)} %get-tuple-element.158), channel_id=1, source_target_pairs={{0,8},{4,12},{8,0},{12,4},{16,24},{20,28},{24,16},{28,20},{1,9},{5... | collective-permute-start | bytes 737288 | tf_op jit(solution)/shard_map/ppermute | solution.py:113
  519.3 37.8 %collective-permute-start.43 = (bf16[3,64,640]{2,1,0:T(8,128)(2,1)S(1)}, bf16[3,64,640]{2,1,0:T(8,128)(2,1)S(1)}, u32[]{:S(2)}, u32[]{:S(2)}) collective-permute-start(bf16[3,64,640]{2,1,0:T(8,128)(2,1)S(1)} %get-tuple-element.157), channel_id=1, source_target_pairs={{0,12},{4,8},{8,4},{12,0},{16,28},{20,24},{24,20},{28,16},{1,13},{... | collective-permute-start | bytes 737288 | tf_op jit(solution)/shard_map/ppermute | solution.py:113
  519.7 38.8 %collective-permute-start.44 = (bf16[3,64,640]{2,1,0:T(8,128)(2,1)S(1)}, bf16[3,64,640]{2,1,0:T(8,128)(2,1)S(1)}, u32[]{:S(2)}, u32[]{:S(2)}) collective-permute-start(bf16[3,64,640]{2,1,0:T(8,128)(2,1)S(1)} %get-tuple-element.156), channel_id=1, source_target_pairs={{0,16},{4,20},{8,24},{12,28},{16,0},{20,4},{24,8},{28,12},{1,17},{... | collective-permute-start | bytes 737288 | tf_op jit(solution)/shard_map/ppermute | solution.py:113
  522.1 37.3 %collective-permute-start.45 = (bf16[3,64,640]{2,1,0:T(8,128)(2,1)S(1)}, bf16[3,64,640]{2,1,0:T(8,128)(2,1)S(1)}, u32[]{:S(2)}, u32[]{:S(2)}) collective-permute-start(bf16[3,64,640]{2,1,0:T(8,128)(2,1)S(1)} %get-tuple-element.155), channel_id=1, source_target_pairs={{0,20},{4,16},{8,28},{12,24},{16,4},{20,0},{24,12},{28,8},{1,21},{... | collective-permute-start | bytes 737288 | tf_op jit(solution)/shard_map/ppermute | solution.py:113
  527.8 39.4 %collective-permute-start.46 = (bf16[3,64,640]{2,1,0:T(8,128)(2,1)S(1)}, bf16[3,64,640]{2,1,0:T(8,128)(2,1)S(1)}, u32[]{:S(2)}, u32[]{:S(2)}) collective-permute-start(bf16[3,64,640]{2,1,0:T(8,128)(2,1)S(1)} %get-tuple-element.154), channel_id=1, source_target_pairs={{0,24},{4,28},{8,16},{12,20},{16,8},{20,12},{24,0},{28,4},{1,25},{... | collective-permute-start | bytes 737288 | tf_op jit(solution)/shard_map/ppermute | solution.py:113
  546.3 25.9 %collective-permute-start.47 = (bf16[3,64,640]{2,1,0:T(8,128)(2,1)S(1)}, bf16[3,64,640]{2,1,0:T(8,128)(2,1)S(1)}, u32[]{:S(2)}, u32[]{:S(2)}) collective-permute-start(bf16[3,64,640]{2,1,0:T(8,128)(2,1)S(1)} %get-tuple-element.153), channel_id=1, source_target_pairs={{0,28},{4,24},{8,20},{12,16},{16,12},{20,8},{24,4},{28,0},{1,29},{... | collective-permute-start | bytes 737288 | tf_op jit(solution)/shard_map/ppermute | solution.py:113
  557.1 22.5 %collective-permute-start.32 = (bf16[4,4,64,256]{3,2,0,1:T(8,128)(2,1)}, bf16[4,4,64,256]{3,2,0,1:T(8,128)(2,1)S(1)}, u32[]{:S(2)}, u32[]{:S(2)}) collective-permute-start(bf16[4,4,64,256]{3,2,0,1:T(8,128)(2,1)} %get-tuple-element.181), channel_id=1, source_target_pairs={{0,2},{1,3},{2,0},{3,1},{4,6},{5,7},{6,4},{7,5},{8,10},{9,11},{10,... | collective-permute-start | bytes 1572872 | tf_op jit(solution)/shard_map/ppermute | solution.py:113
  558.5 24.0 %collective-permute-start.29 = (bf16[4,4,64,256]{3,2,0,1:T(8,128)(2,1)}, bf16[4,4,64,256]{3,2,0,1:T(8,128)(2,1)S(1)}, u32[]{:S(2)}, u32[]{:S(2)}) collective-permute-start(bf16[4,4,64,256]{3,2,0,1:T(8,128)(2,1)} %get-tuple-element.180), channel_id=1, source_target_pairs={{0,1},{1,0},{2,3},{3,2},{4,5},{5,4},{6,7},{7,6},{8,9},{9,8},{10,11... | collective-permute-start | bytes 1572872 | tf_op jit(solution)/shard_map/ppermute | solution.py:113
  559.4 34.2 %collective-permute-start.28 = (bf16[4,4,64,256]{3,2,0,1:T(8,128)(2,1)}, bf16[4,4,64,256]{3,2,0,1:T(8,128)(2,1)}, u32[]{:S(2)}, u32[]{:S(2)}) collective-permute-start(bf16[4,4,64,256]{3,2,0,1:T(8,128)(2,1)} %slice.166), channel_id=1, source_target_pairs={{0,1},{1,0},{2,3},{3,2},{4,5},{5,4},{6,7},{7,6},{8,9},{9,8},{10,11... | collective-permute-start | bytes 1572872 | tf_op jit(solution)/shard_map/ppermute | solution.py:113
  567.2 26.4 %collective-permute-start.31 = (bf16[4,4,64,256]{3,2,0,1:T(8,128)(2,1)}, bf16[4,4,64,256]{3,2,0,1:T(8,128)(2,1)}, u32[]{:S(2)}, u32[]{:S(2)}) collective-permute-start(bf16[4,4,64,256]{3,2,0,1:T(8,128)(2,1)} %slice.170), channel_id=1, source_target_pairs={{0,2},{1,3},{2,0},{3,1},{4,6},{5,7},{6,4},{7,5},{8,10},{9,11},{10,... | collective-permute-start | bytes 1572872 | tf_op jit(solution)/shard_map/ppermute | solution.py:113
  581.0 14.0 %collective-permute-start.33 = (bf16[4,4,64,256]{3,2,0,1:T(8,128)(2,1)S(1)}, bf16[4,4,64,256]{3,2,0,1:T(8,128)(2,1)S(1)}, u32[]{:S(2)}, u32[]{:S(2)}) collective-permute-start(bf16[4,4,64,256]{3,2,0,1:T(8,128)(2,1)S(1)} %add_convert_fusion.7), channel_id=1, source_target_pairs={{0,1},{1,0},{2,3},{3,2},{4,5},{5,4},{6,7},{7,6},{8,9},{9,8},{10,11... | collective-permute-start | bytes 1572872 | tf_op jit(solution)/shard_map/ppermute | solution.py:113
  583.7 13.7 %collective-permute-start.30 = (bf16[4,4,64,256]{3,2,0,1:T(8,128)(2,1)S(1)}, bf16[4,4,64,256]{3,2,0,1:T(8,128)(2,1)S(1)}, u32[]{:S(2)}, u32[]{:S(2)}) collective-permute-start(bf16[4,4,64,256]{3,2,0,1:T(8,128)(2,1)S(1)} %add_convert_fusion.9), channel_id=1, source_target_pairs={{0,2},{1,3},{2,0},{3,1},{4,6},{5,7},{6,4},{7,5},{8,10},{9,11},{10,... | collective-permute-start | bytes 1572872 | tf_op jit(solution)/shard_map/ppermute | solution.py:113
  599.1 41.9 %copy-start.36 = (f32[1,2048]{1,0:T(1,128)S(1)}, f32[1,2048]{1,0:T(1,128)}, u32[]{:S(2)}) copy-start(f32[1,2048]{1,0:T(1,128)} %copy-done.35) | copy-start | bytes 24580
  599.2 41.9 %copy-start.46 = (f32[2,64]{1,0:T(2,128)S(1)}, f32[2,64]{1,0:T(2,128)}, u32[]{:S(2)}) copy-start(f32[2,64]{1,0:T(2,128)} %copy-done.45) | copy-start | bytes 1540
  599.5 14.8 %collective-permute-start.34 = (bf16[4,64,256]{2,1,0:T(8,128)(2,1)S(1)}, bf16[4,64,256]{2,1,0:T(8,128)(2,1)S(1)}, u32[]{:S(2)}, u32[]{:S(2)}) collective-permute-start(bf16[4,64,256]{2,1,0:T(8,128)(2,1)S(1)} %get-tuple-element.173), channel_id=1, source_target_pairs={{0,4},{4,0},{8,12},{12,8},{16,20},{20,16},{24,28},{28,24},{1,5},{5... | collective-permute-start | bytes 393224 | tf_op jit(solution)/shard_map/ppermute | solution.py:113
  599.7 40.7 %collective-permute-start.39 = (bf16[4,64,256]{2,1,0:T(8,128)(2,1)S(1)}, bf16[4,64,256]{2,1,0:T(8,128)(2,1)S(1)}, u32[]{:S(2)}, u32[]{:S(2)}) collective-permute-start(bf16[4,64,256]{2,1,0:T(8,128)(2,1)S(1)} %fusion.54), channel_id=1, source_target_pairs={{0,24},{4,28},{8,16},{12,20},{16,8},{20,12},{24,0},{28,4},{1,25},{... | collective-permute-start | bytes 393224 | tf_op jit(solution)/shard_map/ppermute | solution.py:113
  600.3 18.5 %collective-permute-start.35 = (bf16[4,64,256]{2,1,0:T(8,128)(2,1)S(1)}, bf16[4,64,256]{2,1,0:T(8,128)(2,1)S(1)}, u32[]{:S(2)}, u32[]{:S(2)}) collective-permute-start(bf16[4,64,256]{2,1,0:T(8,128)(2,1)S(1)} %get-tuple-element.174), channel_id=1, source_target_pairs={{0,8},{4,12},{8,0},{12,4},{16,24},{20,28},{24,16},{28,20},{1,9},{5... | collective-permute-start | bytes 393224 | tf_op jit(solution)/shard_map/ppermute | solution.py:113
  610.8 18.4 %collective-permute-start.36 = (bf16[4,64,256]{2,1,0:T(8,128)(2,1)S(1)}, bf16[4,64,256]{2,1,0:T(8,128)(2,1)S(1)}, u32[]{:S(2)}, u32[]{:S(2)}) collective-permute-start(bf16[4,64,256]{2,1,0:T(8,128)(2,1)S(1)} %get-tuple-element.175), channel_id=1, source_target_pairs={{0,12},{4,8},{8,4},{12,0},{16,28},{20,24},{24,20},{28,16},{1,13},{... | collective-permute-start | bytes 393224 | tf_op jit(solution)/shard_map/ppermute | solution.py:113
  610.9 19.0 %collective-permute-start.37 = (bf16[4,64,256]{2,1,0:T(8,128)(2,1)S(1)}, bf16[4,64,256]{2,1,0:T(8,128)(2,1)S(1)}, u32[]{:S(2)}, u32[]{:S(2)}) collective-permute-start(bf16[4,64,256]{2,1,0:T(8,128)(2,1)S(1)} %get-tuple-element.176), channel_id=1, source_target_pairs={{0,16},{4,20},{8,24},{12,28},{16,0},{20,4},{24,8},{28,12},{1,17},{... | collective-permute-start | bytes 393224 | tf_op jit(solution)/shard_map/ppermute | solution.py:113
  614.3 25.4 %collective-permute-start.38 = (bf16[4,64,256]{2,1,0:T(8,128)(2,1)S(1)}, bf16[4,64,256]{2,1,0:T(8,128)(2,1)S(1)}, u32[]{:S(2)}, u32[]{:S(2)}) collective-permute-start(bf16[4,64,256]{2,1,0:T(8,128)(2,1)S(1)} %get-tuple-element.177), channel_id=1, source_target_pairs={{0,20},{4,16},{8,28},{12,24},{16,4},{20,0},{24,12},{28,8},{1,21},{... | collective-permute-start | bytes 393224 | tf_op jit(solution)/shard_map/ppermute | solution.py:113
  618.7 25.1 %collective-permute-start.40 = (bf16[4,64,256]{2,1,0:T(8,128)(2,1)S(1)}, bf16[4,64,256]{2,1,0:T(8,128)(2,1)S(1)}, u32[]{:S(2)}, u32[]{:S(2)}) collective-permute-start(bf16[4,64,256]{2,1,0:T(8,128)(2,1)S(1)} %get-tuple-element.172), channel_id=1, source_target_pairs={{0,28},{4,24},{8,20},{12,16},{16,12},{20,8},{24,4},{28,0},{1,29},{... | collective-permute-start | bytes 393224 | tf_op jit(solution)/shard_map/ppermute | solution.py:113
  642.7 7.0 %collective-permute-start.48 = (f32[40,128]{1,0:T(8,128)S(1)}, f32[40,128]{1,0:T(8,128)S(1)}, u32[]{:S(2)}, u32[]{:S(2)}) collective-permute-start(f32[40,128]{1,0:T(8,128)S(1)} %maximum_bitcast_fusion), channel_id=1, source_target_pairs={{0,4},{4,0},{8,12},{12,8},{16,20},{20,16},{24,28},{28,24},{1,5},{5... | collective-permute-start | bytes 61448 | tf_op jit(solution)/shard_map/ppermute | solution.py:113
  649.7 11.3 %collective-permute-start.49 = (f32[40,128]{1,0:T(8,128)S(1)}, f32[40,128]{1,0:T(8,128)S(1)}, u32[]{:S(2)}, u32[]{:S(2)}) collective-permute-start(f32[40,128]{1,0:T(8,128)S(1)} %fusion.66), channel_id=1, source_target_pairs={{0,8},{4,12},{8,0},{12,4},{16,24},{20,28},{24,16},{28,20},{1,9},{5... | collective-permute-start | bytes 61448 | tf_op jit(solution)/shard_map/ppermute | solution.py:113
  661.0 7.5 %collective-permute-start.50 = (f32[40,128]{1,0:T(8,128)S(1)}, f32[40,128]{1,0:T(8,128)S(1)}, u32[]{:S(2)}, u32[]{:S(2)}) collective-permute-start(f32[40,128]{1,0:T(8,128)S(1)} %fusion.125), channel_id=1, source_target_pairs={{0,16},{4,20},{8,24},{12,28},{16,0},{20,4},{24,8},{28,12},{1,17},{... | collective-permute-start | bytes 61448 | tf_op jit(solution)/shard_map/ppermute | solution.py:113
  668.5 3.8 collective-permute-start.51
  672.4 4.3 collective-permute-start.52
  (59 other events, 471.5 us)
Sparse Core Ops, SparseCore 0:
  11.6 59.8 all-gather.8
  73.0 61.8 all-gather.10
  196.1 57.6 reduce-scatter.4
  257.3 45.2 all-gather.12
  351.1 52.1 reduce-scatter.6
  406.3 45.2 all-gather.14
  491.9 67.3 reduce-scatter.10
  561.7 84.4 reduce-scatter.8

commit v3 on v2

--- a/solution.py
+++ b/solution.py
@@ -113,33 +113,118 @@
     return lax.ppermute(value, axis, partner_pairs(axis, offset))
 
 
-VMEM_LIMIT = 56 * 1024 * 1024
-
-
-def place_columns(stacked, me):
-    seq_size, slots, rows, part = stacked.shape
+MIB = 1024 * 1024
+ADAM_PARAMS = pltpu.CompilerParams(vmem_limit_bytes=32 * MIB)
+
+
+def attention_params(length):
+    return pltpu.CompilerParams(vmem_limit_bytes=min(56, length * length // 8192) * MIB)
+
+
+def adam_values(weight, first, second, grads, rate, decay):
+    first_new = BETA_ONE * first + (1.0 - BETA_ONE) * grads
+    second_new = BETA_TWO * second + (1.0 - BETA_TWO) * grads * grads
+    first_hat = first_new * (1.0 / (1.0 - BETA_ONE**STEP))
+    root = jnp.sqrt(second_new * (1.0 / (1.0 - BETA_TWO**STEP)))
+    weight_new = weight - rate * (first_hat / (root + EPS_ADAM) + decay * weight)
+    return (weight_new, first_new, second_new)
+
+
+def in_columns(grads):
+    seq_size, slots, rows, part = grads.shape
+    return wide(grads).transpose(2, 1, 0, 3).reshape(rows, slots, seq_size * part)
+
+
+def update_attention(weight, first, second, grads):
+    seq_size, slots, rows, part = grads.shape
+    width = seq_size * part
     if part % 128:
-        out = jnp.zeros((slots, rows, seq_size * part), stacked.dtype)
-        for offset in range(seq_size):
-            out = lax.dynamic_update_slice(out, stacked[offset], (0, 0, (me ^ offset) * part))
-        return out
-
-    def body(me_ref, in_ref, out_ref):
-        out_ref[...] = in_ref[0]
-
-    return pl.pallas_call(
+        new = adam_update(weight, first, second, in_columns(grads), attention_rates(), DECAY)
+        return new[0], new[1], new[2][:, :3], new[2][:, 3]
+    chunk = 2
+    scales = [D ** (-0.5), (32 * D) ** (-0.5), D ** (-0.5), (HEADS * HEAD_DIM // 64) ** (-0.5)]
+
+    def body(w_ref, m_ref, v_ref, g_ref, w_out, m_out, v_out, o_out):
+        for slot in range(slots):
+            for item in range(chunk):
+                cols = slice(item * part, (item + 1) * part)
+                new = adam_values(
+                    w_ref[:, slot, cols],
+                    m_ref[:, slot, cols],
+                    v_ref[:, slot, cols],
+                    wide(g_ref[item, slot]),
+                    3.0 * scales[slot],
+                    DECAY,
+                )
+                w_out[:, slot, cols] = new[0]
+                m_out[:, slot, cols] = new[1]
+                if slot < slots - 1:
+                    v_out[slot, :, cols] = new[2]
+                else:
+                    o_out[:, cols] = new[2]
+
+    state_spec = pl.BlockSpec((rows, slots, chunk * part), lambda j: (0, 0, j))
+    new = pl.pallas_call(
         body,
-        grid_spec=pltpu.PrefetchScalarGridSpec(
-            num_scalar_prefetch=1,
-            grid=(seq_size,),
-            in_specs=[
-                pl.BlockSpec((1, slots, rows, part), lambda j, me_ref: (j ^ me_ref[0], 0, 0, 0))
-            ],
-            out_specs=pl.BlockSpec((slots, rows, part), lambda j, me_ref: (0, 0, j)),
+        grid=(seq_size // chunk,),
+        in_specs=[state_spec] * 3
+        + [pl.BlockSpec((chunk, slots, rows, part), lambda j: (j, 0, 0, 0))],
+        out_specs=[
+            state_spec,
+            state_spec,
+            pl.BlockSpec((slots - 1, rows, chunk * part), lambda j: (0, 0, j)),
+            pl.BlockSpec((rows, chunk * part), lambda j: (0, j)),
+        ],
+        out_shape=[
+            jax.ShapeDtypeStruct(weight.shape, jnp.float32),
+            jax.ShapeDtypeStruct(weight.shape, jnp.float32),
+            jax.ShapeDtypeStruct((slots - 1, rows, width), jnp.float32),
+            jax.ShapeDtypeStruct((rows, width), jnp.float32),
+        ],
+        compiler_params=ADAM_PARAMS,
+        cost_estimate=pl.CostEstimate(
+            flops=20 * weight.size, bytes_accessed=26 * weight.size, transcendentals=weight.size
         ),
-        out_shape=jax.ShapeDtypeStruct((slots, rows, seq_size * part), stacked.dtype),
-        compiler_params=pltpu.CompilerParams(vmem_limit_bytes=VMEM_LIMIT),
-    )(me.reshape(1), stacked)
+    )(weight, first, second, grads)
+    return new[0], new[1], new[2].transpose(1, 0, 2), new[3]
+
+
+def update_feed(weight, first, second, grads):
+    seq_size, slots, rows, part = grads.shape
+    if part % 128:
+        return adam_update(weight, first, second, in_columns(grads), feed_rates(), DECAY)
+
+    def body(w_ref, m_ref, v_ref, g_ref, w_out, m_out, v_out):
+        rate = jnp.where(pl.program_id(0) == slots - 1, 3.0 * FF ** (-0.5), 3.0 * D ** (-0.5))
+        for item in range(chunk):
+            cols = slice(item * part, (item + 1) * part)
+            new = adam_values(
+                w_ref[0, :, cols],
+                m_ref[0, :, cols],
+                v_ref[0, :, cols],
+                wide(g_ref[item, 0]),
+                rate,
+                DECAY,
+            )
+            for ref, value in zip((w_out, m_out, v_out), new):
+                ref[0, :, cols] = value
+
+    chunk = 4
+    state_spec = pl.BlockSpec((1, rows, chunk * part), lambda slot, j: (slot, 0, j))
+    state = [item.transpose(1, 0, 2) for item in (weight, first, second)]
+    new = pl.pallas_call(
+        body,
+        grid=(slots, seq_size // chunk),
+        in_specs=[state_spec] * 3
+        + [pl.BlockSpec((chunk, 1, rows, part), lambda slot, j: (j, slot, 0, 0))],
+        out_specs=[state_spec] * 3,
+        out_shape=[jax.ShapeDtypeStruct(state[0].shape, jnp.float32)] * 3,
+        compiler_params=ADAM_PARAMS,
+        cost_estimate=pl.CostEstimate(
+            flops=20 * weight.size, bytes_accessed=26 * weight.size, transcendentals=weight.size
+        ),
+    )(*state, grads)
+    return [item.transpose(1, 0, 2) for item in new]
 
 
 def head_probs(query, key, bias, same_doc):
@@ -183,7 +268,12 @@
         in_specs=[tokens_spec] * 3 + other_specs,
         out_specs=tokens_spec,
         out_shape=jax.ShapeDtypeStruct(query.shape, jnp.bfloat16),
-        compiler_params=pltpu.CompilerParams(vmem_limit_bytes=VMEM_LIMIT),
+        compiler_params=attention_params(length),
+        cost_estimate=pl.CostEstimate(
+            flops=6000 * length * query.size // HEAD_DIM,
+            bytes_accessed=8 * query.size + bias.size * 4,
+            transcendentals=length * query.size // HEAD_DIM,
+        ),
     )(query, key, value, bias, segments[:, :, None], segments[:, None, :])
 
 
@@ -222,45 +312,40 @@
         + [pl.BlockSpec((2, length, length), lambda pair, m: (pair, 0, 0))],
         out_shape=[jax.ShapeDtypeStruct(query.shape, jnp.bfloat16)] * 3
         + [jax.ShapeDtypeStruct((part // HEAD_DIM, length, length), jnp.float32)],
-        compiler_params=pltpu.CompilerParams(vmem_limit_bytes=VMEM_LIMIT),
+        compiler_params=attention_params(length),
+        cost_estimate=pl.CostEstimate(
+            flops=8000 * length * query.size // HEAD_DIM,
+            bytes_accessed=14 * query.size + bias.size * 8,
+            transcendentals=length * query.size // HEAD_DIM,
+        ),
     )(query, key, value, grad_out, bias, segments[:, :, None], segments[:, None, :])
 
 
-def exchange(values, dim, out_dim):
-    seq_size = lax.axis_size("seq")
-    me = lax.axis_index("seq")
-    received = None
-    for offset in range(seq_size):
-        piece = lax.dynamic_index_in_dim(values, me ^ offset, dim, keepdims=False)
-        if offset:
-            piece = swap(piece, "seq", offset)
-        piece = jnp.expand_dims(piece, out_dim)
-        if received is None:
-            shape = piece.shape[:out_dim] + (seq_size,) + piece.shape[out_dim + 1 :]
-            received = jnp.zeros(shape, values.dtype)
-        received = lax.dynamic_update_slice_in_dim(received, piece, me ^ offset, out_dim)
-    return received
-
-
-def gather_dp(mine):
+def gather_dp_first(mine):
     if lax.axis_size("dp") != 4:
-        return lax.all_gather(mine, "dp", axis=2)
-    me = lax.axis_index("dp")
-    half = mine.shape[1] // 2
-    one = swap(mine, "dp", 1)
-    two = swap(mine, "dp", 2)
-    low = swap(one[:, :half], "dp", 2)
-    high = swap(two[:, half:], "dp", 1)
-    full = jnp.zeros(mine.shape[:2] + (4,) + mine.shape[2:], mine.dtype)
-    for piece, source, start in (
-        (mine, 0, 0),
-        (one, 1, 0),
-        (two, 2, 0),
-        (low, 3, 0),
-        (high, 3, half),
-    ):
-        full = lax.dynamic_update_slice(full, piece[:, :, None], (0, start, me ^ source, 0, 0))
-    return full
+        return [lax.all_gather(mine, "dp", axis=2)]
+    return [mine, swap(mine, "dp", 1), swap(mine, "dp", 2)]
+
+
+def gather_dp_second(items):
+    if len(items) == 1:
+        full = items[0]
+    else:
+        mine, one, two = items
+        me = lax.axis_index("dp")
+        half = mine.shape[1] // 2
+        low = swap(one[:, :half], "dp", 2)
+        high = swap(two[:, half:], "dp", 1)
+        full = jnp.zeros(mine.shape[:2] + (4,) + mine.shape[2:], mine.dtype)
+        for piece, source, start in (
+            (mine, 0, 0),
+            (one, 1, 0),
+            (two, 2, 0),
+            (low, 3, 0),
+            (high, 3, half),
+        ):
+            full = lax.dynamic_update_slice(full, piece[:, :, None], (0, start, me ^ source, 0, 0))
+    return full.reshape(full.shape[0], -1, full.shape[-1])
 
 
 def wide(value):
@@ -275,31 +360,37 @@
     pieces = [lax.dynamic_index_in_dim(partial, me ^ k, 2, keepdims=False) for k in range(4)]
     low = [piece[:, :half] for piece in pieces]
     high = [piece[:, half:] for piece in pieces]
-    low_two = (wide(low[2]) + wide(swap(low[3], "dp", 1))).astype(jnp.bfloat16)
-    high_one = (wide(high[1]) + wide(swap(high[3], "dp", 2))).astype(jnp.bfloat16)
-    low_zero = wide(low[0]) + wide(swap(low[1], "dp", 1))
-    high_zero = wide(high[0]) + wide(swap(high[2], "dp", 2))
-    return [low_two, high_one, low_zero, high_zero]
+    return low[:3] + high[:3] + [swap(low[3], "dp", 1), swap(high[3], "dp", 2)]
 
 
 def scatter_dp_second(items):
     if len(items) == 1:
+        return items
+    low = items[:3]
+    high = items[3:6]
+    low_two = (wide(low[2]) + wide(items[6])).astype(jnp.bfloat16)
+    high_one = (wide(high[1]) + wide(items[7])).astype(jnp.bfloat16)
+    return [low[0], high[0], swap(low[1], "dp", 1), swap(high[2], "dp", 2), low_two, high_one]
+
+
+def scatter_dp_third(items):
+    if len(items) == 1:
         return items[0]
-    low_two, high_one, low_zero, high_zero = items
-    low_sum = low_zero + wide(swap(low_two, "dp", 2))
-    high_sum = high_zero + wide(swap(high_one, "dp", 1))
+    low, high, low_more, high_more, low_two, high_one = items
+    low_sum = wide(low) + wide(low_more) + wide(swap(low_two, "dp", 2))
+    high_sum = wide(high) + wide(high_more) + wide(swap(high_one, "dp", 1))
     return jnp.concatenate([low_sum, high_sum], 1).astype(jnp.bfloat16)
 
 
 def to_columns(weight):
     seq_size = lax.axis_size("seq")
     slots, rows, width = weight.shape
-    part = width // seq_size
-    return exchange(weight.astype(jnp.bfloat16).reshape(slots, rows, seq_size, part), 2, 1)
-
-
-def all_rows(mine):
-    return gather_dp(mine).reshape(mine.shape[0], -1, mine.shape[-1])
+    send = weight.reshape(slots, rows, seq_size, width // seq_size).transpose(2, 0, 1, 3)
+    return lax.all_to_all(send, "seq", 0, 0).transpose(1, 0, 2, 3)
+
+
+def to_rows(mine):
+    return lax.all_to_all(mine.transpose(1, 0, 2, 3), "seq", 0, 0)
 
 
 def after(value, *earlier):
@@ -313,15 +404,6 @@
     slots, total, part = partial.shape
     rows = total // (seq_size * dp_size)
     return scatter_dp_first(partial.reshape(slots, seq_size, dp_size, rows, part))
-
-
-def to_rows_last(mine):
-    me = lax.axis_index("seq")
-    pieces = []
-    for offset in range(lax.axis_size("seq")):
-        piece = lax.dynamic_index_in_dim(mine, me ^ offset, 1, keepdims=False)
-        pieces.append(swap(piece, "seq", offset) if offset else piece)
-    return wide(place_columns(jnp.stack(pieces, 0), me))
 
 
 def sum_all(value):
@@ -368,12 +450,18 @@
     part = heads_here * HEAD_DIM
     seq_index = lax.axis_index("seq")
 
-    attention_slots = attention_weight.transpose(1, 0, 2)
+    attention_slots = attention_weight.transpose(1, 0, 2).astype(jnp.bfloat16)
     feed_slots = feed_weight.transpose(1, 0, 2).astype(jnp.bfloat16)
-    attention_mine = to_columns(attention_slots)
-    attention_mine, feed_slots = lax.optimization_barrier((attention_mine, feed_slots))
-    attention_low = all_rows(attention_mine)
-    feed_mine = to_columns(feed_slots)
+    inputs = tokens.astype(jnp.float32)
+    normed_here = rms_norm(inputs, gains[0]).astype(jnp.bfloat16)
+    attention_mine, normed_here = lax.optimization_barrier(
+        (to_columns(attention_slots), normed_here)
+    )
+    normed_one = gather_tokens(normed_here)
+    attention_items, late_cotangent = lax.optimization_barrier(
+        (gather_dp_first(attention_mine), cotangent)
+    )
+    attention_low = gather_dp_second(attention_items)
     weight_out = attention_low[3]
 
     positions = jnp.arange(seq_len, dtype=jnp.int32)
@@ -391,18 +479,20 @@
     def as_blocks(matrix):
         return matrix.astype(jnp.bfloat16).reshape(seq_size, micro_count, local_rows, part)
 
-    inputs = tokens.astype(jnp.float32)
-    normed_one = gather_tokens(rms_norm(inputs, gains[0]).astype(jnp.bfloat16))
-    grad_out = gather_tokens(after(cotangent, normed_one))
+    grad_out = gather_tokens(late_cotangent)
     query, key, value = [
         as_blocks(dot(normed_one, attention_low[slot])) for slot in range(3)
     ]
+    query, key, value, feed_slots = lax.optimization_barrier((query, key, value, feed_slots))
+    feed_mine = to_columns(feed_slots)
     attended = attention_forward(query, key, value, bias, segments).reshape(-1, part)
-    attention_partial, feed_mine, grad_out = lax.optimization_barrier(
-        (dot_t(attended, weight_out).astype(jnp.bfloat16), feed_mine, grad_out)
-    )
-    feed_low = all_rows(feed_mine)
+    attention_partial, grad_out, feed_mine = lax.optimization_barrier(
+        (dot_t(attended, weight_out).astype(jnp.bfloat16), grad_out, feed_mine)
+    )
+    feed_gathered = gather_dp_first(feed_mine)
     attention_out = scatter_tokens(attention_partial, shape)
+    attention_out, feed_gathered = lax.optimization_barrier((attention_out, feed_gathered))
+    feed_low = gather_dp_second(feed_gathered)
     weight_gate, weight_up, weight_down = feed_low[0], feed_low[1], feed_low[2]
     hidden_state = inputs + attention_out
     normed_two = gather_tokens(rms_norm(hidden_state, gains[1]).astype(jnp.bfloat16))
@@ -422,21 +512,20 @@
         outer_sum(normed_two, grad_up).astype(jnp.bfloat16),
         outer_sum(grad_out, inner).astype(jnp.bfloat16),
     ]
-    grad_normed_two, grads_feed = lax.optimization_barrier((grad_normed_two, grads_feed))
-    feed_first_step = to_rows_first(grads_feed)
+    feed_steps = to_rows_first(grads_feed)
+    grad_normed_two, feed_steps = lax.optimization_barrier((grad_normed_two, feed_steps))
+    feed_steps = scatter_dp_second(feed_steps)
     grad_hidden_norm, grad_gain_two = norm_back(hidden_state, gains[1], grad_normed_two)
     grad_hidden = cotangent.astype(jnp.float32) + grad_hidden_norm
     grad_branch = gather_tokens(grad_hidden.astype(jnp.bfloat16))
-    grad_branch, feed_partial, feed_first_step = lax.optimization_barrier(
-        (grad_branch, feed_partial, feed_first_step)
-    )
-    block_rows = (hidden_state + scatter_tokens(feed_partial, shape)).astype(jnp.bfloat16)
+    grad_branch, feed_mine_grad = lax.optimization_barrier(
+        (grad_branch, scatter_dp_third(feed_steps))
+    )
     grad_attended = as_blocks(dot(grad_branch, weight_out))
-    feed_mine_grad = scatter_dp_second(feed_first_step)
+    feed_total = to_rows(feed_mine_grad)
     grad_query, grad_key, grad_value, score_sums = attention_backward(
         query, key, value, grad_attended, bias, segments
     )
-    grad_query, feed_mine_grad = lax.optimization_barrier((grad_query, feed_mine_grad))
     grad_table_here = jnp.einsum(
         "hij,zij->zh",
         score_sums.astype(jnp.bfloat16),
@@ -444,14 +533,17 @@
         preferred_element_type=jnp.float32,
     )
     grad_qkv = [item.reshape(-1, part) for item in (grad_query, grad_key, grad_value)]
-    grad_normed_one = scatter_tokens(
-        sum(dot_t(grad_qkv[slot], attention_low[slot]) for slot in range(3)), shape
-    )
+    normed_partial = sum(dot_t(grad_qkv[slot], attention_low[slot]) for slot in range(3))
+    normed_partial, feed_total = lax.optimization_barrier(
+        (normed_partial.astype(jnp.bfloat16), feed_total)
+    )
+    grad_normed_one = scatter_tokens(normed_partial, shape)
+    block_rows = hidden_state + scatter_tokens(after(feed_partial, grad_normed_one), shape)
+    block_rows = block_rows.astype(jnp.bfloat16)
     attention_steps = to_rows_first(
         [outer_sum(normed_one, item) for item in grad_qkv] + [outer_sum(grad_branch, attended)]
     )
-    feed_total = to_rows_last(feed_mine_grad).transpose(1, 0, 2)
-    attention_total = to_rows_last(scatter_dp_second(attention_steps)).transpose(1, 0, 2)
+    attention_total = to_rows(scatter_dp_third(scatter_dp_second(attention_steps)))
     grad_input_norm, grad_gain_one = norm_back(inputs, gains[0], grad_normed_one)
     grad_rows = (grad_hidden + grad_input_norm).astype(jnp.bfloat16)
     grad_table = lax.dynamic_update_slice_in_dim(
@@ -461,15 +553,10 @@
     small = sum_all(small.reshape(-1, 128)).reshape(-1)
     gains_total = small[: 2 * width].reshape(2, width)
     table_total = small[2 * width :].reshape(NUM_BUCKETS, HEADS)
-    new_attention = adam_update(
-        attention_weight,
-        attention_first,
-        attention_second,
-        attention_total,
-        attention_rates(),
-        DECAY,
-    )
-    new_feed = adam_update(feed_weight, feed_first, feed_second, feed_total, feed_rates(), DECAY)
+    new_attention = update_attention(
+        attention_weight, attention_first, attention_second, attention_total
+    )
+    new_feed = update_feed(feed_weight, feed_first, feed_second, feed_total)
     new_gains = adam_update(gains, gains_first, gains_second, gains_total, 0.6, 0.0)
     new_table = adam_update(rel_table, table_first, table_second, table_total, 1.5, 0.0)
     return (
@@ -477,8 +564,8 @@
         grad_rows,
         new_attention[0],
         new_attention[1],
-        new_attention[2][:, :3, :],
-        new_attention[2][:, 3, :],
+        new_attention[2],
+        new_attention[3],
         new_feed[0],
         new_feed[1],
         new_feed[2],

time: 695 us -> 598 us (0.86)
  waiting for transfers between devices: 338 us -> 309 us
  other arithmetic: 57.3 us -> 32 us
  starting transfers between devices: 78.7 us -> 54.4 us
  matrix products: 99.7 us -> 91.7 us
    all_to_all x0 -> x4, waiting for transfers between devices: none -> 96.4 us  [the longest x2 68.2 us: to_columns(): return lax.all_to_all(send, 'seq', 0, 0).transpose(1, 0, 2, 3)]
    ppermute x53 -> x25, waiting for transfers between devices: 216 us -> 136 us  [swap(): return lax.ppermute(value, axis, partner_pairs(axis, offset))]
    ppermute x53 -> x25, starting transfers between devices: 77.4 us -> 34.4 us  [swap(): return lax.ppermute(value, axis, partner_pairs(axis, offset))]
    reduce_scatter x4, waiting for transfers between devices: 91.8 us -> 66.8 us  [scatter_tokens(): lax.psum_scatter(send, 'seq', scatter_dimension=0).astype(jnp.float32)]
    all_gather x4, waiting for transfers between devices: 29.5 us -> 10.2 us  [gather_tokens(): full = lax.all_gather(local_rows, 'seq', axis=0)]
    all_to_all x0 -> x4, starting transfers between devices: none -> 18.9 us  [the longest x2 10.8 us: to_columns(): return lax.all_to_all(send, 'seq', 0, 0).transpose(1, 0, 2, 3)]
    sub x4 -> x2, other arithmetic: 16.8 us -> 1.31 us  [adam_update(): weight - rate * (first_hat / (jnp.sqrt(second_hat) + EPS_ADAM) + decay *...]
    dot_general x7, matrix products: 30.2 us -> 21.3 us  [outer_sum(): lax.dot_general(left, right, (((0,), (0,)), ((), ())), preferred_element_...]
  transfers between devices with their start and end apart: 61 -> 37, of which waited for: 26 -> 22; matrix products, arithmetic and copies ran while one was open for 24% -> 22% of each run, Pallas kernels for 6% -> 6%
where the time goes in v3:
time: 598 us; the launch traced here: 592 us
  waiting for transfers between devices  309 us (52%)
  matrix products  91.7 us (15%)
  starting transfers between devices  54.4 us (9%)
  local copies, waits for them, and re-layouts  50.8 us (8%)
  Pallas kernels  37.7 us (6%)
  other arithmetic  32 us (5%)
  between operations  15.6 us (3%)
    ppermute x25, waiting for transfers between devices, swap(): return lax.ppermute(value, axis, partner_pairs(axis, offset))  136 us
    all_to_all x2, waiting for transfers between devices, to_columns(): return lax.all_to_all(send, 'seq', 0, 0).transpose(1, 0, 2, 3)  68.2 us
    reduce_scatter x4, waiting for transfers between devices, scatter_tokens(): lax.psum_scatter(send, 'seq', scatter_dimension=0).astype(jnp.float32)  66.8 us
    ppermute x25, starting transfers between devices, swap(): return lax.ppermute(value, axis, partner_pairs(axis, offset))  34.4 us
    all_to_all x2, waiting for transfers between devices, to_rows(): return lax.all_to_all(mine.transpose(1, 0, 2, 3), 'seq', 0, 0)  28.2 us
    dot_general x7, matrix products, dot(): return jnp.dot(left, right, preferred_element_type=jnp.float32)  27.1 us
    dot_general x7, matrix products, dot_t(): lax.dot_general(left, right, (((1,), (1,)), ((), ())), preferred_element_...  25.6 us
    dot_general x7, matrix products, outer_sum(): lax.dot_general(left, right, (((0,), (0,)), ((), ())), preferred_element_...  21.3 us
  transfers between devices with their start and end apart: 37, of which 22 were waited for; matrix products, arithmetic and copies ran while one was open for 22% of the time, Pallas kernels for 6%

profile of v3, /device:TPU:0, one launch (start us, length us, event | category | flops | bytes accessed | tf_op | source)
XLA Modules:
  0.0 591.5 jit_solution(10695052478069479623)
XLA Ops:
  7.2 2.0 convert_bitcast_fusion
  11.6 6.3 %all-to-all-start = ((bf16[8,4,64,256]{3,2,1,0:T(8,128)(2,1)}), bf16[8,4,64,256]{3,2,1,0:T(8,128)(2,1)S(1)}, u32[]{:S(2)}, u32[]{:S(2)}) async-start(bf16[8,4,64,256]{3,2,1,0:T(8,128)(2,1)} %copy.91), calls=%async_computation | async-start | bytes 2097152 | tf_op jit(solution)/shard_map/all_to_all | solution.py:389
  19.2 25.3 %all-to-all-done = bf16[8,4,64,256]{3,2,1,0:T(8,128)(2,1)S(1)} async-done(((bf16[8,4,64,256]{3,2,1,0:T(8,128)(2,1)}), bf16[8,4,64,256]{3,2,1,0:T(8,128)(2,1)S(1)}, u32[]{:S(2)}, u32[]{:S(2)}) %all-to-all-start) | async-done | bytes 1048608 | tf_op jit(solution)/shard_map/all_to_all | solution.py:389
  47.8 21.7 %collective-permute-done = bf16[4,8,64,256]{3,2,1,0:T(8,128)(2,1)S(1)} collective-permute-done((bf16[4,8,64,256]{3,2,1,0:T(8,128)(2,1)S(1)}, bf16[4,8,64,256]{3,2,1,0:T(8,128)(2,1)S(1)}, u32[]{:S(2)}, u32[]{:S(2)}) %collective-permute-start) | collective-permute-done | bytes 1048608 | tf_op jit(solution)/shard_map/ppermute | solution.py:113
  70.8 3.7 bitcast_convert_fusion.3
  79.9 7.0 %collective-permute-done.2 = bf16[4,4,64,256]{3,2,1,0:T(8,128)(2,1)S(1)} collective-permute-done((bf16[4,4,64,256]{3,2,1,0:T(8,128)(2,1)S(1)}, bf16[4,4,64,256]{3,2,1,0:T(8,128)(2,1)S(1)}, u32[]{:S(2)}, u32[]{:S(2)}) %collective-permute-start.2) | collective-permute-done | bytes 524320 | tf_op jit(solution)/shard_map/ppermute | solution.py:113
  87.0 2.4 collective-permute-done.3
  89.4 1.9 fusion.51
  91.2 3.9 convolution_convert_fusion.7
  100.1 4.5 all-to-all-start.1
  105.2 10.4 %fusion.1 = f32[4,512,512]{2,0,1:T(4,128)S(1)} fusion(s32[512,512]{1,0:T(8,128)S(1)} %fusion.30, f32[32,32]{1,0:T(8,128)S(1)} %copy-done.55, s32[]{:T(128)S(6)} %select_n.56), kind=kOutput, calls=%fused_computation.2 | convolution fusion | flops 411041792 | bytes 5246980 | tf_op jit(solution)/shard_map/atj,ao->otj/dot_general | solution.py:471
  115.7 3.3 copy.98.bias_ref
  119.3 2.2 copy-done.5
  121.5 11.1 %shard_map.262 = bf16[8,2,64,256]{3,2,1,0:T(8,128)(2,1)S(1)} custom-call(bf16[8,2,64,256]{3,2,1,0:T(8,128)(2,1)S(1)} %bitcast.219, bf16[8,2,64,256]{3,2,1,0:T(8,128)(2,1)S(1)} %bitcast.217, bf16[8,2,64,256]{3,2,1,0:T(8,128)(2,1)S(1)} %bitcast.215, f32[4,512,512]{2,1,0:T(8,128)S(1)} %copy-done.5, s32[2,512,1]{2,1,0:T(8,128)S(1)} %copy.99.seg_q_ref, ...), custom_call_target="tpu_custom_call" | custom-call | flops 12582912000 | bytes 6291456 | tf_op jit(solution)/shard_map/pallas_call | solution.py:265
  132.7 3.3 convolution_convert_fusion.1
  136.0 42.9 %all-to-all-done.1 = bf16[8,3,64,640]{3,2,1,0:T(8,128)(2,1)} async-done(((bf16[8,3,64,640]{3,2,1,0:T(8,128)(2,1)}), bf16[8,3,64,640]{3,2,1,0:T(8,128)(2,1)}, u32[]{:S(2)}, u32[]{:S(2)}) %all-to-all-start.1) | async-done | bytes 1966112 | tf_op jit(solution)/shard_map/all_to_all | solution.py:389
  178.8 1.7 copy.152
  183.7 45.8 %reduce-scatter.5.cloned.1.call-done = bf16[1,2,64,2048]{3,2,1,0:T(8,128)(2,1)} async-done(((bf16[8,2,64,2048]{3,2,1,0:T(8,128)(2,1)}), bf16[1,2,64,2048]{3,2,1,0:T(8,128)(2,1)}) %reduce-scatter.5.cloned.1.call-update) | async-done | bytes 524304 | tf_op jit(solution)/shard_map/reduce_scatter | solution.py:425
  239.3 1.9 bitcast_dynamic-update-slice_fusion.1
  241.2 1.9 bitcast_dynamic-update-slice_fusion
  243.1 11.7 %collective-permute-done.6 = bf16[3,4,64,640]{3,2,1,0:T(8,128)(2,1)S(1)} collective-permute-done((bf16[3,4,64,640]{3,2,1,0:T(8,128)(2,1)S(1)}, bf16[3,4,64,640]{3,2,1,0:T(8,128)(2,1)S(1)}, u32[]{:S(2)}, u32[]{:S(2)}) %collective-permute-start.6) | collective-permute-done | bytes 983072 | tf_op jit(solution)/shard_map/ppermute | solution.py:113
  255.0 2.4 collective-permute-done.7
  257.5 3.4 fusion.50
  262.4 4.9 fusion.59
  267.3 10.2 %all-gather.13.cloned.1.call-done = bf16[16,64,2048]{2,1,0:T(8,128)(2,1)} async-done(((bf16[2,64,2048]{2,1,0:T(8,128)(2,1)}), bf16[16,64,2048]{2,1,0:T(8,128)(2,1)}) %all-gather.13.cloned.1.call-update) | async-done | bytes 4194320 | tf_op jit(solution)/shard_map/all_gather | solution.py:419
  277.5 6.1 %fusion.58 = f32[1024,640]{1,0:T(8,128)S(1)} fusion(bf16[1024,2048]{1,0:T(8,128)(2,1)} %bitcast.281, bf16[2048,640]{1,0:T(8,128)(2,1)} %bitcast.254), kind=kOutput, calls=%fused_computation.143 | convolution fusion | flops 2684354560 | bytes 9437184 | tf_op jit(solution)/shard_map/dot_general | solution.py:81
  283.7 6.2 %fusion.10 = (bf16[1024,640]{1,0:T(8,128)(2,1)S(1)}, bf16[1024,640]{1,0:T(8,128)(2,1)S(1)}, bf16[1024,640]{1,0:T(8,128)(2,1)}) fusion(f32[1024,640]{1,0:T(8,128)S(1)} %copy-done.71, f32[1024,640]{1,0:T(8,128)S(1)} %fusion.58, bf16[1024,2048]{1,0:T(8,128)(2,1)S(1)} %bitcast.283, bf16[2048,640]{1,0:T(8,128)(2,1)S(1)} %bitcast.252), kind=kOutput, calls=%fused_computation.26 | convolution fusion | flops 2701393920 | bytes 15990784 | tf_op jit(solution)/shard_map/dot_general | solution.py:81
  289.8 3.4 fusion.60
  293.3 5.1 add_convert_fusion.1
  298.7 5.9 convolution_convert_fusion.4
  304.6 3.8 convolution_convert_fusion.3
  308.4 3.8 convolution_convert_fusion.2
  313.3 2.2 constant_dynamic-slice_fusion.4
  315.5 1.9 copy_bitcast_fusion
  326.3 21.0 %reduce-scatter.7.cloned.1.call-done = bf16[1,2,64,2048]{3,2,1,0:T(8,128)(2,1)} async-done(((bf16[8,2,64,2048]{3,2,1,0:T(8,128)(2,1)}), bf16[1,2,64,2048]{3,2,1,0:T(8,128)(2,1)}) %reduce-scatter.7.cloned.1.call-update) | async-done | bytes 524304 | tf_op jit(solution)/shard_map/reduce_scatter | solution.py:425
  350.7 1.9 add_convert_fusion.5
  358.2 19.1 %collective-permute-done.11 = bf16[3,4,64,640]{3,2,0,1:T(8,128)(2,1)S(1)} collective-permute-done((bf16[3,4,64,640]{3,2,0,1:T(8,128)(2,1)S(1)}, bf16[3,4,64,640]{3,2,0,1:T(8,128)(2,1)S(1)}, u32[]{:S(2)}, u32[]{:S(2)}) %collective-permute-start.11) | collective-permute-done | bytes 983072 | tf_op jit(solution)/shard_map/ppermute | solution.py:113
  377.3 1.7 collective-permute-done.10
  379.4 17.0 %collective-permute-done.13 = bf16[3,4,64,640]{3,2,0,1:T(8,128)(2,1)S(1)} collective-permute-done((bf16[3,4,64,640]{3,2,0,1:T(8,128)(2,1)S(1)}, bf16[3,4,64,640]{3,2,0,1:T(8,128)(2,1)S(1)}, u32[]{:S(2)}, u32[]{:S(2)}) %collective-permute-start.13) | collective-permute-done | bytes 983072 | tf_op jit(solution)/shard_map/ppermute | solution.py:113
  398.4 4.3 all-to-all-start.2
  402.8 3.6 convolution_convert_fusion.6
  406.8 12.3 %shard_map.263 = (bf16[8,2,64,256]{3,2,1,0:T(8,128)(2,1)S(1)}, bf16[8,2,64,256]{3,2,1,0:T(8,128)(2,1)S(1)}, bf16[8,2,64,256]{3,2,1,0:T(8,128)(2,1)S(1)}, f32[4,512,512]{2,1,0:T(8,128)S(1)}) custom-call(bf16[8,2,64,256]{3,2,1,0:T(8,128)(2,1)S(1)} %bitcast.220, bf16[8,2,64,256]{3,2,1,0:T(8,128)(2,1)S(1)} %bitcast.218, bf16[8,2,64,256]{3,2,1,0:T(8,128)(2,1)S(1)} %bitcast.216, ...), custom_call_target="tpu_custom_call" | custom-call | flops 16777216000 | bytes 12058624 | tf_op jit(solution)/shard_map/pallas_call | solution.py:307
  422.4 3.4 add_convert_fusion
  425.8 23.1 %all-to-all-done.2.g_ref = bf16[8,3,64,640]{3,2,1,0:T(8,128)(2,1)S(1)} async-done(((bf16[8,3,64,640]{3,2,1,0:T(8,128)(2,1)}), bf16[8,3,64,640]{3,2,1,0:T(8,128)(2,1)S(1)}, u32[]{:S(2)}, u32[]{:S(2)}) %all-to-all-start.2) | async-done | bytes 1966112 | tf_op jit(solution)/shard_map/all_to_all | solution.py:393
  449.4 7.8 %convolution_convert_fusion = bf16[1024,2048]{1,0:T(8,128)(2,1)} fusion(bf16[1024,640]{1,0:T(8,128)(2,1)} %get-tuple-element.120, bf16[2048,640]{1,0:T(8,128)(2,1)} %bitcast.251), kind=kOutput, calls=%fused_computation.9 | convolution fusion | flops 2686451712 | bytes 8126464 | tf_op jit(solution)/shard_map/dot_general | solution.py:85
  457.3 3.7 convolution_convert_fusion.5
  471.1 10.4 %collective-permute-done.18 = bf16[4,4,64,256]{3,2,0,1:T(8,128)(2,1)S(1)} collective-permute-done((bf16[4,4,64,256]{3,2,0,1:T(8,128)(2,1)S(1)}, bf16[4,4,64,256]{3,2,0,1:T(8,128)(2,1)S(1)}, u32[]{:S(2)}, u32[]{:S(2)}) %collective-permute-start.18) | collective-permute-done | bytes 524320 | tf_op jit(solution)/shard_map/ppermute | solution.py:113
  484.0 9.3 %collective-permute-done.14 = bf16[4,4,64,256]{3,2,0,1:T(8,128)(2,1)S(1)} collective-permute-done((bf16[4,4,64,256]{3,2,0,1:T(8,128)(2,1)S(1)}, bf16[4,4,64,256]{3,2,0,1:T(8,128)(2,1)S(1)}, u32[]{:S(2)}, u32[]{:S(2)}) %collective-permute-start.14) | collective-permute-done | bytes 524320 | tf_op jit(solution)/shard_map/ppermute | solution.py:113
  493.3 9.6 %collective-permute-done.19 = bf16[4,4,64,256]{3,2,0,1:T(8,128)(2,1)S(1)} collective-permute-done((bf16[4,4,64,256]{3,2,0,1:T(8,128)(2,1)S(1)}, bf16[4,4,64,256]{3,2,0,1:T(8,128)(2,1)S(1)}, u32[]{:S(2)}, u32[]{:S(2)}) %collective-permute-start.19) | collective-permute-done | bytes 524320 | tf_op jit(solution)/shard_map/ppermute | solution.py:113
  504.5 3.7 all-to-all-start.3
  508.3 3.8 convert_element_type.317
  512.1 7.2 %fusion.19 = f32[32,4]{1,0:T(8,128)S(1)} fusion(bf16[4,512,512]{2,1,0:T(8,128)(2,1)} %convert_element_type.317, s32[512,512]{1,0:T(8,128)} %copy-done.45), kind=kOutput, calls=%fused_computation.60 | convolution fusion | flops 75497472 | bytes 3146240 | tf_op jit(solution)/shard_map/hij,zij->zh/dot_general | solution.py:529
  519.7 1.7 fusion.28
  522.8 1.9 collective-permute-start.21
  524.7 19.3 %collective-permute-done.21 = f32[40,128]{1,0:T(8,128)S(1)} collective-permute-done((f32[40,128]{1,0:T(8,128)S(1)}, f32[40,128]{1,0:T(8,128)S(1)}, u32[]{:S(2)}, u32[]{:S(2)}) %collective-permute-start.21) | collective-permute-done | bytes 20512 | tf_op jit(solution)/shard_map/ppermute | solution.py:113
  543.9 4.0 collective-permute-start.22
  548.0 5.0 all-to-all-done.3.g_ref
  553.0 1.6 copy-done.9
  556.2 7.8 %shard_map.264 = (f32[64,4,2048]{2,1,0:T(4,128)}, f32[64,4,2048]{2,1,0:T(4,128)}, f32[3,64,2048]{2,1,0:T(8,128)}, f32[64,2048]{1,0:T(8,128)}) custom-call(f32[64,4,2048]{2,1,0:T(4,128)S(1)} %copy-done.1, f32[64,4,2048]{2,1,0:T(4,128)S(1)} %copy-done.9, f32[64,4,2048]{2,1,0:T(4,128)S(1)} %copy-done.10, bf16[8,4,64,256]{3,2,1,0:T(8,128)(2,1)S(1)} %all-to-all-done.3.g_ref), custom_call_target="tpu_custom_call" | custom-call | flops 10485760 | bytes 13631488 | tf_op jit(solution)/shard_map/pallas_call | solution.py:167
  564.0 2.2 copy-done.7
  566.2 2.1 copy-done.8
  568.3 6.5 %shard_map.265 = (f32[3,64,5120]{2,1,0:T(8,128)}, f32[3,64,5120]{2,1,0:T(8,128)}, f32[3,64,5120]{2,1,0:T(8,128)}) custom-call(f32[3,64,5120]{2,1,0:T(8,128)S(1)} %bitcast.207, f32[3,64,5120]{2,1,0:T(8,128)S(1)} %bitcast.208, f32[3,64,5120]{2,1,0:T(8,128)S(1)} %bitcast.209, bf16[8,3,64,640]{3,2,1,0:T(8,128)(2,1)S(1)} %copy-done.3), custom_call_target="tpu_custom_call" | custom-call | flops 19660800 | bytes 25559040 | tf_op jit(solution)/shard_map/pallas_call | solution.py:215
  576.4 2.3 collective-permute-done.23
  580.3 2.7 fusion.27
  (277 shorter events, 81.9 us)
Async XLA Ops:
  10.0 8.0 %copy-start.25 = (bf16[2,64,2048]{2,1,0:T(8,128)(2,1)S(1)}, bf16[2,64,2048]{2,1,0:T(8,128)(2,1)}, u32[]{:S(2)}) copy-start(bf16[2,64,2048]{2,1,0:T(8,128)(2,1)} %param.15) | copy-start | bytes 1572868
  10.0 8.2 %copy-start.50 = (f32[2,2048]{1,0:T(2,128)S(1)}, f32[2,2048]{1,0:T(2,128)}, u32[]{:S(2)}) copy-start(f32[2,2048]{1,0:T(2,128)} %param.24) | copy-start | bytes 49156
  11.6 32.9 %all-to-all-start = ((bf16[8,4,64,256]{3,2,1,0:T(8,128)(2,1)}), bf16[8,4,64,256]{3,2,1,0:T(8,128)(2,1)S(1)}, u32[]{:S(2)}, u32[]{:S(2)}) async-start(bf16[8,4,64,256]{3,2,1,0:T(8,128)(2,1)} %copy.91), calls=%async_computation | async-start | bytes 2097152 | tf_op jit(solution)/shard_map/all_to_all | solution.py:389
  17.9 73.3 %all-gather.9.cloned.1.call-start = ((), (), s32[]{:S(2)}) async-start(), calls=%async_computation.12 | async-start | bytes 4718592 | tf_op jit(solution)/shard_map/all_gather | solution.py:419
  18.2 56.3 %copy-start.59 = (f32[2,64]{1,0:T(2,128)}, f32[2,64]{1,0:T(2,128)S(1)}, u32[]{:S(2)}) copy-start(f32[2,64]{1,0:T(2,128)S(1)} %add_rsqrt_fusion.1) | copy-start | bytes 1540
  18.2 56.3 %copy-start.47 = (f32[1,2048]{1,0:T(1,128)}, f32[1,2048]{1,0:T(1,128)S(1)}, u32[]{:S(2)}) copy-start(f32[1,2048]{1,0:T(1,128)S(1)} %get-tuple-element.144) | copy-start | bytes 24580
  44.6 135.9 %all-gather.11.cloned.1.call-start = ((), (), s32[]{:S(2)}) async-start(), calls=%async_computation.13 | async-start | bytes 4718592 | tf_op jit(solution)/shard_map/all_gather | solution.py:419
  44.7 24.8 %collective-permute-start = (bf16[4,8,64,256]{3,2,1,0:T(8,128)(2,1)S(1)}, bf16[4,8,64,256]{3,2,1,0:T(8,128)(2,1)S(1)}, u32[]{:S(2)}, u32[]{:S(2)}) collective-permute-start(bf16[4,8,64,256]{3,2,1,0:T(8,128)(2,1)S(1)} %bitcast.230), channel_id=1, source_target_pairs={{0,1},{1,0},{2,3},{3,2},{4,5},{5,4},{6,7},{7,6},{8,9},{9,8},{10,11... | collective-permute-start | bytes 3145736 | tf_op jit(solution)/shard_map/ppermute | solution.py:113
  46.2 24.5 %collective-permute-start.1 = (bf16[4,8,64,256]{3,2,1,0:T(8,128)(2,1)S(1)}, bf16[4,8,64,256]{3,2,1,0:T(8,128)(2,1)}, u32[]{:S(2)}, u32[]{:S(2)}) collective-permute-start(bf16[4,8,64,256]{3,2,1,0:T(8,128)(2,1)S(1)} %bitcast.231), channel_id=1, source_target_pairs={{0,2},{1,3},{2,0},{3,1},{4,6},{5,7},{6,4},{7,5},{8,10},{9,11},{10,... | collective-permute-start | bytes 3145736 | tf_op jit(solution)/shard_map/ppermute | solution.py:113
  74.5 12.4 %collective-permute-start.2 = (bf16[4,4,64,256]{3,2,1,0:T(8,128)(2,1)S(1)}, bf16[4,4,64,256]{3,2,1,0:T(8,128)(2,1)S(1)}, u32[]{:S(2)}, u32[]{:S(2)}) collective-permute-start(bf16[4,4,64,256]{3,2,1,0:T(8,128)(2,1)S(1)} %slice.108), channel_id=1, source_target_pairs={{0,2},{1,3},{2,0},{3,1},{4,6},{5,7},{6,4},{7,5},{8,10},{9,11},{10,... | collective-permute-start | bytes 1572872 | tf_op jit(solution)/shard_map/ppermute | solution.py:113
  77.2 12.1 %collective-permute-start.3 = (bf16[4,4,64,256]{3,2,1,0:T(8,128)(2,1)S(1)}, bf16[4,4,64,256]{3,2,1,0:T(8,128)(2,1)S(1)}, u32[]{:S(2)}, u32[]{:S(2)}) collective-permute-start(bf16[4,4,64,256]{3,2,1,0:T(8,128)(2,1)S(1)} %slice.109), channel_id=1, source_target_pairs={{0,1},{1,0},{2,3},{3,2},{4,5},{5,4},{6,7},{7,6},{8,9},{9,8},{10,11... | collective-permute-start | bytes 1572872 | tf_op jit(solution)/shard_map/ppermute | solution.py:113
  95.1 24.1 %copy-start.15 = (bf16[1024,256]{1,0:T(8,128)(2,1)}, bf16[1024,256]{1,0:T(8,128)(2,1)S(1)}, u32[]{:S(2)}) copy-start(bf16[1024,256]{1,0:T(8,128)(2,1)S(1)} %convolution_convert_fusion.7) | copy-start | bytes 1572868
  96.6 22.6 %copy-start.17 = (bf16[1024,256]{1,0:T(8,128)(2,1)}, bf16[1024,256]{1,0:T(8,128)(2,1)S(1)}, u32[]{:S(2)}) copy-start(bf16[1024,256]{1,0:T(8,128)(2,1)S(1)} %convolution_convert_fusion.8) | copy-start | bytes 1572868
  97.9 21.3 %copy-start.19 = (bf16[1024,256]{1,0:T(8,128)(2,1)}, bf16[1024,256]{1,0:T(8,128)(2,1)S(1)}, u32[]{:S(2)}) copy-start(bf16[1024,256]{1,0:T(8,128)(2,1)S(1)} %convolution_convert_fusion.9) | copy-start | bytes 1572868
  100.1 78.8 %all-to-all-start.1 = ((bf16[8,3,64,640]{3,2,1,0:T(8,128)(2,1)}), bf16[8,3,64,640]{3,2,1,0:T(8,128)(2,1)}, u32[]{:S(2)}, u32[]{:S(2)}) async-start(bf16[8,3,64,640]{3,2,1,0:T(8,128)(2,1)} %bitcast.228), calls=%async_computation.1 | async-start | bytes 3932160 | tf_op jit(solution)/shard_map/all_to_all | solution.py:389
  104.5 124.9 %reduce-scatter.5.cloned.1.call-start = ((), (), s32[]{:S(2)}) async-start(), calls=%async_computation.8 | async-start | bytes 4718592 | tf_op jit(solution)/shard_map/reduce_scatter | solution.py:425
  105.2 10.4 %copy-start.45 = (s32[512,512]{1,0:T(8,128)}, s32[512,512]{1,0:T(8,128)S(1)}, u32[]{:S(2)}) copy-start(s32[512,512]{1,0:T(8,128)S(1)} %fusion.30) | copy-start | bytes 3145732
  121.5 11.2 %copy-start.13 = (s32[2,512,1]{2,1,0:T(8,128)}, s32[2,512,1]{2,1,0:T(8,128)S(1)}, u32[]{:S(2)}) copy-start(s32[2,512,1]{2,1,0:T(8,128)S(1)} %copy.99.seg_q_ref) | copy-start | bytes 12292
  121.5 11.2 %copy-start.38 = (bf16[1,8,4,64,256]{4,3,2,1,0:T(8,128)(2,1)S(1)}, bf16[1,8,4,64,256]{4,3,2,1,0:T(8,128)(2,1)}, u32[]{:S(2)}) copy-start(bf16[1,8,4,64,256]{4,3,2,1,0:T(8,128)(2,1)} %get-tuple-element.125) | copy-start | bytes 3145732
  180.6 50.0 %copy-start.27 = (bf16[8,3,64,640]{3,2,0,1:T(8,128)(2,1)}, bf16[8,3,64,640]{3,2,0,1:T(8,128)(2,1)S(1)}, u32[]{:S(2)}) copy-start(bf16[8,3,64,640]{3,2,0,1:T(8,128)(2,1)S(1)} %copy.152) | copy-start | bytes 5898244
  180.6 96.9 %all-gather.13.cloned.1.call-start = ((), (), s32[]{:S(2)}) async-start(), calls=%async_computation.14 | async-start | bytes 4718592 | tf_op jit(solution)/shard_map/all_gather | solution.py:419
  180.7 49.9 %collective-permute-start.4 = (bf16[3,8,64,640]{3,2,1,0:T(8,128)(2,1)S(1)}, bf16[3,8,64,640]{3,2,1,0:T(8,128)(2,1)}, u32[]{:S(2)}, u32[]{:S(2)}) collective-permute-start(bf16[3,8,64,640]{3,2,1,0:T(8,128)(2,1)S(1)} %bitcast.224), channel_id=1, source_target_pairs={{0,1},{1,0},{2,3},{3,2},{4,5},{5,4},{6,7},{7,6},{8,9},{9,8},{10,11... | collective-permute-start | bytes 5898248 | tf_op jit(solution)/shard_map/ppermute | solution.py:113
  182.2 48.4 %collective-permute-start.5 = (bf16[3,8,64,640]{3,2,1,0:T(8,128)(2,1)S(1)}, bf16[3,8,64,640]{3,2,1,0:T(8,128)(2,1)}, u32[]{:S(2)}, u32[]{:S(2)}) collective-permute-start(bf16[3,8,64,640]{3,2,1,0:T(8,128)(2,1)S(1)} %bitcast.225), channel_id=1, source_target_pairs={{0,2},{1,3},{2,0},{3,1},{4,6},{5,7},{6,4},{7,5},{8,10},{9,11},{10,... | collective-permute-start | bytes 5898248 | tf_op jit(solution)/shard_map/ppermute | solution.py:113
  230.9 118.6 %copy-start.21 = (f32[2,64,2048]{2,1,0:T(8,128)}, f32[2,64,2048]{2,1,0:T(8,128)S(1)}, u32[]{:S(2)}) copy-start(f32[2,64,2048]{2,1,0:T(8,128)S(1)} %get-tuple-element.110) | copy-start | bytes 3145732
  232.0 115.3 %reduce-scatter.7.cloned.1.call-start = ((), (), s32[]{:S(2)}) async-start(), calls=%async_computation.9 | async-start | bytes 4718592 | tf_op jit(solution)/shard_map/reduce_scatter | solution.py:425
  233.4 21.4 %collective-permute-start.6 = (bf16[3,4,64,640]{3,2,1,0:T(8,128)(2,1)S(1)}, bf16[3,4,64,640]{3,2,1,0:T(8,128)(2,1)S(1)}, u32[]{:S(2)}, u32[]{:S(2)}) collective-permute-start(bf16[3,4,64,640]{3,2,1,0:T(8,128)(2,1)S(1)} %slice.115), channel_id=1, source_target_pairs={{0,2},{1,3},{2,0},{3,1},{4,6},{5,7},{6,4},{7,5},{8,10},{9,11},{10,... | collective-permute-start | bytes 2949128 | tf_op jit(solution)/shard_map/ppermute | solution.py:113
  236.2 21.1 %collective-permute-start.7 = (bf16[3,4,64,640]{3,2,1,0:T(8,128)(2,1)S(1)}, bf16[3,4,64,640]{3,2,1,0:T(8,128)(2,1)S(1)}, u32[]{:S(2)}, u32[]{:S(2)}) collective-permute-start(bf16[3,4,64,640]{3,2,1,0:T(8,128)(2,1)S(1)} %slice.116), channel_id=1, source_target_pairs={{0,1},{1,0},{2,3},{3,2},{4,5},{5,4},{6,7},{7,6},{8,9},{9,8},{10,11... | collective-permute-start | bytes 2949128 | tf_op jit(solution)/shard_map/ppermute | solution.py:113
  298.4 99.9 %all-gather.15.cloned.1.call-start = ((), (), s32[]{:S(2)}) async-start(), calls=%async_computation.15 | async-start | bytes 4718592 | tf_op jit(solution)/shard_map/all_gather | solution.py:419
  318.9 29.6 %collective-permute-start.8 = (bf16[3,4,64,640]{3,2,0,1:T(8,128)(2,1)}, bf16[3,4,64,640]{3,2,0,1:T(8,128)(2,1)}, u32[]{:S(2)}, u32[]{:S(2)}) collective-permute-start(bf16[3,4,64,640]{3,2,0,1:T(8,128)(2,1)} %get-tuple-element.130), channel_id=1, source_target_pairs={{0,1},{1,0},{2,3},{3,2},{4,5},{5,4},{6,7},{7,6},{8,9},{9,8},{10,11... | collective-permute-start | bytes 2949128 | tf_op jit(solution)/shard_map/ppermute | solution.py:113
  320.4 28.1 %collective-permute-start.9 = (bf16[3,4,64,640]{3,2,0,1:T(8,128)(2,1)}, bf16[3,4,64,640]{3,2,0,1:T(8,128)(2,1)}, u32[]{:S(2)}, u32[]{:S(2)}) collective-permute-start(bf16[3,4,64,640]{3,2,0,1:T(8,128)(2,1)} %get-tuple-element.129), channel_id=1, source_target_pairs={{0,2},{1,3},{2,0},{3,1},{4,6},{5,7},{6,4},{7,5},{8,10},{9,11},{10,... | collective-permute-start | bytes 2949128 | tf_op jit(solution)/shard_map/ppermute | solution.py:113
  326.3 23.1 %copy-start.30 = (bf16[2,64,2048]{2,1,0:T(8,128)(2,1)S(1)}, bf16[2,64,2048]{2,1,0:T(8,128)(2,1)}, u32[]{:S(2)}) copy-start(bf16[2,64,2048]{2,1,0:T(8,128)(2,1)} %param.17) | copy-start | bytes 1572868
  350.6 28.4 %copy-start.41 = (bf16[3,4,64,640]{3,2,0,1:T(8,128)(2,1)S(1)}, bf16[3,4,64,640]{3,2,0,1:T(8,128)(2,1)}, u32[]{:S(2)}) copy-start(bf16[3,4,64,640]{3,2,0,1:T(8,128)(2,1)} %get-tuple-element.75) | copy-start | bytes 2949124
  352.6 24.8 %collective-permute-start.11 = (bf16[3,4,64,640]{3,2,0,1:T(8,128)(2,1)S(1)}, bf16[3,4,64,640]{3,2,0,1:T(8,128)(2,1)S(1)}, u32[]{:S(2)}, u32[]{:S(2)}) collective-permute-start(bf16[3,4,64,640]{3,2,0,1:T(8,128)(2,1)S(1)} %add_convert_fusion.5), channel_id=1, source_target_pairs={{0,2},{1,3},{2,0},{3,1},{4,6},{5,7},{6,4},{7,5},{8,10},{9,11},{10,... | collective-permute-start | bytes 2949128 | tf_op jit(solution)/shard_map/ppermute | solution.py:113
  354.1 24.9 %collective-permute-start.10 = (bf16[3,4,64,640]{3,2,0,1:T(8,128)(2,1)}, bf16[3,4,64,640]{3,2,0,1:T(8,128)(2,1)S(1)}, u32[]{:S(2)}, u32[]{:S(2)}) collective-permute-start(bf16[3,4,64,640]{3,2,0,1:T(8,128)(2,1)} %get-tuple-element.76), channel_id=1, source_target_pairs={{0,1},{1,0},{2,3},{3,2},{4,5},{5,4},{6,7},{7,6},{8,9},{9,8},{10,11... | collective-permute-start | bytes 2949128 | tf_op jit(solution)/shard_map/ppermute | solution.py:113
  357.1 39.3 %copy-start.40 = (bf16[3,4,64,640]{3,2,0,1:T(8,128)(2,1)S(1)}, bf16[3,4,64,640]{3,2,0,1:T(8,128)(2,1)}, u32[]{:S(2)}) copy-start(bf16[3,4,64,640]{3,2,0,1:T(8,128)(2,1)} %get-tuple-element.79) | copy-start | bytes 2949124
  357.1 39.3 %collective-permute-start.13 = (bf16[3,4,64,640]{3,2,0,1:T(8,128)(2,1)S(1)}, bf16[3,4,64,640]{3,2,0,1:T(8,128)(2,1)S(1)}, u32[]{:S(2)}, u32[]{:S(2)}) collective-permute-start(bf16[3,4,64,640]{3,2,0,1:T(8,128)(2,1)S(1)} %add_convert_fusion.3), channel_id=1, source_target_pairs={{0,1},{1,0},{2,3},{3,2},{4,5},{5,4},{6,7},{7,6},{8,9},{9,8},{10,11... | collective-permute-start | bytes 2949128 | tf_op jit(solution)/shard_map/ppermute | solution.py:113
  357.7 38.7 %collective-permute-start.12 = (bf16[3,4,64,640]{3,2,0,1:T(8,128)(2,1)S(1)}, bf16[3,4,64,640]{3,2,0,1:T(8,128)(2,1)S(1)}, u32[]{:S(2)}, u32[]{:S(2)}) collective-permute-start(bf16[3,4,64,640]{3,2,0,1:T(8,128)(2,1)S(1)} %copy-done.46), channel_id=1, source_target_pairs={{0,2},{1,3},{2,0},{3,1},{4,6},{5,7},{6,4},{7,5},{8,10},{9,11},{10,... | collective-permute-start | bytes 2949128 | tf_op jit(solution)/shard_map/ppermute | solution.py:113
  398.4 50.6 %all-to-all-start.2 = ((bf16[8,3,64,640]{3,2,1,0:T(8,128)(2,1)}), bf16[8,3,64,640]{3,2,1,0:T(8,128)(2,1)S(1)}, u32[]{:S(2)}, u32[]{:S(2)}) async-start(bf16[8,3,64,640]{3,2,1,0:T(8,128)(2,1)} %bitcast.229), calls=%async_computation.4 | async-start | bytes 3932160 | tf_op jit(solution)/shard_map/all_to_all | solution.py:393
  402.7 117.0 %reduce-scatter.9.cloned.1.call-start = ((), (), s32[]{:S(2)}) async-start(), calls=%async_computation.10 | async-start | bytes 4718592 | tf_op jit(solution)/shard_map/reduce_scatter | solution.py:425
  406.8 12.3 %copy-start.37 = (bf16[1,8,4,64,256]{4,3,2,1,0:T(8,128)(2,1)S(1)}, bf16[1,8,4,64,256]{4,3,2,1,0:T(8,128)(2,1)}, u32[]{:S(2)}) copy-start(bf16[1,8,4,64,256]{4,3,2,1,0:T(8,128)(2,1)} %get-tuple-element.127) | copy-start | bytes 3145732
  449.0 8.3 %copy-start.2 = (bf16[8,3,64,640]{3,2,1,0:T(8,128)(2,1)}, bf16[8,3,64,640]{3,2,1,0:T(8,128)(2,1)S(1)}, u32[]{:S(2)}) copy-start(bf16[8,3,64,640]{3,2,1,0:T(8,128)(2,1)S(1)} %all-to-all-done.2.g_ref) | copy-start | bytes 5898244
  449.0 131.3 %reduce-scatter.11.cloned.1.call-start = ((), (), s32[]{:S(2)}) async-start(), calls=%async_computation.11 | async-start | bytes 4718592 | tf_op jit(solution)/shard_map/reduce_scatter | solution.py:425
  466.6 14.9 %collective-permute-start.18 = (bf16[4,4,64,256]{3,2,0,1:T(8,128)(2,1)S(1)}, bf16[4,4,64,256]{3,2,0,1:T(8,128)(2,1)S(1)}, u32[]{:S(2)}, u32[]{:S(2)}) collective-permute-start(bf16[4,4,64,256]{3,2,0,1:T(8,128)(2,1)S(1)} %get-tuple-element.140), channel_id=1, source_target_pairs={{0,2},{1,3},{2,0},{3,1},{4,6},{5,7},{6,4},{7,5},{8,10},{9,11},{10,... | collective-permute-start | bytes 1572872 | tf_op jit(solution)/shard_map/ppermute | solution.py:113
  467.2 16.0 %collective-permute-start.15 = (bf16[4,4,64,256]{3,2,0,1:T(8,128)(2,1)S(1)}, bf16[4,4,64,256]{3,2,0,1:T(8,128)(2,1)S(1)}, u32[]{:S(2)}, u32[]{:S(2)}) collective-permute-start(bf16[4,4,64,256]{3,2,0,1:T(8,128)(2,1)S(1)} %get-tuple-element.139), channel_id=1, source_target_pairs={{0,1},{1,0},{2,3},{3,2},{4,5},{5,4},{6,7},{7,6},{8,9},{9,8},{10,11... | collective-permute-start | bytes 1572872 | tf_op jit(solution)/shard_map/ppermute | solution.py:113
  468.8 24.4 %collective-permute-start.14 = (bf16[4,4,64,256]{3,2,0,1:T(8,128)(2,1)S(1)}, bf16[4,4,64,256]{3,2,0,1:T(8,128)(2,1)S(1)}, u32[]{:S(2)}, u32[]{:S(2)}) collective-permute-start(bf16[4,4,64,256]{3,2,0,1:T(8,128)(2,1)S(1)} %slice.154), channel_id=1, source_target_pairs={{0,1},{1,0},{2,3},{3,2},{4,5},{5,4},{6,7},{7,6},{8,9},{9,8},{10,11... | collective-permute-start | bytes 1572872 | tf_op jit(solution)/shard_map/ppermute | solution.py:113
  469.5 23.8 %collective-permute-start.17 = (bf16[4,4,64,256]{3,2,0,1:T(8,128)(2,1)S(1)}, bf16[4,4,64,256]{3,2,0,1:T(8,128)(2,1)S(1)}, u32[]{:S(2)}, u32[]{:S(2)}) collective-permute-start(bf16[4,4,64,256]{3,2,0,1:T(8,128)(2,1)S(1)} %slice.158), channel_id=1, source_target_pairs={{0,2},{1,3},{2,0},{3,1},{4,6},{5,7},{6,4},{7,5},{8,10},{9,11},{10,... | collective-permute-start | bytes 1572872 | tf_op jit(solution)/shard_map/ppermute | solution.py:113
  481.6 21.2 %collective-permute-start.19 = (bf16[4,4,64,256]{3,2,0,1:T(8,128)(2,1)S(1)}, bf16[4,4,64,256]{3,2,0,1:T(8,128)(2,1)S(1)}, u32[]{:S(2)}, u32[]{:S(2)}) collective-permute-start(bf16[4,4,64,256]{3,2,0,1:T(8,128)(2,1)S(1)} %add_convert_fusion.7), channel_id=1, source_target_pairs={{0,1},{1,0},{2,3},{3,2},{4,5},{5,4},{6,7},{7,6},{8,9},{9,8},{10,11... | collective-permute-start | bytes 1572872 | tf_op jit(solution)/shard_map/ppermute | solution.py:113
  483.3 19.6 %collective-permute-start.16 = (bf16[4,4,64,256]{3,2,0,1:T(8,128)(2,1)S(1)}, bf16[4,4,64,256]{3,2,0,1:T(8,128)(2,1)S(1)}, u32[]{:S(2)}, u32[]{:S(2)}) collective-permute-start(bf16[4,4,64,256]{3,2,0,1:T(8,128)(2,1)S(1)} %add_convert_fusion.9), channel_id=1, source_target_pairs={{0,2},{1,3},{2,0},{3,1},{4,6},{5,7},{6,4},{7,5},{8,10},{9,11},{10,... | collective-permute-start | bytes 1572872 | tf_op jit(solution)/shard_map/ppermute | solution.py:113
  504.5 48.5 %all-to-all-start.3 = ((bf16[8,4,64,256]{3,2,1,0:T(8,128)(2,1)}), bf16[8,4,64,256]{3,2,1,0:T(8,128)(2,1)S(1)}, u32[]{:S(2)}, u32[]{:S(2)}) async-start(bf16[8,4,64,256]{3,2,1,0:T(8,128)(2,1)} %maximum_bitcast_fusion), calls=%async_computation.7 | async-start | bytes 2097152 | tf_op jit(solution)/shard_map/all_to_all | solution.py:393
  512.1 7.6 %copy-start.60 = (f32[2,64]{1,0:T(2,128)S(1)}, f32[2,64]{1,0:T(2,128)}, u32[]{:S(2)}) copy-start(f32[2,64]{1,0:T(2,128)} %copy-done.59) | copy-start | bytes 1540
  512.1 9.2 %copy-start.49 = (f32[2048]{0:T(1024)S(1)}, f32[2048]{0:T(1024)}, u32[]{:S(2)}) copy-start(f32[2048]{0:T(1024)} %get-tuple-element.99) | copy-start | bytes 24580
  512.1 40.9 %copy-start.1 = (f32[64,4,2048]{2,1,0:T(4,128)S(1)}, f32[64,4,2048]{2,1,0:T(4,128)}, u32[]{:S(2)}) copy-start(f32[64,4,2048]{2,1,0:T(4,128)} %w_ref.1) | copy-start | bytes 6291460
  521.3 1.5 collective-permute-start.20
  522.8 21.1 %collective-permute-start.21 = (f32[40,128]{1,0:T(8,128)S(1)}, f32[40,128]{1,0:T(8,128)S(1)}, u32[]{:S(2)}, u32[]{:S(2)}) collective-permute-start(f32[40,128]{1,0:T(8,128)S(1)} %fusion.47), channel_id=1, source_target_pairs={{0,8},{4,12},{8,0},{12,4},{16,24},{20,28},{24,16},{28,20},{1,9},{5... | collective-permute-start | bytes 61448 | tf_op jit(solution)/shard_map/ppermute | solution.py:113
  543.9 30.9 %collective-permute-start.22 = (f32[40,128]{1,0:T(8,128)S(1)}, f32[40,128]{1,0:T(8,128)S(1)}, u32[]{:S(2)}, u32[]{:S(2)}) collective-permute-start(f32[40,128]{1,0:T(8,128)S(1)} %fusion.105), channel_id=1, source_target_pairs={{0,16},{4,20},{8,24},{12,28},{16,0},{20,4},{24,8},{28,12},{1,17},{... | collective-permute-start | bytes 61448 | tf_op jit(solution)/shard_map/ppermute | solution.py:113
  556.2 7.8 %copy-start = (f32[64,3,5120]{2,0,1:T(8,128)S(1)}, f32[64,3,5120]{2,0,1:T(8,128)}, u32[]{:S(2)}) copy-start(f32[64,3,5120]{2,0,1:T(8,128)} %param.21) | copy-start | bytes 11796484
  556.2 7.8 %copy-start.3 = (bf16[8,3,64,640]{3,2,1,0:T(8,128)(2,1)S(1)}, bf16[8,3,64,640]{3,2,1,0:T(8,128)(2,1)}, u32[]{:S(2)}) copy-start(bf16[8,3,64,640]{3,2,1,0:T(8,128)(2,1)} %copy-done.2) | copy-start | bytes 5898244
  568.3 12.0 %copy-start.22 = (f32[2,64,2048]{2,1,0:T(8,128)S(1)}, f32[2,64,2048]{2,1,0:T(8,128)}, u32[]{:S(2)}) copy-start(f32[2,64,2048]{2,1,0:T(8,128)} %copy-done.21) | copy-start | bytes 3145732
  568.3 12.0 %copy-start.24 = (f32[2,64,2048]{2,1,0:T(8,128)S(1)}, f32[2,64,2048]{2,1,0:T(8,128)}, u32[]{:S(2)}) copy-start(f32[2,64,2048]{2,1,0:T(8,128)} %copy-done.23) | copy-start | bytes 3145732
  568.3 12.0 %copy-start.26 = (bf16[2,64,2048]{2,1,0:T(8,128)(2,1)S(1)}, bf16[2,64,2048]{2,1,0:T(8,128)(2,1)}, u32[]{:S(2)}) copy-start(bf16[2,64,2048]{2,1,0:T(8,128)(2,1)} %param.15) | copy-start | bytes 1572868
  568.3 12.0 %copy-start.31 = (bf16[2,64,2048]{2,1,0:T(8,128)(2,1)S(1)}, bf16[2,64,2048]{2,1,0:T(8,128)(2,1)}, u32[]{:S(2)}) copy-start(bf16[2,64,2048]{2,1,0:T(8,128)(2,1)} %param.17) | copy-start | bytes 1572868
  568.3 12.0 %copy-start.62 = (f32[2,64]{1,0:T(2,128)S(1)}, f32[2,64]{1,0:T(2,128)}, u32[]{:S(2)}) copy-start(f32[2,64]{1,0:T(2,128)} %copy-done.61) | copy-start | bytes 1540
  574.8 3.8 collective-permute-start.23
  578.7 4.3 collective-permute-start.24
  (46 other events, 174.7 us)
Sparse Core Ops, SparseCore 0:
  44.8 46.0 all-gather.8
  92.5 80.7 all-gather.10
  180.7 48.6 reduce-scatter.4
  232.1 45.2 all-gather.12
  298.5 48.7 reduce-scatter.6
  350.8 45.2 all-gather.14
  449.1 47.9 reduce-scatter.8
  499.3 65.7 reduce-scatter.10

commit v4 on v3

--- a/solution.py
+++ b/solution.py
@@ -1,3 +1,5 @@
+import math
+
 import jax
 import jax.numpy as jnp
 from jax import lax
@@ -26,10 +28,6 @@
 def rms_norm(values, gain_vec):
     inv_root = lax.rsqrt(jnp.mean(values * values, axis=-1, keepdims=True) + NORM_EPSILON)
     return values * inv_root * gain_vec
-
-
-def gelu_tanh(values):
-    return jax.nn.gelu(values, approximate=True)
 
 
 def bucket_edges():
@@ -103,6 +101,53 @@
     scaled = grads * gain_vec
     grad_in = inv_root * (scaled - unit * jnp.mean(unit * scaled, axis=-1, keepdims=True))
     return grad_in, jnp.sum(grads * unit, axis=(0, 1))
+
+
+def feed_middle(normed, grad_inner, weight_gate, weight_up):
+    tokens, width = normed.shape
+    hidden = weight_gate.shape[1]
+    block = 256
+    scale = (2.0 / math.pi) ** 0.5
+
+    def body(n_ref, gi_ref, wg_ref, wu_ref, inner_ref, gg_ref, gu_ref, out_ref):
+        gate = dot(n_ref[...], wg_ref[...])
+        up = dot(n_ref[...], wu_ref[...])
+        grad_inner = gi_ref[...]
+        squared = gate * gate
+        tanh = jnp.tanh(scale * (gate + 0.044715 * (squared * gate)))
+        half = 0.5 * (1.0 + tanh)
+        act = gate * half
+        slope = half + 0.5 * gate * (1.0 - tanh * tanh) * (scale * (1.0 + 0.134145 * squared))
+        inner_ref[...] = (act * up).astype(jnp.bfloat16)
+        grad_gate = (grad_inner * up * slope).astype(jnp.bfloat16)
+        grad_up = (grad_inner * act).astype(jnp.bfloat16)
+        gg_ref[...] = grad_gate
+        gu_ref[...] = grad_up
+        total = dot_t(grad_gate, wg_ref[...]) + dot_t(grad_up, wu_ref[...])
+        out_ref[...] = total.astype(jnp.bfloat16)
+
+    rows = pl.BlockSpec((block, width), lambda i: (i, 0))
+    units = pl.BlockSpec((block, hidden), lambda i: (i, 0))
+    weights = pl.BlockSpec((width, hidden), lambda i: (0, 0))
+    low_units = jax.ShapeDtypeStruct((tokens, hidden), jnp.bfloat16)
+    return pl.pallas_call(
+        body,
+        grid=(tokens // block,),
+        in_specs=[rows, units, weights, weights],
+        out_specs=[units, units, units, rows],
+        out_shape=[
+            low_units,
+            low_units,
+            low_units,
+            jax.ShapeDtypeStruct((tokens, width), jnp.bfloat16),
+        ],
+        compiler_params=pltpu.CompilerParams(vmem_limit_bytes=40 * MIB),
+        cost_estimate=pl.CostEstimate(
+            flops=8 * tokens * width * hidden,
+            bytes_accessed=4 * tokens * width + 10 * tokens * hidden + 4 * width * hidden,
+            transcendentals=tokens * hidden,
+        ),
+    )(normed, grad_inner, weight_gate, weight_up)
 
 
 def partner_pairs(axis, offset):
@@ -496,24 +541,21 @@
     weight_gate, weight_up, weight_down = feed_low[0], feed_low[1], feed_low[2]
     hidden_state = inputs + attention_out
     normed_two = gather_tokens(rms_norm(hidden_state, gains[1]).astype(jnp.bfloat16))
-    gate_pre = dot(normed_two, weight_gate)
-    up_pre = dot(normed_two, weight_up)
-    gate_act, gate_back = jax.vjp(gelu_tanh, gate_pre)
-    inner = (gate_act * up_pre).astype(jnp.bfloat16)
+    grad_inner = dot(grad_out, weight_down)
+    inner, grad_gate, grad_up, grad_two = feed_middle(
+        normed_two, grad_inner, weight_gate, weight_up
+    )
     feed_partial = dot_t(inner, weight_down).astype(jnp.bfloat16)
-    grad_inner = dot(grad_out, weight_down)
-    grad_gate = gate_back(grad_inner * up_pre)[0].astype(jnp.bfloat16)
-    grad_up = (grad_inner * gate_act).astype(jnp.bfloat16)
-    grad_normed_two = scatter_tokens(
-        dot_t(grad_gate, weight_gate) + dot_t(grad_up, weight_up), shape
-    )
+    grad_normed_two = scatter_tokens(grad_two, shape)
     grads_feed = [
         outer_sum(normed_two, grad_gate).astype(jnp.bfloat16),
         outer_sum(normed_two, grad_up).astype(jnp.bfloat16),
         outer_sum(grad_out, inner).astype(jnp.bfloat16),
     ]
     feed_steps = to_rows_first(grads_feed)
-    grad_normed_two, feed_steps = lax.optimization_barrier((grad_normed_two, feed_steps))
+    grad_normed_two, feed_steps, feed_partial = lax.optimization_barrier(
+        (grad_normed_two, feed_steps, feed_partial)
+    )
     feed_steps = scatter_dp_second(feed_steps)
     grad_hidden_norm, grad_gain_two = norm_back(hidden_state, gains[1], grad_normed_two)
     grad_hidden = cotangent.astype(jnp.float32) + grad_hidden_norm
@@ -549,14 +591,15 @@
     grad_table = lax.dynamic_update_slice_in_dim(
         jnp.zeros((NUM_BUCKETS, HEADS), jnp.float32), grad_table_here, seq_index * heads_here, 1
     )
+    new_feed = update_feed(feed_weight, feed_first, feed_second, feed_total)
     small = jnp.concatenate([grad_gain_one, grad_gain_two, grad_table.reshape(-1)])
+    small, new_feed = lax.optimization_barrier((small, new_feed))
     small = sum_all(small.reshape(-1, 128)).reshape(-1)
     gains_total = small[: 2 * width].reshape(2, width)
     table_total = small[2 * width :].reshape(NUM_BUCKETS, HEADS)
     new_attention = update_attention(
         attention_weight, attention_first, attention_second, attention_total
     )
-    new_feed = update_feed(feed_weight, feed_first, feed_second, feed_total)
     new_gains = adam_update(gains, gains_first, gains_second, gains_total, 0.6, 0.0)
     new_table = adam_update(rel_table, table_first, table_second, table_total, 1.5, 0.0)
     return (

time: 598 us -> 588 us (0.983)
  matrix products: 91.7 us -> 67.4 us
  Pallas kernels: 37.7 us -> 54.8 us
  waiting for transfers between devices: 309 us -> 296 us
  local copies, waits for them, and re-layouts: 50.8 us -> 57.3 us
    all_gather x4, waiting for transfers between devices: 10.2 us -> 49.9 us  [gather_tokens(): full = lax.all_gather(local_rows, 'seq', axis=0)]
    all_to_all x2, waiting for transfers between devices: 68.2 us -> 30.7 us  [to_columns(): return lax.all_to_all(send, 'seq', 0, 0).transpose(1, 0, 2, 3)]
    pallas_call x0 -> x1, Pallas kernels: none -> 16.9 us  [feed_middle(): pl.pallas_call(body, grid=(tokens // block,), in_specs=[rows, units, weig...]
    ppermute x25, waiting for transfers between devices: 136 us -> 121 us  [swap(): return lax.ppermute(value, axis, partner_pairs(axis, offset))]
    unnamed x150 -> x144, local copies, waits for them, and re-layouts: 13.7 us -> 27 us
    dot_general x7 -> x5, matrix products: 27.1 us -> 14.9 us  [dot(): return jnp.dot(left, right, preferred_element_type=jnp.float32)]
    dot_general x7 -> x5, matrix products: 25.6 us -> 14.2 us  [dot_t(): lax.dot_general(left, right, (((1,), (1,)), ((), ())), preferred_element_...]
  transfers between devices with their start and end apart: 37 -> 37, of which waited for: 22 -> 24; matrix products, arithmetic and copies ran while one was open for 22% -> 21% of each run, Pallas kernels for 6% -> 7%
where the time goes in v4:
time: 588 us; the launch traced here: 577 us
  waiting for transfers between devices  296 us (50%)
  matrix products  67.4 us (11%)
  local copies, waits for them, and re-layouts  57.3 us (10%)
  Pallas kernels  54.8 us (9%)
  starting transfers between devices  53.5 us (9%)
  other arithmetic  32.7 us (6%)
  between operations  15.4 us (3%)
    ppermute x25, waiting for transfers between devices, swap(): return lax.ppermute(value, axis, partner_pairs(axis, offset))  121 us
    reduce_scatter x4, waiting for transfers between devices, scatter_tokens(): lax.psum_scatter(send, 'seq', scatter_dimension=0).astype(jnp.float32)  66.5 us
    all_gather x4, waiting for transfers between devices, gather_tokens(): full = lax.all_gather(local_rows, 'seq', axis=0)  49.9 us
    ppermute x25, starting transfers between devices, swap(): return lax.ppermute(value, axis, partner_pairs(axis, offset))  34.1 us
    all_to_all x2, waiting for transfers between devices, to_columns(): return lax.all_to_all(send, 'seq', 0, 0).transpose(1, 0, 2, 3)  30.7 us
    unnamed x144, local copies, waits for them, and re-layouts  27 us
    all_to_all x2, waiting for transfers between devices, to_rows(): return lax.all_to_all(mine.transpose(1, 0, 2, 3), 'seq', 0, 0)  26.9 us
    dot_general x7, matrix products, outer_sum(): lax.dot_general(left, right, (((0,), (0,)), ((), ())), preferred_element_...  21.5 us
  transfers between devices with their start and end apart: 37, of which 24 were waited for; matrix products, arithmetic and copies ran while one was open for 21% of the time, Pallas kernels for 7%

profile of v4, /device:TPU:0, one launch (start us, length us, event | category | flops | bytes accessed | tf_op | source)
XLA Modules:
  0.0 577.2 jit_solution(17077032161634837717)
XLA Ops:
  7.2 2.0 convert_bitcast_fusion
  11.6 6.3 %all-to-all-start = ((bf16[8,4,64,256]{3,2,1,0:T(8,128)(2,1)}), bf16[8,4,64,256]{3,2,1,0:T(8,128)(2,1)S(1)}, u32[]{:S(2)}, u32[]{:S(2)}) async-start(bf16[8,4,64,256]{3,2,1,0:T(8,128)(2,1)} %copy.96), calls=%async_computation | async-start | bytes 2097152 | tf_op jit(solution)/shard_map/all_to_all | solution.py:434
  19.2 25.3 %all-to-all-done = bf16[8,4,64,256]{3,2,1,0:T(8,128)(2,1)S(1)} async-done(((bf16[8,4,64,256]{3,2,1,0:T(8,128)(2,1)}), bf16[8,4,64,256]{3,2,1,0:T(8,128)(2,1)S(1)}, u32[]{:S(2)}, u32[]{:S(2)}) %all-to-all-start) | async-done | bytes 1048608 | tf_op jit(solution)/shard_map/all_to_all | solution.py:434
  47.8 21.7 %collective-permute-done = bf16[4,8,64,256]{3,2,1,0:T(8,128)(2,1)S(1)} collective-permute-done((bf16[4,8,64,256]{3,2,1,0:T(8,128)(2,1)S(1)}, bf16[4,8,64,256]{3,2,1,0:T(8,128)(2,1)S(1)}, u32[]{:S(2)}, u32[]{:S(2)}) %collective-permute-start) | collective-permute-done | bytes 1048608 | tf_op jit(solution)/shard_map/ppermute | solution.py:158
  70.8 3.7 bitcast_convert_fusion.3
  79.9 7.0 %collective-permute-done.2 = bf16[4,4,64,256]{3,2,1,0:T(8,128)(2,1)S(1)} collective-permute-done((bf16[4,4,64,256]{3,2,1,0:T(8,128)(2,1)S(1)}, bf16[4,4,64,256]{3,2,1,0:T(8,128)(2,1)S(1)}, u32[]{:S(2)}, u32[]{:S(2)}) %collective-permute-start.2) | collective-permute-done | bytes 524320 | tf_op jit(solution)/shard_map/ppermute | solution.py:158
  87.0 2.4 collective-permute-done.3
  89.4 1.8 fusion.43
  91.2 3.9 convolution_convert_fusion.7
  100.0 4.3 all-to-all-start.1
  105.3 10.4 %fusion.1 = f32[4,512,512]{2,0,1:T(4,128)S(1)} fusion(s32[512,512]{1,0:T(8,128)S(1)} %fusion.23, f32[32,32]{1,0:T(8,128)S(1)} %copy-done.57, s32[]{:T(128)S(6)} %select_n.56), kind=kOutput, calls=%fused_computation.2 | convolution fusion | flops 411041792 | bytes 5246980 | tf_op jit(solution)/shard_map/atj,ao->otj/dot_general | solution.py:516
  115.8 3.2 copy.103.bias_ref
  119.3 2.2 copy-done.5
  121.5 11.1 %shard_map.262 = bf16[8,2,64,256]{3,2,1,0:T(8,128)(2,1)S(1)} custom-call(bf16[8,2,64,256]{3,2,1,0:T(8,128)(2,1)S(1)} %bitcast.206, bf16[8,2,64,256]{3,2,1,0:T(8,128)(2,1)S(1)} %bitcast.204, bf16[8,2,64,256]{3,2,1,0:T(8,128)(2,1)S(1)} %bitcast.202, f32[4,512,512]{2,1,0:T(8,128)S(1)} %copy-done.5, s32[2,512,1]{2,1,0:T(8,128)S(1)} %copy.104.seg_q_ref, ...), custom_call_target="tpu_custom_call" | custom-call | flops 12582912000 | bytes 6291456 | tf_op jit(solution)/shard_map/pallas_call | solution.py:310
  132.7 3.2 convolution_convert_fusion.1
  135.9 37.5 %all-gather.11.cloned.1.call-done = bf16[16,64,2048]{2,1,0:T(8,128)(2,1)} async-done(((bf16[2,64,2048]{2,1,0:T(8,128)(2,1)}), bf16[16,64,2048]{2,1,0:T(8,128)(2,1)}) %all-gather.11.cloned.1.call-update) | async-done | bytes 4194320 | tf_op jit(solution)/shard_map/all_gather | solution.py:464
  173.4 5.4 all-to-all-done.1
  181.9 45.8 %reduce-scatter.5.cloned.1.call-done = bf16[1,2,64,2048]{3,2,1,0:T(8,128)(2,1)} async-done(((bf16[8,2,64,2048]{3,2,1,0:T(8,128)(2,1)}), bf16[1,2,64,2048]{3,2,1,0:T(8,128)(2,1)}) %reduce-scatter.5.cloned.1.call-update) | async-done | bytes 524304 | tf_op jit(solution)/shard_map/reduce_scatter | solution.py:470
  236.9 2.2 copy_dynamic-update-slice_fusion.2
  239.5 1.9 copy_dynamic-update-slice_fusion
  241.4 11.4 %collective-permute-done.6 = bf16[3,4,64,640]{3,2,0,1:T(8,128)(2,1)S(1)} collective-permute-done((bf16[3,4,64,640]{3,2,0,1:T(8,128)(2,1)S(1)}, bf16[3,4,64,640]{3,2,0,1:T(8,128)(2,1)S(1)}, u32[]{:S(2)}, u32[]{:S(2)}) %collective-permute-start.6) | collective-permute-done | bytes 983072 | tf_op jit(solution)/shard_map/ppermute | solution.py:158
  252.9 2.4 collective-permute-done.7
  255.5 2.1 fusion.42
  259.1 4.9 fusion.50.gi_ref
  264.0 12.4 %all-gather.13.cloned.1.call-done = bf16[16,64,2048]{2,1,0:T(8,128)(2,1)} async-done(((bf16[2,64,2048]{2,1,0:T(8,128)(2,1)}), bf16[16,64,2048]{2,1,0:T(8,128)(2,1)}) %all-gather.13.cloned.1.call-update) | async-done | bytes 4194320 | tf_op jit(solution)/shard_map/all_gather | solution.py:464
  276.5 1.7 copy-done.9
  278.2 1.7 copy-done.24
  279.9 16.9 %shard_map.263 = (bf16[1024,640]{1,0:T(8,128)(2,1)S(1)}, bf16[1024,640]{1,0:T(8,128)(2,1)S(1)}, bf16[1024,640]{1,0:T(8,128)(2,1)S(1)}, bf16[1024,2048]{1,0:T(8,128)(2,1)}) custom-call(bf16[1024,2048]{1,0:T(8,128)(2,1)} %bitcast.262, f32[1024,640]{1,0:T(8,128)S(1)} %copy-done.24, bf16[2048,640]{1,0:T(8,128)(2,1)S(1)} %bitcast.196, bf16[2048,640]{1,0:T(8,128)(2,1)S(1)} %bitcast.195), custom_call_target="tpu_custom_call" | custom-call | flops 10737418240 | bytes 20185088 | tf_op jit(solution)/shard_map/pallas_call | solution.py:133
  301.3 5.9 %convolution_convert_fusion.4 = bf16[2048,640]{1,0:T(8,128)(2,1)S(1)} fusion(bf16[1024,2048]{1,0:T(8,128)(2,1)} %bitcast.263, bf16[1024,640]{1,0:T(8,128)(2,1)S(1)} %copy-done.30), kind=kOutput, calls=%fused_computation.12 | convolution fusion | flops 2685665280 | bytes 8126464 | tf_op jit(solution)/shard_map/dot_general | solution.py:89
  307.2 4.0 convolution_convert_fusion.3
  311.3 3.8 convolution_convert_fusion.2
  326.3 5.0 convolution_convert_fusion
  331.3 17.6 %reduce-scatter.7.cloned.1.call-done = bf16[1,2,64,2048]{3,2,1,0:T(8,128)(2,1)} async-done(((bf16[8,2,64,2048]{3,2,1,0:T(8,128)(2,1)}), bf16[1,2,64,2048]{3,2,1,0:T(8,128)(2,1)}) %reduce-scatter.7.cloned.1.call-update) | async-done | bytes 524304 | tf_op jit(solution)/shard_map/reduce_scatter | solution.py:470
  352.2 1.8 add_convert_fusion.4
  359.7 19.1 %collective-permute-done.11 = bf16[3,4,64,640]{3,2,0,1:T(8,128)(2,1)S(1)} collective-permute-done((bf16[3,4,64,640]{3,2,0,1:T(8,128)(2,1)S(1)}, bf16[3,4,64,640]{3,2,0,1:T(8,128)(2,1)S(1)}, u32[]{:S(2)}, u32[]{:S(2)}) %collective-permute-start.11) | collective-permute-done | bytes 983072 | tf_op jit(solution)/shard_map/ppermute | solution.py:158
  378.8 1.7 collective-permute-done.10
  380.4 1.6 add_convert_fusion.3
  382.1 15.8 %collective-permute-done.13 = bf16[3,4,64,640]{3,2,0,1:T(8,128)(2,1)S(1)} collective-permute-done((bf16[3,4,64,640]{3,2,0,1:T(8,128)(2,1)S(1)}, bf16[3,4,64,640]{3,2,0,1:T(8,128)(2,1)S(1)}, u32[]{:S(2)}, u32[]{:S(2)}) %collective-permute-start.13) | collective-permute-done | bytes 983072 | tf_op jit(solution)/shard_map/ppermute | solution.py:158
  399.8 4.2 all-to-all-start.2
  404.1 3.6 convolution_convert_fusion.6
  408.1 12.6 %shard_map.264 = (bf16[8,2,64,256]{3,2,1,0:T(8,128)(2,1)S(1)}, bf16[8,2,64,256]{3,2,1,0:T(8,128)(2,1)S(1)}, bf16[8,2,64,256]{3,2,1,0:T(8,128)(2,1)S(1)}, f32[4,512,512]{2,1,0:T(8,128)S(1)}) custom-call(bf16[8,2,64,256]{3,2,1,0:T(8,128)(2,1)S(1)} %bitcast.207, bf16[8,2,64,256]{3,2,1,0:T(8,128)(2,1)S(1)} %bitcast.205, bf16[8,2,64,256]{3,2,1,0:T(8,128)(2,1)S(1)} %bitcast.203, ...), custom_call_target="tpu_custom_call" | custom-call | flops 16777216000 | bytes 12058624 | tf_op jit(solution)/shard_map/pallas_call | solution.py:352
  424.1 3.4 add_convert_fusion
  427.5 22.7 %all-to-all-done.2.g_ref = bf16[8,3,64,640]{3,2,1,0:T(8,128)(2,1)S(1)} async-done(((bf16[8,3,64,640]{3,2,1,0:T(8,128)(2,1)}), bf16[8,3,64,640]{3,2,1,0:T(8,128)(2,1)S(1)}, u32[]{:S(2)}, u32[]{:S(2)}) %all-to-all-start.2) | async-done | bytes 1966112 | tf_op jit(solution)/shard_map/all_to_all | solution.py:438
  451.5 3.7 convolution_convert_fusion.5
  463.9 1.8 collective-permute-start.17
  465.7 10.4 %collective-permute-done.18 = bf16[4,4,64,256]{3,2,0,1:T(8,128)(2,1)S(1)} collective-permute-done((bf16[4,4,64,256]{3,2,0,1:T(8,128)(2,1)S(1)}, bf16[4,4,64,256]{3,2,0,1:T(8,128)(2,1)S(1)}, u32[]{:S(2)}, u32[]{:S(2)}) %collective-permute-start.18) | collective-permute-done | bytes 524320 | tf_op jit(solution)/shard_map/ppermute | solution.py:158
  478.5 9.2 %collective-permute-done.14 = bf16[4,4,64,256]{3,2,0,1:T(8,128)(2,1)S(1)} collective-permute-done((bf16[4,4,64,256]{3,2,0,1:T(8,128)(2,1)S(1)}, bf16[4,4,64,256]{3,2,0,1:T(8,128)(2,1)S(1)}, u32[]{:S(2)}, u32[]{:S(2)}) %collective-permute-start.14) | collective-permute-done | bytes 524320 | tf_op jit(solution)/shard_map/ppermute | solution.py:158
  487.7 9.6 %collective-permute-done.19 = bf16[4,4,64,256]{3,2,0,1:T(8,128)(2,1)S(1)} collective-permute-done((bf16[4,4,64,256]{3,2,0,1:T(8,128)(2,1)S(1)}, bf16[4,4,64,256]{3,2,0,1:T(8,128)(2,1)S(1)}, u32[]{:S(2)}, u32[]{:S(2)}) %collective-permute-start.19) | collective-permute-done | bytes 524320 | tf_op jit(solution)/shard_map/ppermute | solution.py:158
  498.9 3.6 all-to-all-start.3
  502.5 2.5 convert_element_type.301
  505.0 6.4 %fusion.12 = f32[32,4]{1,0:T(8,128)S(1)} fusion(bf16[4,512,512]{2,1,0:T(8,128)(2,1)S(1)} %convert_element_type.301, s32[512,512]{1,0:T(8,128)} %copy-done.48), kind=kOutput, calls=%fused_computation.46 | convolution fusion | flops 75497472 | bytes 3146240 | tf_op jit(solution)/shard_map/hij,zij->zh/dot_general | solution.py:571
  511.6 2.2 copy-done
  515.4 2.1 copy-done.7
  517.5 2.2 copy-done.8
  519.6 6.5 %shard_map.266 = (f32[3,64,5120]{2,1,0:T(8,128)}, f32[3,64,5120]{2,1,0:T(8,128)}, f32[3,64,5120]{2,1,0:T(8,128)}) custom-call(f32[3,64,5120]{2,1,0:T(8,128)S(1)} %bitcast.192, f32[3,64,5120]{2,1,0:T(8,128)S(1)} %bitcast.193, f32[3,64,5120]{2,1,0:T(8,128)S(1)} %bitcast.194, bf16[8,3,64,640]{3,2,1,0:T(8,128)(2,1)S(1)} %copy-done.3), custom_call_target="tpu_custom_call" | custom-call | flops 19660800 | bytes 25559040 | tf_op jit(solution)/shard_map/pallas_call | solution.py:260
  526.1 1.7 fusion.21
  529.2 1.9 collective-permute-start.21
  531.1 6.1 %collective-permute-done.21 = f32[40,128]{1,0:T(8,128)S(1)} collective-permute-done((f32[40,128]{1,0:T(8,128)S(1)}, f32[40,128]{1,0:T(8,128)S(1)}, u32[]{:S(2)}, u32[]{:S(2)}) %collective-permute-start.21) | collective-permute-done | bytes 20512 | tf_op jit(solution)/shard_map/ppermute | solution.py:158
  537.2 4.1 collective-permute-start.22
  541.2 4.2 all-to-all-done.3.g_ref
  548.7 7.8 %shard_map.265 = (f32[64,4,2048]{2,1,0:T(4,128)}, f32[64,4,2048]{2,1,0:T(4,128)}, f32[3,64,2048]{2,1,0:T(8,128)}, f32[64,2048]{1,0:T(8,128)}) custom-call(f32[64,4,2048]{2,1,0:T(4,128)S(1)} %copy-done.1, f32[64,4,2048]{2,1,0:T(4,128)S(1)} %copy-done.10, f32[64,4,2048]{2,1,0:T(4,128)S(1)} %copy-done.11, bf16[8,4,64,256]{3,2,1,0:T(8,128)(2,1)S(1)} %all-to-all-done.3.g_ref), custom_call_target="tpu_custom_call" | custom-call | flops 10485760 | bytes 13631488 | tf_op jit(solution)/shard_map/pallas_call | solution.py:212
  558.1 2.3 collective-permute-done.23
  562.0 3.1 reduce-scatter.11.cloned.1.call-done
  565.1 3.7 fusion.20
  (267 shorter events, 89.2 us)
Async XLA Ops:
  9.2 8.7 %copy-start.34 = (bf16[2,64,2048]{2,1,0:T(8,128)(2,1)S(1)}, bf16[2,64,2048]{2,1,0:T(8,128)(2,1)}, u32[]{:S(2)}) copy-start(bf16[2,64,2048]{2,1,0:T(8,128)(2,1)} %param.15) | copy-start | bytes 1572868
  9.2 8.9 %copy-start.51 = (f32[2,2048]{1,0:T(2,128)S(1)}, f32[2,2048]{1,0:T(2,128)}, u32[]{:S(2)}) copy-start(f32[2,2048]{1,0:T(2,128)} %param.24) | copy-start | bytes 49156
  11.6 32.9 %all-to-all-start = ((bf16[8,4,64,256]{3,2,1,0:T(8,128)(2,1)}), bf16[8,4,64,256]{3,2,1,0:T(8,128)(2,1)S(1)}, u32[]{:S(2)}, u32[]{:S(2)}) async-start(bf16[8,4,64,256]{3,2,1,0:T(8,128)(2,1)} %copy.96), calls=%async_computation | async-start | bytes 2097152 | tf_op jit(solution)/shard_map/all_to_all | solution.py:434
  17.9 73.3 %all-gather.9.cloned.1.call-start = ((), (), s32[]{:S(2)}) async-start(), calls=%async_computation.12 | async-start | bytes 4718592 | tf_op jit(solution)/shard_map/all_gather | solution.py:464
  18.2 56.3 %copy-start.61 = (f32[2,64]{1,0:T(2,128)}, f32[2,64]{1,0:T(2,128)S(1)}, u32[]{:S(2)}) copy-start(f32[2,64]{1,0:T(2,128)S(1)} %add_rsqrt_fusion.1) | copy-start | bytes 1540
  18.2 56.3 %copy-start.49 = (f32[1,2048]{1,0:T(1,128)}, f32[1,2048]{1,0:T(1,128)S(1)}, u32[]{:S(2)}) copy-start(f32[1,2048]{1,0:T(1,128)S(1)} %get-tuple-element.159) | copy-start | bytes 24580
  44.6 128.8 %all-gather.11.cloned.1.call-start = ((), (), s32[]{:S(2)}) async-start(), calls=%async_computation.13 | async-start | bytes 4718592 | tf_op jit(solution)/shard_map/all_gather | solution.py:464
  44.7 24.8 %collective-permute-start = (bf16[4,8,64,256]{3,2,1,0:T(8,128)(2,1)S(1)}, bf16[4,8,64,256]{3,2,1,0:T(8,128)(2,1)S(1)}, u32[]{:S(2)}, u32[]{:S(2)}) collective-permute-start(bf16[4,8,64,256]{3,2,1,0:T(8,128)(2,1)S(1)} %bitcast.214), channel_id=1, source_target_pairs={{0,1},{1,0},{2,3},{3,2},{4,5},{5,4},{6,7},{7,6},{8,9},{9,8},{10,11... | collective-permute-start | bytes 3145736 | tf_op jit(solution)/shard_map/ppermute | solution.py:158
  46.2 24.5 %collective-permute-start.1 = (bf16[4,8,64,256]{3,2,1,0:T(8,128)(2,1)S(1)}, bf16[4,8,64,256]{3,2,1,0:T(8,128)(2,1)}, u32[]{:S(2)}, u32[]{:S(2)}) collective-permute-start(bf16[4,8,64,256]{3,2,1,0:T(8,128)(2,1)S(1)} %bitcast.215), channel_id=1, source_target_pairs={{0,2},{1,3},{2,0},{3,1},{4,6},{5,7},{6,4},{7,5},{8,10},{9,11},{10,... | collective-permute-start | bytes 3145736 | tf_op jit(solution)/shard_map/ppermute | solution.py:158
  74.5 12.4 %collective-permute-start.2 = (bf16[4,4,64,256]{3,2,1,0:T(8,128)(2,1)S(1)}, bf16[4,4,64,256]{3,2,1,0:T(8,128)(2,1)S(1)}, u32[]{:S(2)}, u32[]{:S(2)}) collective-permute-start(bf16[4,4,64,256]{3,2,1,0:T(8,128)(2,1)S(1)} %slice.108), channel_id=1, source_target_pairs={{0,2},{1,3},{2,0},{3,1},{4,6},{5,7},{6,4},{7,5},{8,10},{9,11},{10,... | collective-permute-start | bytes 1572872 | tf_op jit(solution)/shard_map/ppermute | solution.py:158
  77.2 12.1 %collective-permute-start.3 = (bf16[4,4,64,256]{3,2,1,0:T(8,128)(2,1)S(1)}, bf16[4,4,64,256]{3,2,1,0:T(8,128)(2,1)S(1)}, u32[]{:S(2)}, u32[]{:S(2)}) collective-permute-start(bf16[4,4,64,256]{3,2,1,0:T(8,128)(2,1)S(1)} %slice.109), channel_id=1, source_target_pairs={{0,1},{1,0},{2,3},{3,2},{4,5},{5,4},{6,7},{7,6},{8,9},{9,8},{10,11... | collective-permute-start | bytes 1572872 | tf_op jit(solution)/shard_map/ppermute | solution.py:158
  95.1 24.2 %copy-start.18 = (bf16[1024,256]{1,0:T(8,128)(2,1)}, bf16[1024,256]{1,0:T(8,128)(2,1)S(1)}, u32[]{:S(2)}) copy-start(bf16[1024,256]{1,0:T(8,128)(2,1)S(1)} %convolution_convert_fusion.7) | copy-start | bytes 1572868
  96.6 22.7 %copy-start.20 = (bf16[1024,256]{1,0:T(8,128)(2,1)}, bf16[1024,256]{1,0:T(8,128)(2,1)S(1)}, u32[]{:S(2)}) copy-start(bf16[1024,256]{1,0:T(8,128)(2,1)S(1)} %convolution_convert_fusion.8) | copy-start | bytes 1572868
  97.9 21.4 %copy-start.22 = (bf16[1024,256]{1,0:T(8,128)(2,1)}, bf16[1024,256]{1,0:T(8,128)(2,1)S(1)}, u32[]{:S(2)}) copy-start(bf16[1024,256]{1,0:T(8,128)(2,1)S(1)} %convolution_convert_fusion.9) | copy-start | bytes 1572868
  98.5 6.9 %copy-start.57 = (f32[32,32]{1,0:T(8,128)S(1)}, f32[32,32]{1,0:T(8,128)}, u32[]{:S(2)}) copy-start(f32[32,32]{1,0:T(8,128)} %param.27) | copy-start | bytes 12292
  100.0 78.8 %all-to-all-start.1 = ((bf16[8,3,64,640]{3,2,1,0:T(8,128)(2,1)}), bf16[8,3,64,640]{3,2,1,0:T(8,128)(2,1)}, u32[]{:S(2)}, u32[]{:S(2)}) async-start(bf16[8,3,64,640]{3,2,1,0:T(8,128)(2,1)} %bitcast.212), calls=%async_computation.1 | async-start | bytes 3932160 | tf_op jit(solution)/shard_map/all_to_all | solution.py:434
  104.4 123.3 %reduce-scatter.5.cloned.1.call-start = ((), (), s32[]{:S(2)}) async-start(), calls=%async_computation.8 | async-start | bytes 4718592 | tf_op jit(solution)/shard_map/reduce_scatter | solution.py:470
  105.3 10.4 %copy-start.48 = (s32[512,512]{1,0:T(8,128)}, s32[512,512]{1,0:T(8,128)S(1)}, u32[]{:S(2)}) copy-start(s32[512,512]{1,0:T(8,128)S(1)} %fusion.23) | copy-start | bytes 3145732
  121.5 11.2 %copy-start.16 = (s32[2,512,1]{2,1,0:T(8,128)}, s32[2,512,1]{2,1,0:T(8,128)S(1)}, u32[]{:S(2)}) copy-start(s32[2,512,1]{2,1,0:T(8,128)S(1)} %copy.104.seg_q_ref) | copy-start | bytes 12292
  121.5 11.2 %copy-start.43 = (bf16[1,8,4,64,256]{4,3,2,1,0:T(8,128)(2,1)S(1)}, bf16[1,8,4,64,256]{4,3,2,1,0:T(8,128)(2,1)}, u32[]{:S(2)}) copy-start(bf16[1,8,4,64,256]{4,3,2,1,0:T(8,128)(2,1)} %get-tuple-element.140) | copy-start | bytes 3145732
  178.8 97.6 %all-gather.13.cloned.1.call-start = ((), (), s32[]{:S(2)}) async-start(), calls=%async_computation.14 | async-start | bytes 4718592 | tf_op jit(solution)/shard_map/all_gather | solution.py:464
  178.9 49.9 %collective-permute-start.4 = (bf16[3,8,64,640]{3,2,0,1:T(8,128)(2,1)}, bf16[3,8,64,640]{3,2,0,1:T(8,128)(2,1)S(1)}, u32[]{:S(2)}, u32[]{:S(2)}) collective-permute-start(bf16[3,8,64,640]{3,2,0,1:T(8,128)(2,1)} %bitcast.28), channel_id=1, source_target_pairs={{0,1},{1,0},{2,3},{3,2},{4,5},{5,4},{6,7},{7,6},{8,9},{9,8},{10,11... | collective-permute-start | bytes 5898248 | tf_op jit(solution)/shard_map/ppermute | solution.py:158
  180.4 48.4 %collective-permute-start.5 = (bf16[3,8,64,640]{3,2,0,1:T(8,128)(2,1)}, bf16[3,8,64,640]{3,2,0,1:T(8,128)(2,1)}, u32[]{:S(2)}, u32[]{:S(2)}) collective-permute-start(bf16[3,8,64,640]{3,2,0,1:T(8,128)(2,1)} %bitcast.28), channel_id=1, source_target_pairs={{0,2},{1,3},{2,0},{3,1},{4,6},{5,7},{6,4},{7,5},{8,10},{9,11},{10,... | collective-permute-start | bytes 5898248 | tf_op jit(solution)/shard_map/ppermute | solution.py:158
  231.0 117.9 %reduce-scatter.7.cloned.1.call-start = ((), (), s32[]{:S(2)}) async-start(), calls=%async_computation.9 | async-start | bytes 4718592 | tf_op jit(solution)/shard_map/reduce_scatter | solution.py:470
  231.3 21.4 %collective-permute-start.6 = (bf16[3,4,64,640]{3,2,0,1:T(8,128)(2,1)S(1)}, bf16[3,4,64,640]{3,2,0,1:T(8,128)(2,1)S(1)}, u32[]{:S(2)}, u32[]{:S(2)}) collective-permute-start(bf16[3,4,64,640]{3,2,0,1:T(8,128)(2,1)S(1)} %slice.115), channel_id=1, source_target_pairs={{0,2},{1,3},{2,0},{3,1},{4,6},{5,7},{6,4},{7,5},{8,10},{9,11},{10,... | collective-permute-start | bytes 2949128 | tf_op jit(solution)/shard_map/ppermute | solution.py:158
  234.2 21.1 %collective-permute-start.7 = (bf16[3,4,64,640]{3,2,0,1:T(8,128)(2,1)S(1)}, bf16[3,4,64,640]{3,2,0,1:T(8,128)(2,1)S(1)}, u32[]{:S(2)}, u32[]{:S(2)}) collective-permute-start(bf16[3,4,64,640]{3,2,0,1:T(8,128)(2,1)S(1)} %slice.116), channel_id=1, source_target_pairs={{0,1},{1,0},{2,3},{3,2},{4,5},{5,4},{6,7},{7,6},{8,9},{9,8},{10,11... | collective-permute-start | bytes 2949128 | tf_op jit(solution)/shard_map/ppermute | solution.py:158
  300.0 99.8 %all-gather.15.cloned.1.call-start = ((), (), s32[]{:S(2)}) async-start(), calls=%async_computation.15 | async-start | bytes 4718592 | tf_op jit(solution)/shard_map/all_gather | solution.py:464
  318.9 31.2 %collective-permute-start.8 = (bf16[3,4,64,640]{3,2,0,1:T(8,128)(2,1)}, bf16[3,4,64,640]{3,2,0,1:T(8,128)(2,1)}, u32[]{:S(2)}, u32[]{:S(2)}) collective-permute-start(bf16[3,4,64,640]{3,2,0,1:T(8,128)(2,1)} %get-tuple-element.145), channel_id=1, source_target_pairs={{0,1},{1,0},{2,3},{3,2},{4,5},{5,4},{6,7},{7,6},{8,9},{9,8},{10,11... | collective-permute-start | bytes 2949128 | tf_op jit(solution)/shard_map/ppermute | solution.py:158
  320.4 29.7 %collective-permute-start.9 = (bf16[3,4,64,640]{3,2,0,1:T(8,128)(2,1)}, bf16[3,4,64,640]{3,2,0,1:T(8,128)(2,1)}, u32[]{:S(2)}, u32[]{:S(2)}) collective-permute-start(bf16[3,4,64,640]{3,2,0,1:T(8,128)(2,1)} %get-tuple-element.144), channel_id=1, source_target_pairs={{0,2},{1,3},{2,0},{3,1},{4,6},{5,7},{6,4},{7,5},{8,10},{9,11},{10,... | collective-permute-start | bytes 2949128 | tf_op jit(solution)/shard_map/ppermute | solution.py:158
  326.3 23.8 %copy-start.32 = (f32[2,64,2048]{2,1,0:T(8,128)S(1)}, f32[2,64,2048]{2,1,0:T(8,128)}, u32[]{:S(2)}) copy-start(f32[2,64,2048]{2,1,0:T(8,128)} %copy-done.31) | copy-start | bytes 3145732
  331.3 19.8 %copy-start.36 = (bf16[2,64,2048]{2,1,0:T(8,128)(2,1)S(1)}, bf16[2,64,2048]{2,1,0:T(8,128)(2,1)}, u32[]{:S(2)}) copy-start(bf16[2,64,2048]{2,1,0:T(8,128)(2,1)} %param.17) | copy-start | bytes 1572868
  351.1 7.5 %copy-start.63 = (f32[2,64]{1,0:T(2,128)}, f32[2,64]{1,0:T(2,128)S(1)}, u32[]{:S(2)}) copy-start(f32[2,64]{1,0:T(2,128)S(1)} %broadcast_multiply_fusion.1) | copy-start | bytes 1540
  354.0 43.9 %copy-start.45 = (bf16[3,4,64,640]{3,2,0,1:T(8,128)(2,1)S(1)}, bf16[3,4,64,640]{3,2,0,1:T(8,128)(2,1)}, u32[]{:S(2)}) copy-start(bf16[3,4,64,640]{3,2,0,1:T(8,128)(2,1)} %get-tuple-element.93) | copy-start | bytes 2949124
  354.0 24.8 %collective-permute-start.11 = (bf16[3,4,64,640]{3,2,0,1:T(8,128)(2,1)S(1)}, bf16[3,4,64,640]{3,2,0,1:T(8,128)(2,1)S(1)}, u32[]{:S(2)}, u32[]{:S(2)}) collective-permute-start(bf16[3,4,64,640]{3,2,0,1:T(8,128)(2,1)S(1)} %add_convert_fusion.4), channel_id=1, source_target_pairs={{0,2},{1,3},{2,0},{3,1},{4,6},{5,7},{6,4},{7,5},{8,10},{9,11},{10,... | collective-permute-start | bytes 2949128 | tf_op jit(solution)/shard_map/ppermute | solution.py:158
  355.5 24.9 %collective-permute-start.10 = (bf16[3,4,64,640]{3,2,0,1:T(8,128)(2,1)}, bf16[3,4,64,640]{3,2,0,1:T(8,128)(2,1)S(1)}, u32[]{:S(2)}, u32[]{:S(2)}) collective-permute-start(bf16[3,4,64,640]{3,2,0,1:T(8,128)(2,1)} %get-tuple-element.90), channel_id=1, source_target_pairs={{0,1},{1,0},{2,3},{3,2},{4,5},{5,4},{6,7},{7,6},{8,9},{9,8},{10,11... | collective-permute-start | bytes 2949128 | tf_op jit(solution)/shard_map/ppermute | solution.py:158
  358.6 39.3 %collective-permute-start.13 = (bf16[3,4,64,640]{3,2,0,1:T(8,128)(2,1)S(1)}, bf16[3,4,64,640]{3,2,0,1:T(8,128)(2,1)S(1)}, u32[]{:S(2)}, u32[]{:S(2)}) collective-permute-start(bf16[3,4,64,640]{3,2,0,1:T(8,128)(2,1)S(1)} %add_convert_fusion.2), channel_id=1, source_target_pairs={{0,1},{1,0},{2,3},{3,2},{4,5},{5,4},{6,7},{7,6},{8,9},{9,8},{10,11... | collective-permute-start | bytes 2949128 | tf_op jit(solution)/shard_map/ppermute | solution.py:158
  359.1 38.8 %collective-permute-start.12 = (bf16[3,4,64,640]{3,2,0,1:T(8,128)(2,1)}, bf16[3,4,64,640]{3,2,0,1:T(8,128)(2,1)S(1)}, u32[]{:S(2)}, u32[]{:S(2)}) collective-permute-start(bf16[3,4,64,640]{3,2,0,1:T(8,128)(2,1)} %get-tuple-element.94), channel_id=1, source_target_pairs={{0,2},{1,3},{2,0},{3,1},{4,6},{5,7},{6,4},{7,5},{8,10},{9,11},{10,... | collective-permute-start | bytes 2949128 | tf_op jit(solution)/shard_map/ppermute | solution.py:158
  399.8 50.4 %all-to-all-start.2 = ((bf16[8,3,64,640]{3,2,1,0:T(8,128)(2,1)}), bf16[8,3,64,640]{3,2,1,0:T(8,128)(2,1)S(1)}, u32[]{:S(2)}, u32[]{:S(2)}) async-start(bf16[8,3,64,640]{3,2,1,0:T(8,128)(2,1)} %bitcast.213), calls=%async_computation.4 | async-start | bytes 3932160 | tf_op jit(solution)/shard_map/all_to_all | solution.py:438
  404.0 122.1 %reduce-scatter.9.cloned.1.call-start = ((), (), s32[]{:S(2)}) async-start(), calls=%async_computation.10 | async-start | bytes 4718592 | tf_op jit(solution)/shard_map/reduce_scatter | solution.py:470
  408.1 12.6 %copy-start.42 = (bf16[1,8,4,64,256]{4,3,2,1,0:T(8,128)(2,1)S(1)}, bf16[1,8,4,64,256]{4,3,2,1,0:T(8,128)(2,1)}, u32[]{:S(2)}) copy-start(bf16[1,8,4,64,256]{4,3,2,1,0:T(8,128)(2,1)} %get-tuple-element.142) | copy-start | bytes 3145732
  450.3 114.8 %reduce-scatter.11.cloned.1.call-start = ((), (), s32[]{:S(2)}) async-start(), calls=%async_computation.11 | async-start | bytes 4718592 | tf_op jit(solution)/shard_map/reduce_scatter | solution.py:470
  461.2 14.9 %collective-permute-start.18 = (bf16[4,4,64,256]{3,2,0,1:T(8,128)(2,1)S(1)}, bf16[4,4,64,256]{3,2,0,1:T(8,128)(2,1)S(1)}, u32[]{:S(2)}, u32[]{:S(2)}) collective-permute-start(bf16[4,4,64,256]{3,2,0,1:T(8,128)(2,1)S(1)} %get-tuple-element.155), channel_id=1, source_target_pairs={{0,2},{1,3},{2,0},{3,1},{4,6},{5,7},{6,4},{7,5},{8,10},{9,11},{10,... | collective-permute-start | bytes 1572872 | tf_op jit(solution)/shard_map/ppermute | solution.py:158
  461.6 16.3 %collective-permute-start.15 = (bf16[4,4,64,256]{3,2,0,1:T(8,128)(2,1)S(1)}, bf16[4,4,64,256]{3,2,0,1:T(8,128)(2,1)S(1)}, u32[]{:S(2)}, u32[]{:S(2)}) collective-permute-start(bf16[4,4,64,256]{3,2,0,1:T(8,128)(2,1)S(1)} %get-tuple-element.154), channel_id=1, source_target_pairs={{0,1},{1,0},{2,3},{3,2},{4,5},{5,4},{6,7},{7,6},{8,9},{9,8},{10,11... | collective-permute-start | bytes 1572872 | tf_op jit(solution)/shard_map/ppermute | solution.py:158
  463.2 24.4 %collective-permute-start.14 = (bf16[4,4,64,256]{3,2,0,1:T(8,128)(2,1)S(1)}, bf16[4,4,64,256]{3,2,0,1:T(8,128)(2,1)S(1)}, u32[]{:S(2)}, u32[]{:S(2)}) collective-permute-start(bf16[4,4,64,256]{3,2,0,1:T(8,128)(2,1)S(1)} %slice.154), channel_id=1, source_target_pairs={{0,1},{1,0},{2,3},{3,2},{4,5},{5,4},{6,7},{7,6},{8,9},{9,8},{10,11... | collective-permute-start | bytes 1572872 | tf_op jit(solution)/shard_map/ppermute | solution.py:158
  463.9 23.8 %collective-permute-start.17 = (bf16[4,4,64,256]{3,2,0,1:T(8,128)(2,1)S(1)}, bf16[4,4,64,256]{3,2,0,1:T(8,128)(2,1)S(1)}, u32[]{:S(2)}, u32[]{:S(2)}) collective-permute-start(bf16[4,4,64,256]{3,2,0,1:T(8,128)(2,1)S(1)} %slice.158), channel_id=1, source_target_pairs={{0,2},{1,3},{2,0},{3,1},{4,6},{5,7},{6,4},{7,5},{8,10},{9,11},{10,... | collective-permute-start | bytes 1572872 | tf_op jit(solution)/shard_map/ppermute | solution.py:158
  476.3 20.9 %collective-permute-start.19 = (bf16[4,4,64,256]{3,2,0,1:T(8,128)(2,1)S(1)}, bf16[4,4,64,256]{3,2,0,1:T(8,128)(2,1)S(1)}, u32[]{:S(2)}, u32[]{:S(2)}) collective-permute-start(bf16[4,4,64,256]{3,2,0,1:T(8,128)(2,1)S(1)} %add_convert_fusion.6), channel_id=1, source_target_pairs={{0,1},{1,0},{2,3},{3,2},{4,5},{5,4},{6,7},{7,6},{8,9},{9,8},{10,11... | collective-permute-start | bytes 1572872 | tf_op jit(solution)/shard_map/ppermute | solution.py:158
  478.0 19.3 %collective-permute-start.16 = (bf16[4,4,64,256]{3,2,0,1:T(8,128)(2,1)S(1)}, bf16[4,4,64,256]{3,2,0,1:T(8,128)(2,1)S(1)}, u32[]{:S(2)}, u32[]{:S(2)}) collective-permute-start(bf16[4,4,64,256]{3,2,0,1:T(8,128)(2,1)S(1)} %add_convert_fusion.8), channel_id=1, source_target_pairs={{0,2},{1,3},{2,0},{3,1},{4,6},{5,7},{6,4},{7,5},{8,10},{9,11},{10,... | collective-permute-start | bytes 1572872 | tf_op jit(solution)/shard_map/ppermute | solution.py:158
  498.9 46.6 %all-to-all-start.3 = ((bf16[8,4,64,256]{3,2,1,0:T(8,128)(2,1)}), bf16[8,4,64,256]{3,2,1,0:T(8,128)(2,1)S(1)}, u32[]{:S(2)}, u32[]{:S(2)}) async-start(bf16[8,4,64,256]{3,2,1,0:T(8,128)(2,1)} %maximum_bitcast_fusion), calls=%async_computation.7 | async-start | bytes 2097152 | tf_op jit(solution)/shard_map/all_to_all | solution.py:438
  519.6 6.5 %copy-start.50 = (f32[1,2048]{1,0:T(1,128)S(1)}, f32[1,2048]{1,0:T(1,128)}, u32[]{:S(2)}) copy-start(f32[1,2048]{1,0:T(1,128)} %copy-done.49) | copy-start | bytes 24580
  519.6 6.5 %copy-start.62 = (f32[2,64]{1,0:T(2,128)S(1)}, f32[2,64]{1,0:T(2,128)}, u32[]{:S(2)}) copy-start(f32[2,64]{1,0:T(2,128)} %copy-done.61) | copy-start | bytes 1540
  519.6 8.2 %copy-start.53 = (f32[2048]{0:T(1024)S(1)}, f32[2048]{0:T(1024)}, u32[]{:S(2)}) copy-start(f32[2048]{0:T(1024)} %get-tuple-element.117) | copy-start | bytes 24580
  519.6 25.8 %copy-start.1 = (f32[64,4,2048]{2,1,0:T(4,128)S(1)}, f32[64,4,2048]{2,1,0:T(4,128)}, u32[]{:S(2)}) copy-start(f32[64,4,2048]{2,1,0:T(4,128)} %w_ref.1) | copy-start | bytes 6291460
  527.8 37.3 %copy-start.64 = (f32[2,64]{1,0:T(2,128)S(1)}, f32[2,64]{1,0:T(2,128)}, u32[]{:S(2)}) copy-start(f32[2,64]{1,0:T(2,128)} %copy-done.63) | copy-start | bytes 1540
  527.8 1.3 collective-permute-start.20
  529.2 8.0 %collective-permute-start.21 = (f32[40,128]{1,0:T(8,128)S(1)}, f32[40,128]{1,0:T(8,128)S(1)}, u32[]{:S(2)}, u32[]{:S(2)}) collective-permute-start(f32[40,128]{1,0:T(8,128)S(1)} %bitcast_add_fusion), channel_id=1, source_target_pairs={{0,8},{4,12},{8,0},{12,4},{16,24},{20,28},{24,16},{28,20},{1,9},{5... | collective-permute-start | bytes 61448 | tf_op jit(solution)/shard_map/ppermute | solution.py:158
  537.2 19.4 %collective-permute-start.22 = (f32[40,128]{1,0:T(8,128)S(1)}, f32[40,128]{1,0:T(8,128)S(1)}, u32[]{:S(2)}, u32[]{:S(2)}) collective-permute-start(f32[40,128]{1,0:T(8,128)S(1)} %fusion.87), channel_id=1, source_target_pairs={{0,16},{4,20},{8,24},{12,28},{16,0},{20,4},{24,8},{28,12},{1,17},{... | collective-permute-start | bytes 61448 | tf_op jit(solution)/shard_map/ppermute | solution.py:158
  556.5 12.4 %copy-start.52 = (f32[2,2048]{1,0:T(2,128)S(1)}, f32[2,2048]{1,0:T(2,128)}, u32[]{:S(2)}) copy-start(f32[2,2048]{1,0:T(2,128)} %param.24) | copy-start | bytes 49156
  556.5 12.4 %copy-start.55 = (f32[2,2048]{1,0:T(2,128)S(1)}, f32[2,2048]{1,0:T(2,128)}, u32[]{:S(2)}) copy-start(f32[2,2048]{1,0:T(2,128)} %param.25) | copy-start | bytes 49156
  556.5 12.4 %copy-start.56 = (f32[2,2048]{1,0:T(2,128)S(1)}, f32[2,2048]{1,0:T(2,128)}, u32[]{:S(2)}) copy-start(f32[2,2048]{1,0:T(2,128)} %param.26) | copy-start | bytes 49156
  556.5 13.1 %copy-start.58 = (f32[32,32]{1,0:T(8,128)S(1)}, f32[32,32]{1,0:T(8,128)}, u32[]{:S(2)}) copy-start(f32[32,32]{1,0:T(8,128)} %param.27) | copy-start | bytes 12292
  556.5 13.1 %copy-start.59 = (f32[32,32]{1,0:T(8,128)S(1)}, f32[32,32]{1,0:T(8,128)}, u32[]{:S(2)}) copy-start(f32[32,32]{1,0:T(8,128)} %param.28) | copy-start | bytes 12292
  556.5 13.1 %copy-start.60 = (f32[32,32]{1,0:T(8,128)S(1)}, f32[32,32]{1,0:T(8,128)}, u32[]{:S(2)}) copy-start(f32[32,32]{1,0:T(8,128)} %param.29) | copy-start | bytes 12292
  556.6 3.8 collective-permute-start.23
  560.4 8.3 %collective-permute-start.24 = (f32[40,128]{1,0:T(8,128)S(1)}, f32[40,128]{1,0:T(8,128)S(1)}, u32[]{:S(2)}, u32[]{:S(2)}) collective-permute-start(f32[40,128]{1,0:T(8,128)S(1)} %add.255), channel_id=1, source_target_pairs={{0,2},{1,3},{2,0},{3,1},{4,6},{5,7},{6,4},{7,5},{8,10},{9,11},{10,... | collective-permute-start | bytes 61448 | tf_op jit(solution)/shard_map/ppermute | solution.py:158
  (43 other events, 115.6 us)
Sparse Core Ops, SparseCore 0:
  44.8 46.0 all-gather.8
  92.5 80.9 all-gather.10
  179.0 48.6 reduce-scatter.4
  231.1 45.2 all-gather.12
  300.1 48.7 reduce-scatter.6
  352.4 45.2 all-gather.14
  450.4 47.9 reduce-scatter.8
  500.7 64.3 reduce-scatter.10

commit v5 on v4

--- a/solution.py
+++ b/solution.py
@@ -106,7 +106,7 @@
 def feed_middle(normed, grad_inner, weight_gate, weight_up):
     tokens, width = normed.shape
     hidden = weight_gate.shape[1]
-    block = 256
+    block = min(512, tokens)
     scale = (2.0 / math.pi) ** 0.5
 
     def body(n_ref, gi_ref, wg_ref, wu_ref, inner_ref, gg_ref, gu_ref, out_ref):
@@ -141,7 +141,7 @@
             low_units,
             jax.ShapeDtypeStruct((tokens, width), jnp.bfloat16),
         ],
-        compiler_params=pltpu.CompilerParams(vmem_limit_bytes=40 * MIB),
+        compiler_params=pltpu.CompilerParams(vmem_limit_bytes=56 * MIB),
         cost_estimate=pl.CostEstimate(
             flops=8 * tokens * width * hidden,
             bytes_accessed=4 * tokens * width + 10 * tokens * hidden + 4 * width * hidden,

time: 588 us -> 583 us (level)
    unnamed x144 -> x134, local copies, waits for them, and re-layouts: 27 us -> 20.9 us
  transfers between devices with their start and end apart: 37 -> 37, of which waited for: 24 -> 24; matrix products, arithmetic and copies ran while one was open for 21% -> 22% of each run, Pallas kernels for 7% -> 7%
where the time goes in v5:
time: 583 us; the launch traced here: 573 us
  waiting for transfers between devices  294 us (50%)
  matrix products  67.4 us (12%)
  Pallas kernels  56.2 us (10%)
  starting transfers between devices  53.4 us (9%)
  local copies, waits for them, and re-layouts  53.2 us (9%)
  other arithmetic  32.9 us (6%)
  between operations  15.4 us (3%)
    ppermute x25, waiting for transfers between devices, swap(): return lax.ppermute(value, axis, partner_pairs(axis, offset))  121 us
    reduce_scatter x4, waiting for transfers between devices, scatter_tokens(): lax.psum_scatter(send, 'seq', scatter_dimension=0).astype(jnp.float32)  66.2 us
    all_gather x4, waiting for transfers between devices, gather_tokens(): full = lax.all_gather(local_rows, 'seq', axis=0)  47.9 us
    ppermute x25, starting transfers between devices, swap(): return lax.ppermute(value, axis, partner_pairs(axis, offset))  34.1 us
    all_to_all x2, waiting for transfers between devices, to_columns(): return lax.all_to_all(send, 'seq', 0, 0).transpose(1, 0, 2, 3)  30.7 us
    all_to_all x2, waiting for transfers between devices, to_rows(): return lax.all_to_all(mine.transpose(1, 0, 2, 3), 'seq', 0, 0)  27.2 us
    dot_general x7, matrix products, outer_sum(): lax.dot_general(left, right, (((0,), (0,)), ((), ())), preferred_element_...  21.5 us
    unnamed x134, local copies, waits for them, and re-layouts  20.9 us
  transfers between devices with their start and end apart: 37, of which 24 were waited for; matrix products, arithmetic and copies ran while one was open for 22% of the time, Pallas kernels for 7%

profile of v5, /device:TPU:0, one launch (start us, length us, event | category | flops | bytes accessed | tf_op | source)
XLA Modules:
  0.0 572.6 jit_solution(9023663817221041722)
XLA Ops:
  7.2 2.0 convert_bitcast_fusion
  11.6 6.3 %all-to-all-start = ((bf16[8,4,64,256]{3,2,1,0:T(8,128)(2,1)}), bf16[8,4,64,256]{3,2,1,0:T(8,128)(2,1)S(1)}, u32[]{:S(2)}, u32[]{:S(2)}) async-start(bf16[8,4,64,256]{3,2,1,0:T(8,128)(2,1)} %copy.96), calls=%async_computation | async-start | bytes 2097152 | tf_op jit(solution)/shard_map/all_to_all | solution.py:434
  19.2 25.3 %all-to-all-done = bf16[8,4,64,256]{3,2,1,0:T(8,128)(2,1)S(1)} async-done(((bf16[8,4,64,256]{3,2,1,0:T(8,128)(2,1)}), bf16[8,4,64,256]{3,2,1,0:T(8,128)(2,1)S(1)}, u32[]{:S(2)}, u32[]{:S(2)}) %all-to-all-start) | async-done | bytes 1048608 | tf_op jit(solution)/shard_map/all_to_all | solution.py:434
  47.8 21.7 %collective-permute-done = bf16[4,8,64,256]{3,2,1,0:T(8,128)(2,1)S(1)} collective-permute-done((bf16[4,8,64,256]{3,2,1,0:T(8,128)(2,1)S(1)}, bf16[4,8,64,256]{3,2,1,0:T(8,128)(2,1)S(1)}, u32[]{:S(2)}, u32[]{:S(2)}) %collective-permute-start) | collective-permute-done | bytes 1048608 | tf_op jit(solution)/shard_map/ppermute | solution.py:158
  70.8 3.7 bitcast_convert_fusion.3
  79.9 7.0 %collective-permute-done.2 = bf16[4,4,64,256]{3,2,1,0:T(8,128)(2,1)S(1)} collective-permute-done((bf16[4,4,64,256]{3,2,1,0:T(8,128)(2,1)S(1)}, bf16[4,4,64,256]{3,2,1,0:T(8,128)(2,1)S(1)}, u32[]{:S(2)}, u32[]{:S(2)}) %collective-permute-start.2) | collective-permute-done | bytes 524320 | tf_op jit(solution)/shard_map/ppermute | solution.py:158
  87.0 2.4 collective-permute-done.3
  89.4 1.8 fusion.43
  91.2 3.9 convolution_convert_fusion.7
  100.0 4.3 all-to-all-start.1
  105.0 10.4 %fusion.1 = f32[4,512,512]{2,0,1:T(4,128)S(1)} fusion(s32[512,512]{1,0:T(8,128)S(1)} %fusion.23, f32[32,32]{1,0:T(8,128)S(1)} %copy-done.48, s32[]{:T(128)S(6)} %select_n.56), kind=kOutput, calls=%fused_computation.2 | convolution fusion | flops 411041792 | bytes 5246980 | tf_op jit(solution)/shard_map/atj,ao->otj/dot_general | solution.py:516
  115.5 3.2 copy.103.bias_ref
  119.0 2.2 copy-done.5
  121.2 11.1 %shard_map.262 = bf16[8,2,64,256]{3,2,1,0:T(8,128)(2,1)S(1)} custom-call(bf16[8,2,64,256]{3,2,1,0:T(8,128)(2,1)S(1)} %bitcast.204, bf16[8,2,64,256]{3,2,1,0:T(8,128)(2,1)S(1)} %bitcast.202, bf16[8,2,64,256]{3,2,1,0:T(8,128)(2,1)S(1)} %bitcast.200, f32[4,512,512]{2,1,0:T(8,128)S(1)} %copy-done.5, s32[2,512,1]{2,1,0:T(8,128)S(1)} %copy.104.seg_q_ref, ...), custom_call_target="tpu_custom_call" | custom-call | flops 12582912000 | bytes 6291456 | tf_op jit(solution)/shard_map/pallas_call | solution.py:310
  132.3 3.2 convolution_convert_fusion.1
  135.6 37.8 %all-gather.11.cloned.1.call-done = bf16[16,64,2048]{2,1,0:T(8,128)(2,1)} async-done(((bf16[2,64,2048]{2,1,0:T(8,128)(2,1)}), bf16[16,64,2048]{2,1,0:T(8,128)(2,1)}) %all-gather.11.cloned.1.call-update) | async-done | bytes 4194320 | tf_op jit(solution)/shard_map/all_gather | solution.py:464
  173.4 5.4 all-to-all-done.1
  181.9 45.8 %reduce-scatter.5.cloned.1.call-done = bf16[1,2,64,2048]{3,2,1,0:T(8,128)(2,1)} async-done(((bf16[8,2,64,2048]{3,2,1,0:T(8,128)(2,1)}), bf16[1,2,64,2048]{3,2,1,0:T(8,128)(2,1)}) %reduce-scatter.5.cloned.1.call-update) | async-done | bytes 524304 | tf_op jit(solution)/shard_map/reduce_scatter | solution.py:470
  238.8 2.0 copy_dynamic-update-slice_fusion.2
  241.3 1.9 copy_dynamic-update-slice_fusion
  243.2 11.5 %collective-permute-done.6 = bf16[3,4,64,640]{3,2,0,1:T(8,128)(2,1)S(1)} collective-permute-done((bf16[3,4,64,640]{3,2,0,1:T(8,128)(2,1)S(1)}, bf16[3,4,64,640]{3,2,0,1:T(8,128)(2,1)S(1)}, u32[]{:S(2)}, u32[]{:S(2)}) %collective-permute-start.6) | collective-permute-done | bytes 983072 | tf_op jit(solution)/shard_map/ppermute | solution.py:158
  254.8 2.4 collective-permute-done.7
  257.4 3.1 fusion.42
  262.0 4.9 fusion.50.gi_ref
  266.9 10.0 %all-gather.13.cloned.1.call-done = bf16[16,64,2048]{2,1,0:T(8,128)(2,1)} async-done(((bf16[2,64,2048]{2,1,0:T(8,128)(2,1)}), bf16[16,64,2048]{2,1,0:T(8,128)(2,1)}) %all-gather.13.cloned.1.call-update) | async-done | bytes 4194320 | tf_op jit(solution)/shard_map/all_gather | solution.py:464
  277.0 18.3 %shard_map.263 = (bf16[1024,640]{1,0:T(8,128)(2,1)}, bf16[1024,640]{1,0:T(8,128)(2,1)}, bf16[1024,640]{1,0:T(8,128)(2,1)}, bf16[1024,2048]{1,0:T(8,128)(2,1)}) custom-call(bf16[1024,2048]{1,0:T(8,128)(2,1)} %bitcast.262, f32[1024,640]{1,0:T(8,128)} %fusion.50.gi_ref, bf16[2048,640]{1,0:T(8,128)(2,1)} %bitcast.235, bf16[2048,640]{1,0:T(8,128)(2,1)} %bitcast.234), custom_call_target="tpu_custom_call" | custom-call | flops 10737418240 | bytes 20185088 | tf_op jit(solution)/shard_map/pallas_call | solution.py:133
  296.6 5.9 %convolution_convert_fusion.4 = bf16[2048,640]{1,0:T(8,128)(2,1)S(1)} fusion(bf16[1024,2048]{1,0:T(8,128)(2,1)} %bitcast.263, bf16[1024,640]{1,0:T(8,128)(2,1)S(1)} %copy-done.64), kind=kOutput, calls=%fused_computation.12 | convolution fusion | flops 2685665280 | bytes 8126464 | tf_op jit(solution)/shard_map/dot_general | solution.py:89
  302.5 4.0 convolution_convert_fusion.3
  306.6 3.8 convolution_convert_fusion.2
  322.1 5.0 convolution_convert_fusion
  327.1 17.1 %reduce-scatter.7.cloned.1.call-done = bf16[1,2,64,2048]{3,2,1,0:T(8,128)(2,1)} async-done(((bf16[8,2,64,2048]{3,2,1,0:T(8,128)(2,1)}), bf16[1,2,64,2048]{3,2,1,0:T(8,128)(2,1)}) %reduce-scatter.7.cloned.1.call-update) | async-done | bytes 524304 | tf_op jit(solution)/shard_map/reduce_scatter | solution.py:470
  347.6 1.8 add_convert_fusion.4
  355.0 19.1 %collective-permute-done.11 = bf16[3,4,64,640]{3,2,0,1:T(8,128)(2,1)S(1)} collective-permute-done((bf16[3,4,64,640]{3,2,0,1:T(8,128)(2,1)S(1)}, bf16[3,4,64,640]{3,2,0,1:T(8,128)(2,1)S(1)}, u32[]{:S(2)}, u32[]{:S(2)}) %collective-permute-start.11) | collective-permute-done | bytes 983072 | tf_op jit(solution)/shard_map/ppermute | solution.py:158
  374.1 1.7 collective-permute-done.10
  375.8 1.6 add_convert_fusion.3
  377.4 15.8 %collective-permute-done.13 = bf16[3,4,64,640]{3,2,0,1:T(8,128)(2,1)S(1)} collective-permute-done((bf16[3,4,64,640]{3,2,0,1:T(8,128)(2,1)S(1)}, bf16[3,4,64,640]{3,2,0,1:T(8,128)(2,1)S(1)}, u32[]{:S(2)}, u32[]{:S(2)}) %collective-permute-start.13) | collective-permute-done | bytes 983072 | tf_op jit(solution)/shard_map/ppermute | solution.py:158
  395.1 4.2 all-to-all-start.2
  399.5 3.6 convolution_convert_fusion.6
  403.4 12.5 %shard_map.264 = (bf16[8,2,64,256]{3,2,1,0:T(8,128)(2,1)S(1)}, bf16[8,2,64,256]{3,2,1,0:T(8,128)(2,1)S(1)}, bf16[8,2,64,256]{3,2,1,0:T(8,128)(2,1)S(1)}, f32[4,512,512]{2,1,0:T(8,128)S(1)}) custom-call(bf16[8,2,64,256]{3,2,1,0:T(8,128)(2,1)S(1)} %bitcast.205, bf16[8,2,64,256]{3,2,1,0:T(8,128)(2,1)S(1)} %bitcast.203, bf16[8,2,64,256]{3,2,1,0:T(8,128)(2,1)S(1)} %bitcast.201, ...), custom_call_target="tpu_custom_call" | custom-call | flops 16777216000 | bytes 12058624 | tf_op jit(solution)/shard_map/pallas_call | solution.py:352
  419.3 3.4 add_convert_fusion
  422.7 22.9 %all-to-all-done.2.g_ref = bf16[8,3,64,640]{3,2,1,0:T(8,128)(2,1)S(1)} async-done(((bf16[8,3,64,640]{3,2,1,0:T(8,128)(2,1)}), bf16[8,3,64,640]{3,2,1,0:T(8,128)(2,1)S(1)}, u32[]{:S(2)}, u32[]{:S(2)}) %all-to-all-start.2) | async-done | bytes 1966112 | tf_op jit(solution)/shard_map/all_to_all | solution.py:438
  446.9 3.7 convolution_convert_fusion.5
  459.2 1.7 collective-permute-start.17
  460.9 10.4 %collective-permute-done.18 = bf16[4,4,64,256]{3,2,0,1:T(8,128)(2,1)S(1)} collective-permute-done((bf16[4,4,64,256]{3,2,0,1:T(8,128)(2,1)S(1)}, bf16[4,4,64,256]{3,2,0,1:T(8,128)(2,1)S(1)}, u32[]{:S(2)}, u32[]{:S(2)}) %collective-permute-start.18) | collective-permute-done | bytes 524320 | tf_op jit(solution)/shard_map/ppermute | solution.py:158
  473.7 9.3 %collective-permute-done.14 = bf16[4,4,64,256]{3,2,0,1:T(8,128)(2,1)S(1)} collective-permute-done((bf16[4,4,64,256]{3,2,0,1:T(8,128)(2,1)S(1)}, bf16[4,4,64,256]{3,2,0,1:T(8,128)(2,1)S(1)}, u32[]{:S(2)}, u32[]{:S(2)}) %collective-permute-start.14) | collective-permute-done | bytes 524320 | tf_op jit(solution)/shard_map/ppermute | solution.py:158
  483.0 9.6 %collective-permute-done.19 = bf16[4,4,64,256]{3,2,0,1:T(8,128)(2,1)S(1)} collective-permute-done((bf16[4,4,64,256]{3,2,0,1:T(8,128)(2,1)S(1)}, bf16[4,4,64,256]{3,2,0,1:T(8,128)(2,1)S(1)}, u32[]{:S(2)}, u32[]{:S(2)}) %collective-permute-start.19) | collective-permute-done | bytes 524320 | tf_op jit(solution)/shard_map/ppermute | solution.py:158
  494.2 3.6 all-to-all-start.3
  497.8 2.5 convert_element_type.301
  500.3 6.4 %fusion.12 = f32[32,4]{1,0:T(8,128)S(1)} fusion(bf16[4,512,512]{2,1,0:T(8,128)(2,1)S(1)} %convert_element_type.301, s32[512,512]{1,0:T(8,128)} %copy-done.39), kind=kOutput, calls=%fused_computation.46 | convolution fusion | flops 75497472 | bytes 3146240 | tf_op jit(solution)/shard_map/hij,zij->zh/dot_general | solution.py:571
  507.0 2.2 copy-done
  510.7 2.1 copy-done.7
  512.8 2.2 copy-done.8
  515.0 6.5 %shard_map.266 = (f32[3,64,5120]{2,1,0:T(8,128)}, f32[3,64,5120]{2,1,0:T(8,128)}, f32[3,64,5120]{2,1,0:T(8,128)}) custom-call(f32[3,64,5120]{2,1,0:T(8,128)S(1)} %bitcast.192, f32[3,64,5120]{2,1,0:T(8,128)S(1)} %bitcast.193, f32[3,64,5120]{2,1,0:T(8,128)S(1)} %bitcast.194, bf16[8,3,64,640]{3,2,1,0:T(8,128)(2,1)S(1)} %copy-done.3), custom_call_target="tpu_custom_call" | custom-call | flops 19660800 | bytes 25559040 | tf_op jit(solution)/shard_map/pallas_call | solution.py:260
  521.5 1.7 fusion.21
  524.5 1.9 collective-permute-start.21
  526.4 6.1 %collective-permute-done.21 = f32[40,128]{1,0:T(8,128)S(1)} collective-permute-done((f32[40,128]{1,0:T(8,128)S(1)}, f32[40,128]{1,0:T(8,128)S(1)}, u32[]{:S(2)}, u32[]{:S(2)}) %collective-permute-start.21) | collective-permute-done | bytes 20512 | tf_op jit(solution)/shard_map/ppermute | solution.py:158
  532.4 4.1 collective-permute-start.22
  536.5 4.2 all-to-all-done.3.g_ref
  540.8 1.6 copy-done.9
  542.4 1.6 copy-done.10
  544.0 7.8 %shard_map.265 = (f32[64,4,2048]{2,1,0:T(4,128)}, f32[64,4,2048]{2,1,0:T(4,128)}, f32[3,64,2048]{2,1,0:T(8,128)}, f32[64,2048]{1,0:T(8,128)}) custom-call(f32[64,4,2048]{2,1,0:T(4,128)S(1)} %copy-done.1, f32[64,4,2048]{2,1,0:T(4,128)S(1)} %copy-done.9, f32[64,4,2048]{2,1,0:T(4,128)S(1)} %copy-done.10, bf16[8,4,64,256]{3,2,1,0:T(8,128)(2,1)S(1)} %all-to-all-done.3.g_ref), custom_call_target="tpu_custom_call" | custom-call | flops 10485760 | bytes 13631488 | tf_op jit(solution)/shard_map/pallas_call | solution.py:212
  553.3 2.4 collective-permute-done.23
  557.2 3.2 reduce-scatter.11.cloned.1.call-done
  560.4 3.7 fusion.20
  (257 shorter events, 84.7 us)
Async XLA Ops:
  9.2 8.7 %copy-start.23 = (bf16[2,64,2048]{2,1,0:T(8,128)(2,1)S(1)}, bf16[2,64,2048]{2,1,0:T(8,128)(2,1)}, u32[]{:S(2)}) copy-start(bf16[2,64,2048]{2,1,0:T(8,128)(2,1)} %param.15) | copy-start | bytes 1572868
  9.2 8.9 %copy-start.42 = (f32[2,2048]{1,0:T(2,128)S(1)}, f32[2,2048]{1,0:T(2,128)}, u32[]{:S(2)}) copy-start(f32[2,2048]{1,0:T(2,128)} %param.24) | copy-start | bytes 49156
  11.6 32.9 %all-to-all-start = ((bf16[8,4,64,256]{3,2,1,0:T(8,128)(2,1)}), bf16[8,4,64,256]{3,2,1,0:T(8,128)(2,1)S(1)}, u32[]{:S(2)}, u32[]{:S(2)}) async-start(bf16[8,4,64,256]{3,2,1,0:T(8,128)(2,1)} %copy.96), calls=%async_computation | async-start | bytes 2097152 | tf_op jit(solution)/shard_map/all_to_all | solution.py:434
  17.9 73.3 %all-gather.9.cloned.1.call-start = ((), (), s32[]{:S(2)}) async-start(), calls=%async_computation.12 | async-start | bytes 4718592 | tf_op jit(solution)/shard_map/all_gather | solution.py:464
  18.2 56.3 %copy-start.52 = (f32[2,64]{1,0:T(2,128)}, f32[2,64]{1,0:T(2,128)S(1)}, u32[]{:S(2)}) copy-start(f32[2,64]{1,0:T(2,128)S(1)} %add_rsqrt_fusion.1) | copy-start | bytes 1540
  18.2 56.3 %copy-start.40 = (f32[1,2048]{1,0:T(1,128)}, f32[1,2048]{1,0:T(1,128)S(1)}, u32[]{:S(2)}) copy-start(f32[1,2048]{1,0:T(1,128)S(1)} %get-tuple-element.159) | copy-start | bytes 24580
  44.6 128.8 %all-gather.11.cloned.1.call-start = ((), (), s32[]{:S(2)}) async-start(), calls=%async_computation.13 | async-start | bytes 4718592 | tf_op jit(solution)/shard_map/all_gather | solution.py:464
  44.7 24.8 %collective-permute-start = (bf16[4,8,64,256]{3,2,1,0:T(8,128)(2,1)S(1)}, bf16[4,8,64,256]{3,2,1,0:T(8,128)(2,1)S(1)}, u32[]{:S(2)}, u32[]{:S(2)}) collective-permute-start(bf16[4,8,64,256]{3,2,1,0:T(8,128)(2,1)S(1)} %bitcast.212), channel_id=1, source_target_pairs={{0,1},{1,0},{2,3},{3,2},{4,5},{5,4},{6,7},{7,6},{8,9},{9,8},{10,11... | collective-permute-start | bytes 3145736 | tf_op jit(solution)/shard_map/ppermute | solution.py:158
  46.2 24.5 %collective-permute-start.1 = (bf16[4,8,64,256]{3,2,1,0:T(8,128)(2,1)S(1)}, bf16[4,8,64,256]{3,2,1,0:T(8,128)(2,1)}, u32[]{:S(2)}, u32[]{:S(2)}) collective-permute-start(bf16[4,8,64,256]{3,2,1,0:T(8,128)(2,1)S(1)} %bitcast.213), channel_id=1, source_target_pairs={{0,2},{1,3},{2,0},{3,1},{4,6},{5,7},{6,4},{7,5},{8,10},{9,11},{10,... | collective-permute-start | bytes 3145736 | tf_op jit(solution)/shard_map/ppermute | solution.py:158
  74.5 12.4 %collective-permute-start.2 = (bf16[4,4,64,256]{3,2,1,0:T(8,128)(2,1)S(1)}, bf16[4,4,64,256]{3,2,1,0:T(8,128)(2,1)S(1)}, u32[]{:S(2)}, u32[]{:S(2)}) collective-permute-start(bf16[4,4,64,256]{3,2,1,0:T(8,128)(2,1)S(1)} %slice.108), channel_id=1, source_target_pairs={{0,2},{1,3},{2,0},{3,1},{4,6},{5,7},{6,4},{7,5},{8,10},{9,11},{10,... | collective-permute-start | bytes 1572872 | tf_op jit(solution)/shard_map/ppermute | solution.py:158
  77.2 12.1 %collective-permute-start.3 = (bf16[4,4,64,256]{3,2,1,0:T(8,128)(2,1)S(1)}, bf16[4,4,64,256]{3,2,1,0:T(8,128)(2,1)S(1)}, u32[]{:S(2)}, u32[]{:S(2)}) collective-permute-start(bf16[4,4,64,256]{3,2,1,0:T(8,128)(2,1)S(1)} %slice.109), channel_id=1, source_target_pairs={{0,1},{1,0},{2,3},{3,2},{4,5},{5,4},{6,7},{7,6},{8,9},{9,8},{10,11... | collective-permute-start | bytes 1572872 | tf_op jit(solution)/shard_map/ppermute | solution.py:158
  95.1 23.9 %copy-start.15 = (bf16[1024,256]{1,0:T(8,128)(2,1)}, bf16[1024,256]{1,0:T(8,128)(2,1)S(1)}, u32[]{:S(2)}) copy-start(bf16[1024,256]{1,0:T(8,128)(2,1)S(1)} %convolution_convert_fusion.7) | copy-start | bytes 1572868
  96.6 22.4 %copy-start.17 = (bf16[1024,256]{1,0:T(8,128)(2,1)}, bf16[1024,256]{1,0:T(8,128)(2,1)S(1)}, u32[]{:S(2)}) copy-start(bf16[1024,256]{1,0:T(8,128)(2,1)S(1)} %convolution_convert_fusion.8) | copy-start | bytes 1572868
  97.9 21.1 %copy-start.19 = (bf16[1024,256]{1,0:T(8,128)(2,1)}, bf16[1024,256]{1,0:T(8,128)(2,1)S(1)}, u32[]{:S(2)}) copy-start(bf16[1024,256]{1,0:T(8,128)(2,1)S(1)} %convolution_convert_fusion.9) | copy-start | bytes 1572868
  98.5 6.6 %copy-start.48 = (f32[32,32]{1,0:T(8,128)S(1)}, f32[32,32]{1,0:T(8,128)}, u32[]{:S(2)}) copy-start(f32[32,32]{1,0:T(8,128)} %param.27) | copy-start | bytes 12292
  100.0 78.8 %all-to-all-start.1 = ((bf16[8,3,64,640]{3,2,1,0:T(8,128)(2,1)}), bf16[8,3,64,640]{3,2,1,0:T(8,128)(2,1)}, u32[]{:S(2)}, u32[]{:S(2)}) async-start(bf16[8,3,64,640]{3,2,1,0:T(8,128)(2,1)} %bitcast.210), calls=%async_computation.1 | async-start | bytes 3932160 | tf_op jit(solution)/shard_map/all_to_all | solution.py:434
  104.4 123.3 %reduce-scatter.5.cloned.1.call-start = ((), (), s32[]{:S(2)}) async-start(), calls=%async_computation.8 | async-start | bytes 4718592 | tf_op jit(solution)/shard_map/reduce_scatter | solution.py:470
  105.0 10.4 %copy-start.39 = (s32[512,512]{1,0:T(8,128)}, s32[512,512]{1,0:T(8,128)S(1)}, u32[]{:S(2)}) copy-start(s32[512,512]{1,0:T(8,128)S(1)} %fusion.23) | copy-start | bytes 3145732
  121.2 11.2 %copy-start.13 = (s32[2,512,1]{2,1,0:T(8,128)}, s32[2,512,1]{2,1,0:T(8,128)S(1)}, u32[]{:S(2)}) copy-start(s32[2,512,1]{2,1,0:T(8,128)S(1)} %copy.104.seg_q_ref) | copy-start | bytes 12292
  121.2 11.2 %copy-start.34 = (bf16[1,8,4,64,256]{4,3,2,1,0:T(8,128)(2,1)S(1)}, bf16[1,8,4,64,256]{4,3,2,1,0:T(8,128)(2,1)}, u32[]{:S(2)}) copy-start(bf16[1,8,4,64,256]{4,3,2,1,0:T(8,128)(2,1)} %get-tuple-element.140) | copy-start | bytes 3145732
  178.8 98.1 %all-gather.13.cloned.1.call-start = ((), (), s32[]{:S(2)}) async-start(), calls=%async_computation.14 | async-start | bytes 4718592 | tf_op jit(solution)/shard_map/all_gather | solution.py:464
  178.9 49.9 %collective-permute-start.4 = (bf16[3,8,64,640]{3,2,0,1:T(8,128)(2,1)}, bf16[3,8,64,640]{3,2,0,1:T(8,128)(2,1)S(1)}, u32[]{:S(2)}, u32[]{:S(2)}) collective-permute-start(bf16[3,8,64,640]{3,2,0,1:T(8,128)(2,1)} %bitcast.28), channel_id=1, source_target_pairs={{0,1},{1,0},{2,3},{3,2},{4,5},{5,4},{6,7},{7,6},{8,9},{9,8},{10,11... | collective-permute-start | bytes 5898248 | tf_op jit(solution)/shard_map/ppermute | solution.py:158
  180.4 49.7 %collective-permute-start.5 = (bf16[3,8,64,640]{3,2,0,1:T(8,128)(2,1)}, bf16[3,8,64,640]{3,2,0,1:T(8,128)(2,1)}, u32[]{:S(2)}, u32[]{:S(2)}) collective-permute-start(bf16[3,8,64,640]{3,2,0,1:T(8,128)(2,1)} %bitcast.28), channel_id=1, source_target_pairs={{0,2},{1,3},{2,0},{3,1},{4,6},{5,7},{6,4},{7,5},{8,10},{9,11},{10,... | collective-permute-start | bytes 5898248 | tf_op jit(solution)/shard_map/ppermute | solution.py:158
  230.4 116.0 %copy-start.21 = (f32[2,64,2048]{2,1,0:T(8,128)}, f32[2,64,2048]{2,1,0:T(8,128)S(1)}, u32[]{:S(2)}) copy-start(f32[2,64,2048]{2,1,0:T(8,128)S(1)} %get-tuple-element.128) | copy-start | bytes 3145732
  231.5 112.7 %reduce-scatter.7.cloned.1.call-start = ((), (), s32[]{:S(2)}) async-start(), calls=%async_computation.9 | async-start | bytes 4718592 | tf_op jit(solution)/shard_map/reduce_scatter | solution.py:470
  233.3 21.4 %collective-permute-start.6 = (bf16[3,4,64,640]{3,2,0,1:T(8,128)(2,1)S(1)}, bf16[3,4,64,640]{3,2,0,1:T(8,128)(2,1)S(1)}, u32[]{:S(2)}, u32[]{:S(2)}) collective-permute-start(bf16[3,4,64,640]{3,2,0,1:T(8,128)(2,1)S(1)} %slice.115), channel_id=1, source_target_pairs={{0,2},{1,3},{2,0},{3,1},{4,6},{5,7},{6,4},{7,5},{8,10},{9,11},{10,... | collective-permute-start | bytes 2949128 | tf_op jit(solution)/shard_map/ppermute | solution.py:158
  236.1 21.1 %collective-permute-start.7 = (bf16[3,4,64,640]{3,2,0,1:T(8,128)(2,1)S(1)}, bf16[3,4,64,640]{3,2,0,1:T(8,128)(2,1)S(1)}, u32[]{:S(2)}, u32[]{:S(2)}) collective-permute-start(bf16[3,4,64,640]{3,2,0,1:T(8,128)(2,1)S(1)} %slice.116), channel_id=1, source_target_pairs={{0,1},{1,0},{2,3},{3,2},{4,5},{5,4},{6,7},{7,6},{8,9},{9,8},{10,11... | collective-permute-start | bytes 2949128 | tf_op jit(solution)/shard_map/ppermute | solution.py:158
  295.3 99.8 %all-gather.15.cloned.1.call-start = ((), (), s32[]{:S(2)}) async-start(), calls=%async_computation.15 | async-start | bytes 4718592 | tf_op jit(solution)/shard_map/all_gather | solution.py:464
  314.2 31.2 %collective-permute-start.8 = (bf16[3,4,64,640]{3,2,0,1:T(8,128)(2,1)}, bf16[3,4,64,640]{3,2,0,1:T(8,128)(2,1)}, u32[]{:S(2)}, u32[]{:S(2)}) collective-permute-start(bf16[3,4,64,640]{3,2,0,1:T(8,128)(2,1)} %get-tuple-element.145), channel_id=1, source_target_pairs={{0,1},{1,0},{2,3},{3,2},{4,5},{5,4},{6,7},{7,6},{8,9},{9,8},{10,11... | collective-permute-start | bytes 2949128 | tf_op jit(solution)/shard_map/ppermute | solution.py:158
  315.6 29.7 %collective-permute-start.9 = (bf16[3,4,64,640]{3,2,0,1:T(8,128)(2,1)}, bf16[3,4,64,640]{3,2,0,1:T(8,128)(2,1)}, u32[]{:S(2)}, u32[]{:S(2)}) collective-permute-start(bf16[3,4,64,640]{3,2,0,1:T(8,128)(2,1)} %get-tuple-element.144), channel_id=1, source_target_pairs={{0,2},{1,3},{2,0},{3,1},{4,6},{5,7},{6,4},{7,5},{8,10},{9,11},{10,... | collective-permute-start | bytes 2949128 | tf_op jit(solution)/shard_map/ppermute | solution.py:158
  327.1 19.3 %copy-start.25 = (bf16[2,64,2048]{2,1,0:T(8,128)(2,1)S(1)}, bf16[2,64,2048]{2,1,0:T(8,128)(2,1)}, u32[]{:S(2)}) copy-start(bf16[2,64,2048]{2,1,0:T(8,128)(2,1)} %param.17) | copy-start | bytes 1572868
  346.4 7.5 %copy-start.54 = (f32[2,64]{1,0:T(2,128)}, f32[2,64]{1,0:T(2,128)S(1)}, u32[]{:S(2)}) copy-start(f32[2,64]{1,0:T(2,128)S(1)} %broadcast_multiply_fusion.1) | copy-start | bytes 1540
  349.3 43.9 %copy-start.36 = (bf16[3,4,64,640]{3,2,0,1:T(8,128)(2,1)S(1)}, bf16[3,4,64,640]{3,2,0,1:T(8,128)(2,1)}, u32[]{:S(2)}) copy-start(bf16[3,4,64,640]{3,2,0,1:T(8,128)(2,1)} %get-tuple-element.93) | copy-start | bytes 2949124
  349.3 24.8 %collective-permute-start.11 = (bf16[3,4,64,640]{3,2,0,1:T(8,128)(2,1)S(1)}, bf16[3,4,64,640]{3,2,0,1:T(8,128)(2,1)S(1)}, u32[]{:S(2)}, u32[]{:S(2)}) collective-permute-start(bf16[3,4,64,640]{3,2,0,1:T(8,128)(2,1)S(1)} %add_convert_fusion.4), channel_id=1, source_target_pairs={{0,2},{1,3},{2,0},{3,1},{4,6},{5,7},{6,4},{7,5},{8,10},{9,11},{10,... | collective-permute-start | bytes 2949128 | tf_op jit(solution)/shard_map/ppermute | solution.py:158
  350.9 24.9 %collective-permute-start.10 = (bf16[3,4,64,640]{3,2,0,1:T(8,128)(2,1)}, bf16[3,4,64,640]{3,2,0,1:T(8,128)(2,1)S(1)}, u32[]{:S(2)}, u32[]{:S(2)}) collective-permute-start(bf16[3,4,64,640]{3,2,0,1:T(8,128)(2,1)} %get-tuple-element.90), channel_id=1, source_target_pairs={{0,1},{1,0},{2,3},{3,2},{4,5},{5,4},{6,7},{7,6},{8,9},{9,8},{10,11... | collective-permute-start | bytes 2949128 | tf_op jit(solution)/shard_map/ppermute | solution.py:158
  353.9 39.3 %collective-permute-start.13 = (bf16[3,4,64,640]{3,2,0,1:T(8,128)(2,1)S(1)}, bf16[3,4,64,640]{3,2,0,1:T(8,128)(2,1)S(1)}, u32[]{:S(2)}, u32[]{:S(2)}) collective-permute-start(bf16[3,4,64,640]{3,2,0,1:T(8,128)(2,1)S(1)} %add_convert_fusion.2), channel_id=1, source_target_pairs={{0,1},{1,0},{2,3},{3,2},{4,5},{5,4},{6,7},{7,6},{8,9},{9,8},{10,11... | collective-permute-start | bytes 2949128 | tf_op jit(solution)/shard_map/ppermute | solution.py:158
  354.5 38.8 %collective-permute-start.12 = (bf16[3,4,64,640]{3,2,0,1:T(8,128)(2,1)}, bf16[3,4,64,640]{3,2,0,1:T(8,128)(2,1)S(1)}, u32[]{:S(2)}, u32[]{:S(2)}) collective-permute-start(bf16[3,4,64,640]{3,2,0,1:T(8,128)(2,1)} %get-tuple-element.94), channel_id=1, source_target_pairs={{0,2},{1,3},{2,0},{3,1},{4,6},{5,7},{6,4},{7,5},{8,10},{9,11},{10,... | collective-permute-start | bytes 2949128 | tf_op jit(solution)/shard_map/ppermute | solution.py:158
  395.1 50.5 %all-to-all-start.2 = ((bf16[8,3,64,640]{3,2,1,0:T(8,128)(2,1)}), bf16[8,3,64,640]{3,2,1,0:T(8,128)(2,1)S(1)}, u32[]{:S(2)}, u32[]{:S(2)}) async-start(bf16[8,3,64,640]{3,2,1,0:T(8,128)(2,1)} %bitcast.211), calls=%async_computation.4 | async-start | bytes 3932160 | tf_op jit(solution)/shard_map/all_to_all | solution.py:438
  399.3 122.1 %reduce-scatter.9.cloned.1.call-start = ((), (), s32[]{:S(2)}) async-start(), calls=%async_computation.10 | async-start | bytes 4718592 | tf_op jit(solution)/shard_map/reduce_scatter | solution.py:470
  403.4 12.5 %copy-start.33 = (bf16[1,8,4,64,256]{4,3,2,1,0:T(8,128)(2,1)S(1)}, bf16[1,8,4,64,256]{4,3,2,1,0:T(8,128)(2,1)}, u32[]{:S(2)}) copy-start(bf16[1,8,4,64,256]{4,3,2,1,0:T(8,128)(2,1)} %get-tuple-element.142) | copy-start | bytes 3145732
  445.6 114.8 %reduce-scatter.11.cloned.1.call-start = ((), (), s32[]{:S(2)}) async-start(), calls=%async_computation.11 | async-start | bytes 4718592 | tf_op jit(solution)/shard_map/reduce_scatter | solution.py:470
  456.4 14.9 %collective-permute-start.18 = (bf16[4,4,64,256]{3,2,0,1:T(8,128)(2,1)S(1)}, bf16[4,4,64,256]{3,2,0,1:T(8,128)(2,1)S(1)}, u32[]{:S(2)}, u32[]{:S(2)}) collective-permute-start(bf16[4,4,64,256]{3,2,0,1:T(8,128)(2,1)S(1)} %get-tuple-element.155), channel_id=1, source_target_pairs={{0,2},{1,3},{2,0},{3,1},{4,6},{5,7},{6,4},{7,5},{8,10},{9,11},{10,... | collective-permute-start | bytes 1572872 | tf_op jit(solution)/shard_map/ppermute | solution.py:158
  456.9 16.0 %collective-permute-start.15 = (bf16[4,4,64,256]{3,2,0,1:T(8,128)(2,1)S(1)}, bf16[4,4,64,256]{3,2,0,1:T(8,128)(2,1)S(1)}, u32[]{:S(2)}, u32[]{:S(2)}) collective-permute-start(bf16[4,4,64,256]{3,2,0,1:T(8,128)(2,1)S(1)} %get-tuple-element.154), channel_id=1, source_target_pairs={{0,1},{1,0},{2,3},{3,2},{4,5},{5,4},{6,7},{7,6},{8,9},{9,8},{10,11... | collective-permute-start | bytes 1572872 | tf_op jit(solution)/shard_map/ppermute | solution.py:158
  458.5 24.5 %collective-permute-start.14 = (bf16[4,4,64,256]{3,2,0,1:T(8,128)(2,1)S(1)}, bf16[4,4,64,256]{3,2,0,1:T(8,128)(2,1)S(1)}, u32[]{:S(2)}, u32[]{:S(2)}) collective-permute-start(bf16[4,4,64,256]{3,2,0,1:T(8,128)(2,1)S(1)} %slice.154), channel_id=1, source_target_pairs={{0,1},{1,0},{2,3},{3,2},{4,5},{5,4},{6,7},{7,6},{8,9},{9,8},{10,11... | collective-permute-start | bytes 1572872 | tf_op jit(solution)/shard_map/ppermute | solution.py:158
  459.2 23.8 %collective-permute-start.17 = (bf16[4,4,64,256]{3,2,0,1:T(8,128)(2,1)S(1)}, bf16[4,4,64,256]{3,2,0,1:T(8,128)(2,1)S(1)}, u32[]{:S(2)}, u32[]{:S(2)}) collective-permute-start(bf16[4,4,64,256]{3,2,0,1:T(8,128)(2,1)S(1)} %slice.158), channel_id=1, source_target_pairs={{0,2},{1,3},{2,0},{3,1},{4,6},{5,7},{6,4},{7,5},{8,10},{9,11},{10,... | collective-permute-start | bytes 1572872 | tf_op jit(solution)/shard_map/ppermute | solution.py:158
  471.5 21.1 %collective-permute-start.19 = (bf16[4,4,64,256]{3,2,0,1:T(8,128)(2,1)S(1)}, bf16[4,4,64,256]{3,2,0,1:T(8,128)(2,1)S(1)}, u32[]{:S(2)}, u32[]{:S(2)}) collective-permute-start(bf16[4,4,64,256]{3,2,0,1:T(8,128)(2,1)S(1)} %add_convert_fusion.6), channel_id=1, source_target_pairs={{0,1},{1,0},{2,3},{3,2},{4,5},{5,4},{6,7},{7,6},{8,9},{9,8},{10,11... | collective-permute-start | bytes 1572872 | tf_op jit(solution)/shard_map/ppermute | solution.py:158
  473.1 19.5 %collective-permute-start.16 = (bf16[4,4,64,256]{3,2,0,1:T(8,128)(2,1)S(1)}, bf16[4,4,64,256]{3,2,0,1:T(8,128)(2,1)S(1)}, u32[]{:S(2)}, u32[]{:S(2)}) collective-permute-start(bf16[4,4,64,256]{3,2,0,1:T(8,128)(2,1)S(1)} %add_convert_fusion.8), channel_id=1, source_target_pairs={{0,2},{1,3},{2,0},{3,1},{4,6},{5,7},{6,4},{7,5},{8,10},{9,11},{10,... | collective-permute-start | bytes 1572872 | tf_op jit(solution)/shard_map/ppermute | solution.py:158
  494.2 46.5 %all-to-all-start.3 = ((bf16[8,4,64,256]{3,2,1,0:T(8,128)(2,1)}), bf16[8,4,64,256]{3,2,1,0:T(8,128)(2,1)S(1)}, u32[]{:S(2)}, u32[]{:S(2)}) async-start(bf16[8,4,64,256]{3,2,1,0:T(8,128)(2,1)} %maximum_bitcast_fusion), calls=%async_computation.7 | async-start | bytes 2097152 | tf_op jit(solution)/shard_map/all_to_all | solution.py:438
  514.9 6.5 %copy-start.41 = (f32[1,2048]{1,0:T(1,128)S(1)}, f32[1,2048]{1,0:T(1,128)}, u32[]{:S(2)}) copy-start(f32[1,2048]{1,0:T(1,128)} %copy-done.40) | copy-start | bytes 24580
  515.0 6.5 %copy-start.53 = (f32[2,64]{1,0:T(2,128)S(1)}, f32[2,64]{1,0:T(2,128)}, u32[]{:S(2)}) copy-start(f32[2,64]{1,0:T(2,128)} %copy-done.52) | copy-start | bytes 1540
  515.0 8.2 %copy-start.44 = (f32[2048]{0:T(1024)S(1)}, f32[2048]{0:T(1024)}, u32[]{:S(2)}) copy-start(f32[2048]{0:T(1024)} %get-tuple-element.117) | copy-start | bytes 24580
  515.0 25.8 %copy-start.1 = (f32[64,4,2048]{2,1,0:T(4,128)S(1)}, f32[64,4,2048]{2,1,0:T(4,128)}, u32[]{:S(2)}) copy-start(f32[64,4,2048]{2,1,0:T(4,128)} %w_ref.1) | copy-start | bytes 6291460
  523.1 37.3 %copy-start.55 = (f32[2,64]{1,0:T(2,128)S(1)}, f32[2,64]{1,0:T(2,128)}, u32[]{:S(2)}) copy-start(f32[2,64]{1,0:T(2,128)} %copy-done.54) | copy-start | bytes 1540
  523.1 1.3 collective-permute-start.20
  524.5 7.9 %collective-permute-start.21 = (f32[40,128]{1,0:T(8,128)S(1)}, f32[40,128]{1,0:T(8,128)S(1)}, u32[]{:S(2)}, u32[]{:S(2)}) collective-permute-start(f32[40,128]{1,0:T(8,128)S(1)} %bitcast_add_fusion), channel_id=1, source_target_pairs={{0,8},{4,12},{8,0},{12,4},{16,24},{20,28},{24,16},{28,20},{1,9},{5... | collective-permute-start | bytes 61448 | tf_op jit(solution)/shard_map/ppermute | solution.py:158
  532.4 19.4 %collective-permute-start.22 = (f32[40,128]{1,0:T(8,128)S(1)}, f32[40,128]{1,0:T(8,128)S(1)}, u32[]{:S(2)}, u32[]{:S(2)}) collective-permute-start(f32[40,128]{1,0:T(8,128)S(1)} %fusion.87), channel_id=1, source_target_pairs={{0,16},{4,20},{8,24},{12,28},{16,0},{20,4},{24,8},{28,12},{1,17},{... | collective-permute-start | bytes 61448 | tf_op jit(solution)/shard_map/ppermute | solution.py:158
  551.7 12.5 %copy-start.43 = (f32[2,2048]{1,0:T(2,128)S(1)}, f32[2,2048]{1,0:T(2,128)}, u32[]{:S(2)}) copy-start(f32[2,2048]{1,0:T(2,128)} %param.24) | copy-start | bytes 49156
  551.7 12.5 %copy-start.46 = (f32[2,2048]{1,0:T(2,128)S(1)}, f32[2,2048]{1,0:T(2,128)}, u32[]{:S(2)}) copy-start(f32[2,2048]{1,0:T(2,128)} %param.25) | copy-start | bytes 49156
  551.7 12.5 %copy-start.47 = (f32[2,2048]{1,0:T(2,128)S(1)}, f32[2,2048]{1,0:T(2,128)}, u32[]{:S(2)}) copy-start(f32[2,2048]{1,0:T(2,128)} %param.26) | copy-start | bytes 49156
  551.8 13.1 %copy-start.49 = (f32[32,32]{1,0:T(8,128)S(1)}, f32[32,32]{1,0:T(8,128)}, u32[]{:S(2)}) copy-start(f32[32,32]{1,0:T(8,128)} %param.27) | copy-start | bytes 12292
  551.8 13.1 %copy-start.50 = (f32[32,32]{1,0:T(8,128)S(1)}, f32[32,32]{1,0:T(8,128)}, u32[]{:S(2)}) copy-start(f32[32,32]{1,0:T(8,128)} %param.28) | copy-start | bytes 12292
  551.8 13.1 %copy-start.51 = (f32[32,32]{1,0:T(8,128)S(1)}, f32[32,32]{1,0:T(8,128)}, u32[]{:S(2)}) copy-start(f32[32,32]{1,0:T(8,128)} %param.29) | copy-start | bytes 12292
  551.8 3.8 collective-permute-start.23
  555.7 8.4 %collective-permute-start.24 = (f32[40,128]{1,0:T(8,128)S(1)}, f32[40,128]{1,0:T(8,128)S(1)}, u32[]{:S(2)}, u32[]{:S(2)}) collective-permute-start(f32[40,128]{1,0:T(8,128)S(1)} %add.255), channel_id=1, source_target_pairs={{0,2},{1,3},{2,0},{3,1},{4,6},{5,7},{6,4},{7,5},{8,10},{9,11},{10,... | collective-permute-start | bytes 61448 | tf_op jit(solution)/shard_map/ppermute | solution.py:158
  (38 other events, 109.1 us)
Sparse Core Ops, SparseCore 0:
  44.8 46.0 all-gather.8
  92.5 80.9 all-gather.10
  179.0 48.6 reduce-scatter.4
  231.7 45.2 all-gather.12
  295.5 48.7 reduce-scatter.6
  347.7 45.2 all-gather.14
  445.8 47.9 reduce-scatter.8
  496.0 64.3 reduce-scatter.10

commit v6 on v5

--- a/solution.py
+++ b/solution.py
@@ -495,20 +495,6 @@
     part = heads_here * HEAD_DIM
     seq_index = lax.axis_index("seq")
 
-    attention_slots = attention_weight.transpose(1, 0, 2).astype(jnp.bfloat16)
-    feed_slots = feed_weight.transpose(1, 0, 2).astype(jnp.bfloat16)
-    inputs = tokens.astype(jnp.float32)
-    normed_here = rms_norm(inputs, gains[0]).astype(jnp.bfloat16)
-    attention_mine, normed_here = lax.optimization_barrier(
-        (to_columns(attention_slots), normed_here)
-    )
-    normed_one = gather_tokens(normed_here)
-    attention_items, late_cotangent = lax.optimization_barrier(
-        (gather_dp_first(attention_mine), cotangent)
-    )
-    attention_low = gather_dp_second(attention_items)
-    weight_out = attention_low[3]
-
     positions = jnp.arange(seq_len, dtype=jnp.int32)
     buckets = rel_bucket(positions[None, :] - positions[:, None])
     bucket_match = buckets[None, :, :] == jnp.arange(NUM_BUCKETS, dtype=jnp.int32)[:, None, None]
@@ -520,15 +506,28 @@
         precision=HIGHEST,
         preferred_element_type=jnp.float32,
     )
+    attention_slots = attention_weight.transpose(1, 0, 2).astype(jnp.bfloat16)
+    feed_slots = feed_weight.transpose(1, 0, 2).astype(jnp.bfloat16)
+    inputs = tokens.astype(jnp.float32)
+    normed_here = rms_norm(inputs, gains[0]).astype(jnp.bfloat16)
+    attention_mine, normed_here, bias, feed_slots = lax.optimization_barrier(
+        (to_columns(attention_slots), normed_here, bias, feed_slots)
+    )
+    normed_one = gather_tokens(normed_here)
+    attention_items, late_cotangent = lax.optimization_barrier(
+        (gather_dp_first(attention_mine), cotangent)
+    )
+    attention_low = gather_dp_second(attention_items)
+    weight_out = attention_low[3]
 
     def as_blocks(matrix):
         return matrix.astype(jnp.bfloat16).reshape(seq_size, micro_count, local_rows, part)
 
     grad_out = gather_tokens(late_cotangent)
+    normed_one, feed_slots = lax.optimization_barrier((normed_one, feed_slots))
     query, key, value = [
         as_blocks(dot(normed_one, attention_low[slot])) for slot in range(3)
     ]
-    query, key, value, feed_slots = lax.optimization_barrier((query, key, value, feed_slots))
     feed_mine = to_columns(feed_slots)
     attended = attention_forward(query, key, value, bias, segments).reshape(-1, part)
     attention_partial, grad_out, feed_mine = lax.optimization_barrier(

time: 583 us -> 584 us (level)
  the two profiles are of different devices: /device:TPU:0 before, /device:TPU:11 now
where the time goes in v6:
time: 584 us; the launch traced here: 575 us
  waiting for transfers between devices  295 us (51%)
  local copies, waits for them, and re-layouts  66.3 us (11%)
  matrix products  66.1 us (11%)
  Pallas kernels  56.2 us (10%)
  starting transfers between devices  42.7 us (7%)
  other arithmetic  32.9 us (6%)
  between operations  15.4 us (3%)
    ppermute x25, waiting for transfers between devices, swap(): return lax.ppermute(value, axis, partner_pairs(axis, offset))  122 us
    reduce_scatter x4, waiting for transfers between devices, scatter_tokens(): lax.psum_scatter(send, 'seq', scatter_dimension=0).astype(jnp.float32)  80 us
    all_gather x4, waiting for transfers between devices, gather_tokens(): full = lax.all_gather(local_rows, 'seq', axis=0)  58.5 us
    all_to_all x2, waiting for transfers between devices, to_rows(): return lax.all_to_all(mine.transpose(1, 0, 2, 3), 'seq', 0, 0)  23.4 us
    dot_general x7, matrix products, outer_sum(): lax.dot_general(left, right, (((0,), (0,)), ((), ())), preferred_element_...  21.5 us
    unnamed x132, local copies, waits for them, and re-layouts  19.1 us
    pallas_call x1, Pallas kernels, feed_middle(): pl.pallas_call(body, grid=(tokens // block,), in_specs=[rows, units, weig...  18.3 us
    ppermute x25, starting transfers between devices, swap(): return lax.ppermute(value, axis, partner_pairs(axis, offset))  17.5 us
  transfers between devices with their start and end apart: 37, of which 25 were waited for; matrix products, arithmetic and copies ran while one was open for 24% of the time, Pallas kernels for 7%

profile of v6, /device:TPU:11, one launch (start us, length us, event | category | flops | bytes accessed | tf_op | source)
XLA Modules:
  0.0 574.6 jit_solution(4463334529211080296)
XLA Ops:
  7.2 2.0 convert_bitcast_fusion
  10.0 1.6 copy.96
  11.6 5.6 all-to-all-start
  17.9 11.8 %fusion.1 = f32[4,512,512]{2,0,1:T(4,128)} fusion(s32[512,512]{1,0:T(8,128)S(1)} %fusion.20, f32[32,32]{1,0:T(8,128)S(1)} %copy-done.47, s32[]{:T(128)S(6)} %select_n.52), kind=kOutput, calls=%fused_computation.2 | convolution fusion | flops 411041792 | bytes 5246980 | tf_op jit(solution)/shard_map/atj,ao->otj/dot_general | solution.py:502
  30.7 3.6 bitcast_convert_fusion.3
  34.4 5.9 %all-to-all-done = bf16[8,4,64,256]{3,2,1,0:T(8,128)(2,1)S(1)} async-done(((bf16[8,4,64,256]{3,2,1,0:T(8,128)(2,1)}), bf16[8,4,64,256]{3,2,1,0:T(8,128)(2,1)S(1)}, u32[]{:S(2)}, u32[]{:S(2)}) %all-to-all-start) | async-done | bytes 1048608 | tf_op jit(solution)/shard_map/all_to_all | solution.py:434
  42.0 22.9 %collective-permute-done = bf16[4,8,64,256]{3,2,1,0:T(8,128)(2,1)S(1)} collective-permute-done((bf16[4,8,64,256]{3,2,1,0:T(8,128)(2,1)S(1)}, bf16[4,8,64,256]{3,2,1,0:T(8,128)(2,1)S(1)}, u32[]{:S(2)}, u32[]{:S(2)}) %collective-permute-start) | collective-permute-done | bytes 1048608 | tf_op jit(solution)/shard_map/ppermute | solution.py:158
  66.2 5.9 %copy.103.bias_ref = f32[4,512,512]{2,1,0:T(8,128)} copy(f32[4,512,512]{2,0,1:T(4,128)} %fusion.1) | data formatting | bytes 8388608 | tf_op jit(solution)/shard_map/optimization_barrier | solution.py:513
  74.9 2.5 broadcast_in_dim.58
  79.6 2.4 bitcast_dynamic-update-slice_fusion
  82.0 2.6 collective-permute-done.2
  85.5 2.7 all-gather.9.cloned.1.call-done
  88.2 3.1 copy.157
  91.3 6.2 %all-to-all-start.1 = ((bf16[8,3,64,640]{3,2,1,0:T(8,128)(2,1)}), bf16[8,3,64,640]{3,2,1,0:T(8,128)(2,1)}, u32[]{:S(2)}, u32[]{:S(2)}) async-start(bf16[8,3,64,640]{3,2,1,0:T(8,128)(2,1)} %bitcast.195), calls=%async_computation.1 | async-start | bytes 3932160 | tf_op jit(solution)/shard_map/all_to_all | solution.py:434
  97.7 1.9 bitcast_dynamic-update-slice_fusion.4
  99.7 2.9 fusion.40
  108.2 11.1 %shard_map.262 = bf16[8,2,64,256]{3,2,1,0:T(8,128)(2,1)S(1)} custom-call(bf16[8,2,64,256]{3,2,1,0:T(8,128)(2,1)S(1)} %bitcast.188, bf16[8,2,64,256]{3,2,1,0:T(8,128)(2,1)S(1)} %bitcast.186, bf16[8,2,64,256]{3,2,1,0:T(8,128)(2,1)S(1)} %bitcast.184, f32[4,512,512]{2,1,0:T(8,128)S(1)} %copy-done.5, s32[2,512,1]{2,1,0:T(8,128)S(1)} %copy.104.seg_q_ref, ...), custom_call_target="tpu_custom_call" | custom-call | flops 12582912000 | bytes 6291456 | tf_op jit(solution)/shard_map/pallas_call | solution.py:310
  119.4 3.2 convolution_convert_fusion.1
  122.7 47.1 %all-gather.11.cloned.1.call-done = bf16[16,64,2048]{2,1,0:T(8,128)(2,1)} async-done(((bf16[2,64,2048]{2,1,0:T(8,128)(2,1)}), bf16[16,64,2048]{2,1,0:T(8,128)(2,1)}) %all-gather.11.cloned.1.call-update) | async-done | bytes 4194320 | tf_op jit(solution)/shard_map/all_gather | solution.py:464
  169.7 4.1 all-to-all-done.1
  175.5 48.7 %reduce-scatter.5.cloned.1.call-done = bf16[1,2,64,2048]{3,2,1,0:T(8,128)(2,1)} async-done(((bf16[8,2,64,2048]{3,2,1,0:T(8,128)(2,1)}), bf16[1,2,64,2048]{3,2,1,0:T(8,128)(2,1)}) %reduce-scatter.5.cloned.1.call-update) | async-done | bytes 524304 | tf_op jit(solution)/shard_map/reduce_scatter | solution.py:470
  232.6 2.0 copy_dynamic-update-slice_fusion.2
  234.6 2.0 copy_dynamic-update-slice_fusion.1
  236.7 1.9 copy_dynamic-update-slice_fusion
  238.6 13.1 %collective-permute-done.6 = bf16[3,4,64,640]{3,2,0,1:T(8,128)(2,1)S(1)} collective-permute-done((bf16[3,4,64,640]{3,2,0,1:T(8,128)(2,1)S(1)}, bf16[3,4,64,640]{3,2,0,1:T(8,128)(2,1)S(1)}, u32[]{:S(2)}, u32[]{:S(2)}) %collective-permute-start.6) | collective-permute-done | bytes 983072 | tf_op jit(solution)/shard_map/ppermute | solution.py:158
  251.9 2.4 collective-permute-done.7
  254.5 3.2 fusion.39
  259.1 4.9 fusion.47.gi_ref
  264.0 8.7 %all-gather.13.cloned.1.call-done = bf16[16,64,2048]{2,1,0:T(8,128)(2,1)} async-done(((bf16[2,64,2048]{2,1,0:T(8,128)(2,1)}), bf16[16,64,2048]{2,1,0:T(8,128)(2,1)}) %all-gather.13.cloned.1.call-update) | async-done | bytes 4194320 | tf_op jit(solution)/shard_map/all_gather | solution.py:464
  272.7 18.3 %shard_map.263 = (bf16[1024,640]{1,0:T(8,128)(2,1)}, bf16[1024,640]{1,0:T(8,128)(2,1)}, bf16[1024,640]{1,0:T(8,128)(2,1)}, bf16[1024,2048]{1,0:T(8,128)(2,1)}) custom-call(bf16[1024,2048]{1,0:T(8,128)(2,1)} %bitcast.246, f32[1024,640]{1,0:T(8,128)} %fusion.47.gi_ref, bf16[2048,640]{1,0:T(8,128)(2,1)} %bitcast.219, bf16[2048,640]{1,0:T(8,128)(2,1)} %bitcast.218), custom_call_target="tpu_custom_call" | custom-call | flops 10737418240 | bytes 20185088 | tf_op jit(solution)/shard_map/pallas_call | solution.py:133
  292.4 5.9 %convolution_convert_fusion.4 = bf16[2048,640]{1,0:T(8,128)(2,1)S(1)} fusion(bf16[1024,2048]{1,0:T(8,128)(2,1)} %bitcast.247, bf16[1024,640]{1,0:T(8,128)(2,1)S(1)} %copy-done.63), kind=kOutput, calls=%fused_computation.12 | convolution fusion | flops 2685665280 | bytes 8126464 | tf_op jit(solution)/shard_map/dot_general | solution.py:89
  298.3 4.0 convolution_convert_fusion.3
  302.3 3.8 convolution_convert_fusion.2
  316.3 5.0 convolution_convert_fusion
  321.4 18.2 %reduce-scatter.7.cloned.1.call-done = bf16[1,2,64,2048]{3,2,1,0:T(8,128)(2,1)} async-done(((bf16[8,2,64,2048]{3,2,1,0:T(8,128)(2,1)}), bf16[1,2,64,2048]{3,2,1,0:T(8,128)(2,1)}) %reduce-scatter.7.cloned.1.call-update) | async-done | bytes 524304 | tf_op jit(solution)/shard_map/reduce_scatter | solution.py:470
  342.9 1.8 add_convert_fusion.4
  349.2 19.4 %collective-permute-done.11 = bf16[3,4,64,640]{3,2,0,1:T(8,128)(2,1)S(1)} collective-permute-done((bf16[3,4,64,640]{3,2,0,1:T(8,128)(2,1)S(1)}, bf16[3,4,64,640]{3,2,0,1:T(8,128)(2,1)S(1)}, u32[]{:S(2)}, u32[]{:S(2)}) %collective-permute-start.11) | collective-permute-done | bytes 983072 | tf_op jit(solution)/shard_map/ppermute | solution.py:158
  370.0 1.7 add_convert_fusion.3
  371.6 18.5 %collective-permute-done.13 = bf16[3,4,64,640]{3,2,0,1:T(8,128)(2,1)S(1)} collective-permute-done((bf16[3,4,64,640]{3,2,0,1:T(8,128)(2,1)S(1)}, bf16[3,4,64,640]{3,2,0,1:T(8,128)(2,1)S(1)}, u32[]{:S(2)}, u32[]{:S(2)}) %collective-permute-start.13) | collective-permute-done | bytes 983072 | tf_op jit(solution)/shard_map/ppermute | solution.py:158
  392.1 4.9 all-to-all-start.2
  397.1 3.6 convolution_convert_fusion.9
  401.1 12.5 %shard_map.264 = (bf16[8,2,64,256]{3,2,1,0:T(8,128)(2,1)S(1)}, bf16[8,2,64,256]{3,2,1,0:T(8,128)(2,1)S(1)}, bf16[8,2,64,256]{3,2,1,0:T(8,128)(2,1)S(1)}, f32[4,512,512]{2,1,0:T(8,128)S(1)}) custom-call(bf16[8,2,64,256]{3,2,1,0:T(8,128)(2,1)S(1)} %bitcast.189, bf16[8,2,64,256]{3,2,1,0:T(8,128)(2,1)S(1)} %bitcast.187, bf16[8,2,64,256]{3,2,1,0:T(8,128)(2,1)S(1)} %bitcast.185, ...), custom_call_target="tpu_custom_call" | custom-call | flops 16777216000 | bytes 12058624 | tf_op jit(solution)/shard_map/pallas_call | solution.py:352
  417.0 3.4 add_convert_fusion
  420.4 19.4 %all-to-all-done.2.g_ref = bf16[8,3,64,640]{3,2,1,0:T(8,128)(2,1)S(1)} async-done(((bf16[8,3,64,640]{3,2,1,0:T(8,128)(2,1)}), bf16[8,3,64,640]{3,2,1,0:T(8,128)(2,1)S(1)}, u32[]{:S(2)}, u32[]{:S(2)}) %all-to-all-start.2) | async-done | bytes 1966112 | tf_op jit(solution)/shard_map/all_to_all | solution.py:438
  441.0 3.7 convolution_convert_fusion.5
  453.8 9.8 %collective-permute-done.18 = bf16[4,4,64,256]{3,2,0,1:T(8,128)(2,1)S(1)} collective-permute-done((bf16[4,4,64,256]{3,2,0,1:T(8,128)(2,1)S(1)}, bf16[4,4,64,256]{3,2,0,1:T(8,128)(2,1)S(1)}, u32[]{:S(2)}, u32[]{:S(2)}) %collective-permute-start.18) | collective-permute-done | bytes 524320 | tf_op jit(solution)/shard_map/ppermute | solution.py:158
  465.1 9.7 %collective-permute-done.14 = bf16[4,4,64,256]{3,2,0,1:T(8,128)(2,1)S(1)} collective-permute-done((bf16[4,4,64,256]{3,2,0,1:T(8,128)(2,1)S(1)}, bf16[4,4,64,256]{3,2,0,1:T(8,128)(2,1)S(1)}, u32[]{:S(2)}, u32[]{:S(2)}) %collective-permute-start.14) | collective-permute-done | bytes 524320 | tf_op jit(solution)/shard_map/ppermute | solution.py:158
  474.9 11.2 %collective-permute-done.19 = bf16[4,4,64,256]{3,2,0,1:T(8,128)(2,1)S(1)} collective-permute-done((bf16[4,4,64,256]{3,2,0,1:T(8,128)(2,1)S(1)}, bf16[4,4,64,256]{3,2,0,1:T(8,128)(2,1)S(1)}, u32[]{:S(2)}, u32[]{:S(2)}) %collective-permute-start.19) | collective-permute-done | bytes 524320 | tf_op jit(solution)/shard_map/ppermute | solution.py:158
  487.8 7.6 %all-to-all-start.3 = ((bf16[8,4,64,256]{3,2,1,0:T(8,128)(2,1)}), bf16[8,4,64,256]{3,2,1,0:T(8,128)(2,1)S(1)}, u32[]{:S(2)}, u32[]{:S(2)}) async-start(bf16[8,4,64,256]{3,2,1,0:T(8,128)(2,1)} %maximum_bitcast_fusion), calls=%async_computation.7 | async-start | bytes 2097152 | tf_op jit(solution)/shard_map/all_to_all | solution.py:438
  495.4 2.5 convert_element_type.301
  497.9 6.4 %fusion.9 = f32[32,4]{1,0:T(8,128)S(1)} fusion(bf16[4,512,512]{2,1,0:T(8,128)(2,1)S(1)} %convert_element_type.301, s32[512,512]{1,0:T(8,128)} %copy-done.38), kind=kOutput, calls=%fused_computation.43 | convolution fusion | flops 75497472 | bytes 3146240 | tf_op jit(solution)/shard_map/hij,zij->zh/dot_general | solution.py:570
  504.7 2.1 copy-done
  508.3 2.1 copy-done.7
  510.5 2.1 copy-done.8
  512.6 6.5 %shard_map.266 = (f32[3,64,5120]{2,1,0:T(8,128)}, f32[3,64,5120]{2,1,0:T(8,128)}, f32[3,64,5120]{2,1,0:T(8,128)}) custom-call(f32[3,64,5120]{2,1,0:T(8,128)S(1)} %bitcast.173, f32[3,64,5120]{2,1,0:T(8,128)S(1)} %bitcast.174, f32[3,64,5120]{2,1,0:T(8,128)S(1)} %bitcast.175, bf16[8,3,64,640]{3,2,1,0:T(8,128)(2,1)S(1)} %copy-done.3), custom_call_target="tpu_custom_call" | custom-call | flops 19660800 | bytes 25559040 | tf_op jit(solution)/shard_map/pallas_call | solution.py:260
  519.1 1.7 fusion.18
  522.1 7.6 %collective-permute-done.21 = f32[40,128]{1,0:T(8,128)S(1)} collective-permute-done((f32[40,128]{1,0:T(8,128)S(1)}, f32[40,128]{1,0:T(8,128)S(1)}, u32[]{:S(2)}, u32[]{:S(2)}) %collective-permute-start.21) | collective-permute-done | bytes 20512 | tf_op jit(solution)/shard_map/ppermute | solution.py:158
  530.0 4.0 all-to-all-done.3.g_ref
  534.0 1.6 copy-done.9
  535.6 1.6 copy-done.10
  537.2 7.8 %shard_map.265 = (f32[64,4,2048]{2,1,0:T(4,128)}, f32[64,4,2048]{2,1,0:T(4,128)}, f32[3,64,2048]{2,1,0:T(8,128)}, f32[64,2048]{1,0:T(8,128)}) custom-call(f32[64,4,2048]{2,1,0:T(4,128)S(1)} %copy-done.1, f32[64,4,2048]{2,1,0:T(4,128)S(1)} %copy-done.9, f32[64,4,2048]{2,1,0:T(4,128)S(1)} %copy-done.10, bf16[8,4,64,256]{3,2,1,0:T(8,128)(2,1)S(1)} %all-to-all-done.3.g_ref), custom_call_target="tpu_custom_call" | custom-call | flops 10485760 | bytes 13631488 | tf_op jit(solution)/shard_map/pallas_call | solution.py:212
  545.5 2.7 collective-permute-done.23
  549.4 13.0 %reduce-scatter.11.cloned.1.call-done = bf16[1,2,64,2048]{3,2,1,0:T(8,128)(2,1)} async-done(((bf16[8,2,64,2048]{3,2,1,0:T(8,128)(2,1)}), bf16[1,2,64,2048]{3,2,1,0:T(8,128)(2,1)}) %reduce-scatter.11.cloned.1.call-update) | async-done | bytes 524304 | tf_op jit(solution)/shard_map/reduce_scatter | solution.py:470
  562.5 3.7 fusion.17
  (255 shorter events, 75.2 us)
Async XLA Ops:
  9.2 8.4 %copy-start.41 = (f32[2,2048]{1,0:T(2,128)S(1)}, f32[2,2048]{1,0:T(2,128)}, u32[]{:S(2)}) copy-start(f32[2,2048]{1,0:T(2,128)} %param.24) | copy-start | bytes 49156
  9.2 8.5 %copy-start.23 = (bf16[2,64,2048]{2,1,0:T(8,128)(2,1)S(1)}, bf16[2,64,2048]{2,1,0:T(8,128)(2,1)}, u32[]{:S(2)}) copy-start(bf16[2,64,2048]{2,1,0:T(8,128)(2,1)} %param.15) | copy-start | bytes 1572868
  9.3 8.7 %copy-start.47 = (f32[32,32]{1,0:T(8,128)S(1)}, f32[32,32]{1,0:T(8,128)}, u32[]{:S(2)}) copy-start(f32[32,32]{1,0:T(8,128)} %param.27) | copy-start | bytes 12292
  11.6 28.7 %all-to-all-start = ((bf16[8,4,64,256]{3,2,1,0:T(8,128)(2,1)}), bf16[8,4,64,256]{3,2,1,0:T(8,128)(2,1)S(1)}, u32[]{:S(2)}, u32[]{:S(2)}) async-start(bf16[8,4,64,256]{3,2,1,0:T(8,128)(2,1)} %copy.96), calls=%async_computation | async-start | bytes 2097152 | tf_op jit(solution)/shard_map/all_to_all | solution.py:434
  17.2 71.0 %all-gather.9.cloned.1.call-start = ((), (), s32[]{:S(2)}) async-start(), calls=%async_computation.12 | async-start | bytes 4718592 | tf_op jit(solution)/shard_map/all_gather | solution.py:464
  17.7 12.1 %copy-start.38 = (s32[512,512]{1,0:T(8,128)}, s32[512,512]{1,0:T(8,128)S(1)}, u32[]{:S(2)}) copy-start(s32[512,512]{1,0:T(8,128)S(1)} %fusion.20) | copy-start | bytes 3145732
  17.7 12.0 %copy-start.39 = (f32[1,2048]{1,0:T(1,128)}, f32[1,2048]{1,0:T(1,128)S(1)}, u32[]{:S(2)}) copy-start(f32[1,2048]{1,0:T(1,128)S(1)} %get-tuple-element.159) | copy-start | bytes 24580
  29.7 10.7 %copy-start.51 = (f32[2,64]{1,0:T(2,128)}, f32[2,64]{1,0:T(2,128)S(1)}, u32[]{:S(2)}) copy-start(f32[2,64]{1,0:T(2,128)S(1)} %add_rsqrt_fusion.1) | copy-start | bytes 1540
  30.7 35.2 %copy-start.44 = (s32[2,512]{1,0:T(2,128)S(1)}, s32[2,512]{1,0:T(2,128)}, u32[]{:S(2)}) copy-start(s32[2,512]{1,0:T(2,128)} %param.16) | copy-start | bytes 12292
  40.4 129.3 %all-gather.11.cloned.1.call-start = ((), (), s32[]{:S(2)}) async-start(), calls=%async_computation.13 | async-start | bytes 4718592 | tf_op jit(solution)/shard_map/all_gather | solution.py:464
  40.5 24.5 %collective-permute-start = (bf16[4,8,64,256]{3,2,1,0:T(8,128)(2,1)S(1)}, bf16[4,8,64,256]{3,2,1,0:T(8,128)(2,1)S(1)}, u32[]{:S(2)}, u32[]{:S(2)}) collective-permute-start(bf16[4,8,64,256]{3,2,1,0:T(8,128)(2,1)S(1)} %bitcast.196), channel_id=1, source_target_pairs={{0,1},{1,0},{2,3},{3,2},{4,5},{5,4},{6,7},{7,6},{8,9},{9,8},{10,11... | collective-permute-start | bytes 3145736 | tf_op jit(solution)/shard_map/ppermute | solution.py:158
  40.8 25.1 %collective-permute-start.1 = (bf16[4,8,64,256]{3,2,1,0:T(8,128)(2,1)S(1)}, bf16[4,8,64,256]{3,2,1,0:T(8,128)(2,1)}, u32[]{:S(2)}, u32[]{:S(2)}) collective-permute-start(bf16[4,8,64,256]{3,2,1,0:T(8,128)(2,1)S(1)} %bitcast.197), channel_id=1, source_target_pairs={{0,2},{1,3},{2,0},{3,1},{4,6},{5,7},{6,4},{7,5},{8,10},{9,11},{10,... | collective-permute-start | bytes 3145736 | tf_op jit(solution)/shard_map/ppermute | solution.py:158
  66.2 40.8 %copy-start.13 = (s32[2,512,1]{2,1,0:T(8,128)}, s32[2,512,1]{2,1,0:T(8,128)S(1)}, u32[]{:S(2)}) copy-start(s32[2,512,1]{2,1,0:T(8,128)S(1)} %copy.104.seg_q_ref) | copy-start | bytes 12292
  72.2 12.5 %collective-permute-start.2 = (bf16[4,4,64,256]{3,2,1,0:T(8,128)(2,1)S(1)}, bf16[4,4,64,256]{3,2,1,0:T(8,128)(2,1)S(1)}, u32[]{:S(2)}, u32[]{:S(2)}) collective-permute-start(bf16[4,4,64,256]{3,2,1,0:T(8,128)(2,1)S(1)} %slice.108), channel_id=1, source_target_pairs={{0,2},{1,3},{2,0},{3,1},{4,6},{5,7},{6,4},{7,5},{8,10},{9,11},{10,... | collective-permute-start | bytes 1572872 | tf_op jit(solution)/shard_map/ppermute | solution.py:158
  74.6 23.1 %collective-permute-start.3 = (bf16[4,4,64,256]{3,2,1,0:T(8,128)(2,1)S(1)}, bf16[4,4,64,256]{3,2,1,0:T(8,128)(2,1)}, u32[]{:S(2)}, u32[]{:S(2)}) collective-permute-start(bf16[4,4,64,256]{3,2,1,0:T(8,128)(2,1)S(1)} %slice.109), channel_id=1, source_target_pairs={{0,1},{1,0},{2,3},{3,2},{4,5},{5,4},{6,7},{7,6},{8,9},{9,8},{10,11... | collective-permute-start | bytes 1572872 | tf_op jit(solution)/shard_map/ppermute | solution.py:158
  91.3 82.6 %all-to-all-start.1 = ((bf16[8,3,64,640]{3,2,1,0:T(8,128)(2,1)}), bf16[8,3,64,640]{3,2,1,0:T(8,128)(2,1)}, u32[]{:S(2)}, u32[]{:S(2)}) async-start(bf16[8,3,64,640]{3,2,1,0:T(8,128)(2,1)} %bitcast.195), calls=%async_computation.1 | async-start | bytes 3932160 | tf_op jit(solution)/shard_map/all_to_all | solution.py:434
  97.5 126.7 %reduce-scatter.5.cloned.1.call-start = ((), (), s32[]{:S(2)}) async-start(), calls=%async_computation.8 | async-start | bytes 4718592 | tf_op jit(solution)/shard_map/reduce_scatter | solution.py:470
  102.6 16.8 %copy-start.31 = (bf16[1,8,4,64,256]{4,3,2,1,0:T(8,128)(2,1)}, bf16[1,8,4,64,256]{4,3,2,1,0:T(8,128)(2,1)S(1)}, u32[]{:S(2)}) copy-start(bf16[1,8,4,64,256]{4,3,2,1,0:T(8,128)(2,1)S(1)} %get-tuple-element.140) | copy-start | bytes 3145732
  105.6 13.7 %copy-start.17 = (bf16[1024,256]{1,0:T(8,128)(2,1)}, bf16[1024,256]{1,0:T(8,128)(2,1)S(1)}, u32[]{:S(2)}) copy-start(bf16[1024,256]{1,0:T(8,128)(2,1)S(1)} %convolution_convert_fusion.11) | copy-start | bytes 1572868
  106.9 12.5 %copy-start.19 = (bf16[1024,256]{1,0:T(8,128)(2,1)}, bf16[1024,256]{1,0:T(8,128)(2,1)S(1)}, u32[]{:S(2)}) copy-start(bf16[1024,256]{1,0:T(8,128)(2,1)S(1)} %convolution_convert_fusion.12) | copy-start | bytes 1572868
  173.9 98.8 %all-gather.13.cloned.1.call-start = ((), (), s32[]{:S(2)}) async-start(), calls=%async_computation.14 | async-start | bytes 4718592 | tf_op jit(solution)/shard_map/all_gather | solution.py:464
  174.0 51.4 %collective-permute-start.4 = (bf16[3,8,64,640]{3,2,0,1:T(8,128)(2,1)}, bf16[3,8,64,640]{3,2,0,1:T(8,128)(2,1)}, u32[]{:S(2)}, u32[]{:S(2)}) collective-permute-start(bf16[3,8,64,640]{3,2,0,1:T(8,128)(2,1)} %bitcast.28), channel_id=1, source_target_pairs={{0,1},{1,0},{2,3},{3,2},{4,5},{5,4},{6,7},{7,6},{8,9},{9,8},{10,11... | collective-permute-start | bytes 5898248 | tf_op jit(solution)/shard_map/ppermute | solution.py:158
  174.3 51.1 %collective-permute-start.5 = (bf16[3,8,64,640]{3,2,0,1:T(8,128)(2,1)}, bf16[3,8,64,640]{3,2,0,1:T(8,128)(2,1)}, u32[]{:S(2)}, u32[]{:S(2)}) collective-permute-start(bf16[3,8,64,640]{3,2,0,1:T(8,128)(2,1)} %bitcast.28), channel_id=1, source_target_pairs={{0,2},{1,3},{2,0},{3,1},{4,6},{5,7},{6,4},{7,5},{8,10},{9,11},{10,... | collective-permute-start | bytes 5898248 | tf_op jit(solution)/shard_map/ppermute | solution.py:158
  225.6 116.1 %copy-start.21 = (f32[2,64,2048]{2,1,0:T(8,128)}, f32[2,64,2048]{2,1,0:T(8,128)S(1)}, u32[]{:S(2)}) copy-start(f32[2,64,2048]{2,1,0:T(8,128)S(1)} %get-tuple-element.128) | copy-start | bytes 3145732
  226.9 112.7 %reduce-scatter.7.cloned.1.call-start = ((), (), s32[]{:S(2)}) async-start(), calls=%async_computation.9 | async-start | bytes 4718592 | tf_op jit(solution)/shard_map/reduce_scatter | solution.py:470
  228.6 23.1 %collective-permute-start.6 = (bf16[3,4,64,640]{3,2,0,1:T(8,128)(2,1)S(1)}, bf16[3,4,64,640]{3,2,0,1:T(8,128)(2,1)S(1)}, u32[]{:S(2)}, u32[]{:S(2)}) collective-permute-start(bf16[3,4,64,640]{3,2,0,1:T(8,128)(2,1)S(1)} %slice.115), channel_id=1, source_target_pairs={{0,2},{1,3},{2,0},{3,1},{4,6},{5,7},{6,4},{7,5},{8,10},{9,11},{10,... | collective-permute-start | bytes 2949128 | tf_op jit(solution)/shard_map/ppermute | solution.py:158
  231.1 23.2 %collective-permute-start.7 = (bf16[3,4,64,640]{3,2,0,1:T(8,128)(2,1)S(1)}, bf16[3,4,64,640]{3,2,0,1:T(8,128)(2,1)S(1)}, u32[]{:S(2)}, u32[]{:S(2)}) collective-permute-start(bf16[3,4,64,640]{3,2,0,1:T(8,128)(2,1)S(1)} %slice.116), channel_id=1, source_target_pairs={{0,1},{1,0},{2,3},{3,2},{4,5},{5,4},{6,7},{7,6},{8,9},{9,8},{10,11... | collective-permute-start | bytes 2949128 | tf_op jit(solution)/shard_map/ppermute | solution.py:158
  291.1 101.0 %all-gather.15.cloned.1.call-start = ((), (), s32[]{:S(2)}) async-start(), calls=%async_computation.15 | async-start | bytes 4718592 | tf_op jit(solution)/shard_map/all_gather | solution.py:464
  309.9 30.8 %collective-permute-start.8 = (bf16[3,4,64,640]{3,2,0,1:T(8,128)(2,1)}, bf16[3,4,64,640]{3,2,0,1:T(8,128)(2,1)}, u32[]{:S(2)}, u32[]{:S(2)}) collective-permute-start(bf16[3,4,64,640]{3,2,0,1:T(8,128)(2,1)} %get-tuple-element.145), channel_id=1, source_target_pairs={{0,1},{1,0},{2,3},{3,2},{4,5},{5,4},{6,7},{7,6},{8,9},{9,8},{10,11... | collective-permute-start | bytes 2949128 | tf_op jit(solution)/shard_map/ppermute | solution.py:158
  310.2 30.5 %collective-permute-start.9 = (bf16[3,4,64,640]{3,2,0,1:T(8,128)(2,1)}, bf16[3,4,64,640]{3,2,0,1:T(8,128)(2,1)}, u32[]{:S(2)}, u32[]{:S(2)}) collective-permute-start(bf16[3,4,64,640]{3,2,0,1:T(8,128)(2,1)} %get-tuple-element.144), channel_id=1, source_target_pairs={{0,2},{1,3},{2,0},{3,1},{4,6},{5,7},{6,4},{7,5},{8,10},{9,11},{10,... | collective-permute-start | bytes 2949128 | tf_op jit(solution)/shard_map/ppermute | solution.py:158
  321.4 20.3 %copy-start.24 = (bf16[2,64,2048]{2,1,0:T(8,128)(2,1)S(1)}, bf16[2,64,2048]{2,1,0:T(8,128)(2,1)}, u32[]{:S(2)}) copy-start(bf16[2,64,2048]{2,1,0:T(8,128)(2,1)} %param.17) | copy-start | bytes 1572868
  344.7 45.5 %copy-start.33 = (bf16[3,4,64,640]{3,2,0,1:T(8,128)(2,1)S(1)}, bf16[3,4,64,640]{3,2,0,1:T(8,128)(2,1)}, u32[]{:S(2)}) copy-start(bf16[3,4,64,640]{3,2,0,1:T(8,128)(2,1)} %get-tuple-element.93) | copy-start | bytes 2949124
  344.7 23.9 %collective-permute-start.11 = (bf16[3,4,64,640]{3,2,0,1:T(8,128)(2,1)S(1)}, bf16[3,4,64,640]{3,2,0,1:T(8,128)(2,1)S(1)}, u32[]{:S(2)}, u32[]{:S(2)}) collective-permute-start(bf16[3,4,64,640]{3,2,0,1:T(8,128)(2,1)S(1)} %add_convert_fusion.4), channel_id=1, source_target_pairs={{0,2},{1,3},{2,0},{3,1},{4,6},{5,7},{6,4},{7,5},{8,10},{9,11},{10,... | collective-permute-start | bytes 2949128 | tf_op jit(solution)/shard_map/ppermute | solution.py:158
  345.9 24.0 %collective-permute-start.10 = (bf16[3,4,64,640]{3,2,0,1:T(8,128)(2,1)}, bf16[3,4,64,640]{3,2,0,1:T(8,128)(2,1)S(1)}, u32[]{:S(2)}, u32[]{:S(2)}) collective-permute-start(bf16[3,4,64,640]{3,2,0,1:T(8,128)(2,1)} %get-tuple-element.90), channel_id=1, source_target_pairs={{0,1},{1,0},{2,3},{3,2},{4,5},{5,4},{6,7},{7,6},{8,9},{9,8},{10,11... | collective-permute-start | bytes 2949128 | tf_op jit(solution)/shard_map/ppermute | solution.py:158
  347.7 42.5 %collective-permute-start.13 = (bf16[3,4,64,640]{3,2,0,1:T(8,128)(2,1)S(1)}, bf16[3,4,64,640]{3,2,0,1:T(8,128)(2,1)S(1)}, u32[]{:S(2)}, u32[]{:S(2)}) collective-permute-start(bf16[3,4,64,640]{3,2,0,1:T(8,128)(2,1)S(1)} %add_convert_fusion.2), channel_id=1, source_target_pairs={{0,1},{1,0},{2,3},{3,2},{4,5},{5,4},{6,7},{7,6},{8,9},{9,8},{10,11... | collective-permute-start | bytes 2949128 | tf_op jit(solution)/shard_map/ppermute | solution.py:158
  349.0 41.2 %collective-permute-start.12 = (bf16[3,4,64,640]{3,2,0,1:T(8,128)(2,1)}, bf16[3,4,64,640]{3,2,0,1:T(8,128)(2,1)S(1)}, u32[]{:S(2)}, u32[]{:S(2)}) collective-permute-start(bf16[3,4,64,640]{3,2,0,1:T(8,128)(2,1)} %get-tuple-element.94), channel_id=1, source_target_pairs={{0,2},{1,3},{2,0},{3,1},{4,6},{5,7},{6,4},{7,5},{8,10},{9,11},{10,... | collective-permute-start | bytes 2949128 | tf_op jit(solution)/shard_map/ppermute | solution.py:158
  390.6 6.4 %copy-start.32 = (bf16[1,8,4,64,256]{4,3,2,1,0:T(8,128)(2,1)S(1)}, bf16[1,8,4,64,256]{4,3,2,1,0:T(8,128)(2,1)}, u32[]{:S(2)}) copy-start(bf16[1,8,4,64,256]{4,3,2,1,0:T(8,128)(2,1)} %copy-done.31) | copy-start | bytes 3145732
  392.1 47.6 %all-to-all-start.2 = ((bf16[8,3,64,640]{3,2,1,0:T(8,128)(2,1)}), bf16[8,3,64,640]{3,2,1,0:T(8,128)(2,1)S(1)}, u32[]{:S(2)}, u32[]{:S(2)}) async-start(bf16[8,3,64,640]{3,2,1,0:T(8,128)(2,1)} %bitcast.194), calls=%async_computation.4 | async-start | bytes 3932160 | tf_op jit(solution)/shard_map/all_to_all | solution.py:438
  397.1 122.0 %reduce-scatter.9.cloned.1.call-start = ((), (), s32[]{:S(2)}) async-start(), calls=%async_computation.10 | async-start | bytes 4718592 | tf_op jit(solution)/shard_map/reduce_scatter | solution.py:470
  401.1 12.5 %copy-start.30 = (bf16[1,8,4,64,256]{4,3,2,1,0:T(8,128)(2,1)S(1)}, bf16[1,8,4,64,256]{4,3,2,1,0:T(8,128)(2,1)}, u32[]{:S(2)}) copy-start(bf16[1,8,4,64,256]{4,3,2,1,0:T(8,128)(2,1)} %copy-done.29) | copy-start | bytes 3145732
  439.8 122.7 %reduce-scatter.11.cloned.1.call-start = ((), (), s32[]{:S(2)}) async-start(), calls=%async_computation.11 | async-start | bytes 4718592 | tf_op jit(solution)/shard_map/reduce_scatter | solution.py:470
  450.4 13.2 %collective-permute-start.18 = (bf16[4,4,64,256]{3,2,0,1:T(8,128)(2,1)S(1)}, bf16[4,4,64,256]{3,2,0,1:T(8,128)(2,1)S(1)}, u32[]{:S(2)}, u32[]{:S(2)}) collective-permute-start(bf16[4,4,64,256]{3,2,0,1:T(8,128)(2,1)S(1)} %get-tuple-element.155), channel_id=1, source_target_pairs={{0,2},{1,3},{2,0},{3,1},{4,6},{5,7},{6,4},{7,5},{8,10},{9,11},{10,... | collective-permute-start | bytes 1572872 | tf_op jit(solution)/shard_map/ppermute | solution.py:158
  450.8 13.4 %collective-permute-start.15 = (bf16[4,4,64,256]{3,2,0,1:T(8,128)(2,1)S(1)}, bf16[4,4,64,256]{3,2,0,1:T(8,128)(2,1)S(1)}, u32[]{:S(2)}, u32[]{:S(2)}) collective-permute-start(bf16[4,4,64,256]{3,2,0,1:T(8,128)(2,1)S(1)} %get-tuple-element.154), channel_id=1, source_target_pairs={{0,1},{1,0},{2,3},{3,2},{4,5},{5,4},{6,7},{7,6},{8,9},{9,8},{10,11... | collective-permute-start | bytes 1572872 | tf_op jit(solution)/shard_map/ppermute | solution.py:158
  451.3 23.6 %collective-permute-start.14 = (bf16[4,4,64,256]{3,2,0,1:T(8,128)(2,1)S(1)}, bf16[4,4,64,256]{3,2,0,1:T(8,128)(2,1)S(1)}, u32[]{:S(2)}, u32[]{:S(2)}) collective-permute-start(bf16[4,4,64,256]{3,2,0,1:T(8,128)(2,1)S(1)} %slice.154), channel_id=1, source_target_pairs={{0,1},{1,0},{2,3},{3,2},{4,5},{5,4},{6,7},{7,6},{8,9},{9,8},{10,11... | collective-permute-start | bytes 1572872 | tf_op jit(solution)/shard_map/ppermute | solution.py:158
  452.5 22.4 %collective-permute-start.17 = (bf16[4,4,64,256]{3,2,0,1:T(8,128)(2,1)S(1)}, bf16[4,4,64,256]{3,2,0,1:T(8,128)(2,1)S(1)}, u32[]{:S(2)}, u32[]{:S(2)}) collective-permute-start(bf16[4,4,64,256]{3,2,0,1:T(8,128)(2,1)S(1)} %slice.158), channel_id=1, source_target_pairs={{0,2},{1,3},{2,0},{3,1},{4,6},{5,7},{6,4},{7,5},{8,10},{9,11},{10,... | collective-permute-start | bytes 1572872 | tf_op jit(solution)/shard_map/ppermute | solution.py:158
  463.8 22.3 %collective-permute-start.19 = (bf16[4,4,64,256]{3,2,0,1:T(8,128)(2,1)S(1)}, bf16[4,4,64,256]{3,2,0,1:T(8,128)(2,1)S(1)}, u32[]{:S(2)}, u32[]{:S(2)}) collective-permute-start(bf16[4,4,64,256]{3,2,0,1:T(8,128)(2,1)S(1)} %add_convert_fusion.6), channel_id=1, source_target_pairs={{0,1},{1,0},{2,3},{3,2},{4,5},{5,4},{6,7},{7,6},{8,9},{9,8},{10,11... | collective-permute-start | bytes 1572872 | tf_op jit(solution)/shard_map/ppermute | solution.py:158
  464.4 21.8 %collective-permute-start.16 = (bf16[4,4,64,256]{3,2,0,1:T(8,128)(2,1)S(1)}, bf16[4,4,64,256]{3,2,0,1:T(8,128)(2,1)S(1)}, u32[]{:S(2)}, u32[]{:S(2)}) collective-permute-start(bf16[4,4,64,256]{3,2,0,1:T(8,128)(2,1)S(1)} %add_convert_fusion.8), channel_id=1, source_target_pairs={{0,2},{1,3},{2,0},{3,1},{4,6},{5,7},{6,4},{7,5},{8,10},{9,11},{10,... | collective-permute-start | bytes 1572872 | tf_op jit(solution)/shard_map/ppermute | solution.py:158
  487.8 46.2 %all-to-all-start.3 = ((bf16[8,4,64,256]{3,2,1,0:T(8,128)(2,1)}), bf16[8,4,64,256]{3,2,1,0:T(8,128)(2,1)S(1)}, u32[]{:S(2)}, u32[]{:S(2)}) async-start(bf16[8,4,64,256]{3,2,1,0:T(8,128)(2,1)} %maximum_bitcast_fusion), calls=%async_computation.7 | async-start | bytes 2097152 | tf_op jit(solution)/shard_map/all_to_all | solution.py:438
  512.6 6.5 %copy-start.40 = (f32[1,2048]{1,0:T(1,128)S(1)}, f32[1,2048]{1,0:T(1,128)}, u32[]{:S(2)}) copy-start(f32[1,2048]{1,0:T(1,128)} %copy-done.39) | copy-start | bytes 24580
  512.6 6.5 %copy-start.52 = (f32[2,64]{1,0:T(2,128)S(1)}, f32[2,64]{1,0:T(2,128)}, u32[]{:S(2)}) copy-start(f32[2,64]{1,0:T(2,128)} %copy-done.51) | copy-start | bytes 1540
  512.6 8.2 %copy-start.43 = (f32[2048]{0:T(1024)S(1)}, f32[2048]{0:T(1024)}, u32[]{:S(2)}) copy-start(f32[2048]{0:T(1024)} %get-tuple-element.117) | copy-start | bytes 24580
  512.6 21.5 %copy-start.1 = (f32[64,4,2048]{2,1,0:T(4,128)S(1)}, f32[64,4,2048]{2,1,0:T(4,128)}, u32[]{:S(2)}) copy-start(f32[64,4,2048]{2,1,0:T(4,128)} %w_ref.1) | copy-start | bytes 6291460
  520.7 41.7 %copy-start.54 = (f32[2,64]{1,0:T(2,128)S(1)}, f32[2,64]{1,0:T(2,128)}, u32[]{:S(2)}) copy-start(f32[2,64]{1,0:T(2,128)} %copy-done.53) | copy-start | bytes 1540
  520.8 1.3 collective-permute-start.20
  522.1 7.6 %collective-permute-start.21 = (f32[40,128]{1,0:T(8,128)S(1)}, f32[40,128]{1,0:T(8,128)S(1)}, u32[]{:S(2)}, u32[]{:S(2)}) collective-permute-start(f32[40,128]{1,0:T(8,128)S(1)} %bitcast_add_fusion), channel_id=1, source_target_pairs={{0,8},{4,12},{8,0},{12,4},{16,24},{20,28},{24,16},{28,20},{1,9},{5... | collective-permute-start | bytes 61448 | tf_op jit(solution)/shard_map/ppermute | solution.py:158
  529.7 15.4 %collective-permute-start.22 = (f32[40,128]{1,0:T(8,128)S(1)}, f32[40,128]{1,0:T(8,128)S(1)}, u32[]{:S(2)}, u32[]{:S(2)}) collective-permute-start(f32[40,128]{1,0:T(8,128)S(1)} %fusion.84), channel_id=1, source_target_pairs={{0,16},{4,20},{8,24},{12,28},{16,0},{20,4},{24,8},{28,12},{1,17},{... | collective-permute-start | bytes 61448 | tf_op jit(solution)/shard_map/ppermute | solution.py:158
  545.0 21.2 %copy-start.42 = (f32[2,2048]{1,0:T(2,128)S(1)}, f32[2,2048]{1,0:T(2,128)}, u32[]{:S(2)}) copy-start(f32[2,2048]{1,0:T(2,128)} %param.24) | copy-start | bytes 49156
  545.0 21.2 %copy-start.45 = (f32[2,2048]{1,0:T(2,128)S(1)}, f32[2,2048]{1,0:T(2,128)}, u32[]{:S(2)}) copy-start(f32[2,2048]{1,0:T(2,128)} %param.25) | copy-start | bytes 49156
  545.0 21.2 %copy-start.46 = (f32[2,2048]{1,0:T(2,128)S(1)}, f32[2,2048]{1,0:T(2,128)}, u32[]{:S(2)}) copy-start(f32[2,2048]{1,0:T(2,128)} %param.26) | copy-start | bytes 49156
  545.0 21.9 %copy-start.48 = (f32[32,32]{1,0:T(8,128)S(1)}, f32[32,32]{1,0:T(8,128)}, u32[]{:S(2)}) copy-start(f32[32,32]{1,0:T(8,128)} %param.27) | copy-start | bytes 12292
  545.0 21.9 %copy-start.49 = (f32[32,32]{1,0:T(8,128)S(1)}, f32[32,32]{1,0:T(8,128)}, u32[]{:S(2)}) copy-start(f32[32,32]{1,0:T(8,128)} %param.28) | copy-start | bytes 12292
  545.1 21.9 %copy-start.50 = (f32[32,32]{1,0:T(8,128)S(1)}, f32[32,32]{1,0:T(8,128)}, u32[]{:S(2)}) copy-start(f32[32,32]{1,0:T(8,128)} %param.29) | copy-start | bytes 12292
  545.1 3.1 collective-permute-start.23
  548.2 17.9 %collective-permute-start.24 = (f32[40,128]{1,0:T(8,128)S(1)}, f32[40,128]{1,0:T(8,128)S(1)}, u32[]{:S(2)}, u32[]{:S(2)}) collective-permute-start(f32[40,128]{1,0:T(8,128)S(1)} %add.255), channel_id=1, source_target_pairs={{0,2},{1,3},{2,0},{3,1},{4,6},{5,7},{6,4},{7,5},{8,10},{9,11},{10,... | collective-permute-start | bytes 61448 | tf_op jit(solution)/shard_map/ppermute | solution.py:158
  (37 other events, 109.8 us)
Sparse Core Ops, SparseCore 0:
  40.5 47.6 all-gather.8
  89.8 79.9 all-gather.10
  174.0 50.1 reduce-scatter.4
  227.0 45.6 all-gather.12
  291.2 48.3 reduce-scatter.6
  343.0 45.6 all-gather.14
  439.9 49.1 reduce-scatter.8
  491.4 71.0 reduce-scatter.10

commit v7 on v5

--- a/solution.py
+++ b/solution.py
@@ -159,11 +159,11 @@
 
 
 MIB = 1024 * 1024
-ADAM_PARAMS = pltpu.CompilerParams(vmem_limit_bytes=32 * MIB)
+ADAM_PARAMS = pltpu.CompilerParams(vmem_limit_bytes=56 * MIB)
 
 
 def attention_params(length):
-    return pltpu.CompilerParams(vmem_limit_bytes=min(56, length * length // 8192) * MIB)
+    return pltpu.CompilerParams(vmem_limit_bytes=56 * MIB)
 
 
 def adam_values(weight, first, second, grads, rate, decay):

time: 583 us -> 580 us (level)
  local copies, waits for them, and re-layouts: 53.2 us -> 38.2 us
  Pallas kernels: 56.2 us -> 67.6 us
  matrix products: 67.4 us -> 73.4 us
    unnamed x134 -> x96, local copies, waits for them, and re-layouts: 20.9 us -> 4.13 us
  transfers between devices with their start and end apart: 37 -> 37, of which waited for: 24 -> 25; matrix products, arithmetic and copies ran while one was open for 22% -> 23% of each run, Pallas kernels for 7% -> 9%
where the time goes in v7:
time: 580 us; the launch traced here: 570 us
  waiting for transfers between devices  291 us (50%)
  matrix products  73.4 us (13%)
  Pallas kernels  67.6 us (12%)
  starting transfers between devices  53.8 us (9%)
  local copies, waits for them, and re-layouts  38.2 us (7%)
  other arithmetic  30.5 us (5%)
  between operations  15.3 us (3%)
    ppermute x25, waiting for transfers between devices, swap(): return lax.ppermute(value, axis, partner_pairs(axis, offset))  123 us
    reduce_scatter x4, waiting for transfers between devices, scatter_tokens(): lax.psum_scatter(send, 'seq', scatter_dimension=0).astype(jnp.float32)  68 us
    all_gather x4, waiting for transfers between devices, gather_tokens(): full = lax.all_gather(local_rows, 'seq', axis=0)  45.6 us
    ppermute x25, starting transfers between devices, swap(): return lax.ppermute(value, axis, partner_pairs(axis, offset))  34.4 us
    all_to_all x2, waiting for transfers between devices, to_columns(): return lax.all_to_all(send, 'seq', 0, 0).transpose(1, 0, 2, 3)  30.8 us
    all_to_all x2, waiting for transfers between devices, to_rows(): return lax.all_to_all(mine.transpose(1, 0, 2, 3), 'seq', 0, 0)  23 us
    dot_general x7, matrix products, outer_sum(): lax.dot_general(left, right, (((0,), (0,)), ((), ())), preferred_element_...  21.5 us
    pallas_call x1, Pallas kernels, feed_middle(): pl.pallas_call(body, grid=(tokens // block,), in_specs=[rows, units, weig...  18.3 us
  transfers between devices with their start and end apart: 37, of which 25 were waited for; matrix products, arithmetic and copies ran while one was open for 23% of the time, Pallas kernels for 9%

profile of v7, /device:TPU:0, one launch (start us, length us, event | category | flops | bytes accessed | tf_op | source)
XLA Modules:
  0.0 570.2 jit_solution(10953378303845082170)
XLA Ops:
  7.2 2.0 convert_bitcast_fusion
  11.6 6.3 %all-to-all-start = ((bf16[8,4,64,256]{3,2,1,0:T(8,128)(2,1)}), bf16[8,4,64,256]{3,2,1,0:T(8,128)(2,1)S(1)}, u32[]{:S(2)}, u32[]{:S(2)}) async-start(bf16[8,4,64,256]{3,2,1,0:T(8,128)(2,1)} %copy.96), calls=%async_computation | async-start | bytes 2097152 | tf_op jit(solution)/shard_map/all_to_all | solution.py:434
  19.2 25.3 %all-to-all-done = bf16[8,4,64,256]{3,2,1,0:T(8,128)(2,1)S(1)} async-done(((bf16[8,4,64,256]{3,2,1,0:T(8,128)(2,1)}), bf16[8,4,64,256]{3,2,1,0:T(8,128)(2,1)S(1)}, u32[]{:S(2)}, u32[]{:S(2)}) %all-to-all-start) | async-done | bytes 1048608 | tf_op jit(solution)/shard_map/all_to_all | solution.py:434
  44.7 1.6 collective-permute-start
  47.8 21.7 %collective-permute-done = bf16[4,8,64,256]{3,2,1,0:T(8,128)(2,1)S(1)} collective-permute-done((bf16[4,8,64,256]{3,2,1,0:T(8,128)(2,1)S(1)}, bf16[4,8,64,256]{3,2,1,0:T(8,128)(2,1)S(1)}, u32[]{:S(2)}, u32[]{:S(2)}) %collective-permute-start) | collective-permute-done | bytes 1048608 | tf_op jit(solution)/shard_map/ppermute | solution.py:158
  70.8 2.5 bitcast_convert_fusion.3
  73.3 1.6 collective-permute-start.2
  79.3 6.5 %collective-permute-done.2 = bf16[4,4,64,256]{3,2,1,0:T(8,128)(2,1)S(1)} collective-permute-done((bf16[4,4,64,256]{3,2,1,0:T(8,128)(2,1)S(1)}, bf16[4,4,64,256]{3,2,1,0:T(8,128)(2,1)S(1)}, u32[]{:S(2)}, u32[]{:S(2)}) %collective-permute-start.2) | collective-permute-done | bytes 524320 | tf_op jit(solution)/shard_map/ppermute | solution.py:158
  85.9 2.3 collective-permute-done.3
  88.2 1.8 fusion.43
  90.9 4.4 convolution_convert_fusion.7
  95.2 2.0 convolution_convert_fusion.8
  97.3 2.0 convolution_convert_fusion.9
  99.3 1.6 copy.160
  100.9 3.6 all-to-all-start.1
  105.2 10.4 %fusion.1 = f32[4,512,512]{2,0,1:T(4,128)S(1)} fusion(s32[512,512]{1,0:T(8,128)S(1)} %fusion.23, f32[32,32]{1,0:T(8,128)S(1)} %copy-done.31, s32[]{:T(128)S(6)} %select_n.56), kind=kOutput, calls=%fused_computation.2 | convolution fusion | flops 411041792 | bytes 5246980 | tf_op jit(solution)/shard_map/atj,ao->otj/dot_general | solution.py:516
  115.6 3.3 copy.103.bias_ref
  120.6 13.5 %shard_map.262 = bf16[8,2,64,256]{3,2,1,0:T(8,128)(2,1)} custom-call(bf16[8,2,64,256]{3,2,1,0:T(8,128)(2,1)} %bitcast.269, bf16[8,2,64,256]{3,2,1,0:T(8,128)(2,1)} %bitcast.267, bf16[8,2,64,256]{3,2,1,0:T(8,128)(2,1)} %bitcast.265, f32[4,512,512]{2,1,0:T(8,128)} %copy.103.bias_ref, s32[2,512,1]{2,1,0:T(8,128)} %copy.104.seg_q_ref, ...), custom_call_target="tpu_custom_call" | custom-call | flops 12582912000 | bytes 6291456 | tf_op jit(solution)/shard_map/pallas_call | solution.py:310
  134.1 4.4 convolution_convert_fusion.1
  138.5 34.7 %all-gather.11.cloned.1.call-done = bf16[16,64,2048]{2,1,0:T(8,128)(2,1)} async-done(((bf16[2,64,2048]{2,1,0:T(8,128)(2,1)}), bf16[16,64,2048]{2,1,0:T(8,128)(2,1)}) %all-gather.11.cloned.1.call-update) | async-done | bytes 4194320 | tf_op jit(solution)/shard_map/all_gather | solution.py:464
  173.3 5.5 all-to-all-done.1
  181.8 45.8 %reduce-scatter.5.cloned.1.call-done = bf16[1,2,64,2048]{3,2,1,0:T(8,128)(2,1)} async-done(((bf16[8,2,64,2048]{3,2,1,0:T(8,128)(2,1)}), bf16[1,2,64,2048]{3,2,1,0:T(8,128)(2,1)}) %reduce-scatter.5.cloned.1.call-update) | async-done | bytes 524304 | tf_op jit(solution)/shard_map/reduce_scatter | solution.py:470
  237.6 1.9 copy_dynamic-update-slice_fusion.1
  239.5 1.9 copy_dynamic-update-slice_fusion
  241.5 11.7 %collective-permute-done.6 = bf16[3,4,64,640]{3,2,0,1:T(8,128)(2,1)S(1)} collective-permute-done((bf16[3,4,64,640]{3,2,0,1:T(8,128)(2,1)S(1)}, bf16[3,4,64,640]{3,2,0,1:T(8,128)(2,1)S(1)}, u32[]{:S(2)}, u32[]{:S(2)}) %collective-permute-start.6) | collective-permute-done | bytes 983072 | tf_op jit(solution)/shard_map/ppermute | solution.py:158
  253.3 2.4 collective-permute-done.7
  255.8 3.1 fusion.42
  260.5 4.9 fusion.50.gi_ref
  265.4 10.1 %all-gather.13.cloned.1.call-done = bf16[16,64,2048]{2,1,0:T(8,128)(2,1)} async-done(((bf16[2,64,2048]{2,1,0:T(8,128)(2,1)}), bf16[16,64,2048]{2,1,0:T(8,128)(2,1)}) %all-gather.13.cloned.1.call-update) | async-done | bytes 4194320 | tf_op jit(solution)/shard_map/all_gather | solution.py:464
  275.4 18.3 %shard_map.263 = (bf16[1024,640]{1,0:T(8,128)(2,1)}, bf16[1024,640]{1,0:T(8,128)(2,1)}, bf16[1024,640]{1,0:T(8,128)(2,1)}, bf16[1024,2048]{1,0:T(8,128)(2,1)}) custom-call(bf16[1024,2048]{1,0:T(8,128)(2,1)} %bitcast.258, f32[1024,640]{1,0:T(8,128)} %fusion.50.gi_ref, bf16[2048,640]{1,0:T(8,128)(2,1)} %bitcast.226, bf16[2048,640]{1,0:T(8,128)(2,1)} %bitcast.225), custom_call_target="tpu_custom_call" | custom-call | flops 10737418240 | bytes 20185088 | tf_op jit(solution)/shard_map/pallas_call | solution.py:133
  295.0 5.8 %convolution_convert_fusion.4 = bf16[2048,640]{1,0:T(8,128)(2,1)S(1)} fusion(bf16[1024,2048]{1,0:T(8,128)(2,1)} %bitcast.259, bf16[1024,640]{1,0:T(8,128)(2,1)S(1)} %copy-done.45), kind=kOutput, calls=%fused_computation.12 | convolution fusion | flops 2685665280 | bytes 8126464 | tf_op jit(solution)/shard_map/dot_general | solution.py:89
  300.9 4.0 convolution_convert_fusion.3
  305.0 3.8 convolution_convert_fusion.2
  318.8 1.6 fusion.47
  320.8 5.0 convolution_convert_fusion
  325.8 16.8 %reduce-scatter.7.cloned.1.call-done = bf16[1,2,64,2048]{3,2,1,0:T(8,128)(2,1)} async-done(((bf16[8,2,64,2048]{3,2,1,0:T(8,128)(2,1)}), bf16[1,2,64,2048]{3,2,1,0:T(8,128)(2,1)}) %reduce-scatter.7.cloned.1.call-update) | async-done | bytes 524304 | tf_op jit(solution)/shard_map/reduce_scatter | solution.py:470
  345.3 1.9 add_convert_fusion.4
  350.2 1.9 add_convert_fusion.2
  353.2 18.8 %collective-permute-done.11 = bf16[3,4,64,640]{3,2,0,1:T(8,128)(2,1)S(1)} collective-permute-done((bf16[3,4,64,640]{3,2,0,1:T(8,128)(2,1)S(1)}, bf16[3,4,64,640]{3,2,0,1:T(8,128)(2,1)S(1)}, u32[]{:S(2)}, u32[]{:S(2)}) %collective-permute-start.11) | collective-permute-done | bytes 983072 | tf_op jit(solution)/shard_map/ppermute | solution.py:158
  372.0 1.7 collective-permute-done.10
  374.1 17.0 %collective-permute-done.13 = bf16[3,4,64,640]{3,2,0,1:T(8,128)(2,1)S(1)} collective-permute-done((bf16[3,4,64,640]{3,2,0,1:T(8,128)(2,1)S(1)}, bf16[3,4,64,640]{3,2,0,1:T(8,128)(2,1)S(1)}, u32[]{:S(2)}, u32[]{:S(2)}) %collective-permute-start.13) | collective-permute-done | bytes 983072 | tf_op jit(solution)/shard_map/ppermute | solution.py:158
  393.0 4.3 all-to-all-start.2
  397.4 4.5 convolution_convert_fusion.6
  401.9 15.7 %shard_map.264 = (bf16[8,2,64,256]{3,2,1,0:T(8,128)(2,1)}, bf16[8,2,64,256]{3,2,1,0:T(8,128)(2,1)}, bf16[8,2,64,256]{3,2,1,0:T(8,128)(2,1)}, f32[4,512,512]{2,1,0:T(8,128)}) custom-call(bf16[8,2,64,256]{3,2,1,0:T(8,128)(2,1)} %bitcast.270, bf16[8,2,64,256]{3,2,1,0:T(8,128)(2,1)} %bitcast.268, bf16[8,2,64,256]{3,2,1,0:T(8,128)(2,1)} %bitcast.266, ...), custom_call_target="tpu_custom_call" | custom-call | flops 16777216000 | bytes 12058624 | tf_op jit(solution)/shard_map/pallas_call | solution.py:352
  417.7 2.4 fusion.52
  421.5 3.4 add_convert_fusion
  424.9 18.8 %all-to-all-done.2.g_ref = bf16[8,3,64,640]{3,2,1,0:T(8,128)(2,1)} async-done(((bf16[8,3,64,640]{3,2,1,0:T(8,128)(2,1)}), bf16[8,3,64,640]{3,2,1,0:T(8,128)(2,1)}, u32[]{:S(2)}, u32[]{:S(2)}) %all-to-all-start.2) | async-done | bytes 1966112 | tf_op jit(solution)/shard_map/all_to_all | solution.py:438
  444.7 3.7 convolution_convert_fusion.5
  457.1 1.8 collective-permute-start.17
  458.9 10.4 %collective-permute-done.18 = bf16[4,4,64,256]{3,2,0,1:T(8,128)(2,1)S(1)} collective-permute-done((bf16[4,4,64,256]{3,2,0,1:T(8,128)(2,1)S(1)}, bf16[4,4,64,256]{3,2,0,1:T(8,128)(2,1)S(1)}, u32[]{:S(2)}, u32[]{:S(2)}) %collective-permute-start.18) | collective-permute-done | bytes 524320 | tf_op jit(solution)/shard_map/ppermute | solution.py:158
  471.6 9.2 %collective-permute-done.14 = bf16[4,4,64,256]{3,2,0,1:T(8,128)(2,1)S(1)} collective-permute-done((bf16[4,4,64,256]{3,2,0,1:T(8,128)(2,1)S(1)}, bf16[4,4,64,256]{3,2,0,1:T(8,128)(2,1)S(1)}, u32[]{:S(2)}, u32[]{:S(2)}) %collective-permute-start.14) | collective-permute-done | bytes 524320 | tf_op jit(solution)/shard_map/ppermute | solution.py:158
  480.8 9.5 %collective-permute-done.19 = bf16[4,4,64,256]{3,2,0,1:T(8,128)(2,1)S(1)} collective-permute-done((bf16[4,4,64,256]{3,2,0,1:T(8,128)(2,1)S(1)}, bf16[4,4,64,256]{3,2,0,1:T(8,128)(2,1)S(1)}, u32[]{:S(2)}, u32[]{:S(2)}) %collective-permute-start.19) | collective-permute-done | bytes 524320 | tf_op jit(solution)/shard_map/ppermute | solution.py:158
  492.0 4.2 all-to-all-start.3
  496.3 4.1 convert_element_type.301
  500.3 7.0 %fusion.12 = f32[32,4]{1,0:T(8,128)S(1)} fusion(bf16[4,512,512]{2,1,0:T(8,128)(2,1)} %convert_element_type.301, s32[512,512]{1,0:T(8,128)} %copy-done.17), kind=kOutput, calls=%fused_computation.46 | convolution fusion | flops 75497472 | bytes 3146240 | tf_op jit(solution)/shard_map/hij,zij->zh/dot_general | solution.py:571
  507.7 11.4 %shard_map.266 = (f32[3,64,5120]{2,1,0:T(8,128)}, f32[3,64,5120]{2,1,0:T(8,128)}, f32[3,64,5120]{2,1,0:T(8,128)}) custom-call(f32[3,64,5120]{2,1,0:T(8,128)} %bitcast.194, f32[3,64,5120]{2,1,0:T(8,128)} %bitcast.221, f32[3,64,5120]{2,1,0:T(8,128)} %bitcast.222, bf16[8,3,64,640]{3,2,1,0:T(8,128)(2,1)} %all-to-all-done.2.g_ref), custom_call_target="tpu_custom_call" | custom-call | flops 19660800 | bytes 25559040 | tf_op jit(solution)/shard_map/pallas_call | solution.py:260
  522.0 1.8 collective-permute-start.21
  523.9 7.6 %collective-permute-done.21 = f32[40,128]{1,0:T(8,128)S(1)} collective-permute-done((f32[40,128]{1,0:T(8,128)S(1)}, f32[40,128]{1,0:T(8,128)S(1)}, u32[]{:S(2)}, u32[]{:S(2)}) %collective-permute-start.21) | collective-permute-done | bytes 20512 | tf_op jit(solution)/shard_map/ppermute | solution.py:158
  531.4 3.8 collective-permute-start.22
  535.3 4.2 all-to-all-done.3.g_ref
  539.5 8.7 %shard_map.265 = (f32[64,4,2048]{2,1,0:T(4,128)}, f32[64,4,2048]{2,1,0:T(4,128)}, f32[3,64,2048]{2,1,0:T(8,128)}, f32[64,2048]{1,0:T(8,128)}) custom-call(f32[64,4,2048]{2,1,0:T(4,128)} %w_ref.1, f32[64,4,2048]{2,1,0:T(4,128)} %m_ref.1, f32[64,4,2048]{2,1,0:T(4,128)} %v_ref.1, bf16[8,4,64,256]{3,2,1,0:T(8,128)(2,1)} %all-to-all-done.3.g_ref), custom_call_target="tpu_custom_call" | custom-call | flops 10485760 | bytes 13631488 | tf_op jit(solution)/shard_map/pallas_call | solution.py:212
  549.9 2.3 collective-permute-done.23
  553.7 5.4 reduce-scatter.11.cloned.1.call-done
  559.1 2.7 fusion.20
  (219 shorter events, 72.3 us)
Async XLA Ops:
  9.2 8.7 %copy-start = (bf16[2,64,2048]{2,1,0:T(8,128)(2,1)S(1)}, bf16[2,64,2048]{2,1,0:T(8,128)(2,1)}, u32[]{:S(2)}) copy-start(bf16[2,64,2048]{2,1,0:T(8,128)(2,1)} %param.15) | copy-start | bytes 1572868
  9.2 8.9 %copy-start.26 = (f32[2,2048]{1,0:T(2,128)S(1)}, f32[2,2048]{1,0:T(2,128)}, u32[]{:S(2)}) copy-start(f32[2,2048]{1,0:T(2,128)} %param.24) | copy-start | bytes 49156
  11.6 32.9 %all-to-all-start = ((bf16[8,4,64,256]{3,2,1,0:T(8,128)(2,1)}), bf16[8,4,64,256]{3,2,1,0:T(8,128)(2,1)S(1)}, u32[]{:S(2)}, u32[]{:S(2)}) async-start(bf16[8,4,64,256]{3,2,1,0:T(8,128)(2,1)} %copy.96), calls=%async_computation | async-start | bytes 2097152 | tf_op jit(solution)/shard_map/all_to_all | solution.py:434
  17.9 72.9 %all-gather.9.cloned.1.call-start = ((), (), s32[]{:S(2)}) async-start(), calls=%async_computation.12 | async-start | bytes 4718592 | tf_op jit(solution)/shard_map/all_gather | solution.py:464
  18.2 52.6 %copy-start.35 = (f32[2,64]{1,0:T(2,128)}, f32[2,64]{1,0:T(2,128)S(1)}, u32[]{:S(2)}) copy-start(f32[2,64]{1,0:T(2,128)S(1)} %add_rsqrt_fusion.1) | copy-start | bytes 1540
  18.2 52.6 %copy-start.24 = (f32[1,2048]{1,0:T(1,128)}, f32[1,2048]{1,0:T(1,128)S(1)}, u32[]{:S(2)}) copy-start(f32[1,2048]{1,0:T(1,128)S(1)} %get-tuple-element.159) | copy-start | bytes 24580
  44.6 128.6 %all-gather.11.cloned.1.call-start = ((), (), s32[]{:S(2)}) async-start(), calls=%async_computation.13 | async-start | bytes 4718592 | tf_op jit(solution)/shard_map/all_gather | solution.py:464
  44.7 24.8 %collective-permute-start = (bf16[4,8,64,256]{3,2,1,0:T(8,128)(2,1)S(1)}, bf16[4,8,64,256]{3,2,1,0:T(8,128)(2,1)S(1)}, u32[]{:S(2)}, u32[]{:S(2)}) collective-permute-start(bf16[4,8,64,256]{3,2,1,0:T(8,128)(2,1)S(1)} %bitcast.201), channel_id=1, source_target_pairs={{0,1},{1,0},{2,3},{3,2},{4,5},{5,4},{6,7},{7,6},{8,9},{9,8},{10,11... | collective-permute-start | bytes 3145736 | tf_op jit(solution)/shard_map/ppermute | solution.py:158
  46.2 24.5 %collective-permute-start.1 = (bf16[4,8,64,256]{3,2,1,0:T(8,128)(2,1)S(1)}, bf16[4,8,64,256]{3,2,1,0:T(8,128)(2,1)}, u32[]{:S(2)}, u32[]{:S(2)}) collective-permute-start(bf16[4,8,64,256]{3,2,1,0:T(8,128)(2,1)S(1)} %bitcast.202), channel_id=1, source_target_pairs={{0,2},{1,3},{2,0},{3,1},{4,6},{5,7},{6,4},{7,5},{8,10},{9,11},{10,... | collective-permute-start | bytes 3145736 | tf_op jit(solution)/shard_map/ppermute | solution.py:158
  73.3 12.4 %collective-permute-start.2 = (bf16[4,4,64,256]{3,2,1,0:T(8,128)(2,1)S(1)}, bf16[4,4,64,256]{3,2,1,0:T(8,128)(2,1)S(1)}, u32[]{:S(2)}, u32[]{:S(2)}) collective-permute-start(bf16[4,4,64,256]{3,2,1,0:T(8,128)(2,1)S(1)} %slice.108), channel_id=1, source_target_pairs={{0,2},{1,3},{2,0},{3,1},{4,6},{5,7},{6,4},{7,5},{8,10},{9,11},{10,... | collective-permute-start | bytes 1572872 | tf_op jit(solution)/shard_map/ppermute | solution.py:158
  76.0 12.2 %collective-permute-start.3 = (bf16[4,4,64,256]{3,2,1,0:T(8,128)(2,1)S(1)}, bf16[4,4,64,256]{3,2,1,0:T(8,128)(2,1)S(1)}, u32[]{:S(2)}, u32[]{:S(2)}) collective-permute-start(bf16[4,4,64,256]{3,2,1,0:T(8,128)(2,1)S(1)} %slice.109), channel_id=1, source_target_pairs={{0,1},{1,0},{2,3},{3,2},{4,5},{5,4},{6,7},{7,6},{8,9},{9,8},{10,11... | collective-permute-start | bytes 1572872 | tf_op jit(solution)/shard_map/ppermute | solution.py:158
  90.1 7.2 %copy-start.3 = (bf16[1,8,4,64,256]{4,3,2,1,0:T(8,128)(2,1)}, bf16[1,8,4,64,256]{4,3,2,1,0:T(8,128)(2,1)S(1)}, u32[]{:S(2)}) copy-start(bf16[1,8,4,64,256]{4,3,2,1,0:T(8,128)(2,1)S(1)} %get-tuple-element.141) | copy-start | bytes 3145732
  90.9 4.4 copy-start.7
  90.9 4.4 copy-start.37
  99.3 5.8 %copy-start.31 = (f32[32,32]{1,0:T(8,128)S(1)}, f32[32,32]{1,0:T(8,128)}, u32[]{:S(2)}) copy-start(f32[32,32]{1,0:T(8,128)} %param.27) | copy-start | bytes 12292
  100.9 77.8 %all-to-all-start.1 = ((bf16[8,3,64,640]{3,2,1,0:T(8,128)(2,1)}), bf16[8,3,64,640]{3,2,1,0:T(8,128)(2,1)S(1)}, u32[]{:S(2)}, u32[]{:S(2)}) async-start(bf16[8,3,64,640]{3,2,1,0:T(8,128)(2,1)} %bitcast.199), calls=%async_computation.1 | async-start | bytes 3932160 | tf_op jit(solution)/shard_map/all_to_all | solution.py:434
  104.5 123.1 %reduce-scatter.5.cloned.1.call-start = ((), (), s32[]{:S(2)}) async-start(), calls=%async_computation.8 | async-start | bytes 4718592 | tf_op jit(solution)/shard_map/reduce_scatter | solution.py:470
  105.2 10.4 %copy-start.17 = (s32[512,512]{1,0:T(8,128)}, s32[512,512]{1,0:T(8,128)S(1)}, u32[]{:S(2)}) copy-start(s32[512,512]{1,0:T(8,128)S(1)} %fusion.23) | copy-start | bytes 3145732
  120.6 13.5 %copy-start.9 = (bf16[1,8,4,64,256]{4,3,2,1,0:T(8,128)(2,1)S(1)}, bf16[1,8,4,64,256]{4,3,2,1,0:T(8,128)(2,1)}, u32[]{:S(2)}) copy-start(bf16[1,8,4,64,256]{4,3,2,1,0:T(8,128)(2,1)} %get-tuple-element.140) | copy-start | bytes 3145732
  178.7 96.7 %all-gather.13.cloned.1.call-start = ((), (), s32[]{:S(2)}) async-start(), calls=%async_computation.14 | async-start | bytes 4718592 | tf_op jit(solution)/shard_map/all_gather | solution.py:464
  178.8 49.9 %collective-permute-start.4 = (bf16[3,8,64,640]{3,2,0,1:T(8,128)(2,1)S(1)}, bf16[3,8,64,640]{3,2,0,1:T(8,128)(2,1)}, u32[]{:S(2)}, u32[]{:S(2)}) collective-permute-start(bf16[3,8,64,640]{3,2,0,1:T(8,128)(2,1)S(1)} %bitcast.195), channel_id=1, source_target_pairs={{0,1},{1,0},{2,3},{3,2},{4,5},{5,4},{6,7},{7,6},{8,9},{9,8},{10,11... | collective-permute-start | bytes 5898248 | tf_op jit(solution)/shard_map/ppermute | solution.py:158
  180.3 48.4 %collective-permute-start.5 = (bf16[3,8,64,640]{3,2,0,1:T(8,128)(2,1)S(1)}, bf16[3,8,64,640]{3,2,0,1:T(8,128)(2,1)}, u32[]{:S(2)}, u32[]{:S(2)}) collective-permute-start(bf16[3,8,64,640]{3,2,0,1:T(8,128)(2,1)S(1)} %bitcast.196), channel_id=1, source_target_pairs={{0,2},{1,3},{2,0},{3,1},{4,6},{5,7},{6,4},{7,5},{8,10},{9,11},{10,... | collective-permute-start | bytes 5898248 | tf_op jit(solution)/shard_map/ppermute | solution.py:158
  230.0 112.7 %reduce-scatter.7.cloned.1.call-start = ((), (), s32[]{:S(2)}) async-start(), calls=%async_computation.9 | async-start | bytes 4718592 | tf_op jit(solution)/shard_map/reduce_scatter | solution.py:470
  231.7 21.4 %collective-permute-start.6 = (bf16[3,4,64,640]{3,2,0,1:T(8,128)(2,1)S(1)}, bf16[3,4,64,640]{3,2,0,1:T(8,128)(2,1)S(1)}, u32[]{:S(2)}, u32[]{:S(2)}) collective-permute-start(bf16[3,4,64,640]{3,2,0,1:T(8,128)(2,1)S(1)} %slice.115), channel_id=1, source_target_pairs={{0,2},{1,3},{2,0},{3,1},{4,6},{5,7},{6,4},{7,5},{8,10},{9,11},{10,... | collective-permute-start | bytes 2949128 | tf_op jit(solution)/shard_map/ppermute | solution.py:158
  234.6 21.1 %collective-permute-start.7 = (bf16[3,4,64,640]{3,2,0,1:T(8,128)(2,1)S(1)}, bf16[3,4,64,640]{3,2,0,1:T(8,128)(2,1)S(1)}, u32[]{:S(2)}, u32[]{:S(2)}) collective-permute-start(bf16[3,4,64,640]{3,2,0,1:T(8,128)(2,1)S(1)} %slice.116), channel_id=1, source_target_pairs={{0,1},{1,0},{2,3},{3,2},{4,5},{5,4},{6,7},{7,6},{8,9},{9,8},{10,11... | collective-permute-start | bytes 2949128 | tf_op jit(solution)/shard_map/ppermute | solution.py:158
  255.8 4.6 copy-start.39
  293.7 99.3 %all-gather.15.cloned.1.call-start = ((), (), s32[]{:S(2)}) async-start(), calls=%async_computation.15 | async-start | bytes 4718592 | tf_op jit(solution)/shard_map/all_gather | solution.py:464
  295.0 5.8 %copy-start.41 = (bf16[16,64,2048]{2,1,0:T(8,128)(2,1)S(1)}, bf16[16,64,2048]{2,1,0:T(8,128)(2,1)}, u32[]{:S(2)}) copy-start(bf16[16,64,2048]{2,1,0:T(8,128)(2,1)} %all-gather.13.cloned.1.call-done) | copy-start | bytes 12582916
  295.0 5.9 %copy-start.44 = (bf16[1024,640]{1,0:T(8,128)(2,1)S(1)}, bf16[1024,640]{1,0:T(8,128)(2,1)}, u32[]{:S(2)}) copy-start(bf16[1024,640]{1,0:T(8,128)(2,1)} %get-tuple-element.85) | copy-start | bytes 3932164
  312.6 31.2 %collective-permute-start.8 = (bf16[3,4,64,640]{3,2,0,1:T(8,128)(2,1)}, bf16[3,4,64,640]{3,2,0,1:T(8,128)(2,1)}, u32[]{:S(2)}, u32[]{:S(2)}) collective-permute-start(bf16[3,4,64,640]{3,2,0,1:T(8,128)(2,1)} %get-tuple-element.145), channel_id=1, source_target_pairs={{0,1},{1,0},{2,3},{3,2},{4,5},{5,4},{6,7},{7,6},{8,9},{9,8},{10,11... | collective-permute-start | bytes 2949128 | tf_op jit(solution)/shard_map/ppermute | solution.py:158
  314.0 29.7 %collective-permute-start.9 = (bf16[3,4,64,640]{3,2,0,1:T(8,128)(2,1)}, bf16[3,4,64,640]{3,2,0,1:T(8,128)(2,1)}, u32[]{:S(2)}, u32[]{:S(2)}) collective-permute-start(bf16[3,4,64,640]{3,2,0,1:T(8,128)(2,1)} %get-tuple-element.144), channel_id=1, source_target_pairs={{0,2},{1,3},{2,0},{3,1},{4,6},{5,7},{6,4},{7,5},{8,10},{9,11},{10,... | collective-permute-start | bytes 2949128 | tf_op jit(solution)/shard_map/ppermute | solution.py:158
  325.8 18.3 %copy-start.2 = (bf16[2,64,2048]{2,1,0:T(8,128)(2,1)S(1)}, bf16[2,64,2048]{2,1,0:T(8,128)(2,1)}, u32[]{:S(2)}) copy-start(bf16[2,64,2048]{2,1,0:T(8,128)(2,1)} %param.17) | copy-start | bytes 1572868
  345.3 7.4 %copy-start.18 = (bf16[3,4,64,640]{3,2,0,1:T(8,128)(2,1)S(1)}, bf16[3,4,64,640]{3,2,0,1:T(8,128)(2,1)}, u32[]{:S(2)}) copy-start(bf16[3,4,64,640]{3,2,0,1:T(8,128)(2,1)} %get-tuple-element.94) | copy-start | bytes 2949124
  345.3 28.4 %copy-start.11 = (bf16[3,4,64,640]{3,2,0,1:T(8,128)(2,1)S(1)}, bf16[3,4,64,640]{3,2,0,1:T(8,128)(2,1)}, u32[]{:S(2)}) copy-start(bf16[3,4,64,640]{3,2,0,1:T(8,128)(2,1)} %get-tuple-element.89) | copy-start | bytes 2949124
  347.2 43.9 %copy-start.10 = (bf16[3,4,64,640]{3,2,0,1:T(8,128)(2,1)S(1)}, bf16[3,4,64,640]{3,2,0,1:T(8,128)(2,1)}, u32[]{:S(2)}) copy-start(bf16[3,4,64,640]{3,2,0,1:T(8,128)(2,1)} %get-tuple-element.93) | copy-start | bytes 2949124
  347.2 24.8 %collective-permute-start.11 = (bf16[3,4,64,640]{3,2,0,1:T(8,128)(2,1)S(1)}, bf16[3,4,64,640]{3,2,0,1:T(8,128)(2,1)S(1)}, u32[]{:S(2)}, u32[]{:S(2)}) collective-permute-start(bf16[3,4,64,640]{3,2,0,1:T(8,128)(2,1)S(1)} %add_convert_fusion.4), channel_id=1, source_target_pairs={{0,2},{1,3},{2,0},{3,1},{4,6},{5,7},{6,4},{7,5},{8,10},{9,11},{10,... | collective-permute-start | bytes 2949128 | tf_op jit(solution)/shard_map/ppermute | solution.py:158
  348.8 24.9 %collective-permute-start.10 = (bf16[3,4,64,640]{3,2,0,1:T(8,128)(2,1)}, bf16[3,4,64,640]{3,2,0,1:T(8,128)(2,1)S(1)}, u32[]{:S(2)}, u32[]{:S(2)}) collective-permute-start(bf16[3,4,64,640]{3,2,0,1:T(8,128)(2,1)} %get-tuple-element.90), channel_id=1, source_target_pairs={{0,1},{1,0},{2,3},{3,2},{4,5},{5,4},{6,7},{7,6},{8,9},{9,8},{10,11... | collective-permute-start | bytes 2949128 | tf_op jit(solution)/shard_map/ppermute | solution.py:158
  352.1 39.0 %collective-permute-start.13 = (bf16[3,4,64,640]{3,2,0,1:T(8,128)(2,1)S(1)}, bf16[3,4,64,640]{3,2,0,1:T(8,128)(2,1)S(1)}, u32[]{:S(2)}, u32[]{:S(2)}) collective-permute-start(bf16[3,4,64,640]{3,2,0,1:T(8,128)(2,1)S(1)} %add_convert_fusion.2), channel_id=1, source_target_pairs={{0,1},{1,0},{2,3},{3,2},{4,5},{5,4},{6,7},{7,6},{8,9},{9,8},{10,11... | collective-permute-start | bytes 2949128 | tf_op jit(solution)/shard_map/ppermute | solution.py:158
  352.7 38.4 %collective-permute-start.12 = (bf16[3,4,64,640]{3,2,0,1:T(8,128)(2,1)S(1)}, bf16[3,4,64,640]{3,2,0,1:T(8,128)(2,1)S(1)}, u32[]{:S(2)}, u32[]{:S(2)}) collective-permute-start(bf16[3,4,64,640]{3,2,0,1:T(8,128)(2,1)S(1)} %copy-done.18), channel_id=1, source_target_pairs={{0,2},{1,3},{2,0},{3,1},{4,6},{5,7},{6,4},{7,5},{8,10},{9,11},{10,... | collective-permute-start | bytes 2949128 | tf_op jit(solution)/shard_map/ppermute | solution.py:158
  393.0 50.6 %all-to-all-start.2 = ((bf16[8,3,64,640]{3,2,1,0:T(8,128)(2,1)}), bf16[8,3,64,640]{3,2,1,0:T(8,128)(2,1)}, u32[]{:S(2)}, u32[]{:S(2)}) async-start(bf16[8,3,64,640]{3,2,1,0:T(8,128)(2,1)} %bitcast.200), calls=%async_computation.4 | async-start | bytes 3932160 | tf_op jit(solution)/shard_map/all_to_all | solution.py:438
  397.4 121.7 %reduce-scatter.9.cloned.1.call-start = ((), (), s32[]{:S(2)}) async-start(), calls=%async_computation.10 | async-start | bytes 4718592 | tf_op jit(solution)/shard_map/reduce_scatter | solution.py:470
  401.9 15.7 %copy-start.8 = (bf16[1,8,4,64,256]{4,3,2,1,0:T(8,128)(2,1)S(1)}, bf16[1,8,4,64,256]{4,3,2,1,0:T(8,128)(2,1)}, u32[]{:S(2)}) copy-start(bf16[1,8,4,64,256]{4,3,2,1,0:T(8,128)(2,1)} %get-tuple-element.142) | copy-start | bytes 3145732
  443.6 115.4 %reduce-scatter.11.cloned.1.call-start = ((), (), s32[]{:S(2)}) async-start(), calls=%async_computation.11 | async-start | bytes 4718592 | tf_op jit(solution)/shard_map/reduce_scatter | solution.py:470
  454.4 14.9 %collective-permute-start.18 = (bf16[4,4,64,256]{3,2,0,1:T(8,128)(2,1)S(1)}, bf16[4,4,64,256]{3,2,0,1:T(8,128)(2,1)S(1)}, u32[]{:S(2)}, u32[]{:S(2)}) collective-permute-start(bf16[4,4,64,256]{3,2,0,1:T(8,128)(2,1)S(1)} %get-tuple-element.155), channel_id=1, source_target_pairs={{0,2},{1,3},{2,0},{3,1},{4,6},{5,7},{6,4},{7,5},{8,10},{9,11},{10,... | collective-permute-start | bytes 1572872 | tf_op jit(solution)/shard_map/ppermute | solution.py:158
  454.7 16.1 %collective-permute-start.15 = (bf16[4,4,64,256]{3,2,0,1:T(8,128)(2,1)S(1)}, bf16[4,4,64,256]{3,2,0,1:T(8,128)(2,1)S(1)}, u32[]{:S(2)}, u32[]{:S(2)}) collective-permute-start(bf16[4,4,64,256]{3,2,0,1:T(8,128)(2,1)S(1)} %get-tuple-element.154), channel_id=1, source_target_pairs={{0,1},{1,0},{2,3},{3,2},{4,5},{5,4},{6,7},{7,6},{8,9},{9,8},{10,11... | collective-permute-start | bytes 1572872 | tf_op jit(solution)/shard_map/ppermute | solution.py:158
  456.4 24.4 %collective-permute-start.14 = (bf16[4,4,64,256]{3,2,0,1:T(8,128)(2,1)S(1)}, bf16[4,4,64,256]{3,2,0,1:T(8,128)(2,1)S(1)}, u32[]{:S(2)}, u32[]{:S(2)}) collective-permute-start(bf16[4,4,64,256]{3,2,0,1:T(8,128)(2,1)S(1)} %slice.154), channel_id=1, source_target_pairs={{0,1},{1,0},{2,3},{3,2},{4,5},{5,4},{6,7},{7,6},{8,9},{9,8},{10,11... | collective-permute-start | bytes 1572872 | tf_op jit(solution)/shard_map/ppermute | solution.py:158
  457.1 23.8 %collective-permute-start.17 = (bf16[4,4,64,256]{3,2,0,1:T(8,128)(2,1)S(1)}, bf16[4,4,64,256]{3,2,0,1:T(8,128)(2,1)S(1)}, u32[]{:S(2)}, u32[]{:S(2)}) collective-permute-start(bf16[4,4,64,256]{3,2,0,1:T(8,128)(2,1)S(1)} %slice.158), channel_id=1, source_target_pairs={{0,2},{1,3},{2,0},{3,1},{4,6},{5,7},{6,4},{7,5},{8,10},{9,11},{10,... | collective-permute-start | bytes 1572872 | tf_op jit(solution)/shard_map/ppermute | solution.py:158
  469.5 20.9 %collective-permute-start.19 = (bf16[4,4,64,256]{3,2,0,1:T(8,128)(2,1)S(1)}, bf16[4,4,64,256]{3,2,0,1:T(8,128)(2,1)S(1)}, u32[]{:S(2)}, u32[]{:S(2)}) collective-permute-start(bf16[4,4,64,256]{3,2,0,1:T(8,128)(2,1)S(1)} %add_convert_fusion.6), channel_id=1, source_target_pairs={{0,1},{1,0},{2,3},{3,2},{4,5},{5,4},{6,7},{7,6},{8,9},{9,8},{10,11... | collective-permute-start | bytes 1572872 | tf_op jit(solution)/shard_map/ppermute | solution.py:158
  471.0 19.3 %collective-permute-start.16 = (bf16[4,4,64,256]{3,2,0,1:T(8,128)(2,1)S(1)}, bf16[4,4,64,256]{3,2,0,1:T(8,128)(2,1)S(1)}, u32[]{:S(2)}, u32[]{:S(2)}) collective-permute-start(bf16[4,4,64,256]{3,2,0,1:T(8,128)(2,1)S(1)} %add_convert_fusion.8), channel_id=1, source_target_pairs={{0,2},{1,3},{2,0},{3,1},{4,6},{5,7},{6,4},{7,5},{8,10},{9,11},{10,... | collective-permute-start | bytes 1572872 | tf_op jit(solution)/shard_map/ppermute | solution.py:158
  492.0 47.5 %all-to-all-start.3 = ((bf16[8,4,64,256]{3,2,1,0:T(8,128)(2,1)}), bf16[8,4,64,256]{3,2,1,0:T(8,128)(2,1)}, u32[]{:S(2)}, u32[]{:S(2)}) async-start(bf16[8,4,64,256]{3,2,1,0:T(8,128)(2,1)} %maximum_bitcast_fusion), calls=%async_computation.7 | async-start | bytes 2097152 | tf_op jit(solution)/shard_map/all_to_all | solution.py:438
  507.7 11.4 %copy-start.1 = (bf16[2,64,2048]{2,1,0:T(8,128)(2,1)S(1)}, bf16[2,64,2048]{2,1,0:T(8,128)(2,1)}, u32[]{:S(2)}) copy-start(bf16[2,64,2048]{2,1,0:T(8,128)(2,1)} %param.15) | copy-start | bytes 1572868
  507.7 11.4 %copy-start.25 = (f32[1,2048]{1,0:T(1,128)S(1)}, f32[1,2048]{1,0:T(1,128)}, u32[]{:S(2)}) copy-start(f32[1,2048]{1,0:T(1,128)} %copy-done.24) | copy-start | bytes 24580
  507.7 11.4 %copy-start.36 = (f32[2,64]{1,0:T(2,128)S(1)}, f32[2,64]{1,0:T(2,128)}, u32[]{:S(2)}) copy-start(f32[2,64]{1,0:T(2,128)} %copy-done.35) | copy-start | bytes 1540
  520.6 1.4 collective-permute-start.20
  522.0 9.4 %collective-permute-start.21 = (f32[40,128]{1,0:T(8,128)S(1)}, f32[40,128]{1,0:T(8,128)S(1)}, u32[]{:S(2)}, u32[]{:S(2)}) collective-permute-start(f32[40,128]{1,0:T(8,128)S(1)} %bitcast_add_fusion), channel_id=1, source_target_pairs={{0,8},{4,12},{8,0},{12,4},{16,24},{20,28},{24,16},{28,20},{1,9},{5... | collective-permute-start | bytes 61448 | tf_op jit(solution)/shard_map/ppermute | solution.py:158
  531.4 16.9 %collective-permute-start.22 = (f32[40,128]{1,0:T(8,128)S(1)}, f32[40,128]{1,0:T(8,128)S(1)}, u32[]{:S(2)}, u32[]{:S(2)}) collective-permute-start(f32[40,128]{1,0:T(8,128)S(1)} %fusion.87), channel_id=1, source_target_pairs={{0,16},{4,20},{8,24},{12,28},{16,0},{20,4},{24,8},{28,12},{1,17},{... | collective-permute-start | bytes 61448 | tf_op jit(solution)/shard_map/ppermute | solution.py:158
  548.2 13.6 %copy-start.27 = (f32[2,2048]{1,0:T(2,128)S(1)}, f32[2,2048]{1,0:T(2,128)}, u32[]{:S(2)}) copy-start(f32[2,2048]{1,0:T(2,128)} %param.24) | copy-start | bytes 49156
  548.3 13.6 %copy-start.29 = (f32[2,2048]{1,0:T(2,128)S(1)}, f32[2,2048]{1,0:T(2,128)}, u32[]{:S(2)}) copy-start(f32[2,2048]{1,0:T(2,128)} %param.25) | copy-start | bytes 49156
  548.3 13.6 %copy-start.30 = (f32[2,2048]{1,0:T(2,128)S(1)}, f32[2,2048]{1,0:T(2,128)}, u32[]{:S(2)}) copy-start(f32[2,2048]{1,0:T(2,128)} %param.26) | copy-start | bytes 49156
  548.3 14.3 %copy-start.32 = (f32[32,32]{1,0:T(8,128)S(1)}, f32[32,32]{1,0:T(8,128)}, u32[]{:S(2)}) copy-start(f32[32,32]{1,0:T(8,128)} %param.27) | copy-start | bytes 12292
  548.3 14.3 %copy-start.33 = (f32[32,32]{1,0:T(8,128)S(1)}, f32[32,32]{1,0:T(8,128)}, u32[]{:S(2)}) copy-start(f32[32,32]{1,0:T(8,128)} %param.28) | copy-start | bytes 12292
  548.3 14.3 %copy-start.34 = (f32[32,32]{1,0:T(8,128)S(1)}, f32[32,32]{1,0:T(8,128)}, u32[]{:S(2)}) copy-start(f32[32,32]{1,0:T(8,128)} %param.29) | copy-start | bytes 12292
  548.3 3.8 collective-permute-start.23
  552.2 9.6 %collective-permute-start.24 = (f32[40,128]{1,0:T(8,128)S(1)}, f32[40,128]{1,0:T(8,128)S(1)}, u32[]{:S(2)}, u32[]{:S(2)}) collective-permute-start(f32[40,128]{1,0:T(8,128)S(1)} %add.255), channel_id=1, source_target_pairs={{0,2},{1,3},{2,0},{3,1},{4,6},{5,7},{6,4},{7,5},{8,10},{9,11},{10,... | collective-permute-start | bytes 61448 | tf_op jit(solution)/shard_map/ppermute | solution.py:158
  (19 other events, 45.7 us)
Sparse Core Ops, SparseCore 0:
  44.8 46.0 all-gather.8
  92.4 80.7 all-gather.10
  178.9 48.6 reduce-scatter.4
  230.1 45.2 all-gather.12
  293.9 48.7 reduce-scatter.6
  345.4 45.2 all-gather.14
  443.8 47.9 reduce-scatter.8
  494.0 65.0 reduce-scatter.10
